TPU v7x, 32 devices: a whole 2x2x4 slice. The times are simulated.
32 devices in a mesh: section: 2 (over core), dp: 4 (over z), tensor: 4 (over y, x).
Axes of the slice: x: 2, y: 2, z: 4, core: 2. Of those that a mesh axis runs over, the one named last changes fastest.
Arguments:
- ends_in: bfloat16 [2, 2, 8, 2048, 1024], P('section', None, 'dp', 'tensor'), may hold values from -6 to 6
- lengths: int32 [2, 8], P(None, 'dp'), may hold values from 32 to 2048, as said below
- ln_gains: float32 [2, 2, 1024], P('section'), may hold values from 0.5 to 1.5
- ln_biases: float32 [2, 2, 1024], P('section'), may hold values from -1.5 to 1.5
- w_qkv: bfloat16 [2, 3, 1024, 1024], P('section', None, None, 'tensor'), may hold values from -0.1875 to 0.1875
- qv_bias: float32 [2, 2, 1024], P('section', None, 'tensor'), may hold values from -1.5 to 1.5
- w_out: bfloat16 [2, 1024, 1024], P('section', 'tensor'), may hold values from -0.75 to 0.75
- w_up: bfloat16 [2, 1024, 4096], P('section', None, 'tensor'), may hold values from -0.1875 to 0.1875
- up_bias: float32 [2, 4096], P('section', 'tensor'), may hold values from -1.5 to 1.5
- w_down: bfloat16 [2, 4096, 1024], P('section', 'tensor'), may hold values from -0.09375 to 0.09375
- out_biases: float32 [2, 2, 1024], P('section'), may hold values from -1.5 to 1.5
Outputs:
- ends_out: float32 [2, 2, 8, 2048, 1024], P('section', None, 'dp', 'tensor')
- grad_ln_gains: float32 [2, 2, 1024], P('section')
- grad_ln_biases: float32 [2, 2, 1024], P('section')
- grad_qkv: float32 [2, 3, 1024, 1024], P('section', None, None, 'tensor')
- grad_qv_bias: float32 [2, 2, 1024], P('section', None, 'tensor')
- grad_out: float32 [2, 1024, 1024], P('section', 'tensor')
- grad_up: float32 [2, 1024, 4096], P('section', None, 'tensor')
- grad_up_bias: float32 [2, 4096], P('section', 'tensor')
- grad_down: float32 [2, 4096, 1024], P('section', 'tensor')
- grad_out_biases: float32 [2, 2, 1024], P('section')
Inputs may be any that keep to these rules, and one draw needn't show every extreme that they name: `lengths`: in every micro-batch each aligned block of 2 rows (the rows of one index of dp) holds one row of length 2048.
All inputs are finite; a program needn't handle non-finite values.
Results may differ from a plain program's by a relative error of at most 0.017.
Values may be sent and summed in bfloat16 or wider, within the bound.
No kernel may reach another device: no remote copies, remote signals or barrier semaphores. Data moves between devices by JAX's collectives and lax.ppermute only.
A program may use at most 512 MiB of HBM per device.

v0:
```python
from functools import partial

import jax
import jax.numpy as jnp
from jax import lax
from jax.sharding import PartitionSpec as P

D = 1024
HEADS = 16


eps = 1e-05
widest = 512


def shifted(shard, axis, by):
    devices = lax.axis_size(axis)
    pairs = [(i, i + by) for i in range(devices) if 0 <= i + by < devices]
    return lax.ppermute(shard, axis, pairs)


def layer_norm(inputs, gain, bias):
    center = jnp.mean(inputs, axis=-1, keepdims=True)
    centred = inputs - center
    spread = jnp.mean(centred * centred, axis=-1, keepdims=True)
    factor = lax.rsqrt(spread + eps)
    normal = centred * factor
    return (normal * gain + bias, normal, factor)


def norm_back(grad_norm, normal, factor, gain):
    scaled = grad_norm * gain
    first_mean = jnp.mean(scaled, axis=-1, keepdims=True)
    second_mean = jnp.mean(scaled * normal, axis=-1, keepdims=True)
    return factor * (scaled - first_mean - normal * second_mean)


def gather_tokens(values):
    return lax.all_gather(values, "tensor", axis=1, tiled=True)


def scatter_tokens(values):
    return lax.psum_scatter(values, "tensor", scatter_dimension=1, tiled=True)


def gather_grads(values):
    return lax.all_gather(values, "tensor", axis=1, tiled=True)


def scatter_grads(values):
    return lax.psum_scatter(
        values.astype(jnp.bfloat16), "tensor", scatter_dimension=1, tiled=True
    ).astype(jnp.float32)


def project(whole_rows, w_proj, proj_bias):
    combined = jnp.einsum("rld,cde->crle", whole_rows, w_proj, preferred_element_type=jnp.float32)
    queries = (combined[0] + proj_bias[0]).astype(jnp.bfloat16)
    key_rows = combined[1].astype(jnp.bfloat16)
    value_rows = (combined[2] + proj_bias[1]).astype(jnp.bfloat16)
    return (queries, key_rows, value_rows)


def score_block(query_block, key_heads, row_start, row_lengths, slopes_here):
    block_rows = query_block.shape[1]
    seq_len = key_heads.shape[1]
    head_size = key_heads.shape[-1]
    scores = jnp.einsum(
        "rqhd,rkhd->rhqk", query_block, key_heads, preferred_element_type=jnp.float32
    ) * head_size ** (-0.5)
    rowpos = row_start + jnp.arange(block_rows)
    keypos = jnp.arange(seq_len)
    distance = (rowpos[:, None] - keypos[None, :]).astype(jnp.float32)
    scores = scores - slopes_here[None, :, None, None] * distance[None, None]
    causal = keypos[None, :] <= rowpos[:, None]
    inside = keypos[None, :] < row_lengths[:, None]
    allowed = causal[None, None] & inside[:, None, None, :]
    return jnp.where(allowed, scores, -1e30)


def attention(queries, key_rows, value_rows, row_lengths, slopes_here):
    row_count, seq_len, width = queries.shape
    head_count = slopes_here.shape[0]
    head_size = width // head_count
    block_rows = min(widest, seq_len)
    query_heads = queries.reshape(row_count, seq_len, head_count, head_size)
    key_heads = key_rows.reshape(row_count, seq_len, head_count, head_size)
    value_heads = value_rows.reshape(row_count, seq_len, head_count, head_size)

    def one_block(row_start):
        query_block = lax.dynamic_slice_in_dim(query_heads, row_start, block_rows, 1)
        scores = score_block(query_block, key_heads, row_start, row_lengths, slopes_here)
        row_max = jnp.max(scores, axis=-1, keepdims=True)
        powers = jnp.exp(scores - row_max)
        row_total = jnp.sum(powers, axis=-1, keepdims=True)
        probs = (powers / row_total).astype(jnp.bfloat16)
        block_out = jnp.einsum(
            "rhqk,rkhd->rqhd", probs, value_heads, preferred_element_type=jnp.float32
        )
        return (block_out.astype(jnp.bfloat16), (row_max + jnp.log(row_total))[..., 0])

    starts = jnp.arange(seq_len // block_rows) * block_rows
    blocks_out, log_totals = lax.map(one_block, starts)
    attended = jnp.moveaxis(blocks_out, 0, 1).reshape(row_count, seq_len, width)
    log_totals = jnp.moveaxis(log_totals, 0, 2).reshape(row_count, head_count, seq_len)
    return (attended, log_totals)


def attention_back(
    queries, key_rows, value_rows, grad_attended, log_totals, row_lengths, slopes_here
):
    row_count, seq_len, width = queries.shape
    head_count = slopes_here.shape[0]
    head_size = width // head_count
    scale = head_size ** (-0.5)
    block_rows = min(widest, seq_len)
    query_heads = queries.reshape(row_count, seq_len, head_count, head_size)
    key_heads = key_rows.reshape(row_count, seq_len, head_count, head_size)
    value_heads = value_rows.reshape(row_count, seq_len, head_count, head_size)
    grad_heads = grad_attended.reshape(row_count, seq_len, head_count, head_size)

    def one_block(carry, row_start):
        grad_keys, grad_values = carry
        query_block = lax.dynamic_slice_in_dim(query_heads, row_start, block_rows, 1)
        grad_block = lax.dynamic_slice_in_dim(grad_heads, row_start, block_rows, 1)
        scores = score_block(query_block, key_heads, row_start, row_lengths, slopes_here)
        block_logs = lax.dynamic_slice_in_dim(log_totals, row_start, block_rows, 2)
        probs = jnp.exp(scores - block_logs[..., None])
        grad_values = grad_values + jnp.einsum(
            "rhqk,rqhd->rkhd",
            probs.astype(jnp.bfloat16),
            grad_block,
            preferred_element_type=jnp.float32,
        )
        grad_probs = jnp.einsum(
            "rqhd,rkhd->rhqk", grad_block, value_heads, preferred_element_type=jnp.float32
        )
        inner = jnp.sum(probs * grad_probs, axis=-1, keepdims=True)
        grad_scores = (probs * (grad_probs - inner)).astype(jnp.bfloat16)
        grad_query = (
            jnp.einsum(
                "rhqk,rkhd->rqhd", grad_scores, key_heads, preferred_element_type=jnp.float32
            )
            * scale
        )
        grad_keys = (
            grad_keys
            + jnp.einsum(
                "rhqk,rqhd->rkhd", grad_scores, query_block, preferred_element_type=jnp.float32
            )
            * scale
        )
        return ((grad_keys, grad_values), grad_query.astype(jnp.bfloat16))

    zeros_heads = jnp.zeros((row_count, seq_len, head_count, head_size), jnp.float32)
    starts = jnp.arange(seq_len // block_rows) * block_rows
    (grad_keys, grad_values), grad_queries = lax.scan(one_block, (zeros_heads, zeros_heads), starts)
    grad_queries = jnp.moveaxis(grad_queries, 0, 1).reshape(row_count, seq_len, width)
    grad_keys = grad_keys.reshape(row_count, seq_len, width).astype(jnp.bfloat16)
    grad_values = grad_values.reshape(row_count, seq_len, width).astype(jnp.bfloat16)
    return (grad_queries, grad_keys, grad_values)


def layer_forward(inputs, row_lengths, weights, slopes_here):
    gains, biases, w_proj, proj_bias, w_attn, w_first, first_bias, w_second, end_biases = weights
    normed, _, _ = layer_norm(inputs, gains[0], biases[0])
    whole_rows = gather_tokens(normed.astype(jnp.bfloat16))
    queries, key_rows, value_rows = project(whole_rows, w_proj, proj_bias)
    attended, log_totals = attention(queries, key_rows, value_rows, row_lengths, slopes_here)
    attn_part = jnp.dot(attended, w_attn, preferred_element_type=jnp.float32)
    after_attn = inputs + scatter_tokens(attn_part) + end_biases[0]
    middle, _, _ = layer_norm(after_attn, gains[1], biases[1])
    middle_rows = gather_tokens(middle.astype(jnp.bfloat16))
    pre_act = jnp.dot(middle_rows, w_first, preferred_element_type=jnp.float32) + first_bias
    hidden = jax.nn.gelu(pre_act, approximate=True).astype(jnp.bfloat16)
    ffn_part = jnp.dot(hidden, w_second, preferred_element_type=jnp.float32)
    result = after_attn + scatter_tokens(ffn_part) + end_biases[1]
    return (result, after_attn, attended, log_totals, whole_rows, middle_rows)


def layer_backward(grad_result, stored, row_lengths, weights, slopes_here):
    gains, biases, w_proj, proj_bias, w_attn, w_first, first_bias, w_second, end_biases = weights
    inputs = stored[0].astype(jnp.float32)
    after_attn = stored[1]
    attended = stored[2]
    log_totals = stored[3]
    normed, normal_one, factor_one = layer_norm(inputs, gains[0], biases[0])
    middle, normal_two, factor_two = layer_norm(after_attn, gains[1], biases[1])
    whole_rows = gather_tokens(normed.astype(jnp.bfloat16))
    middle_rows = gather_tokens(middle.astype(jnp.bfloat16))
    pre_act = jnp.dot(middle_rows, w_first, preferred_element_type=jnp.float32) + first_bias
    hidden, gelu_pull = jax.vjp(partial(jax.nn.gelu, approximate=True), pre_act)
    hidden = hidden.astype(jnp.bfloat16)
    grad_end_two = jnp.sum(grad_result, axis=(0, 1))
    grad_branch = gather_grads(grad_result.astype(jnp.bfloat16))
    grad_second = jnp.einsum("rlf,rld->fd", hidden, grad_branch, preferred_element_type=jnp.float32)
    grad_hidden = jnp.einsum(
        "rld,fd->rlf", grad_branch, w_second, preferred_element_type=jnp.float32
    )
    grad_pre = gelu_pull(grad_hidden)[0].astype(jnp.bfloat16)
    grad_first_bias = jnp.sum(grad_pre, axis=(0, 1), dtype=jnp.float32)
    grad_first = jnp.einsum(
        "rld,rlf->df", middle_rows, grad_pre, preferred_element_type=jnp.float32
    )
    grad_middle = scatter_grads(
        jnp.einsum("rlf,df->rld", grad_pre, w_first, preferred_element_type=jnp.float32)
    )
    grad_gain_two = jnp.sum(grad_middle * normal_two, axis=(0, 1))
    grad_bias_two = jnp.sum(grad_middle, axis=(0, 1))
    grad_after = grad_result + norm_back(grad_middle, normal_two, factor_two, gains[1])
    grad_end_one = jnp.sum(grad_after, axis=(0, 1))
    grad_attn_rows = gather_grads(grad_after.astype(jnp.bfloat16))
    grad_attn = jnp.einsum(
        "rle,rld->ed", attended, grad_attn_rows, preferred_element_type=jnp.float32
    )
    grad_attended = jnp.einsum(
        "rld,ed->rle", grad_attn_rows, w_attn, preferred_element_type=jnp.float32
    ).astype(jnp.bfloat16)
    queries, key_rows, value_rows = project(whole_rows, w_proj, proj_bias)
    grad_queries, grad_keys, grad_values = attention_back(
        queries, key_rows, value_rows, grad_attended, log_totals, row_lengths, slopes_here
    )
    stacked = jnp.stack([grad_queries, grad_keys, grad_values])
    grad_proj = jnp.einsum("rld,crle->cde", whole_rows, stacked, preferred_element_type=jnp.float32)
    grad_proj_bias = jnp.stack(
        [
            jnp.sum(grad_queries, axis=(0, 1), dtype=jnp.float32),
            jnp.sum(grad_values, axis=(0, 1), dtype=jnp.float32),
        ]
    )
    grad_normed = scatter_grads(
        jnp.einsum("crle,cde->rld", stacked, w_proj, preferred_element_type=jnp.float32)
    )
    grad_gain_one = jnp.sum(grad_normed * normal_one, axis=(0, 1))
    grad_bias_one = jnp.sum(grad_normed, axis=(0, 1))
    grad_inputs = grad_after + norm_back(grad_normed, normal_one, factor_one, gains[0])
    sharded = (grad_proj, grad_proj_bias, grad_attn, grad_first, grad_first_bias, grad_second)
    shared = (
        jnp.stack([grad_gain_one, grad_gain_two]),
        jnp.stack([grad_bias_one, grad_bias_two]),
        jnp.stack([grad_end_one, grad_end_two]),
    )
    return (grad_inputs, sharded, shared)


def on_device(
    ends_in, lengths, ln_gains, ln_biases, w_qkv, qv_bias, w_out, w_up, up_bias, w_down, out_biases
):
    section_index = lax.axis_index("section")
    weights = tuple(
        (
            stored[0]
            for stored in (
                ln_gains,
                ln_biases,
                w_qkv,
                qv_bias,
                w_out,
                w_up,
                up_bias,
                w_down,
                out_biases,
            )
        )
    )
    local_ends = ends_in[0]
    micro_count = local_ends.shape[0]
    heads_here = w_qkv.shape[-1] // (D // HEADS)
    first_head = lax.axis_index("tensor") * heads_here
    slopes_here = jnp.exp2(
        -8.0 * (first_head + jnp.arange(heads_here) + 1).astype(jnp.float32) / HEADS
    )
    padded = jnp.concatenate([local_ends, jnp.zeros_like(local_ends[:1])], axis=0)
    tick_list = jnp.arange(micro_count + 1)

    def forward_tick(received, item):
        arriving, tick_index = item
        entering = jnp.where(section_index == 0, arriving, received)
        slot_index = jnp.clip(tick_index - section_index, 0, micro_count - 1)
        row_lengths = lax.dynamic_index_in_dim(lengths, slot_index, 0, keepdims=False)
        result, after_attn, attended, log_totals, whole_rows, middle_rows = layer_forward(
            entering.astype(jnp.float32), row_lengths, weights, slopes_here
        )
        outgoing = shifted(result.astype(jnp.bfloat16), "section", 1)
        stored = (entering, after_attn, attended, log_totals)
        return (outgoing, (result, stored))

    _, (results, kept_all) = lax.scan(
        forward_tick, jnp.zeros_like(local_ends[0]), (padded, tick_list)
    )
    sharded_zero = (
        jnp.zeros(w_qkv.shape[1:], jnp.float32),
        jnp.zeros(qv_bias.shape[1:], jnp.float32),
        jnp.zeros(w_out.shape[1:], jnp.float32),
        jnp.zeros(w_up.shape[1:], jnp.float32),
        jnp.zeros(up_bias.shape[1:], jnp.float32),
        jnp.zeros(w_down.shape[1:], jnp.float32),
    )
    shared_zero = (
        jnp.zeros(ln_gains.shape[1:], jnp.float32),
        jnp.zeros(ln_biases.shape[1:], jnp.float32),
        jnp.zeros(out_biases.shape[1:], jnp.float32),
    )

    def backward_tick(carry, item):
        received, sharded_total, shared_total = carry
        arriving, tick_index = item
        grad_result = jnp.where(section_index == 1, arriving, received).astype(jnp.float32)
        slot_index = tick_index - 1 + section_index
        is_valid = ((slot_index >= 0) & (slot_index < micro_count)).astype(jnp.float32)
        slot_index = jnp.clip(slot_index, 0, micro_count - 1)
        stored = tuple(
            (
                lax.dynamic_index_in_dim(kept, slot_index + section_index, 0, keepdims=False)
                for kept in kept_all
            )
        )
        row_lengths = lax.dynamic_index_in_dim(lengths, slot_index, 0, keepdims=False)
        grad_inputs, sharded, shared = layer_backward(
            grad_result, stored, row_lengths, weights, slopes_here
        )
        outgoing = shifted(grad_inputs.astype(jnp.bfloat16), "section", -1)
        sharded = tuple((value * is_valid for value in sharded))
        shared = tuple((value * is_valid for value in shared))
        sharded_total = tuple((left + right for left, right in zip(sharded_total, sharded)))
        shared_total = tuple((left + right for left, right in zip(shared_total, shared)))
        return ((outgoing, sharded_total, shared_total), grad_inputs)

    start_carry = (jnp.zeros_like(local_ends[0]), sharded_zero, shared_zero)
    (_, sharded_total, shared_total), grads_in = lax.scan(
        backward_tick, start_carry, (padded, tick_list)
    )
    sharded_total = (
        lax.psum(sharded_total[0].astype(jnp.bfloat16), "dp").astype(jnp.float32),
        lax.psum(sharded_total[1].astype(jnp.bfloat16), "dp").astype(jnp.float32),
        lax.psum(sharded_total[2].astype(jnp.bfloat16), "dp").astype(jnp.float32),
        lax.psum(sharded_total[3].astype(jnp.bfloat16), "dp").astype(jnp.float32),
        lax.psum(sharded_total[4].astype(jnp.bfloat16), "dp").astype(jnp.float32),
        lax.psum(sharded_total[5].astype(jnp.bfloat16), "dp").astype(jnp.float32),
    )
    shared_total = lax.psum((shared_total[0], shared_total[1], shared_total[2]), ("dp", "tensor"))
    ends_local = jnp.where(section_index == 0, grads_in[1:], results[1:])
    return (
        ends_local[None],
        shared_total[0][None],
        shared_total[1][None],
        sharded_total[0][None],
        sharded_total[1][None],
        sharded_total[2][None],
        sharded_total[3][None],
        sharded_total[4][None],
        sharded_total[5][None],
        shared_total[2][None],
    )


def solution(mesh):
    return jax.shard_map(
        on_device,
        mesh=mesh,
        in_specs=(
            P("section", None, "dp", "tensor", None),
            P(None, "dp"),
            P("section", None, None),
            P("section", None, None),
            P("section", None, None, "tensor"),
            P("section", None, "tensor"),
            P("section", "tensor", None),
            P("section", None, "tensor"),
            P("section", "tensor"),
            P("section", "tensor", None),
            P("section", None, None),
        ),
        out_specs=(
            P("section", None, "dp", "tensor", None),
            P("section", None, None),
            P("section", None, None),
            P("section", None, None, "tensor"),
            P("section", None, "tensor"),
            P("section", "tensor", None),
            P("section", None, "tensor"),
            P("section", "tensor"),
            P("section", "tensor", None),
            P("section", None, None),
        ),
        check_vma=False,
    )
```

profile of v0, /device:TPU:0, one launch (start us, length us, event | category | flops | bytes accessed | tf_op | source)
XLA Modules:
  0.0 6350.9 jit_solution(14176301926737137506)
XLA Ops:
  29.2 2650.9 %while.104 = (s32[]{:T(128)}, bf16[2,512,1024]{2,1,0:T(8,128)(2,1)}, f32[3,2,512,1024]{3,2,1,0:T(8,128)}, bf16[3,2,512,1024]{3,2,1,0:T(8,128)(2,1)}, f32[3,2,512...) while((s32[]{:T(128)}, bf16[2,512,1024]{2,1,0:T(8,128)(2,1)}, ...), condition=%wide.region_11.12_spmd.clone, body=%wide.region_0.11_spmd.clone.sunk | while | flops 28130414592 | bytes 729597696 | solution.py:288
  41.2 87.6 %all-gather.7.cloned.1.call-done = bf16[2,2048,1024]{2,1,0:T(8,128)(2,1)} async-done(((bf16[2,512,1024]{2,1,0:T(8,128)(2,1)}), bf16[2,2048,1024]{2,1,0:T(8,128)(2,1)}) %all-gather.7.cloned.1.call-update) | async-done | bytes 8388624 | tf_op jit(solution)/shard_map/while/body/eval_jaxpr/all_gather | solution.py:39
  150.8 288.3 %while.107 = (s32[]{:T(128)}, bf16[4,2,512,4,64]{2,4,3,1,0:T(8,128)(2,1)}, f32[4,2,4,512]{3,2,1,0:T(4,128)S(1)}, s32[4]{0:T(128)S(1)}, s32[2]{0:T(128)S(1)}, /*i...) while((s32[]{:T(128)}, ...), condition=%wide.region_6.6_spmd, body=%wide.region_3.5_spmd.sunk | while | flops 2283012608 | bytes 200423664 | solution.py:103
  455.9 153.3 %reduce-scatter.5.cloned.1.call-done = f32[2,512,1024]{2,1,0:T(8,128)} async-done(((f32[2,2048,1024]{2,1,0:T(8,128)}), f32[2,512,1024]{2,1,0:T(8,128)}) %reduce-scatter.5.cloned.1.call-update) | async-done | bytes 4194320 | tf_op jit(solution)/shard_map/while/body/eval_jaxpr/reduce_scatter | solution.py:43
  624.3 87.7 %all-gather.9.cloned.1.call-done = bf16[2,2048,1024]{2,1,0:T(8,128)(2,1)} async-done(((bf16[2,512,1024]{2,1,0:T(8,128)(2,1)}), bf16[2,2048,1024]{2,1,0:T(8,128)(2,1)}) %all-gather.9.cloned.1.call-update) | async-done | bytes 8388624 | tf_op jit(solution)/shard_map/while/body/eval_jaxpr/all_gather | solution.py:39
  739.0 154.0 %reduce-scatter.7.cloned.1.call-done = f32[2,512,1024]{2,1,0:T(8,128)} async-done(((f32[2,2048,1024]{2,1,0:T(8,128)}), f32[2,512,1024]{2,1,0:T(8,128)}) %reduce-scatter.7.cloned.1.call-update) | async-done | bytes 4194320 | tf_op jit(solution)/shard_map/while/body/eval_jaxpr/reduce_scatter | solution.py:43
  925.9 84.8 %all-gather.7.cloned.1.call-done = bf16[2,2048,1024]{2,1,0:T(8,128)(2,1)} async-done(((bf16[2,512,1024]{2,1,0:T(8,128)(2,1)}), bf16[2,2048,1024]{2,1,0:T(8,128)(2,1)}) %all-gather.7.cloned.1.call-update) | async-done | bytes 8388624 | tf_op jit(solution)/shard_map/while/body/eval_jaxpr/all_gather | solution.py:39
  1032.6 288.5 %while.107 = (s32[]{:T(128)}, bf16[4,2,512,4,64]{2,4,3,1,0:T(8,128)(2,1)}, f32[4,2,4,512]{3,2,1,0:T(4,128)S(1)}, s32[4]{0:T(128)S(1)}, s32[2]{0:T(128)S(1)}, /*i...) while((s32[]{:T(128)}, ...), condition=%wide.region_6.6_spmd, body=%wide.region_3.5_spmd.sunk | while | flops 2283012608 | bytes 200423664 | solution.py:103
  1338.0 153.3 %reduce-scatter.5.cloned.1.call-done = f32[2,512,1024]{2,1,0:T(8,128)} async-done(((f32[2,2048,1024]{2,1,0:T(8,128)}), f32[2,512,1024]{2,1,0:T(8,128)}) %reduce-scatter.5.cloned.1.call-update) | async-done | bytes 4194320 | tf_op jit(solution)/shard_map/while/body/eval_jaxpr/reduce_scatter | solution.py:43
  1506.4 87.7 %all-gather.9.cloned.1.call-done = bf16[2,2048,1024]{2,1,0:T(8,128)(2,1)} async-done(((bf16[2,512,1024]{2,1,0:T(8,128)(2,1)}), bf16[2,2048,1024]{2,1,0:T(8,128)(2,1)}) %all-gather.9.cloned.1.call-update) | async-done | bytes 8388624 | tf_op jit(solution)/shard_map/while/body/eval_jaxpr/all_gather | solution.py:39
  1620.8 154.0 %reduce-scatter.7.cloned.1.call-done = f32[2,512,1024]{2,1,0:T(8,128)} async-done(((f32[2,2048,1024]{2,1,0:T(8,128)}), f32[2,512,1024]{2,1,0:T(8,128)}) %reduce-scatter.7.cloned.1.call-update) | async-done | bytes 4194320 | tf_op jit(solution)/shard_map/while/body/eval_jaxpr/reduce_scatter | solution.py:43
  1808.1 84.8 %all-gather.7.cloned.1.call-done = bf16[2,2048,1024]{2,1,0:T(8,128)(2,1)} async-done(((bf16[2,512,1024]{2,1,0:T(8,128)(2,1)}), bf16[2,2048,1024]{2,1,0:T(8,128)(2,1)}) %all-gather.7.cloned.1.call-update) | async-done | bytes 8388624 | tf_op jit(solution)/shard_map/while/body/eval_jaxpr/all_gather | solution.py:39
  1914.8 288.3 %while.107 = (s32[]{:T(128)}, bf16[4,2,512,4,64]{2,4,3,1,0:T(8,128)(2,1)}, f32[4,2,4,512]{3,2,1,0:T(4,128)S(1)}, s32[4]{0:T(128)S(1)}, s32[2]{0:T(128)S(1)}, /*i...) while((s32[]{:T(128)}, ...), condition=%wide.region_6.6_spmd, body=%wide.region_3.5_spmd.sunk | while | flops 2283012608 | bytes 200423664 | solution.py:103
  2219.9 153.3 %reduce-scatter.5.cloned.1.call-done = f32[2,512,1024]{2,1,0:T(8,128)} async-done(((f32[2,2048,1024]{2,1,0:T(8,128)}), f32[2,512,1024]{2,1,0:T(8,128)}) %reduce-scatter.5.cloned.1.call-update) | async-done | bytes 4194320 | tf_op jit(solution)/shard_map/while/body/eval_jaxpr/reduce_scatter | solution.py:43
  2388.5 87.7 %all-gather.9.cloned.1.call-done = bf16[2,2048,1024]{2,1,0:T(8,128)(2,1)} async-done(((bf16[2,512,1024]{2,1,0:T(8,128)(2,1)}), bf16[2,2048,1024]{2,1,0:T(8,128)(2,1)}) %all-gather.9.cloned.1.call-update) | async-done | bytes 8388624 | tf_op jit(solution)/shard_map/while/body/eval_jaxpr/all_gather | solution.py:39
  2503.1 154.0 %reduce-scatter.7.cloned.1.call-done = f32[2,512,1024]{2,1,0:T(8,128)} async-done(((f32[2,2048,1024]{2,1,0:T(8,128)}), f32[2,512,1024]{2,1,0:T(8,128)}) %reduce-scatter.7.cloned.1.call-update) | async-done | bytes 4194320 | tf_op jit(solution)/shard_map/while/body/eval_jaxpr/reduce_scatter | solution.py:43
  2687.0 3408.3 %while.106 = (s32[]{:T(128)}, bf16[2,512,1024]{2,1,0:T(8,128)(2,1)S(1)}, f32[3,1024,256]{1,2,0:T(8,128)}, f32[2,256]{1,0:T(2,128)}, f32[256,1024]{1,0:T(8,128)},...) while((s32[]{:T(128)}, ...), condition=%wide.region_35.36_spmd.clone, body=%wide.region_12.35_spmd.clone.sunk | while | flops 72301961216 | bytes 1148200320 | solution.py:330
  2704.9 83.1 %all-gather.11.cloned.1.call-done = bf16[2,2048,1024]{2,1,0:T(8,128)(2,1)} async-done(((bf16[2,512,1024]{2,1,0:T(8,128)(2,1)}), bf16[2,2048,1024]{2,1,0:T(8,128)(2,1)}) %all-gather.11.cloned.1.call-update) | async-done | bytes 8388624 | tf_op jit(solution)/shard_map/while/body/eval_jaxpr/all_gather | solution.py:39
  2804.3 73.1 %all-gather.13.cloned.1.call-done = bf16[2,2048,1024]{2,1,0:T(8,128)(2,1)} async-done(((bf16[2,512,1024]{2,1,0:T(8,128)(2,1)}), bf16[2,2048,1024]{2,1,0:T(8,128)(2,1)}) %all-gather.13.cloned.1.call-update) | async-done | bytes 8388624 | tf_op jit(solution)/shard_map/while/body/eval_jaxpr/all_gather | solution.py:47
  2934.6 77.8 %reduce-scatter.9.cloned.1.call-done = bf16[2,512,1024]{2,1,0:T(8,128)(2,1)} async-done(((bf16[2,2048,1024]{2,1,0:T(8,128)(2,1)}), bf16[2,512,1024]{2,1,0:T(8,128)(2,1)}) %reduce-scatter.9.cloned.1.call-update) | async-done | bytes 2097168 | tf_op jit(solution)/shard_map/while/body/eval_jaxpr/reduce_scatter | solution.py:51
  3027.7 74.2 %all-gather.15.cloned.1.call-done = bf16[2,2048,1024]{2,1,0:T(8,128)(2,1)} async-done(((bf16[2,512,1024]{2,1,0:T(8,128)(2,1)}), bf16[2,2048,1024]{2,1,0:T(8,128)(2,1)}) %all-gather.15.cloned.1.call-update) | async-done | bytes 8388624 | tf_op jit(solution)/shard_map/while/body/eval_jaxpr/all_gather | solution.py:39
  3118.6 72.8 %all-gather.17.cloned.1.call-done = bf16[2,2048,1024]{2,1,0:T(8,128)(2,1)} async-done(((bf16[2,512,1024]{2,1,0:T(8,128)(2,1)}), bf16[2,2048,1024]{2,1,0:T(8,128)(2,1)}) %all-gather.17.cloned.1.call-update) | async-done | bytes 8388624 | tf_op jit(solution)/shard_map/while/body/eval_jaxpr/all_gather | solution.py:47
  3198.5 481.1 %while.108 = (s32[]{:T(128)}, f32[2,2048,4,64]{1,3,2,0:T(8,128)}, f32[2,2048,4,64]{1,3,2,0:T(8,128)}, bf16[4,2,512,4,64]{2,4,3,1,0:T(8,128)(2,1)}, s32[4]{0:T(12...) while((s32[]{:T(128)}, f32[2,2048,4,64]{1,3,2,0:T(8,128)}, ...), condition=%wide.region_22.22_spmd.clone, body=%wide.region_20.21_spmd.clone.sunk | while | flops 5467800064 | bytes 409565504 | solution.py:157
  3345.0 30.0 multiply_reduce_fusion.8
  3465.8 30.0 multiply_reduce_fusion.8
  3756.6 45.4 reduce-scatter.11.cloned.1.call-done
  3845.5 84.2 %all-gather.11.cloned.1.call-done = bf16[2,2048,1024]{2,1,0:T(8,128)(2,1)} async-done(((bf16[2,512,1024]{2,1,0:T(8,128)(2,1)}), bf16[2,2048,1024]{2,1,0:T(8,128)(2,1)}) %all-gather.11.cloned.1.call-update) | async-done | bytes 8388624 | tf_op jit(solution)/shard_map/while/body/eval_jaxpr/all_gather | solution.py:39
  3945.9 73.1 %all-gather.13.cloned.1.call-done = bf16[2,2048,1024]{2,1,0:T(8,128)(2,1)} async-done(((bf16[2,512,1024]{2,1,0:T(8,128)(2,1)}), bf16[2,2048,1024]{2,1,0:T(8,128)(2,1)}) %all-gather.13.cloned.1.call-update) | async-done | bytes 8388624 | tf_op jit(solution)/shard_map/while/body/eval_jaxpr/all_gather | solution.py:47
  4066.4 77.8 %reduce-scatter.9.cloned.1.call-done = bf16[2,512,1024]{2,1,0:T(8,128)(2,1)} async-done(((bf16[2,2048,1024]{2,1,0:T(8,128)(2,1)}), bf16[2,512,1024]{2,1,0:T(8,128)(2,1)}) %reduce-scatter.9.cloned.1.call-update) | async-done | bytes 2097168 | tf_op jit(solution)/shard_map/while/body/eval_jaxpr/reduce_scatter | solution.py:51
  4159.6 74.3 %all-gather.15.cloned.1.call-done = bf16[2,2048,1024]{2,1,0:T(8,128)(2,1)} async-done(((bf16[2,512,1024]{2,1,0:T(8,128)(2,1)}), bf16[2,2048,1024]{2,1,0:T(8,128)(2,1)}) %all-gather.15.cloned.1.call-update) | async-done | bytes 8388624 | tf_op jit(solution)/shard_map/while/body/eval_jaxpr/all_gather | solution.py:39
  4250.6 73.0 %all-gather.17.cloned.1.call-done = bf16[2,2048,1024]{2,1,0:T(8,128)(2,1)} async-done(((bf16[2,512,1024]{2,1,0:T(8,128)(2,1)}), bf16[2,2048,1024]{2,1,0:T(8,128)(2,1)}) %all-gather.17.cloned.1.call-update) | async-done | bytes 8388624 | tf_op jit(solution)/shard_map/while/body/eval_jaxpr/all_gather | solution.py:47
  4330.7 480.9 %while.108 = (s32[]{:T(128)}, f32[2,2048,4,64]{1,3,2,0:T(8,128)}, f32[2,2048,4,64]{1,3,2,0:T(8,128)}, bf16[4,2,512,4,64]{2,4,3,1,0:T(8,128)(2,1)}, s32[4]{0:T(12...) while((s32[]{:T(128)}, f32[2,2048,4,64]{1,3,2,0:T(8,128)}, ...), condition=%wide.region_22.22_spmd.clone, body=%wide.region_20.21_spmd.clone.sunk | while | flops 5467800064 | bytes 409565504 | solution.py:157
  4358.6 30.0 multiply_reduce_fusion.8
  4476.9 30.0 multiply_reduce_fusion.8
  4597.7 30.0 multiply_reduce_fusion.8
  4890.6 43.4 reduce-scatter.11.cloned.1.call-done
  4977.2 84.1 %all-gather.11.cloned.1.call-done = bf16[2,2048,1024]{2,1,0:T(8,128)(2,1)} async-done(((bf16[2,512,1024]{2,1,0:T(8,128)(2,1)}), bf16[2,2048,1024]{2,1,0:T(8,128)(2,1)}) %all-gather.11.cloned.1.call-update) | async-done | bytes 8388624 | tf_op jit(solution)/shard_map/while/body/eval_jaxpr/all_gather | solution.py:39
  5077.5 73.1 %all-gather.13.cloned.1.call-done = bf16[2,2048,1024]{2,1,0:T(8,128)(2,1)} async-done(((bf16[2,512,1024]{2,1,0:T(8,128)(2,1)}), bf16[2,2048,1024]{2,1,0:T(8,128)(2,1)}) %all-gather.13.cloned.1.call-update) | async-done | bytes 8388624 | tf_op jit(solution)/shard_map/while/body/eval_jaxpr/all_gather | solution.py:47
  5198.2 77.8 %reduce-scatter.9.cloned.1.call-done = bf16[2,512,1024]{2,1,0:T(8,128)(2,1)} async-done(((bf16[2,2048,1024]{2,1,0:T(8,128)(2,1)}), bf16[2,512,1024]{2,1,0:T(8,128)(2,1)}) %reduce-scatter.9.cloned.1.call-update) | async-done | bytes 2097168 | tf_op jit(solution)/shard_map/while/body/eval_jaxpr/reduce_scatter | solution.py:51
  5291.3 74.3 %all-gather.15.cloned.1.call-done = bf16[2,2048,1024]{2,1,0:T(8,128)(2,1)} async-done(((bf16[2,512,1024]{2,1,0:T(8,128)(2,1)}), bf16[2,2048,1024]{2,1,0:T(8,128)(2,1)}) %all-gather.15.cloned.1.call-update) | async-done | bytes 8388624 | tf_op jit(solution)/shard_map/while/body/eval_jaxpr/all_gather | solution.py:39
  5382.4 73.0 %all-gather.17.cloned.1.call-done = bf16[2,2048,1024]{2,1,0:T(8,128)(2,1)} async-done(((bf16[2,512,1024]{2,1,0:T(8,128)(2,1)}), bf16[2,2048,1024]{2,1,0:T(8,128)(2,1)}) %all-gather.17.cloned.1.call-update) | async-done | bytes 8388624 | tf_op jit(solution)/shard_map/while/body/eval_jaxpr/all_gather | solution.py:47
  5462.5 480.9 %while.108 = (s32[]{:T(128)}, f32[2,2048,4,64]{1,3,2,0:T(8,128)}, f32[2,2048,4,64]{1,3,2,0:T(8,128)}, bf16[4,2,512,4,64]{2,4,3,1,0:T(8,128)(2,1)}, s32[4]{0:T(12...) while((s32[]{:T(128)}, f32[2,2048,4,64]{1,3,2,0:T(8,128)}, ...), condition=%wide.region_22.22_spmd.clone, body=%wide.region_20.21_spmd.clone.sunk | while | flops 5467800064 | bytes 409565504 | solution.py:157
  5490.4 30.0 multiply_reduce_fusion.8
  5608.7 30.0 multiply_reduce_fusion.8
  5729.5 30.0 multiply_reduce_fusion.8
  6022.3 43.4 reduce-scatter.11.cloned.1.call-done
  6120.9 76.8 %all-reduce.1 = (f32[1,2,1024]{2,1,0:T(2,128)}, f32[1,2,1024]{2,1,0:T(2,128)}, f32[1,2,1024]{2,1,0:T(2,128)}) all-reduce(f32[1,2,1024]{2,1,0:T(2,128)S(1)} %bitcast.491, f32[1,2,1024]{2,1,0:T(2,128)S(1)} %bitcast.490, f32[1,2,1024]{2,1,0:T(2,128)S(1)} %bitcast.489), channel_id=1, replica_groups=mesh['section'=2,'dp'=4,'tensor'=4] {'dp','tensor'}, use_global_device_ids=true, to_apply=%region_36.37 | all-reduce | flops 6144 | bytes 49152 | tf_op jit(solution)/shard_map/psum | solution.py:341
  6209.9 122.7 %all-reduce.6.cloned.1.call-done = (bf16[1,3,1024,256]{3,2,1,0:T(8,128)(2,1)}, bf16[1,256,1024]{2,1,0:T(8,128)(2,1)}, bf16[1,1024,1024]{2,1,0:T(8,128)(2,1)}, bf16[1,1024,1024]{2,1,0:T(8,128)(2,1)}) async-done(((bf16[1,3,1024,256]{3,2,1,0:T(8,128)(2,1)}, bf16[1,256,1024]{2,1,0:T(8,128)(2,1)}, bf16[1,1024,1024]{2,1,0:T(8,128)(2,1)}, bf16[1,1024,1024]{2,1,0:T(8,128)(2,1)}), ...) | async-done | bytes 6291472 | tf_op jit(solution)/shard_map/psum | solution.py:334
  (1138 shorter events, 3116.1 us)
Async XLA Ops:
  29.8 99.0 %copy-start.33 = (bf16[3,1024,256]{1,2,0:T(8,128)(2,1)}, bf16[3,1024,256]{1,2,0:T(8,128)(2,1)S(1)}, u32[]{:S(2)}) copy-start(bf16[3,1024,256]{1,2,0:T(8,128)(2,1)S(1)} %get-tuple-element.1921) | copy-start | bytes 4718596 | tf_op jit(solution)/shard_map/while
  29.8 99.0 %all-gather.7.cloned.1.call-start = ((), (), s32[]{:S(2)}) async-start(), calls=%async_computation.5 | async-start | bytes 10485760 | tf_op jit(solution)/shard_map/while/body/eval_jaxpr/all_gather | solution.py:39
  38.3 570.9 %reduce-scatter.5.cloned.1.call-start = ((), (), s32[]{:S(2)}) async-start(), calls=%async_computation.6 | async-start | bytes 20971520 | tf_op jit(solution)/shard_map/while/body/eval_jaxpr/reduce_scatter | solution.py:43
  455.2 154.0 %copy-start.8 = (bf16[2,512,1024]{2,1,0:T(8,128)(2,1)S(1)}, bf16[2,512,1024]{2,1,0:T(8,128)(2,1)}, u32[]{:S(2)}) copy-start(bf16[2,512,1024]{2,1,0:T(8,128)(2,1)} %copy-done.7) | copy-start | bytes 6291460 | tf_op jit(solution)/shard_map/while
  455.2 256.9 %all-gather.9.cloned.1.call-start = ((), (), s32[]{:S(2)}) async-start(), calls=%async_computation.7 | async-start | bytes 10485760 | tf_op jit(solution)/shard_map/while/body/eval_jaxpr/all_gather | solution.py:39
  622.2 89.8 %copy-start.62 = (bf16[1024,1024]{1,0:T(8,128)(2,1)S(1)}, bf16[1024,1024]{1,0:T(8,128)(2,1)}, u32[]{:S(2)}) copy-start(bf16[1024,1024]{1,0:T(8,128)(2,1)} %get-tuple-element.1928) | copy-start | bytes 6291460 | tf_op jit(solution)/shard_map/while
  624.3 268.7 %reduce-scatter.7.cloned.1.call-start = ((), (), s32[]{:S(2)}) async-start(), calls=%async_computation.8 | async-start | bytes 20971520 | tf_op jit(solution)/shard_map/while/body/eval_jaxpr/reduce_scatter | solution.py:43
  899.0 15.4 collective-permute-start.1
  914.6 96.2 %copy-start.33 = (bf16[3,1024,256]{1,2,0:T(8,128)(2,1)}, bf16[3,1024,256]{1,2,0:T(8,128)(2,1)S(1)}, u32[]{:S(2)}) copy-start(bf16[3,1024,256]{1,2,0:T(8,128)(2,1)S(1)} %get-tuple-element.1921) | copy-start | bytes 4718596 | tf_op jit(solution)/shard_map/while
  914.6 96.1 %all-gather.7.cloned.1.call-start = ((), (), s32[]{:S(2)}) async-start(), calls=%async_computation.5 | async-start | bytes 10485760 | tf_op jit(solution)/shard_map/while/body/eval_jaxpr/all_gather | solution.py:39
  923.0 568.3 %reduce-scatter.5.cloned.1.call-start = ((), (), s32[]{:S(2)}) async-start(), calls=%async_computation.6 | async-start | bytes 20971520 | tf_op jit(solution)/shard_map/while/body/eval_jaxpr/reduce_scatter | solution.py:43
  1337.2 154.0 %copy-start.8 = (bf16[2,512,1024]{2,1,0:T(8,128)(2,1)S(1)}, bf16[2,512,1024]{2,1,0:T(8,128)(2,1)}, u32[]{:S(2)}) copy-start(bf16[2,512,1024]{2,1,0:T(8,128)(2,1)} %copy-done.7) | copy-start | bytes 6291460 | tf_op jit(solution)/shard_map/while
  1337.3 256.9 %all-gather.9.cloned.1.call-start = ((), (), s32[]{:S(2)}) async-start(), calls=%async_computation.7 | async-start | bytes 10485760 | tf_op jit(solution)/shard_map/while/body/eval_jaxpr/all_gather | solution.py:39
  1504.3 89.8 %copy-start.62 = (bf16[1024,1024]{1,0:T(8,128)(2,1)S(1)}, bf16[1024,1024]{1,0:T(8,128)(2,1)}, u32[]{:S(2)}) copy-start(bf16[1024,1024]{1,0:T(8,128)(2,1)} %get-tuple-element.1928) | copy-start | bytes 6291460 | tf_op jit(solution)/shard_map/while
  1506.4 268.4 %reduce-scatter.7.cloned.1.call-start = ((), (), s32[]{:S(2)}) async-start(), calls=%async_computation.8 | async-start | bytes 20971520 | tf_op jit(solution)/shard_map/while/body/eval_jaxpr/reduce_scatter | solution.py:43
  1780.8 15.4 collective-permute-start.1
  1796.7 96.2 %copy-start.33 = (bf16[3,1024,256]{1,2,0:T(8,128)(2,1)}, bf16[3,1024,256]{1,2,0:T(8,128)(2,1)S(1)}, u32[]{:S(2)}) copy-start(bf16[3,1024,256]{1,2,0:T(8,128)(2,1)S(1)} %get-tuple-element.1921) | copy-start | bytes 4718596 | tf_op jit(solution)/shard_map/while
  1796.7 96.2 %all-gather.7.cloned.1.call-start = ((), (), s32[]{:S(2)}) async-start(), calls=%async_computation.5 | async-start | bytes 10485760 | tf_op jit(solution)/shard_map/while/body/eval_jaxpr/all_gather | solution.py:39
  1805.1 568.1 %reduce-scatter.5.cloned.1.call-start = ((), (), s32[]{:S(2)}) async-start(), calls=%async_computation.6 | async-start | bytes 20971520 | tf_op jit(solution)/shard_map/while/body/eval_jaxpr/reduce_scatter | solution.py:43
  2219.2 154.0 %copy-start.8 = (bf16[2,512,1024]{2,1,0:T(8,128)(2,1)S(1)}, bf16[2,512,1024]{2,1,0:T(8,128)(2,1)}, u32[]{:S(2)}) copy-start(bf16[2,512,1024]{2,1,0:T(8,128)(2,1)} %copy-done.7) | copy-start | bytes 6291460 | tf_op jit(solution)/shard_map/while
  2219.2 256.9 %all-gather.9.cloned.1.call-start = ((), (), s32[]{:S(2)}) async-start(), calls=%async_computation.7 | async-start | bytes 10485760 | tf_op jit(solution)/shard_map/while/body/eval_jaxpr/all_gather | solution.py:39
  2388.4 268.7 %reduce-scatter.7.cloned.1.call-start = ((), (), s32[]{:S(2)}) async-start(), calls=%async_computation.8 | async-start | bytes 20971520 | tf_op jit(solution)/shard_map/while/body/eval_jaxpr/reduce_scatter | solution.py:43
  2663.1 15.3 collective-permute-start.1
  2687.2 100.8 %all-gather.11.cloned.1.call-start = ((), (), s32[]{:S(2)}) async-start(), calls=%async_computation.9 | async-start | bytes 10485760 | tf_op jit(solution)/shard_map/while/body/eval_jaxpr/all_gather | solution.py:39
  2696.0 234.2 %copy-start.29 = (f32[1,1024]{1,0:T(1,128)}, f32[1,1024]{1,0:T(1,128)S(1)}, u32[]{:S(2)}) copy-start(f32[1,1024]{1,0:T(1,128)S(1)} %get-tuple-element.1724) | copy-start | bytes 12292 | tf_op jit(solution)/shard_map/while
  2700.3 177.1 %all-gather.13.cloned.1.call-start = ((), (), s32[]{:S(2)}) async-start(), calls=%async_computation.10 | async-start | bytes 10485760 | tf_op jit(solution)/shard_map/while/body/eval_jaxpr/all_gather | solution.py:47
  2704.5 307.9 %reduce-scatter.9.cloned.1.call-start = ((), (), s32[]{:S(2)}) async-start(), calls=%async_computation.11 | async-start | bytes 10485760 | tf_op jit(solution)/shard_map/while/body/eval_jaxpr/reduce_scatter | solution.py:51
  2925.8 176.1 %all-gather.15.cloned.1.call-start = ((), (), s32[]{:S(2)}) async-start(), calls=%async_computation.12 | async-start | bytes 10485760 | tf_op jit(solution)/shard_map/while/body/eval_jaxpr/all_gather | solution.py:39
  2934.5 256.9 %all-gather.17.cloned.1.call-start = ((), (), s32[]{:S(2)}) async-start(), calls=%async_computation.13 | async-start | bytes 10485760 | tf_op jit(solution)/shard_map/while/body/eval_jaxpr/all_gather | solution.py:47
  3025.1 776.9 %reduce-scatter.11.cloned.1.call-start = ((), (), s32[]{:S(2)}) async-start(), calls=%async_computation.14 | async-start | bytes 10485760 | tf_op jit(solution)/shard_map/while/body/eval_jaxpr/reduce_scatter | solution.py:51
  3809.4 18.1 collective-permute-start
  3828.0 101.7 %all-gather.11.cloned.1.call-start = ((), (), s32[]{:S(2)}) async-start(), calls=%async_computation.9 | async-start | bytes 10485760 | tf_op jit(solution)/shard_map/while/body/eval_jaxpr/all_gather | solution.py:39
  3836.7 225.3 %copy-start.29 = (f32[1,1024]{1,0:T(1,128)}, f32[1,1024]{1,0:T(1,128)S(1)}, u32[]{:S(2)}) copy-start(f32[1,1024]{1,0:T(1,128)S(1)} %get-tuple-element.1724) | copy-start | bytes 12292 | tf_op jit(solution)/shard_map/while
  3841.0 178.0 %all-gather.13.cloned.1.call-start = ((), (), s32[]{:S(2)}) async-start(), calls=%async_computation.10 | async-start | bytes 10485760 | tf_op jit(solution)/shard_map/while/body/eval_jaxpr/all_gather | solution.py:47
  3845.2 299.0 %reduce-scatter.9.cloned.1.call-start = ((), (), s32[]{:S(2)}) async-start(), calls=%async_computation.11 | async-start | bytes 10485760 | tf_op jit(solution)/shard_map/while/body/eval_jaxpr/reduce_scatter | solution.py:51
  4057.7 176.2 %all-gather.15.cloned.1.call-start = ((), (), s32[]{:S(2)}) async-start(), calls=%async_computation.12 | async-start | bytes 10485760 | tf_op jit(solution)/shard_map/while/body/eval_jaxpr/all_gather | solution.py:39
  4066.4 257.2 %all-gather.17.cloned.1.call-start = ((), (), s32[]{:S(2)}) async-start(), calls=%async_computation.13 | async-start | bytes 10485760 | tf_op jit(solution)/shard_map/while/body/eval_jaxpr/all_gather | solution.py:47
  4157.0 777.0 %reduce-scatter.11.cloned.1.call-start = ((), (), s32[]{:S(2)}) async-start(), calls=%async_computation.14 | async-start | bytes 10485760 | tf_op jit(solution)/shard_map/while/body/eval_jaxpr/reduce_scatter | solution.py:51
  4941.4 18.0 collective-permute-start
  4959.6 101.6 %all-gather.11.cloned.1.call-start = ((), (), s32[]{:S(2)}) async-start(), calls=%async_computation.9 | async-start | bytes 10485760 | tf_op jit(solution)/shard_map/while/body/eval_jaxpr/all_gather | solution.py:39
  4968.4 225.4 %copy-start.29 = (f32[1,1024]{1,0:T(1,128)}, f32[1,1024]{1,0:T(1,128)S(1)}, u32[]{:S(2)}) copy-start(f32[1,1024]{1,0:T(1,128)S(1)} %get-tuple-element.1724) | copy-start | bytes 12292 | tf_op jit(solution)/shard_map/while
  4972.6 178.0 %all-gather.13.cloned.1.call-start = ((), (), s32[]{:S(2)}) async-start(), calls=%async_computation.10 | async-start | bytes 10485760 | tf_op jit(solution)/shard_map/while/body/eval_jaxpr/all_gather | solution.py:47
  4976.9 299.1 %reduce-scatter.9.cloned.1.call-start = ((), (), s32[]{:S(2)}) async-start(), calls=%async_computation.11 | async-start | bytes 10485760 | tf_op jit(solution)/shard_map/while/body/eval_jaxpr/reduce_scatter | solution.py:51
  5189.5 176.2 %all-gather.15.cloned.1.call-start = ((), (), s32[]{:S(2)}) async-start(), calls=%async_computation.12 | async-start | bytes 10485760 | tf_op jit(solution)/shard_map/while/body/eval_jaxpr/all_gather | solution.py:39
  5198.1 257.2 %all-gather.17.cloned.1.call-start = ((), (), s32[]{:S(2)}) async-start(), calls=%async_computation.13 | async-start | bytes 10485760 | tf_op jit(solution)/shard_map/while/body/eval_jaxpr/all_gather | solution.py:47
  5288.8 777.0 %reduce-scatter.11.cloned.1.call-start = ((), (), s32[]{:S(2)}) async-start(), calls=%async_computation.14 | async-start | bytes 10485760 | tf_op jit(solution)/shard_map/while/body/eval_jaxpr/reduce_scatter | solution.py:51
  6073.2 18.0 collective-permute-start
  6095.3 237.4 %all-reduce.6.cloned.1.call-start = ((), (), s32[]{:S(2)}) async-start(), calls=%async_computation.4 | async-start | bytes 12582912 | tf_op jit(solution)/shard_map/psum | solution.py:334
  (209 other events, 2780.5 us)
Sparse Core Ops, SparseCore 0:
  38.4 90.4 all-gather.6
  455.3 153.8 reduce-scatter.4
  624.4 87.5 all-gather.8
  739.1 153.8 reduce-scatter.6
  923.1 87.5 all-gather.6
  1337.4 153.8 reduce-scatter.4
  1506.5 87.5 all-gather.8
  1621.0 153.8 reduce-scatter.6
  1805.3 87.5 all-gather.6
  2219.4 153.8 reduce-scatter.4
  2388.5 87.5 all-gather.8
  2503.2 153.8 reduce-scatter.6
  2700.4 87.5 all-gather.10
  2789.7 87.5 all-gather.12
  2925.9 86.4 reduce-scatter.8
  3014.2 87.5 all-gather.14
  3103.7 87.5 all-gather.16
  3715.6 86.3 reduce-scatter.10
  3841.1 88.4 all-gather.10
  3931.3 87.6 all-gather.12
  4057.8 86.4 reduce-scatter.8
  4146.3 87.5 all-gather.14
  4235.9 87.5 all-gather.16
  4847.5 86.4 reduce-scatter.10
  4972.8 88.4 all-gather.10
  5063.0 87.6 all-gather.12
  5189.6 86.4 reduce-scatter.8
  5278.0 87.5 all-gather.14
  5367.7 87.6 all-gather.16
  5979.3 86.4 reduce-scatter.10
Sparse Core Ops, SparseCore 1:
  6106.7 225.9 all-reduce.5
where the time goes:
time: 6360 us; the launch traced here: 6350 us
  waiting for transfers between devices  2840 us (45%)
  matrix products  1960 us (31%)
  other arithmetic  1130 us (18%)
  local copies, waits for them, and re-layouts  237 us (4%)
  blocking collectives  89.2 us (1%)
    all_gather x12, waiting for transfers between devices, gather_tokens(): return lax.all_gather(values, 'tensor', axis=1, tiled=True)  995 us
    reduce_scatter x6, waiting for transfers between devices, scatter_tokens(): return lax.psum_scatter(values, 'tensor', scatter_dimension=1, tiled=True)  922 us
    dot_general x24, matrix products, score_block(): jnp.einsum('rqhd,rkhd->rhqk', query_block, key_heads, preferred_element_t...  603 us
    all_gather x6, waiting for transfers between devices, gather_grads(): return lax.all_gather(values, 'tensor', axis=1, tiled=True)  438 us
    reduce_scatter x6, waiting for transfers between devices, scatter_grads(): lax.psum_scatter(values.astype(jnp.bfloat16), 'tensor', scatter_dimension...  366 us
    convert_element_type x12, other arithmetic, one_block(): grad_scores = (probs * (grad_probs - inner)).astype(jnp.bfloat16)  329 us
    dot_general x12, matrix products, one_block(): jnp.einsum('rhqk,rkhd->rqhd', probs, value_heads, preferred_element_type=...  233 us
    reduce_sum x12, other arithmetic, one_block(): row_total = jnp.sum(powers, axis=-1, keepdims=True)  226 us
  transfers between devices with their start and end apart: 37, of which 31 were waited for; matrix products, arithmetic and copies ran while one was open for 6% of the time, Pallas kernels for 0%

commit v1 on v0

--- a/solution.py
+++ b/solution.py
@@ -3,6 +3,8 @@
 import jax
 import jax.numpy as jnp
 from jax import lax
+from jax.experimental import pallas as pl
+from jax.experimental.pallas import tpu as pltpu
 from jax.sharding import PartitionSpec as P
 
 D = 1024
@@ -354,9 +356,976 @@
     )
 
 
+bf16, f32 = jnp.bfloat16, jnp.float32
+HEAD = D // HEADS
+LOG2E = 1.4426950408889634
+GROUP = 4
+ST = ("section", "tensor")
+MIB = 2**20
+
+
+def one_row_a_chip(mesh):
+    return mesh.shape["section"] == 2 and mesh.shape["tensor"] == GROUP
+
+
+def core_of(segment):
+    return (segment & 1) ^ (segment >> 1)
+
+
+def place(core, chip):
+    return core * GROUP + chip
+
+
+CHIPS = range(GROUP)
+FIRST_HOP = [(place(0, t), place(0, t ^ 1)) for t in CHIPS] + [(place(1, t), place(1, t ^ 2)) for t in CHIPS]
+SECOND_HOP = [(place(0, t), place(0, t ^ 2)) for t in CHIPS] + [(place(1, t), place(1, t ^ 1)) for t in CHIPS]
+
+
+def hop(value, pairs):
+    return lax.ppermute(value, ST, pairs)
+
+
+def swap(value):
+    return lax.ppermute(value, "section", [(0, 1), (1, 0)])
+
+
+def half_of(value, axis, index):
+    size = value.shape[axis] // 2
+    return lax.dynamic_slice_in_dim(value, index * size, size, axis)
+
+
+def dot_nn(left, right):
+    return lax.dot_general(left, right, (((1,), (0,)), ((), ())), preferred_element_type=f32)
+
+
+def dot_nt(left, right):
+    return lax.dot_general(left, right, (((1,), (1,)), ((), ())), preferred_element_type=f32)
+
+
+def dot_tn(left, right):
+    return lax.dot_general(left, right, (((0,), (0,)), ((), ())), preferred_element_type=f32)
+
+
+def three_parts(value):
+    first = value.astype(bf16)
+    rest = value - first.astype(f32)
+    second = rest.astype(bf16)
+    third = (rest - second.astype(f32)).astype(bf16)
+    return first, second, third
+
+
+def key_columns(positions, length):
+    high = (positions // 8 * 8).astype(f32)
+    low = (positions % 8).astype(f32)
+    mask = jnp.where(positions < length, 0.0, -1e30).astype(f32)
+    one = jnp.ones_like(high)
+    columns = jnp.stack([high, high, high, low, low, low, mask, one, one, one], axis=1)
+    half = jnp.pad(columns, ((0, 0), (0, HEAD - 10)))
+    return jnp.concatenate([half, half], axis=1).astype(bf16)
+
+
+def query_columns(slopes):
+    first, second, third = three_parts(slopes * 8.0)
+    one = jnp.ones_like(first)
+    columns = jnp.stack([first, second, third, first, second, third, one], axis=1)
+    half = jnp.pad(columns, ((0, 0), (0, HEAD - 7))).reshape(-1, 2, HEAD)
+    row = jnp.concatenate([half[:, 1], half[:, 0]], axis=1).astype(f32)
+    return jnp.broadcast_to(row[:, None, :], (row.shape[0], 8, 2 * HEAD))
+
+
+def attend_kernel(seg, meta, q, kv, kvo, kcol, qcol, o, qx, qp, kp, vp, st_m, st_a):
+    other = 1 - meta[0]
+    lane = lax.broadcasted_iota(jnp.int32, (1, 128), 1)
+    low = lane < 64
+    base = qcol[0, 0:1, :].astype(bf16)
+    scale = LOG2E / 8
+    one = jnp.ones((1, 128), bf16)
+    for h in range(2):
+        mine = low if h == 0 else ~low
+        qp[h] = jnp.where(mine, q[...], base)
+        kp[h, 0 : 2 * seg] = jnp.where(mine, kv[0], kcol[0 : 2 * seg])
+        kp[h, 2 * seg :] = jnp.where(mine, kvo[0], kcol[2 * seg :])
+        vp[h, 0 : 2 * seg] = jnp.where(mine, kv[1], one)
+        vp[h, 2 * seg :] = jnp.where(mine, kvo[1], one)
+
+    def scores_of(h, start, keys, masked):
+        queries = qp[h, pl.ds(start, seg)]
+        scores = []
+        for n, (key_start, key_count) in enumerate(keys):
+            part = dot_nt(queries, kp[h, pl.ds(key_start, key_count)])
+            if masked and n == len(keys) - 1:
+                row = lax.broadcasted_iota(jnp.int32, (seg, key_count), 0)
+                column = lax.broadcasted_iota(jnp.int32, (seg, key_count), 1)
+                part = jnp.where(column <= row, part, -1e30)
+            scores.append(part)
+        top = scores[0].max(axis=1, keepdims=True)
+        for part in scores[1:]:
+            top = jnp.maximum(top, part.max(axis=1, keepdims=True))
+        return scores, top
+
+    def weigh(h, scores, top, keys):
+        total = None
+        for part, (key_start, key_count) in zip(scores, keys):
+            powers = jnp.exp2((part - top) * scale).astype(bf16)
+            term = dot_nn(powers, vp[h, pl.ds(key_start, key_count)])
+            total = term if total is None else total + term
+        return total
+
+    for h in range(2):
+        start = pl.multiple_of(other * seg, seg)
+        keys = [(pl.multiple_of(2 * seg + other * seg, seg), seg)]
+        scores, top = scores_of(h, start, keys, False)
+        st_a[h] = weigh(h, scores, top, keys)
+        st_m[h] = jnp.broadcast_to(top, (seg, 128))
+    for segment in range(2):
+        use = other == segment
+        rows = slice(segment * seg, (segment + 1) * seg)
+        totals, tops = [], []
+        for h in range(2):
+            keys = [(segment * seg, seg)]
+            if segment == 1:
+                keys = [(0, seg), (2 * seg, seg)] + keys
+            scores, top = scores_of(h, segment * seg, keys, True)
+            fifth = jnp.where(use, st_m[h][:, 0:1], -1e30)
+            top = jnp.maximum(top, fifth)
+            weight = jnp.where(use, jnp.exp2((fifth - top) * scale), 0.0)
+            totals.append(weigh(h, scores, top, keys) + weight * st_a[h])
+            tops.append(top)
+        number = jnp.where(low, totals[0], totals[1])
+        sums = jnp.where(low, totals[1], totals[0])
+        o[rows] = (number / pltpu.roll(sums, 64, 1)).astype(bf16)
+        logs = jnp.where(low, tops[1], tops[0]) + jnp.log(sums) * 8.0
+        first, second, third = three_parts(logs)
+        at = lane & 63
+        qx[rows] = jnp.where(at == 7, -first, jnp.where(at == 8, -second, jnp.where(at == 9, -third, base)))
+
+
+def attend(meta, q, kv, kvo, kcol, qcol):
+    rows, width = q.shape
+    seg = rows // 2
+    pairs = width // 128
+    block = pl.BlockSpec((rows, 128), lambda i, m: (0, i))
+    return pl.pallas_call(
+        partial(attend_kernel, seg),
+        grid_spec=pltpu.PrefetchScalarGridSpec(
+            num_scalar_prefetch=1,
+            grid=(pairs,),
+            in_specs=[
+                block,
+                pl.BlockSpec((2, rows, 128), lambda i, m: (0, 0, i)),
+                pl.BlockSpec((2, rows, 128), lambda i, m: (0, 0, m[1 + i])),
+                pl.BlockSpec((2 * rows, 128), lambda i, m: (0, 0)),
+                pl.BlockSpec((1, 8, 128), lambda i, m: (i, 0, 0)),
+            ],
+            out_specs=[block, block],
+            scratch_shapes=[
+                pltpu.VMEM((2, rows, 128), bf16),
+                pltpu.VMEM((2, 2 * rows, 128), bf16),
+                pltpu.VMEM((2, 2 * rows, 128), bf16),
+                pltpu.VMEM((2, seg, 128), f32),
+                pltpu.VMEM((2, seg, 128), f32),
+            ],
+        ),
+        out_shape=[jax.ShapeDtypeStruct((rows, width), bf16)] * 2,
+        compiler_params=pltpu.CompilerParams(vmem_limit_bytes=40 * MIB),
+        cost_estimate=pl.CostEstimate(
+            flops=40 * 256 * seg * seg * pairs, bytes_accessed=rows * width * 14, transcendentals=10 * seg * seg * pairs
+        ),
+        name="attend",
+    )(meta, q, kv, kvo, kcol, qcol)
+
+
+def attend_back_kernel(
+    seg, meta, q, kv, kvo, kcol, qx, do, o, dq, dkv, dkvo, qp, kp, vp, dp, kt, qm, dm, aq, ak, av
+):
+    other = 1 - meta[0]
+    lane = lax.broadcasted_iota(jnp.int32, (1, 128), 1)
+    low = lane < 64
+    at = lane & 63
+    scale = LOG2E / 8
+    zero = jnp.zeros((1, 128), bf16)
+    product = do[...].astype(f32) * o[...].astype(f32)
+    for h in range(2):
+        mine = low if h == 0 else ~low
+        qp[h] = jnp.where(mine, q[...], qx[...])
+        kp[h, 0 : 2 * seg] = jnp.where(mine, kv[0], kcol[0 : 2 * seg])
+        kp[h, 2 * seg :] = jnp.where(mine, kvo[0], kcol[2 * seg :])
+        vp[h, 0 : 2 * seg] = jnp.where(mine, kv[1], kcol[0 : 2 * seg])
+        vp[h, 2 * seg :] = jnp.where(mine, kvo[1], kcol[2 * seg :])
+        first, second, third = three_parts(jnp.sum(jnp.where(mine, product, 0.0), axis=1, keepdims=True))
+        extra = jnp.where(at == 7, -first, jnp.where(at == 8, -second, jnp.where(at == 9, -third, zero)))
+        dp[h] = jnp.where(mine, do[...], extra)
+        qm[h] = jnp.where(mine, q[...], zero)
+        dm[h] = jnp.where(mine, do[...], zero)
+    kt[:, 0 : 2 * seg] = kv[0].T
+    kt[:, 2 * seg :] = kvo[0].T
+    aq[...] = jnp.zeros_like(aq)
+    ak[...] = jnp.zeros_like(ak)
+    av[...] = jnp.zeros_like(av)
+
+    def block(query_start, query_count, key_start, key_count, masked):
+        queries, keys = pl.ds(query_start, query_count), pl.ds(key_start, key_count)
+        for h in range(2):
+            probs = jnp.exp2(dot_nt(kp[h, keys], qp[h, queries]) * scale)
+            if masked:
+                row = lax.broadcasted_iota(jnp.int32, (key_count, query_count), 0)
+                column = lax.broadcasted_iota(jnp.int32, (key_count, query_count), 1)
+                probs = jnp.where(row <= column, probs, 0.0)
+            grads = (probs * dot_nt(vp[h, keys], dp[h, queries])).astype(bf16)
+            av[keys] += dot_nn(probs.astype(bf16), dm[h, queries])
+            ak[keys] += dot_nn(grads, qm[h, queries])
+            aq[h * 64 : (h + 1) * 64, queries] += dot_nn(kt[h * 64 : (h + 1) * 64, keys], grads)
+
+    half = seg // 2
+    for segment in range(2):
+        start = segment * seg
+        block(start, half, start, half, True)
+        block(start + half, half, start, half, False)
+        block(start + half, half, start + half, half, True)
+    block(seg, seg, 0, seg, False)
+    block(seg, seg, 2 * seg, seg, False)
+    block(pl.multiple_of(other * seg, seg), seg, pl.multiple_of(2 * seg + other * seg, seg), seg, False)
+    dq[...] = (aq[...] * 0.125).T.astype(bf16)
+    dkv[0] = (ak[0 : 2 * seg] * 0.125).astype(bf16)
+    dkvo[0] = (ak[2 * seg :] * 0.125).astype(bf16)
+    dkv[1] = av[0 : 2 * seg].astype(bf16)
+    dkvo[1] = av[2 * seg :].astype(bf16)
+
+
+def attend_back(meta, q, kv, kvo, kcol, qx, do, o):
+    rows, width = q.shape
+    seg = rows // 2
+    pairs = width // 128
+    block = pl.BlockSpec((rows, 128), lambda i, m: (0, i))
+    mine = pl.BlockSpec((2, rows, 128), lambda i, m: (0, 0, i))
+    theirs = pl.BlockSpec((2, rows, 128), lambda i, m: (0, 0, m[1 + i]))
+    return pl.pallas_call(
+        partial(attend_back_kernel, seg),
+        grid_spec=pltpu.PrefetchScalarGridSpec(
+            num_scalar_prefetch=1,
+            grid=(pairs,),
+            in_specs=[block, mine, theirs, pl.BlockSpec((2 * rows, 128), lambda i, m: (0, 0))] + [block] * 3,
+            out_specs=[block, mine, theirs],
+            scratch_shapes=[
+                pltpu.VMEM((2, rows, 128), bf16),
+                pltpu.VMEM((2, 2 * rows, 128), bf16),
+                pltpu.VMEM((2, 2 * rows, 128), bf16),
+                pltpu.VMEM((2, rows, 128), bf16),
+                pltpu.VMEM((128, 2 * rows), bf16),
+                pltpu.VMEM((2, rows, 128), bf16),
+                pltpu.VMEM((2, rows, 128), bf16),
+                pltpu.VMEM((128, rows), f32),
+                pltpu.VMEM((2 * rows, 128), f32),
+                pltpu.VMEM((2 * rows, 128), f32),
+            ],
+        ),
+        out_shape=[
+            jax.ShapeDtypeStruct((rows, width), bf16),
+            jax.ShapeDtypeStruct((2, rows, width), bf16),
+            jax.ShapeDtypeStruct((2, rows, width), bf16),
+        ],
+        compiler_params=pltpu.CompilerParams(vmem_limit_bytes=48 * MIB),
+        cost_estimate=pl.CostEstimate(
+            flops=100 * 256 * seg * seg * pairs, bytes_accessed=rows * width * 26, transcendentals=10 * seg * seg * pairs
+        ),
+        name="attend_back",
+    )(meta, q, kv, kvo, kcol, qx, do, o)
+
+
+def fixed(shape):
+    return pl.BlockSpec(shape, lambda *_: (0,) * len(shape), pipeline_mode=pl.Buffered(1))
+
+
+def joined(refs, *index):
+    return jnp.concatenate([ref[index] if index else ref[...] for ref in refs], axis=0) if len(refs) > 1 else refs[0][index] if index else refs[0][...]
+
+
+def project_kernel(count, a, *refs):
+    pieces, bias, q, kv = refs[:count], refs[count], refs[count + 1], refs[count + 2]
+    step = pl.program_id(0)
+    result = (dot_nt(a[...], joined(pieces, 0)) + bias[0]).astype(bf16)
+
+    @pl.when(step == 0)
+    def _():
+        q[...] = result
+
+    @pl.when(step > 0)
+    def _():
+        kv[0] = result
+
+
+def project_heads(a, pieces, bias):
+    rows, width = a.shape
+    columns = sum(piece.shape[1] for piece in pieces)
+    return pl.pallas_call(
+        partial(project_kernel, len(pieces)),
+        grid=(3,),
+        in_specs=[fixed(a.shape)]
+        + [pl.BlockSpec((1,) + piece.shape[1:], lambda i: (i, 0, 0)) for piece in pieces]
+        + [pl.BlockSpec((1, 1, columns), lambda i: (i, 0, 0))],
+        out_specs=[
+            pl.BlockSpec((rows, columns), lambda i: (0, 0)),
+            pl.BlockSpec((1, rows, columns), lambda i: (jnp.maximum(i - 1, 0), 0, 0)),
+        ],
+        out_shape=[jax.ShapeDtypeStruct((rows, columns), bf16), jax.ShapeDtypeStruct((2, rows, columns), bf16)],
+        cost_estimate=pl.CostEstimate(
+            flops=6 * rows * width * columns, bytes_accessed=2 * rows * width + 6 * width * columns + 6 * rows * columns, transcendentals=0
+        ),
+        compiler_params=pltpu.CompilerParams(vmem_limit_bytes=40 * MIB),
+        name="project",
+    )(a, *pieces, bias)
+
+
+def normalize(value):
+    center = jnp.mean(value, axis=-1, keepdims=True)
+    centred = value - center
+    spread = jnp.mean(centred * centred, axis=-1, keepdims=True)
+    factor = lax.rsqrt(spread + eps)
+    return centred * factor, factor
+
+
+def normed_rows(value, vectors):
+    normal, _ = normalize(value)
+    return (normal * vectors[1:2] + vectors[2:3]).astype(bf16)
+
+
+def first_norm_kernel(x, vectors, out):
+    out[...] = normed_rows(x[...].astype(f32), vectors)
+
+
+def first_norm(x, vectors):
+    rows, width = x.shape
+    tile = rows // 4
+    return pl.pallas_call(
+        first_norm_kernel,
+        grid=(rows // tile,),
+        in_specs=[pl.BlockSpec((tile, width), lambda i: (i, 0)), fixed(vectors.shape)],
+        out_specs=pl.BlockSpec((tile, width), lambda i: (i, 0)),
+        out_shape=jax.ShapeDtypeStruct((rows, width), bf16),
+        name="first_norm",
+    )(x, vectors)
+
+
+def eight_rows(*rows):
+    return jnp.concatenate([jnp.stack(rows), jnp.zeros((8 - len(rows), rows[0].shape[-1]), f32)])
+
+
+def mix_kernel(counts, *refs):
+    heads, weights = refs[: counts[0]], refs[counts[0] : sum(counts)]
+    x, vectors, out, normed = refs[sum(counts) :]
+    left = jnp.concatenate([ref[...] for ref in heads], axis=1) if len(heads) > 1 else heads[0][...]
+    total = x[...].astype(f32) + vectors[0:1] + dot_nn(left, joined(weights, 0))
+    out[...] = total
+    normed[...] = normed_rows(total, vectors)
+
+
+def mix(x, heads, pieces, vectors):
+    rows, width = x.shape
+    tile = rows // 2
+    return pl.pallas_call(
+        partial(mix_kernel, (len(heads), len(pieces))),
+        grid=(rows // tile,),
+        in_specs=[pl.BlockSpec((tile, h.shape[1]), lambda i: (i, 0)) for h in heads]
+        + [pl.BlockSpec((1,) + p.shape[1:], lambda i: (3, 0, 0), pipeline_mode=pl.Buffered(1)) for p in pieces]
+        + [pl.BlockSpec((tile, width), lambda i: (i, 0)), fixed(vectors.shape)],
+        out_specs=[pl.BlockSpec((tile, width), lambda i: (i, 0))] * 2,
+        out_shape=[jax.ShapeDtypeStruct((rows, width), f32), jax.ShapeDtypeStruct((rows, width), bf16)],
+        cost_estimate=pl.CostEstimate(flops=2 * rows * width * width, bytes_accessed=14 * rows * width, transcendentals=0),
+        compiler_params=pltpu.CompilerParams(vmem_limit_bytes=40 * MIB),
+        name="mix",
+    )(*heads, *pieces, x, vectors)
+
+
+STEPS = 8
+GELU_A = 0.7978845608028654
+GELU_B = 0.044715
+
+
+def share_specs(pieces, steps):
+    specs = [pl.BlockSpec((2, 2, pieces[0].shape[2] // steps, pieces[0].shape[3]), lambda i, m: (0, 0, i, 0))]
+    for piece in pieces[1:]:
+        specs.append(pl.BlockSpec((2, piece.shape[1] // steps, piece.shape[2]), lambda i, m: (0, i, 0)))
+    return specs
+
+
+def share(refs, matrix, core):
+    own = refs[0]
+    return jnp.concatenate([own[matrix, core], own[matrix, 1 - core]] + [ref[matrix] for ref in refs[1:]], axis=0)
+
+
+def feed_kernel(meta, middle, after, vectors, bias, own, near, near_too, far, far_too, pre, hidden, out, normed, total):
+    core = meta[0]
+    step = pl.program_id(0)
+    refs = (own, near, near_too, far, far_too)
+    up, down = share(refs, 0, core), share(refs, 1, core)
+    units = up.shape[0]
+    parts = []
+    count = max(units // 256, 1)
+    size = units // count
+    for n in range(count):
+        at = slice(n * size, (n + 1) * size)
+        u = dot_nt(middle[...], up[at]) + bias[0, 0:1, at]
+        pre[0, :, at] = u.astype(bf16)
+        h = (0.5 * u * (1.0 + jnp.tanh(GELU_A * (u + GELU_B * u * u * u)))).astype(bf16)
+        hidden[0, :, at] = h
+        parts.append(dot_nn(h, down[at]))
+    term = parts[0]
+    for part in parts[1:]:
+        term = term + part
+
+    @pl.when(step == 0)
+    def _():
+        total[...] = term
+
+    @pl.when(step > 0)
+    def _():
+        total[...] += term
+
+    @pl.when(step == pl.num_programs(0) - 1)
+    def _():
+        tile = total.shape[0] // 4
+        for n in range(4):
+            at = slice(n * tile, (n + 1) * tile)
+            value = (total[at] + after[at] + vectors[0:1]).astype(bf16)
+            out[at] = value
+            normed[at] = normed_rows(value.astype(f32), vectors)
+
+
+def feed(meta, middle, after, vectors, bias, pieces):
+    rows, width = middle.shape
+    units = 4 * pieces[1].shape[1]
+    steps = STEPS
+    wide = units // steps
+    return pl.pallas_call(
+        feed_kernel,
+        grid_spec=pltpu.PrefetchScalarGridSpec(
+            num_scalar_prefetch=1,
+            grid=(steps,),
+            in_specs=[fixed(middle.shape), fixed(after.shape), fixed(vectors.shape), pl.BlockSpec((1, 1, wide), lambda i, m: (i, 0, 0))]
+            + share_specs(pieces, steps),
+            out_specs=[pl.BlockSpec((1, rows, wide), lambda i, m: (i, 0, 0))] * 2 + [pl.BlockSpec((rows, width), lambda i, m: (0, 0))] * 2,
+            scratch_shapes=[pltpu.VMEM((rows, width), f32)],
+        ),
+        out_shape=[jax.ShapeDtypeStruct((steps, rows, wide), bf16)] * 2 + [jax.ShapeDtypeStruct((rows, width), bf16)] * 2,
+        cost_estimate=pl.CostEstimate(
+            flops=4 * rows * width * units, bytes_accessed=4 * units * (rows + width) + 10 * rows * width, transcendentals=rows * units
+        ),
+        compiler_params=pltpu.CompilerParams(vmem_limit_bytes=52 * MIB),
+        name="feed",
+    )(meta, middle, after, vectors, bias, *pieces)
+
+
+def norm_back_rows(total, value, above, gain):
+    normal, factor = normalize(value)
+    scaled = total * gain
+    first = jnp.mean(scaled, axis=-1, keepdims=True)
+    second = jnp.mean(scaled * normal, axis=-1, keepdims=True)
+    return above + factor * (scaled - first - normal * second), normal
+
+
+def norm_back_all(total, value, above, gain, out, low, sums):
+    tile = total.shape[0] // 4
+    rows = []
+    for n in range(4):
+        at = slice(n * tile, (n + 1) * tile)
+        part = total[at]
+        top = above[at].astype(f32)
+        grad, normal = norm_back_rows(part, value[at].astype(f32), top, gain)
+        if out is not None:
+            out[at] = grad
+        low[at] = grad.astype(bf16)
+        rows.append([jnp.sum(v, axis=0, keepdims=True) for v in (part * normal, part, grad, top)])
+    for n in range(4):
+        sums[n : n + 1] = rows[0][n] + rows[1][n] + rows[2][n] + rows[3][n]
+
+
+def feed_back_kernel(
+    meta, above, middle, after, vectors, pre, hidden, own, near, near_too, far, far_too, keep, send, bias_sums, out, low, sums, total
+):
+    core = meta[0]
+    step = pl.program_id(0)
+    refs = (own, near, near_too, far, far_too)
+    up, down = share(refs, 0, core), share(refs, 1, core)
+    u = pre[0].astype(f32)
+    inner = GELU_A * (u + GELU_B * u * u * u)
+    t = jnp.tanh(inner)
+    slope = 0.5 * (1.0 + t) + 0.5 * u * (1.0 - t * t) * (GELU_A * (1.0 + 3.0 * GELU_B * u * u))
+    grad = dot_nt(above[...], down) * slope
+    low_grad = grad.astype(bf16)
+    bias_sums[0] = jnp.broadcast_to(jnp.sum(low_grad.astype(f32), axis=0, keepdims=True), bias_sums.shape[1:])
+    term = dot_nn(low_grad, up)
+
+    @pl.when(step == 0)
+    def _():
+        total[...] = term
+
+    @pl.when(step > 0)
+    def _():
+        total[...] += term
+
+    grads = (dot_tn(low_grad, middle[...]).astype(bf16), dot_tn(hidden[0], above[...]).astype(bf16))
+    part = up.shape[0] // 8
+    for n, value in enumerate(grads):
+        keep[n, 0, 0 : 2 * part] = value[2 * part : 4 * part]
+        keep[n, 0, 2 * part : 3 * part] = value[6 * part : 7 * part]
+        keep[n, 0, 3 * part :] = value[0:part]
+        send[n, 0, 0 : 2 * part] = value[4 * part : 6 * part]
+        send[n, 0, 2 * part : 3 * part] = value[7 * part :]
+        send[n, 0, 3 * part :] = value[part : 2 * part]
+
+    @pl.when(step == pl.num_programs(0) - 1)
+    def _():
+        norm_back_all(total, after, above, vectors[0:1], out, low, sums)
+
+
+def feed_back(meta, above, middle, after, gain, pre, hidden, pieces):
+    rows, width = middle.shape
+    units = 4 * pieces[1].shape[1]
+    steps = STEPS
+    wide = units // steps
+    vectors = jnp.broadcast_to(gain[None], (8, width))
+    per_step = pl.BlockSpec((1, rows, wide), lambda i, m: (i, 0, 0))
+    grads = pl.BlockSpec((2, 1, wide // 2, width), lambda i, m: (0, i, 0, 0))
+    whole = pl.BlockSpec((rows, width), lambda i, m: (0, 0))
+    return pl.pallas_call(
+        feed_back_kernel,
+        grid_spec=pltpu.PrefetchScalarGridSpec(
+            num_scalar_prefetch=1,
+            grid=(steps,),
+            in_specs=[fixed(above.shape), fixed(middle.shape), fixed(after.shape), fixed(vectors.shape), per_step, per_step]
+            + share_specs(pieces, steps),
+            out_specs=[grads, grads, pl.BlockSpec((1, 8, wide), lambda i, m: (i, 0, 0)), whole, whole, pl.BlockSpec((8, width), lambda i, m: (0, 0))],
+            scratch_shapes=[pltpu.VMEM((rows, width), f32)],
+        ),
+        out_shape=[jax.ShapeDtypeStruct((2, steps, wide // 2, width), bf16)] * 2
+        + [
+            jax.ShapeDtypeStruct((steps, 8, wide), f32),
+            jax.ShapeDtypeStruct((rows, width), f32),
+            jax.ShapeDtypeStruct((rows, width), bf16),
+            jax.ShapeDtypeStruct((8, width), f32),
+        ],
+        cost_estimate=pl.CostEstimate(
+            flops=8 * rows * width * units, bytes_accessed=12 * units * (rows + width) + 14 * rows * width, transcendentals=rows * units
+        ),
+        compiler_params=pltpu.CompilerParams(vmem_limit_bytes=58 * MIB),
+        name="feed_back",
+    )(meta, above, middle, after, vectors, pre, hidden, *pieces)
+
+
+def heads_back_kernel(count, low, *refs):
+    pieces, out = refs[:count], refs[count]
+    out[...] = dot_nt(low[...], joined(pieces, 0)).astype(bf16)
+
+
+def heads_back(low, pieces):
+    rows, width = low.shape
+    columns = sum(piece.shape[1] for piece in pieces)
+    tile = rows // 2
+    return pl.pallas_call(
+        partial(heads_back_kernel, len(pieces)),
+        grid=(rows // tile,),
+        in_specs=[pl.BlockSpec((tile, width), lambda i: (i, 0))]
+        + [pl.BlockSpec((1,) + p.shape[1:], lambda i: (3, 0, 0), pipeline_mode=pl.Buffered(1)) for p in pieces],
+        out_specs=pl.BlockSpec((tile, columns), lambda i: (i, 0)),
+        out_shape=jax.ShapeDtypeStruct((rows, columns), bf16),
+        cost_estimate=pl.CostEstimate(
+            flops=2 * rows * width * columns, bytes_accessed=2 * (rows * width + width * columns + rows * columns), transcendentals=0
+        ),
+        compiler_params=pltpu.CompilerParams(vmem_limit_bytes=40 * MIB),
+        name="heads_back",
+    )(low, *pieces)
+
+
+def project_back_kernel(groups, first, last, meta, *refs):
+    refs = list(refs)
+    take = lambda n: [refs.pop(0) for _ in range(n)]
+    dq, dkv, dkv_got, o, a, low = take(6)
+    pieces = take(len(groups))
+    so_far = None if first else refs.pop(0)
+    if last:
+        value, above, vectors = take(3)
+    keep, send, bias_sums = take(3)
+    outs = take(2) if last else take(1)
+    lefts, flipped = take(2)
+    total = refs.pop(0) if last else None
+    step = pl.program_id(0)
+    core = meta[0]
+
+    @pl.when(step == 0)
+    def _():
+        lefts[0] = dq[...]
+        for n in range(2):
+            lefts[1 + n] = (dkv[n].astype(f32) + dkv_got[n].astype(f32)).astype(bf16)
+        for n in range(3):
+            flipped[n] = lefts[n].T
+        flipped[3] = o[...].T
+        for n, c in enumerate((0, 2)):
+            bias_sums[n : n + 1] = jnp.sum(lefts[c].astype(f32), axis=0, keepdims=True)
+
+    for c in range(4):
+        value_c = dot_nn(flipped[c], (low if c == 3 else a)[...]).astype(bf16)
+        keep_at = send_at = at = 0
+        for name, size in groups:
+            if name == "own":
+                half = size // 2
+                keep[c, keep_at : keep_at + half] = jnp.where(core == 0, value_c[at : at + half], value_c[at + half : at + size])
+                send[c, send_at : send_at + half] = jnp.where(core == 0, value_c[at + half : at + size], value_c[at : at + half])
+                keep_at, send_at = keep_at + half, send_at + half
+            elif name in ("near", "far"):
+                keep[c, keep_at : keep_at + size] = value_c[at : at + size]
+                keep_at += size
+            else:
+                send[c, send_at : send_at + size] = value_c[at : at + size]
+                send_at += size
+            at += size
+    term = None
+    for c in range(3):
+        part = dot_nn(lefts[c], joined(pieces, c))
+        term = part if term is None else term + part
+    if not first:
+        term = term + so_far[...]
+    if not last:
+        outs[0][...] = term
+        return
+    tile = total.shape[1] // pl.num_programs(0) if isinstance(pl.num_programs(0), int) else term.shape[1]
+    total[:, pl.ds(pl.multiple_of(step * tile, tile), tile)] = term
+
+    @pl.when(step == pl.num_programs(0) - 1)
+    def _():
+        norm_back_all(total, value, above, vectors[0:1], None, outs[0], outs[1])
+
+
+def project_back(meta, names, dq, dkv, dkv_got, o, a, low, pieces, so_far, norm):
+    rows, width = a.shape
+    columns = dq.shape[1]
+    groups = [(name, piece.shape[1]) for name, piece in zip(names, pieces)]
+    tiles = 4
+    tile = width // tiles
+    slim = pl.BlockSpec((rows, tile), lambda i, m: (0, i))
+    grads = pl.BlockSpec((4, columns // 2, tile), lambda i, m: (0, 0, i))
+    args = [dq, dkv, dkv_got, o, a, low, *pieces]
+    specs = [fixed(dq.shape), fixed(dkv.shape), fixed(dkv.shape), fixed(o.shape), slim, slim]
+    specs += [pl.BlockSpec((3, p.shape[1], tile), lambda i, m: (0, 0, i)) for p in pieces]
+    if so_far is not None:
+        args.append(so_far)
+        specs.append(slim)
+    out_specs = [grads, grads, pl.BlockSpec((8, columns), lambda i, m: (0, 0))]
+    out_shape = [jax.ShapeDtypeStruct((4, columns // 2, width), bf16)] * 2 + [jax.ShapeDtypeStruct((8, columns), f32)]
+    scratch = [pltpu.VMEM((3, rows, columns), bf16), pltpu.VMEM((4, columns, rows), bf16)]
+    if norm is None:
+        out_specs.append(slim)
+        out_shape.append(jax.ShapeDtypeStruct((rows, width), f32))
+    else:
+        value, above, gain = norm
+        args += [value, above, jnp.broadcast_to(gain[None], (8, width))]
+        specs += [fixed(value.shape), fixed(above.shape), fixed((8, width))]
+        out_specs += [pl.BlockSpec((rows, width), lambda i, m: (0, 0)), pl.BlockSpec((8, width), lambda i, m: (0, 0))]
+        out_shape += [jax.ShapeDtypeStruct((rows, width), bf16), jax.ShapeDtypeStruct((8, width), f32)]
+        scratch.append(pltpu.VMEM((rows, width), f32))
+    return pl.pallas_call(
+        partial(project_back_kernel, groups, so_far is None, norm is not None),
+        grid_spec=pltpu.PrefetchScalarGridSpec(
+            num_scalar_prefetch=1, grid=(tiles,), in_specs=specs, out_specs=out_specs, scratch_shapes=scratch
+        ),
+        out_shape=out_shape,
+        cost_estimate=pl.CostEstimate(
+            flops=14 * rows * width * columns, bytes_accessed=2 * (6 * rows * columns + 7 * width * columns + 6 * rows * width), transcendentals=0
+        ),
+        compiler_params=pltpu.CompilerParams(vmem_limit_bytes=58 * MIB),
+        name="project_back",
+    )(meta, *args)
+
+
+def gathered(own, core):
+    near = hop(own, FIRST_HOP)
+    near_too = swap(near)
+    far = hop(half_of(near, 1, core), SECOND_HOP)
+    far_too = swap(far)
+    return {"own": own, "near": near, "near_too": near_too, "far": far, "far_too": far_too}
+
+
+def plus(*values):
+    total = values[0].astype(f32)
+    for value in values[1:]:
+        total = total + value.astype(f32)
+    return total.astype(bf16)
+
+
+def summed(near, far, own, core):
+    relayed = hop(far, SECOND_HOP)
+    matrices, units, width = near.shape
+    place_of_half = jnp.arange(2)[None, :, None, None] == core
+    near = near.reshape(matrices, 2, units // 2, width)
+    near = plus(near, jnp.where(place_of_half, relayed[:, None], jnp.zeros((), bf16)))
+    got = hop(near.reshape(matrices, units, width), FIRST_HOP)
+    total = plus(own, half_of(got, 1, core), swap(half_of(got, 1, 1 - core)))
+    return lax.psum(total, "dp")
+
+
+def in_order(own, near, near_too, far, far_too, core, chip):
+    first = core == 0
+    last = jnp.concatenate([jnp.where(first, far, far_too), jnp.where(first, far_too, far)], axis=-1)
+    by_distance = jnp.stack([own, jnp.where(first, near, near_too), jnp.where(first, near_too, near), last])
+    rows = [lax.dynamic_index_in_dim(by_distance, quarter ^ chip, 0, keepdims=False) for quarter in CHIPS]
+    return jnp.concatenate(rows, axis=-1)
+
+
+PIECES = ("own", "near", "near_too", "far", "far_too")
+GROUPS = ((("own",), ("near", "near_too"), ("far", "far_too")), (PIECES,))
+
+
+def on_row(
+    ends_in, lengths, ln_gains, ln_biases, w_qkv, qv_bias, w_out, w_up, up_bias, w_down, out_biases
+):
+    core = lax.axis_index("section")
+    chip = lax.axis_index("tensor")
+    first_core = core == 0
+    micro, rows_here, seg = ends_in.shape[1:4]
+    ends = ends_in.reshape(micro * rows_here, seg, D)
+    lo_segment, hi_segment = core, 3 - core
+    n_qv = qv_bias.shape[-1]
+    n_up = up_bias.shape[-1]
+
+    def row_from(section):
+        got = [
+            hop(
+                lax.dynamic_index_in_dim(ends, chip ^ k, 0, keepdims=False),
+                [(place(section, t), place(core_of(t), t ^ k)) for t in CHIPS],
+            )
+            for k in CHIPS
+        ]
+
+        def pick(k):
+            return jnp.where(k == 0, got[0], jnp.where(k == 1, got[1], jnp.where(k == 2, got[2], got[3])))
+
+        return jnp.concatenate([pick(chip ^ lo_segment), pick(chip ^ hi_segment)])
+
+    def row_to(section, row):
+        got = []
+        for k in CHIPS:
+            segment = chip ^ k
+            sent = jnp.where(segment == lo_segment, row[:seg], row[seg:])
+            got.append(hop(sent, [(place(core_of(t), t ^ k), place(section, t)) for t in CHIPS]))
+        return got
+
+    def both(mine):
+        theirs = swap(mine)
+        return (jnp.where(first_core, mine, theirs), jnp.where(first_core, theirs, mine))
+
+    vectors = jnp.concatenate(
+        [ln_gains[0].reshape(-1), ln_biases[0].reshape(-1), out_biases[0].reshape(-1), qv_bias[0].reshape(-1), up_bias[0]]
+    )
+    vectors = both(vectors[None])
+    x = row_from(0)
+    attention_own = both(jnp.concatenate([jnp.swapaxes(w_qkv[0], 1, 2), w_out]))
+    feed_own = both(jnp.concatenate([w_up[0].T[None], w_down]))
+    biases = jnp.concatenate([v[:, 6 * D :] for v in vectors])
+    near = hop(biases, FIRST_HOP)
+    far = hop(near, SECOND_HOP)
+    bias_quarters = {"own": biases, "near": near, "near_too": swap(near), "far": far, "far_too": far}
+
+    def bias_of(name, layer, start, size):
+        part = bias_quarters[name][layer, start : start + size]
+        if name == "far":
+            part = half_of(part, 0, core)
+        if name == "far_too":
+            part = half_of(part, 0, 1 - core)
+        return part
+
+    weights = []
+    for layer in range(2):
+        own_bias = bias_quarters["own"][layer, 2 * n_qv :]
+        shares = [half_of(own_bias, 0, core), half_of(own_bias, 0, 1 - core)]
+        shares += [bias_of(name, layer, 2 * n_qv, n_up) for name in PIECES[1:]]
+        six = vectors[layer][0, : 6 * D].reshape(6, D)
+        attention, feeding = gathered(attention_own[layer], core), gathered(feed_own[layer], core)
+        feeding["own"] = feeding["own"].reshape(2, 2, -1, D)
+        weights.append(
+            dict(
+                gains=six[0:2],
+                shifts=six[2:4],
+                ends=six[4:6],
+                attention=attention,
+                feed=[feeding[name] for name in PIECES],
+                feed_bias=jnp.concatenate([part.reshape(STEPS, -1) for part in shares], axis=1)[:, None],
+            )
+        )
+
+    length = lax.dynamic_index_in_dim(lengths.reshape(-1), chip, 0, keepdims=False)
+    segments = jnp.stack([lo_segment, hi_segment, 1 - core, 2 + core])
+    positions = (segments[:, None] * seg + jnp.arange(seg)[None]).reshape(-1)
+    kcol = key_columns(positions, length)
+    heads_here = n_qv // HEAD
+    quarters = {"own": chip, "near": chip ^ (1 + core), "near_too": chip ^ (2 - core), "far": chip ^ 3, "far_too": chip ^ 3}
+    pairs_of = {name: n_qv // 128 // (2 if name.startswith("far") else 1) for name in PIECES}
+    across = {"own": "own", "near": "near_too", "near_too": "near", "far": "far_too", "far_too": "far"}
+
+    def head_slopes(name):
+        head = quarters[name] * heads_here + jnp.arange(heads_here)
+        if name == "far":
+            head = half_of(head, 0, core)
+        if name == "far_too":
+            head = half_of(head, 0, 1 - core)
+        return jnp.exp2(-8.0 * (head + 1).astype(f32) / HEADS)
+
+    slopes = {name: head_slopes(name) for name in PIECES}
+
+    def group_meta(names):
+        starts, at = {}, 0
+        for name in names:
+            starts[name] = at
+            at += pairs_of[name]
+        table = [starts[across[name]] + n for name in names for n in range(pairs_of[name])]
+        return jnp.concatenate([core[None].astype(jnp.int32), jnp.array(table, jnp.int32)])
+
+    groups = [
+        [
+            dict(
+                names=names,
+                meta=group_meta(names),
+                qcol=query_columns(jnp.concatenate([slopes[name] for name in names])),
+                pieces=[weights[layer]["attention"][name] for name in names],
+                bias=jnp.stack(
+                    [
+                        jnp.concatenate([bias_of(name, layer, 0, n_qv) for name in names]),
+                        jnp.zeros((sum(pairs_of[name] for name in names) * 128,), f32),
+                        jnp.concatenate([bias_of(name, layer, n_qv, n_qv) for name in names]),
+                    ]
+                )[:, None],
+            )
+            for names in GROUPS[layer]
+        ]
+        for layer in range(2)
+    ]
+    meta = core[None].astype(jnp.int32)
+
+    kept = []
+    normed = first_norm(x, eight_rows(jnp.zeros((D,), f32), weights[0]["gains"][0], weights[0]["shifts"][0]))
+    for layer in range(2):
+        w = weights[layer]
+        saved = []
+        for group in groups[layer]:
+            q, kv = project_heads(normed, group["pieces"], group["bias"])
+            kvo = swap(kv)
+            o, qx = attend(group["meta"], q, kv, kvo, kcol, group["qcol"])
+            saved.append((q, kv, kvo, o, qx))
+        after, middle = mix(
+            x,
+            [s[3] for s in saved],
+            [p for group in groups[layer] for p in group["pieces"]],
+            eight_rows(w["ends"][0], w["gains"][1], w["shifts"][1]),
+        )
+        following = weights[min(layer + 1, 1)]
+        pre, hidden, result, normed_next = feed(
+            meta, middle, after, eight_rows(w["ends"][1], following["gains"][0], following["shifts"][0]), w["feed_bias"], w["feed"]
+        )
+        kept.append((x, normed, saved, after, middle, pre, hidden))
+        x, normed = result, normed_next
+
+    sent_back = row_to(1, x)
+    grad = row_from(1)
+
+    matrices, vector_sums = [None, None], [None, None]
+    for layer in (1, 0):
+        w = weights[layer]
+        x_in, normed, saved, after, middle, pre, hidden = kept[layer]
+        keep, send, unit_sums, grad_after, low, sums_two = feed_back(
+            meta, grad, middle, after, w["gains"][1], pre, hidden, w["feed"]
+        )
+        total = plus(keep, swap(send))
+        part = total.shape[2] // 4
+        feed_grads = summed(
+            total[:, :, : 2 * part].reshape(2, -1, D), total[:, :, 2 * part : 3 * part].reshape(2, -1, D), total[:, :, 3 * part :].reshape(2, -1, D), core
+        )
+        so_far = None
+        sums_of, kept_rows = {}, {}
+        order = list(reversed(range(len(groups[layer]))))
+        for index in order:
+            group = groups[layer][index]
+            q, kv, kvo, o, qx = saved[index]
+            grad_heads = heads_back(low, group["pieces"])
+            dq, dkv, dkvo = attend_back(group["meta"], q, kv, kvo, kcol, qx, grad_heads, o)
+            got = swap(dkvo)
+            last = index == order[-1]
+            norm = (x_in, grad_after, w["gains"][0]) if last else None
+            results = project_back(meta, group["names"], dq, dkv, got, o, normed, low, group["pieces"], so_far, norm)
+            keep, send, bias_sums = results[:3]
+            if last:
+                grad, sums_one = results[3:]
+            else:
+                so_far = results[3]
+            total = plus(keep, swap(send))
+            at = at_kept = 0
+            for name in group["names"]:
+                size = pairs_of[name] * 128
+                sums_of[name] = bias_sums[0:2, at : at + size]
+                at += size
+                if not name.endswith("_too"):
+                    size = size // 2 if name == "own" else size
+                    kept_rows[name] = total[:, at_kept : at_kept + size]
+                    at_kept += size
+        attention_grads = summed(kept_rows["near"], kept_rows["far"], kept_rows["own"], core)
+        matrices[layer] = (attention_grads, feed_grads)
+        unit_sums = unit_sums[:, 0]
+        part = unit_sums.shape[1] // 8
+
+        def unit_part(start, count):
+            return unit_sums[:, start * part : (start + count) * part].reshape(-1)
+
+        own_keep, own_send = unit_part(0, 1), unit_part(1, 1)
+        own = jnp.concatenate([jnp.where(first_core, own_keep, own_send), jnp.where(first_core, own_send, own_keep)])
+        flat = jnp.concatenate(
+            [
+                jnp.stack([sums_one[0], sums_two[0], sums_one[1], sums_two[1], sums_two[2], sums_two[3]]),
+                in_order(*[sums_of[name] for name in PIECES], core, chip),
+                in_order(own, unit_part(2, 2), unit_part(4, 2), unit_part(6, 1), unit_part(7, 1), core, chip).reshape(-1, D),
+            ]
+        )
+        vector_sums[layer] = lax.psum(flat, ("section", "dp", "tensor"))
+
+    first_rows = row_to(0, grad)
+
+    def rows_of(got):
+        return [
+            jnp.where(
+                row == chip, got[0], jnp.where(row == chip ^ 1, got[1], jnp.where(row == chip ^ 2, got[2], got[3]))
+            )
+            for row in CHIPS
+        ]
+
+    ends_out = jnp.stack([jnp.where(first_core, a, b) for a, b in zip(rows_of(first_rows), rows_of(sent_back))])
+    ends_out = ends_out.astype(f32).reshape(1, micro, rows_here, seg, D)
+
+    def finished(lower, upper):
+        to_upper = lax.ppermute(upper, "section", [(0, 1)])
+        to_lower = lax.ppermute(lower, "section", [(1, 0)])
+        return jnp.where(
+            first_core,
+            jnp.concatenate([lower, to_lower], axis=1),
+            jnp.concatenate([to_upper, upper], axis=1),
+        ).astype(f32)
+
+    attention_grads, feed_grads = (finished(a, b) for a, b in zip(*matrices))
+    sums = jnp.where(first_core, vector_sums[0], vector_sums[1])
+    grad_qv = lax.dynamic_slice_in_dim(sums[6:8], chip * n_qv, n_qv, 1)[None]
+    grad_up_bias = lax.dynamic_slice_in_dim(sums[8:].reshape(-1), chip * n_up, n_up, 0)[None]
+    return (
+        ends_out,
+        sums[0:2][None],
+        sums[2:4][None],
+        jnp.swapaxes(attention_grads[:3], 1, 2)[None],
+        grad_qv,
+        attention_grads[3:],
+        feed_grads[0].T[None],
+        grad_up_bias,
+        feed_grads[1:],
+        sums[4:6][None],
+    )
+
+
 def solution(mesh):
     return jax.shard_map(
-        on_device,
+        on_row if one_row_a_chip(mesh) else on_device,
         mesh=mesh,
         in_specs=(
             P("section", None, "dp", "tensor", None),

time: 6360 us -> 1400 us (0.22)
  waiting for transfers between devices: 2840 us -> 533 us
  matrix products: 1960 us -> 0 us
  other arithmetic: 1130 us -> 100 us
  Pallas kernels: 0 us -> 541 us
  local copies, waits for them, and re-layouts: 237 us -> 101 us
  blocking collectives: 89.2 us -> 0 us
  starting transfers between devices: 16.1 us -> 102 us
    dot_general x123 -> x0, matrix products: 1960 us -> none  [the longest x24 603 us: score_block(): jnp.einsum('rqhd,rkhd->rhqk', query_block, key_heads, preferred_element_t...]
    all_gather x18 -> x0, waiting for transfers between devices: 1430 us -> none  [the longest x12 995 us: gather_tokens(): return lax.all_gather(values, 'tensor', axis=1, tiled=True)]
    reduce_scatter x12 -> x0, waiting for transfers between devices: 1290 us -> none  [the longest x6 922 us: scatter_tokens(): return lax.psum_scatter(values, 'tensor', scatter_dimension=1, tiled=True)]
    pallas_call x0 -> x27, Pallas kernels: none -> 541 us  [the longest x4 136 us: attend_back(): pl.pallas_call(partial(attend_back_kernel, seg), grid_spec=pltpu.Prefetch...]
    convert_element_type x73 -> x26, other arithmetic: 439 us -> 62.1 us  [the longest x10 51.7 us: plus(): return total.astype(bf16)]
    reduce_sum x54 -> x0, other arithmetic: 337 us -> none  [the longest x12 226 us: one_block(): row_total = jnp.sum(powers, axis=-1, keepdims=True)]
    ppermute x6 -> x68, waiting for transfers between devices: 0.02 us -> 234 us  [the longest x34 221 us: hop(): return lax.ppermute(value, ST, pairs)]
    mul x30 -> x1, other arithmetic: 196 us -> 0.08 us  [on_row(): positions = (segments[:, None] * seg + jnp.arange(seg)[None]).reshape(-1)]
  transfers between devices with their start and end apart: 37 -> 70, of which waited for: 31 -> 14; matrix products, arithmetic and copies ran while one was open for 6% -> 10% of each run, Pallas kernels for 0% -> 27%
where the time goes in v1:
time: 1400 us; the launch traced here: 1390 us
  Pallas kernels  541 us (39%)
  waiting for transfers between devices  533 us (38%)
  starting transfers between devices  102 us (7%)
  local copies, waits for them, and re-layouts  101 us (7%)
  other arithmetic  100 us (7%)
  between operations  16.3 us (1%)
    psum x1, waiting for transfers between devices, summed(): return lax.psum(total, 'dp')  223 us
    ppermute x34, waiting for transfers between devices, hop(): return lax.ppermute(value, ST, pairs)  221 us
    pallas_call x4, Pallas kernels, attend_back(): pl.pallas_call(partial(attend_back_kernel, seg), grid_spec=pltpu.Prefetch...  136 us
    pallas_call x2, Pallas kernels, feed_back(): pl.pallas_call(feed_back_kernel, grid_spec=pltpu.PrefetchScalarGridSpec(n...  124 us
    pallas_call x4, Pallas kernels, attend(): pl.pallas_call(partial(attend_kernel, seg), grid_spec=pltpu.PrefetchScala...  92.1 us
    psum x1, waiting for transfers between devices, on_row(): vector_sums[layer] = lax.psum(flat, ('section', 'dp', 'tensor'))  75.4 us
    ppermute x34, starting transfers between devices, hop(): return lax.ppermute(value, ST, pairs)  74.8 us
    pallas_call x4, Pallas kernels, project_back(): pl.pallas_call(partial(project_back_kernel, groups, so_far is None, norm...  73.2 us
  transfers between devices with their start and end apart: 70, of which 14 were waited for; matrix products, arithmetic and copies ran while one was open for 10% of the time, Pallas kernels for 27%

profile of v1, /device:TPU:0, one launch (start us, length us, event | category | flops | bytes accessed | tf_op | source)
XLA Modules:
  0.0 1392.8 jit_solution(8290527167377638660)
XLA Ops:
  7.3 4.3 dynamic-slice_bitcast_fusion
  11.7 9.5 collective-permute-start
  42.1 5.5 broadcast_select_fusion
  54.7 64.2 %collective-permute-done.9 = f32[2,1536]{1,0:T(2,128)S(1)} collective-permute-done((f32[2,1536]{1,0:T(2,128)S(1)}, f32[2,1536]{1,0:T(2,128)S(1)}, u32[]{:S(2)}, u32[]{:S(2)}) %collective-permute-start.9) | collective-permute-done | bytes 12320 | tf_op jit(solution)/shard_map/ppermute | solution.py:385
  138.5 42.9 %collective-permute-done.12.refs_0_.refs_6_ = bf16[4,128,1024]{2,1,0:T(8,128)(2,1)S(1)} collective-permute-done((bf16[4,128,1024]{2,1,0:T(8,128)(2,1)S(1)}, bf16[4,128,1024]{2,1,0:T(8,128)(2,1)S(1)}, u32[]{:S(2)}, u32[]{:S(2)}) %collective-permute-start.12) | collective-permute-done | bytes 1048608 | tf_op jit(solution)/shard_map/ppermute | solution.py:385
  187.5 4.5 first_norm.1.a.refs_4_
  197.2 6.4 project.5
  217.7 11.5 attend.4
  231.2 12.7 attend.6
  245.3 22.9 %attend.5 = (bf16[1024,512]{1,0:T(8,128)(2,1)S(1)}, bf16[1024,512]{1,0:T(8,128)(2,1)S(1)}) custom-call(s32[5]{0:T(128)S(1)} %pad_add_fusion.2.meta, bf16[1024,512]{1,0:T(8,128)(2,1)S(1)} %copy-done.46, bf16[2,1024,512]{2,1,0:T(8,128)(2,1)} %get-tuple-element.84.kv, bf16[2,1024,512]{2,1,0:T(8,128)(2,1)} %collective-permute-done.11.kvo, ...), custom_call_target="tpu_custom_call" | custom-call | flops 10737418240 | bytes 7340032 | tf_op jit(solution)/shard_map/attend/pallas_call | solution.py:508
  269.2 6.8 mix.2
  278.6 31.9 %feed.2 = (bf16[8,1024,512]{2,1,0:T(8,128)(2,1)}, bf16[8,1024,512]{2,1,0:T(8,128)(2,1)}, bf16[1024,1024]{1,0:T(8,128)(2,1)}, bf16[1024,1024]{1,0:T(8,128)(2,1)}) custom-call(s32[1]{0:T(128)} %bitcast.meta, bf16[1024,1024]{1,0:T(8,128)(2,1)} %copy-done.32, f32[1024,1024]{1,0:T(8,128)} %get-tuple-element.90.after, f32[8,1024]{1,0:T(8,128)S(1)} %get-tuple-element.321.vectors, ...), custom_call_target="tpu_custom_call" | custom-call | flops 17179869184 | bytes 44040192 | tf_op jit(solution)/shard_map/feed/pallas_call | solution.py:799
  313.3 10.1 project.7
  331.7 9.0 collective-permute-start.31
  344.5 33.3 %collective-permute-done.29 = bf16[512,1024]{1,0:T(8,128)(2,1)} collective-permute-done((bf16[512,1024]{1,0:T(8,128)(2,1)}, bf16[512,1024]{1,0:T(8,128)(2,1)}, u32[]{:S(2)}, u32[]{:S(2)}) %collective-permute-start.29) | collective-permute-done | bytes 1048608 | tf_op jit(solution)/shard_map/ppermute | solution.py:385
  383.3 45.0 %attend.7 = (bf16[1024,1024]{1,0:T(8,128)(2,1)S(1)}, bf16[1024,1024]{1,0:T(8,128)(2,1)S(1)}) custom-call(s32[9]{0:T(128)S(1)} %pad_add_fusion.1.meta, bf16[1024,1024]{1,0:T(8,128)(2,1)S(1)} %copy-done.52, bf16[2,1024,1024]{2,1,0:T(8,128)(2,1)S(1)} %copy-done.31, bf16[2,1024,1024]{2,1,0:T(8,128)(2,1)} %collective-permute-done.25.kvo, ...), custom_call_target="tpu_custom_call" | custom-call | flops 21474836480 | bytes 14680064 | tf_op jit(solution)/shard_map/attend/pallas_call | solution.py:508
  428.3 7.3 mix.3
  438.3 31.6 %feed.3 = (bf16[8,1024,512]{2,1,0:T(8,128)(2,1)}, bf16[8,1024,512]{2,1,0:T(8,128)(2,1)}, bf16[1024,1024]{1,0:T(8,128)(2,1)}, bf16[1024,1024]{1,0:T(8,128)(2,1)}) custom-call(s32[1]{0:T(128)} %bitcast.meta, bf16[1024,1024]{1,0:T(8,128)(2,1)} %copy-done.33, f32[1024,1024]{1,0:T(8,128)} %get-tuple-element.98.after, f32[8,1024]{1,0:T(8,128)S(1)} %get-tuple-element.320.vectors, ...), custom_call_target="tpu_custom_call" | custom-call | flops 17179869184 | bytes 44040192 | tf_op jit(solution)/shard_map/feed/pallas_call | solution.py:799
  470.4 62.2 %feed_back.2 = (bf16[2,8,256,1024]{3,2,1,0:T(8,128)(2,1)}, bf16[2,8,256,1024]{3,2,1,0:T(8,128)(2,1)}, f32[8,8,512]{2,1,0:T(8,128)}, f32[1024,1024]{1,0:T(8,128)}...) custom-call(s32[1]{0:T(128)} %bitcast.meta, bf16[1024,1024]{1,0:T(8,128)(2,1)} %pad_maximum_fusion.4.above, ...), custom_call_target="tpu_custom_call" | custom-call | flops 34359738368 | bytes 115343360 | tf_op jit(solution)/shard_map/feed_back/pallas_call | solution.py:890
  540.5 65.4 %attend_back.4 = (bf16[1024,1024]{1,0:T(8,128)(2,1)S(1)}, bf16[2,1024,1024]{2,1,0:T(8,128)(2,1)}, bf16[2,1024,1024]{2,1,0:T(8,128)(2,1)}) custom-call(s32[9]{0:T(128)S(1)} %pad_add_fusion.1.meta, bf16[1024,1024]{1,0:T(8,128)(2,1)S(1)} %copy-done.53, bf16[2,1024,1024]{2,1,0:T(8,128)(2,1)} %get-tuple-element.93.kv, ...), custom_call_target="tpu_custom_call" | custom-call | flops 53687091200 | bytes 27262976 | tf_op jit(solution)/shard_map/attend_back/pallas_call | solution.py:602
  607.9 7.0 collective-permute-done.34.refs_2_
  615.5 32.3 %project_back.4 = (bf16[4,512,1024]{2,1,0:T(8,128)(2,1)}, bf16[4,512,1024]{2,1,0:T(8,128)(2,1)}, f32[8,1024]{1,0:T(8,128)}, bf16[1024,1024]{1,0:T(8,128)(2,1)}, f32[8,1024]{1,0:T(8,128)}) custom-call(s32[1]{0:T(128)} %bitcast.meta, bf16[1024,1024]{1,0:T(8,128)(2,1)} %copy-done.54, bf16[2,1024,1024]{2,1,0:T(8,128)(2,1)} %get-tuple-element.103.refs_1_, ...), custom_call_target="tpu_custom_call" | custom-call | flops 15032385536 | bytes 39845888 | tf_op jit(solution)/shard_map/project_back/pallas_call | solution.py:1025
  648.4 62.3 %feed_back.3 = (bf16[2,8,256,1024]{3,2,1,0:T(8,128)(2,1)}, bf16[2,8,256,1024]{3,2,1,0:T(8,128)(2,1)}, f32[8,8,512]{2,1,0:T(8,128)}, f32[1024,1024]{1,0:T(8,128)}...) custom-call(s32[1]{0:T(128)} %bitcast.meta, bf16[1024,1024]{1,0:T(8,128)(2,1)} %get-tuple-element.106.above, ...), custom_call_target="tpu_custom_call" | custom-call | flops 34359738368 | bytes 115343360 | tf_op jit(solution)/shard_map/feed_back/pallas_call | solution.py:890
  718.8 34.3 %attend_back.6 = (bf16[1024,512]{1,0:T(8,128)(2,1)S(1)}, bf16[2,1024,512]{2,1,0:T(8,128)(2,1)}, bf16[2,1024,512]{2,1,0:T(8,128)(2,1)}) custom-call(s32[5]{0:T(128)S(1)} %pad_add_fusion.2.meta, bf16[1024,512]{1,0:T(8,128)(2,1)S(1)} %copy-done.47, bf16[2,1024,512]{2,1,0:T(8,128)(2,1)} %get-tuple-element.84.kv, ...), custom_call_target="tpu_custom_call" | custom-call | flops 26843545600 | bytes 13631488 | tf_op jit(solution)/shard_map/attend_back/pallas_call | solution.py:602
  755.4 9.3 add_convert_fusion
  769.4 4.8 collective-permute-start.64
  774.2 6.3 add_convert_fusion.1
  785.2 17.9 %attend_back.7 = (bf16[1024,256]{1,0:T(8,128)(2,1)S(1)}, bf16[2,1024,256]{2,1,0:T(8,128)(2,1)S(1)}, bf16[2,1024,256]{2,1,0:T(8,128)(2,1)S(1)}) custom-call(s32[3]{0:T(128)S(1)} %pad_add_fusion.3.meta, bf16[1024,256]{1,0:T(8,128)(2,1)S(1)} %copy-done.43, bf16[2,1024,256]{2,1,0:T(8,128)(2,1)} %get-tuple-element.87.kv, ...), custom_call_target="tpu_custom_call" | custom-call | flops 13421772800 | bytes 6815744 | tf_op jit(solution)/shard_map/attend_back/pallas_call | solution.py:602
  807.7 9.7 project_back.5
  822.0 6.4 fusion
  830.4 15.1 %project_back.6 = (bf16[4,256,1024]{2,1,0:T(8,128)(2,1)}, bf16[4,256,1024]{2,1,0:T(8,128)(2,1)}, f32[8,512]{1,0:T(8,128)}, f32[1024,1024]{1,0:T(8,128)}) custom-call(s32[1]{0:T(128)} %bitcast.meta, bf16[1024,512]{1,0:T(8,128)(2,1)} %copy-done.49, bf16[2,1024,512]{2,1,0:T(8,128)(2,1)} %get-tuple-element.115.refs_1_, ...), custom_call_target="tpu_custom_call" | custom-call | flops 7516192768 | bytes 26214400 | tf_op jit(solution)/shard_map/project_back/pallas_call | solution.py:1025
  849.3 5.7 add_convert_fusion.2
  856.6 18.4 %attend_back.5 = (bf16[1024,256]{1,0:T(8,128)(2,1)S(1)}, bf16[2,1024,256]{2,1,0:T(8,128)(2,1)S(1)}, bf16[2,1024,256]{2,1,0:T(8,128)(2,1)}) custom-call(s32[3]{0:T(128)S(1)} %pad_add_fusion.meta, bf16[1024,256]{1,0:T(8,128)(2,1)S(1)} %copy-done.40, bf16[2,1024,256]{2,1,0:T(8,128)(2,1)} %copy-done.34, bf16[2,1024,256]{2,1,0:T(8,128)(2,1)} %copy-done.36, ...), custom_call_target="tpu_custom_call" | custom-call | flops 13421772800 | bytes 6815744 | tf_op jit(solution)/shard_map/attend_back/pallas_call | solution.py:602
  875.0 21.2 %collective-permute-done.54 = bf16[4,128,1024]{2,1,0:T(8,128)(2,1)} collective-permute-done((bf16[4,128,1024]{2,1,0:T(8,128)(2,1)}, bf16[4,128,1024]{2,1,0:T(8,128)(2,1)}, u32[]{:S(2)}, u32[]{:S(2)}) %collective-permute-start.54) | collective-permute-done | bytes 1048608 | tf_op jit(solution)/shard_map/ppermute | solution.py:385
  896.3 4.9 add_convert_fusion.3
  911.8 16.1 %project_back.7 = (bf16[4,128,1024]{2,1,0:T(8,128)(2,1)}, bf16[4,128,1024]{2,1,0:T(8,128)(2,1)}, f32[8,256]{1,0:T(8,128)}, bf16[1024,1024]{1,0:T(8,128)(2,1)}, f32[8,1024]{1,0:T(8,128)}) custom-call(s32[1]{0:T(128)} %bitcast.meta, bf16[1024,256]{1,0:T(8,128)(2,1)} %copy-done.26, bf16[2,1024,256]{2,1,0:T(8,128)(2,1)} %copy-done.23, ...), custom_call_target="tpu_custom_call" | custom-call | flops 3758096384 | bytes 19398656 | tf_op jit(solution)/shard_map/project_back/pallas_call | solution.py:1025
  928.5 38.5 %collective-permute-done.55 = bf16[4,256,1024]{2,1,0:T(8,128)(2,1)S(1)} collective-permute-done((bf16[4,256,1024]{2,1,0:T(8,128)(2,1)}, bf16[4,256,1024]{2,1,0:T(8,128)(2,1)S(1)}, u32[]{:S(2)}, u32[]{:S(2)}) %collective-permute-start.55) | collective-permute-done | bytes 2097184 | tf_op jit(solution)/shard_map/ppermute | solution.py:385
  972.4 17.2 %collective-permute-done.50 = bf16[4,256,1024]{2,1,0:T(8,128)(2,1)} collective-permute-done((bf16[4,256,1024]{2,1,0:T(8,128)(2,1)}, bf16[4,256,1024]{2,1,0:T(8,128)(2,1)}, u32[]{:S(2)}, u32[]{:S(2)}) %collective-permute-start.50) | collective-permute-done | bytes 2097184 | tf_op jit(solution)/shard_map/ppermute | solution.py:385
  1001.9 5.2 fusion.4
  1007.1 5.1 fusion.6
  1019.2 6.8 collective-permute-start.45
  1028.3 9.5 collective-permute-start.38
  1043.8 75.4 %all-reduce.10.cloned.1.call-done = (f32[12,1024]{1,0:T(8,128)}, f32[12,1024]{1,0:T(8,128)}) async-done(((f32[12,1024]{1,0:T(8,128)}, f32[12,1024]{1,0:T(8,128)}), (f32[12,1024]{1,0:T(8,128)}, f32[12,1024]{1,0:T(8,128)})) %all-reduce.10.cloned.1.call-update) | async-done | bytes 98320 | tf_op jit(solution)/shard_map/psum | solution.py:1284
  1121.8 223.4 %all-reduce.12.cloned.1.call-done = (bf16[4,128,1024]{2,1,0:T(8,128)(2,1)}, bf16[4,128,1024]{2,1,0:T(8,128)(2,1)}, bf16[2,512,1024]{2,1,0:T(8,128)(2,1)}, bf16[2,512,1024]{2,1,0:T(8,128)(2,1)}) async-done(((bf16[4,128,1024]{2,1,0:T(8,128)(2,1)}, bf16[4,128,1024]{2,1,0:T(8,128)(2,1)}, bf16[2,512,1024]{2,1,0:T(8,128)(2,1)}, bf16[2,512,1024]{2,1,0:T(8,128)(2,1)}), (bf16[4,128,1024]{2,1,0:T(8,128)(2,1)}, ...) | async-done | bytes 6291472 | tf_op jit(solution)/shard_map/psum | solution.py:1062
  1346.5 5.7 collective-permute-start.67
  1362.4 4.4 convert.10
  1371.6 4.4 fusion.2
  1380.2 5.3 copy.106
  (564 shorter events, 216.7 us)
Async XLA Ops:
  7.2 1112.0 %all-reduce.10.cloned.1.call-start = ((), (), s32[]{:S(2)}) async-start(), calls=%async_computation | async-start | bytes 262144 | tf_op jit(solution)/shard_map/psum | solution.py:1284
  11.7 117.9 %collective-permute-start = (bf16[512,1024]{1,0:T(8,128)(2,1)}, bf16[512,1024]{1,0:T(8,128)(2,1)}, u32[]{:S(2)}, u32[]{:S(2)}) collective-permute-start(bf16[512,1024]{1,0:T(8,128)(2,1)} %get-tuple-element.238), channel_id=1, source_target_pairs={{0,0},{1,17},{2,18},{3,3},{4,4},{5,21},{6,22},{7,7},{8,8},{9,25},{... | collective-permute-start | bytes 3145736 | tf_op jit(solution)/shard_map/ppermute | solution.py:385
  21.2 112.0 %collective-permute-start.1 = (bf16[512,1024]{1,0:T(8,128)(2,1)}, bf16[512,1024]{1,0:T(8,128)(2,1)}, u32[]{:S(2)}, u32[]{:S(2)}) collective-permute-start(bf16[512,1024]{1,0:T(8,128)(2,1)} %get-tuple-element.237), channel_id=1, source_target_pairs={{0,1},{1,16},{2,19},{3,2},{4,5},{5,20},{6,23},{7,6},{8,9},{9,24},{... | collective-permute-start | bytes 3145736 | tf_op jit(solution)/shard_map/ppermute | solution.py:385
  47.5 86.5 %collective-permute-start.17 = (bf16[2,1024,1024]{2,1,0:T(8,128)(2,1)}, bf16[2,1024,1024]{2,1,0:T(8,128)(2,1)}, u32[]{:S(2)}, u32[]{:S(2)}) collective-permute-start(bf16[2,1024,1024]{2,1,0:T(8,128)(2,1)} %get-tuple-element.228), channel_id=1, source_target_pairs={{0,1},{1,0},{2,3},{3,2},{16,18},{17,19},{18,16},{19,17},{4,5},{5,4... | collective-permute-start | bytes 12582920 | tf_op jit(solution)/shard_map/ppermute | solution.py:385
  51.1 77.1 %collective-permute-start.7 = (bf16[4,256,1024]{2,1,0:T(8,128)(2,1)S(1)}, bf16[4,256,1024]{2,1,0:T(8,128)(2,1)}, u32[]{:S(2)}, u32[]{:S(2)}) collective-permute-start(bf16[4,256,1024]{2,1,0:T(8,128)(2,1)S(1)} %get-tuple-element.232.refs_0_.refs_3_.refs_6_), channel_id=1, source_target_pairs={{0,1},{1,0},{2,3},{3,2},{16,18},{17,19},{18,16},{19,17},{4,5},{5,4... | collective-permute-start | bytes 6291464 | tf_op jit(solution)/shard_map/ppermute | solution.py:385
  53.1 65.8 %collective-permute-start.9 = (f32[2,1536]{1,0:T(2,128)S(1)}, f32[2,1536]{1,0:T(2,128)S(1)}, u32[]{:S(2)}, u32[]{:S(2)}) collective-permute-start(f32[2,1536]{1,0:T(2,128)S(1)} %pad_maximum_fusion.14), channel_id=1, source_target_pairs={{0,1},{1,0},{2,3},{3,2},{16,18},{17,19},{18,16},{19,17},{4,5},{5,4... | collective-permute-start | bytes 36872 | tf_op jit(solution)/shard_map/ppermute | solution.py:385
  124.1 57.4 %collective-permute-start.2 = (bf16[512,1024]{1,0:T(8,128)(2,1)}, bf16[512,1024]{1,0:T(8,128)(2,1)S(1)}, u32[]{:S(2)}, u32[]{:S(2)}) collective-permute-start(bf16[512,1024]{1,0:T(8,128)(2,1)} %get-tuple-element.236), channel_id=1, source_target_pairs={{0,2},{1,19},{2,16},{3,1},{4,6},{5,23},{6,20},{7,5},{8,10},{9,27},... | collective-permute-start | bytes 3145736 | tf_op jit(solution)/shard_map/ppermute | solution.py:385
  128.1 68.7 %collective-permute-start.8 = (bf16[4,256,1024]{2,1,0:T(8,128)(2,1)}, bf16[4,256,1024]{2,1,0:T(8,128)(2,1)}, u32[]{:S(2)}, u32[]{:S(2)}) collective-permute-start(bf16[4,256,1024]{2,1,0:T(8,128)(2,1)} %collective-permute-done.7.refs_0_.refs_4_.refs_6_), channel_id=1, source_target_pairs={{0,16},{16,0},{1,17},{17,1},{2,18},{18,2},{3,19},{19,3},{4,20},{20... | collective-permute-start | bytes 6291464 | tf_op jit(solution)/shard_map/ppermute | solution.py:389
  129.6 54.5 %collective-permute-start.3 = (bf16[512,1024]{1,0:T(8,128)(2,1)}, bf16[512,1024]{1,0:T(8,128)(2,1)S(1)}, u32[]{:S(2)}, u32[]{:S(2)}) collective-permute-start(bf16[512,1024]{1,0:T(8,128)(2,1)} %get-tuple-element.235), channel_id=1, source_target_pairs={{0,3},{1,18},{2,17},{3,0},{4,7},{5,22},{6,21},{7,4},{8,11},{9,26},... | collective-permute-start | bytes 3145736 | tf_op jit(solution)/shard_map/ppermute | solution.py:385
  133.2 48.3 %collective-permute-start.12 = (bf16[4,128,1024]{2,1,0:T(8,128)(2,1)S(1)}, bf16[4,128,1024]{2,1,0:T(8,128)(2,1)S(1)}, u32[]{:S(2)}, u32[]{:S(2)}) collective-permute-start(bf16[4,128,1024]{2,1,0:T(8,128)(2,1)S(1)} %constant_dynamic-slice_fusion.40), channel_id=1, source_target_pairs={{0,2},{1,3},{2,0},{3,1},{16,17},{17,16},{18,19},{19,18},{4,6},{5,7... | collective-permute-start | bytes 3145736 | tf_op jit(solution)/shard_map/ppermute | solution.py:385
  134.1 74.4 %collective-permute-start.21 = (bf16[4,256,1024]{2,1,0:T(8,128)(2,1)}, bf16[4,256,1024]{2,1,0:T(8,128)(2,1)}, u32[]{:S(2)}, u32[]{:S(2)}) collective-permute-start(bf16[4,256,1024]{2,1,0:T(8,128)(2,1)} %get-tuple-element.231.refs_0_.refs_1_.refs_6_), channel_id=1, source_target_pairs={{0,1},{1,0},{2,3},{3,2},{16,18},{17,19},{18,16},{19,17},{4,5},{5,4... | collective-permute-start | bytes 6291464 | tf_op jit(solution)/shard_map/ppermute | solution.py:385
  181.5 31.5 %collective-permute-start.19 = (bf16[2,512,1024]{2,1,0:T(8,128)(2,1)}, bf16[2,512,1024]{2,1,0:T(8,128)(2,1)}, u32[]{:S(2)}, u32[]{:S(2)}) collective-permute-start(bf16[2,512,1024]{2,1,0:T(8,128)(2,1)} %constant_dynamic-slice_fusion.31), channel_id=1, source_target_pairs={{0,2},{1,3},{2,0},{3,1},{16,17},{17,16},{18,19},{19,18},{4,6},{5,7... | collective-permute-start | bytes 6291464 | tf_op jit(solution)/shard_map/ppermute | solution.py:385
  184.1 93.2 %collective-permute-start.18 = (bf16[2,1024,1024]{2,1,0:T(8,128)(2,1)}, bf16[2,1024,1024]{2,1,0:T(8,128)(2,1)}, u32[]{:S(2)}, u32[]{:S(2)}) collective-permute-start(bf16[2,1024,1024]{2,1,0:T(8,128)(2,1)} %collective-permute-done.17.near), channel_id=1, source_target_pairs={{0,16},{16,0},{1,17},{17,1},{2,18},{18,2},{3,19},{19,3},{4,20},{20... | collective-permute-start | bytes 12582920 | tf_op jit(solution)/shard_map/ppermute | solution.py:389
  203.6 41.3 %collective-permute-start.11 = (bf16[2,1024,512]{2,1,0:T(8,128)(2,1)}, bf16[2,1024,512]{2,1,0:T(8,128)(2,1)}, u32[]{:S(2)}, u32[]{:S(2)}) collective-permute-start(bf16[2,1024,512]{2,1,0:T(8,128)(2,1)} %get-tuple-element.84.kv), channel_id=1, source_target_pairs={{0,16},{16,0},{1,17},{17,1},{2,18},{18,2},{3,19},{19,3},{4,20},{20... | collective-permute-start | bytes 6291464 | tf_op jit(solution)/shard_map/ppermute | solution.py:389
  211.9 32.8 %collective-permute-start.23 = (bf16[4,128,1024]{2,1,0:T(8,128)(2,1)}, bf16[4,128,1024]{2,1,0:T(8,128)(2,1)S(1)}, u32[]{:S(2)}, u32[]{:S(2)}) collective-permute-start(bf16[4,128,1024]{2,1,0:T(8,128)(2,1)} %constant_dynamic-slice_fusion.30), channel_id=1, source_target_pairs={{0,2},{1,3},{2,0},{3,1},{16,17},{17,16},{18,19},{19,18},{4,6},{5,7... | collective-permute-start | bytes 3145736 | tf_op jit(solution)/shard_map/ppermute | solution.py:385
  213.0 64.3 %collective-permute-start.20 = (bf16[2,512,1024]{2,1,0:T(8,128)(2,1)}, bf16[2,512,1024]{2,1,0:T(8,128)(2,1)S(1)}, u32[]{:S(2)}, u32[]{:S(2)}) collective-permute-start(bf16[2,512,1024]{2,1,0:T(8,128)(2,1)} %collective-permute-done.19.far), channel_id=1, source_target_pairs={{0,16},{16,0},{1,17},{17,1},{2,18},{18,2},{3,19},{19,3},{4,20},{20... | collective-permute-start | bytes 6291464 | tf_op jit(solution)/shard_map/ppermute | solution.py:389
  230.0 97.9 %collective-permute-start.30 = (bf16[2,1024,1024]{2,1,0:T(8,128)(2,1)}, bf16[2,1024,1024]{2,1,0:T(8,128)(2,1)}, u32[]{:S(2)}, u32[]{:S(2)}) collective-permute-start(bf16[2,1024,1024]{2,1,0:T(8,128)(2,1)} %get-tuple-element.227), channel_id=1, source_target_pairs={{0,1},{1,0},{2,3},{3,2},{16,18},{17,19},{18,16},{19,17},{4,5},{5,4... | collective-permute-start | bytes 12582920 | tf_op jit(solution)/shard_map/ppermute | solution.py:385
  244.7 65.8 %collective-permute-start.22 = (bf16[4,256,1024]{2,1,0:T(8,128)(2,1)}, bf16[4,256,1024]{2,1,0:T(8,128)(2,1)S(1)}, u32[]{:S(2)}, u32[]{:S(2)}) collective-permute-start(bf16[4,256,1024]{2,1,0:T(8,128)(2,1)} %collective-permute-done.21.refs_1_.refs_2_.refs_7_), channel_id=1, source_target_pairs={{0,16},{16,0},{1,17},{17,1},{2,18},{18,2},{3,19},{19,3},{4,20},{20... | collective-permute-start | bytes 6291464 | tf_op jit(solution)/shard_map/ppermute | solution.py:389
  244.9 65.6 %collective-permute-start.24 = (bf16[4,128,1024]{2,1,0:T(8,128)(2,1)S(1)}, bf16[4,128,1024]{2,1,0:T(8,128)(2,1)S(1)}, u32[]{:S(2)}, u32[]{:S(2)}) collective-permute-start(bf16[4,128,1024]{2,1,0:T(8,128)(2,1)S(1)} %collective-permute-done.23.refs_3_.refs_4_.refs_9_), channel_id=1, source_target_pairs={{0,16},{16,0},{1,17},{17,1},{2,18},{18,2},{3,19},{19,3},{4,20},{20... | collective-permute-start | bytes 3145736 | tf_op jit(solution)/shard_map/ppermute | solution.py:389
  324.7 58.5 %collective-permute-start.25 = (bf16[2,1024,1024]{2,1,0:T(8,128)(2,1)}, bf16[2,1024,1024]{2,1,0:T(8,128)(2,1)}, u32[]{:S(2)}, u32[]{:S(2)}) collective-permute-start(bf16[2,1024,1024]{2,1,0:T(8,128)(2,1)} %get-tuple-element.93.kv), channel_id=1, source_target_pairs={{0,16},{16,0},{1,17},{17,1},{2,18},{18,2},{3,19},{19,3},{4,20},{20... | collective-permute-start | bytes 12582920 | tf_op jit(solution)/shard_map/ppermute | solution.py:389
  331.0 50.7 %collective-permute-start.32 = (bf16[2,512,1024]{2,1,0:T(8,128)(2,1)}, bf16[2,512,1024]{2,1,0:T(8,128)(2,1)}, u32[]{:S(2)}, u32[]{:S(2)}) collective-permute-start(bf16[2,512,1024]{2,1,0:T(8,128)(2,1)} %constant_dynamic-slice_fusion.21), channel_id=1, source_target_pairs={{0,2},{1,3},{2,0},{3,1},{16,17},{17,16},{18,19},{19,18},{4,6},{5,7... | collective-permute-start | bytes 6291464 | tf_op jit(solution)/shard_map/ppermute | solution.py:385
  331.7 105.2 %collective-permute-start.31 = (bf16[2,1024,1024]{2,1,0:T(8,128)(2,1)}, bf16[2,1024,1024]{2,1,0:T(8,128)(2,1)}, u32[]{:S(2)}, u32[]{:S(2)}) collective-permute-start(bf16[2,1024,1024]{2,1,0:T(8,128)(2,1)} %collective-permute-done.30.near), channel_id=1, source_target_pairs={{0,16},{16,0},{1,17},{17,1},{2,18},{18,2},{3,19},{19,3},{4,20},{20... | collective-permute-start | bytes 12582920 | tf_op jit(solution)/shard_map/ppermute | solution.py:389
  342.3 35.6 %collective-permute-start.29 = (bf16[512,1024]{1,0:T(8,128)(2,1)}, bf16[512,1024]{1,0:T(8,128)(2,1)}, u32[]{:S(2)}, u32[]{:S(2)}) collective-permute-start(bf16[512,1024]{1,0:T(8,128)(2,1)} %get-tuple-element.235), channel_id=1, source_target_pairs={{16,3},{17,18},{18,17},{19,0},{20,7},{21,22},{22,21},{23,4},{24,11... | collective-permute-start | bytes 3145736 | tf_op jit(solution)/shard_map/ppermute | solution.py:385
  381.8 55.2 %collective-permute-start.33 = (bf16[2,512,1024]{2,1,0:T(8,128)(2,1)}, bf16[2,512,1024]{2,1,0:T(8,128)(2,1)S(1)}, u32[]{:S(2)}, u32[]{:S(2)}) collective-permute-start(bf16[2,512,1024]{2,1,0:T(8,128)(2,1)} %collective-permute-done.32.far), channel_id=1, source_target_pairs={{0,16},{16,0},{1,17},{17,1},{2,18},{18,2},{3,19},{19,3},{4,20},{20... | collective-permute-start | bytes 6291464 | tf_op jit(solution)/shard_map/ppermute | solution.py:389
  607.4 147.9 %collective-permute-start.63 = (bf16[2,8,256,1024]{3,2,1,0:T(8,128)(2,1)}, bf16[2,8,256,1024]{3,2,1,0:T(8,128)(2,1)}, u32[]{:S(2)}, u32[]{:S(2)}) collective-permute-start(bf16[2,8,256,1024]{3,2,1,0:T(8,128)(2,1)} %get-tuple-element.147), channel_id=1, source_target_pairs={{0,16},{16,0},{1,17},{17,1},{2,18},{18,2},{3,19},{19,3},{4,20},{20... | collective-permute-start | bytes 25165832 | tf_op jit(solution)/shard_map/ppermute | solution.py:389
  710.8 63.5 %collective-permute-start.58 = (bf16[2,8,256,1024]{3,2,1,0:T(8,128)(2,1)}, bf16[2,8,256,1024]{3,2,1,0:T(8,128)(2,1)}, u32[]{:S(2)}, u32[]{:S(2)}) collective-permute-start(bf16[2,8,256,1024]{3,2,1,0:T(8,128)(2,1)} %get-tuple-element.145), channel_id=1, source_target_pairs={{0,16},{16,0},{1,17},{17,1},{2,18},{18,2},{3,19},{19,3},{4,20},{20... | collective-permute-start | bytes 25165832 | tf_op jit(solution)/shard_map/ppermute | solution.py:389
  711.6 137.7 %collective-permute-start.53 = (bf16[4,512,1024]{2,1,0:T(8,128)(2,1)}, bf16[4,512,1024]{2,1,0:T(8,128)(2,1)}, u32[]{:S(2)}, u32[]{:S(2)}) collective-permute-start(bf16[4,512,1024]{2,1,0:T(8,128)(2,1)} %get-tuple-element.143), channel_id=1, source_target_pairs={{0,16},{16,0},{1,17},{17,1},{2,18},{18,2},{3,19},{19,3},{4,20},{20... | collective-permute-start | bytes 12582920 | tf_op jit(solution)/shard_map/ppermute | solution.py:389
  753.1 77.3 %collective-permute-start.36 = (bf16[2,1024,512]{2,1,0:T(8,128)(2,1)}, bf16[2,1024,512]{2,1,0:T(8,128)(2,1)}, u32[]{:S(2)}, u32[]{:S(2)}) collective-permute-start(bf16[2,1024,512]{2,1,0:T(8,128)(2,1)} %get-tuple-element.116), channel_id=1, source_target_pairs={{0,16},{16,0},{1,17},{17,1},{2,18},{18,2},{3,19},{19,3},{4,20},{20... | collective-permute-start | bytes 6291464 | tf_op jit(solution)/shard_map/ppermute | solution.py:389
  769.4 49.2 %collective-permute-start.64 = (bf16[2,512,1024]{2,1,0:T(8,128)(2,1)}, bf16[2,512,1024]{2,1,0:T(8,128)(2,1)}, u32[]{:S(2)}, u32[]{:S(2)}) collective-permute-start(bf16[2,512,1024]{2,1,0:T(8,128)(2,1)} %bitcast.114), channel_id=1, source_target_pairs={{0,2},{1,3},{2,0},{3,1},{16,17},{17,16},{18,19},{19,18},{4,6},{5,7... | collective-permute-start | bytes 6291464 | tf_op jit(solution)/shard_map/ppermute | solution.py:385
  785.2 35.8 %collective-permute-start.59 = (bf16[2,512,1024]{2,1,0:T(8,128)(2,1)}, bf16[2,512,1024]{2,1,0:T(8,128)(2,1)}, u32[]{:S(2)}, u32[]{:S(2)}) collective-permute-start(bf16[2,512,1024]{2,1,0:T(8,128)(2,1)} %bitcast.110), channel_id=1, source_target_pairs={{0,2},{1,3},{2,0},{3,1},{16,17},{17,16},{18,19},{19,18},{4,6},{5,7... | collective-permute-start | bytes 6291464 | tf_op jit(solution)/shard_map/ppermute | solution.py:385
  817.4 28.5 %collective-permute-start.48 = (bf16[4,128,1024]{2,1,0:T(8,128)(2,1)}, bf16[4,128,1024]{2,1,0:T(8,128)(2,1)}, u32[]{:S(2)}, u32[]{:S(2)}) collective-permute-start(bf16[4,128,1024]{2,1,0:T(8,128)(2,1)} %get-tuple-element.141), channel_id=1, source_target_pairs={{0,16},{16,0},{1,17},{17,1},{2,18},{18,2},{3,19},{19,3},{4,20},{20... | collective-permute-start | bytes 3145736 | tf_op jit(solution)/shard_map/ppermute | solution.py:389
  828.4 79.3 %collective-permute-start.65 = (bf16[2,1024,1024]{2,1,0:T(8,128)(2,1)}, bf16[2,1024,1024]{2,1,0:T(8,128)(2,1)}, u32[]{:S(2)}, u32[]{:S(2)}) collective-permute-start(bf16[2,1024,1024]{2,1,0:T(8,128)(2,1)} %get-tuple-element.336), channel_id=1, source_target_pairs={{0,1},{1,0},{2,3},{3,2},{16,18},{17,19},{18,16},{19,17},{4,5},{5,4... | collective-permute-start | bytes 12582920 | tf_op jit(solution)/shard_map/ppermute | solution.py:385
  845.5 29.5 %collective-permute-start.47 = (bf16[4,256,1024]{2,1,0:T(8,128)(2,1)}, bf16[4,256,1024]{2,1,0:T(8,128)(2,1)S(1)}, u32[]{:S(2)}, u32[]{:S(2)}) collective-permute-start(bf16[4,256,1024]{2,1,0:T(8,128)(2,1)} %get-tuple-element.139), channel_id=1, source_target_pairs={{0,16},{16,0},{1,17},{17,1},{2,18},{18,2},{3,19},{19,3},{4,20},{20... | collective-permute-start | bytes 6291464 | tf_op jit(solution)/shard_map/ppermute | solution.py:389
  845.6 122.5 %collective-permute-start.60 = (bf16[2,1024,1024]{2,1,0:T(8,128)(2,1)}, bf16[2,1024,1024]{2,1,0:T(8,128)(2,1)}, u32[]{:S(2)}, u32[]{:S(2)}) collective-permute-start(bf16[2,1024,1024]{2,1,0:T(8,128)(2,1)} %get-tuple-element.337), channel_id=1, source_target_pairs={{0,1},{1,0},{2,3},{3,2},{16,18},{17,19},{18,16},{19,17},{4,5},{5,4... | collective-permute-start | bytes 12582920 | tf_op jit(solution)/shard_map/ppermute | solution.py:385
  847.5 27.4 %collective-permute-start.49 = (bf16[4,128,1024]{2,1,0:T(8,128)(2,1)S(1)}, bf16[4,128,1024]{2,1,0:T(8,128)(2,1)S(1)}, u32[]{:S(2)}, u32[]{:S(2)}) collective-permute-start(bf16[4,128,1024]{2,1,0:T(8,128)(2,1)S(1)} %add_convert_fusion.8), channel_id=1, source_target_pairs={{0,2},{1,3},{2,0},{3,1},{16,17},{17,16},{18,19},{19,18},{4,6},{5,7... | collective-permute-start | bytes 3145736 | tf_op jit(solution)/shard_map/ppermute | solution.py:385
  856.2 40.1 %collective-permute-start.54 = (bf16[4,128,1024]{2,1,0:T(8,128)(2,1)}, bf16[4,128,1024]{2,1,0:T(8,128)(2,1)}, u32[]{:S(2)}, u32[]{:S(2)}) collective-permute-start(bf16[4,128,1024]{2,1,0:T(8,128)(2,1)} %slice.543), channel_id=1, source_target_pairs={{0,2},{1,3},{2,0},{3,1},{16,17},{17,16},{18,19},{19,18},{4,6},{5,7... | collective-permute-start | bytes 3145736 | tf_op jit(solution)/shard_map/ppermute | solution.py:385
  874.9 35.9 %collective-permute-start.35 = (bf16[2,1024,256]{2,1,0:T(8,128)(2,1)}, bf16[2,1024,256]{2,1,0:T(8,128)(2,1)S(1)}, u32[]{:S(2)}, u32[]{:S(2)}) collective-permute-start(bf16[2,1024,256]{2,1,0:T(8,128)(2,1)} %get-tuple-element.112), channel_id=1, source_target_pairs={{0,16},{16,0},{1,17},{17,1},{2,18},{18,2},{3,19},{19,3},{4,20},{20... | collective-permute-start | bytes 3145736 | tf_op jit(solution)/shard_map/ppermute | solution.py:389
  901.3 65.8 %collective-permute-start.55 = (bf16[4,256,1024]{2,1,0:T(8,128)(2,1)}, bf16[4,256,1024]{2,1,0:T(8,128)(2,1)S(1)}, u32[]{:S(2)}, u32[]{:S(2)}) collective-permute-start(bf16[4,256,1024]{2,1,0:T(8,128)(2,1)} %get-tuple-element.346), channel_id=1, source_target_pairs={{0,1},{1,0},{2,3},{3,2},{16,18},{17,19},{18,16},{19,17},{4,5},{5,4... | collective-permute-start | bytes 6291464 | tf_op jit(solution)/shard_map/ppermute | solution.py:385
  904.5 85.1 %collective-permute-start.50 = (bf16[4,256,1024]{2,1,0:T(8,128)(2,1)}, bf16[4,256,1024]{2,1,0:T(8,128)(2,1)}, u32[]{:S(2)}, u32[]{:S(2)}) collective-permute-start(bf16[4,256,1024]{2,1,0:T(8,128)(2,1)} %get-tuple-element.347), channel_id=1, source_target_pairs={{0,1},{1,0},{2,3},{3,2},{16,18},{17,19},{18,16},{19,17},{4,5},{5,4... | collective-permute-start | bytes 6291464 | tf_op jit(solution)/shard_map/ppermute | solution.py:385
  910.8 91.1 %collective-permute-start.66 = (bf16[2,512,1024]{2,1,0:T(8,128)(2,1)}, bf16[2,512,1024]{2,1,0:T(8,128)(2,1)}, u32[]{:S(2)}, u32[]{:S(2)}) collective-permute-start(bf16[2,512,1024]{2,1,0:T(8,128)(2,1)} %constant_dynamic-slice_fusion), channel_id=1, source_target_pairs={{0,16},{16,0},{1,17},{17,1},{2,18},{18,2},{3,19},{19,3},{4,20},{20... | collective-permute-start | bytes 6291464 | tf_op jit(solution)/shard_map/ppermute | solution.py:389
  927.9 70.2 %collective-permute-start.46 = (bf16[4,128,1024]{2,1,0:T(8,128)(2,1)}, bf16[4,128,1024]{2,1,0:T(8,128)(2,1)}, u32[]{:S(2)}, u32[]{:S(2)}) collective-permute-start(bf16[4,128,1024]{2,1,0:T(8,128)(2,1)} %get-tuple-element.137), channel_id=1, source_target_pairs={{0,16},{16,0},{1,17},{17,1},{2,18},{18,2},{3,19},{19,3},{4,20},{20... | collective-permute-start | bytes 3145736 | tf_op jit(solution)/shard_map/ppermute | solution.py:389
  971.2 35.9 %collective-permute-start.61 = (bf16[2,512,1024]{2,1,0:T(8,128)(2,1)}, bf16[2,512,1024]{2,1,0:T(8,128)(2,1)}, u32[]{:S(2)}, u32[]{:S(2)}) collective-permute-start(bf16[2,512,1024]{2,1,0:T(8,128)(2,1)} %constant_dynamic-slice_fusion.1), channel_id=1, source_target_pairs={{0,16},{16,0},{1,17},{17,1},{2,18},{18,2},{3,19},{19,3},{4,20},{20... | collective-permute-start | bytes 6291464 | tf_op jit(solution)/shard_map/ppermute | solution.py:389
  994.7 350.5 %all-reduce.12.cloned.1.call-start = ((), (), s32[]{:S(2)}) async-start(), calls=%async_computation.1 | async-start | bytes 12582912 | tf_op jit(solution)/shard_map/psum | solution.py:1062
  1019.2 102.6 %collective-permute-start.45 = (bf16[512,1024]{1,0:T(8,128)(2,1)}, bf16[512,1024]{1,0:T(8,128)(2,1)}, u32[]{:S(2)}, u32[]{:S(2)}) collective-permute-start(bf16[512,1024]{1,0:T(8,128)(2,1)} %get-tuple-element.243), channel_id=1, source_target_pairs={{3,16},{18,17},{17,18},{0,19},{7,20},{22,21},{21,22},{4,23},{11,24... | collective-permute-start | bytes 3145736 | tf_op jit(solution)/shard_map/ppermute | solution.py:385
  1028.3 318.2 %collective-permute-start.38 = (bf16[512,1024]{1,0:T(8,128)(2,1)}, bf16[512,1024]{1,0:T(8,128)(2,1)}, u32[]{:S(2)}, u32[]{:S(2)}) collective-permute-start(bf16[512,1024]{1,0:T(8,128)(2,1)} %get-tuple-element.241), channel_id=1, source_target_pairs={{0,0},{17,1},{18,2},{3,3},{4,4},{21,5},{22,6},{7,7},{8,8},{25,9},{... | collective-permute-start | bytes 3145736 | tf_op jit(solution)/shard_map/ppermute | solution.py:385
  1037.8 314.4 %collective-permute-start.39 = (bf16[512,1024]{1,0:T(8,128)(2,1)}, bf16[512,1024]{1,0:T(8,128)(2,1)}, u32[]{:S(2)}, u32[]{:S(2)}) collective-permute-start(bf16[512,1024]{1,0:T(8,128)(2,1)} %get-tuple-element.242), channel_id=1, source_target_pairs={{1,0},{16,1},{19,2},{2,3},{5,4},{20,5},{23,6},{6,7},{9,8},{24,9},{... | collective-permute-start | bytes 3145736 | tf_op jit(solution)/shard_map/ppermute | solution.py:385
  1039.1 314.4 %collective-permute-start.40 = (bf16[512,1024]{1,0:T(8,128)(2,1)}, bf16[512,1024]{1,0:T(8,128)(2,1)}, u32[]{:S(2)}, u32[]{:S(2)}) collective-permute-start(bf16[512,1024]{1,0:T(8,128)(2,1)} %get-tuple-element.240), channel_id=1, source_target_pairs={{2,0},{19,1},{16,2},{1,3},{6,4},{23,5},{20,6},{5,7},{10,8},{27,9},... | collective-permute-start | bytes 3145736 | tf_op jit(solution)/shard_map/ppermute | solution.py:385
  1040.4 316.3 %collective-permute-start.41 = (bf16[512,1024]{1,0:T(8,128)(2,1)}, bf16[512,1024]{1,0:T(8,128)(2,1)}, u32[]{:S(2)}, u32[]{:S(2)}) collective-permute-start(bf16[512,1024]{1,0:T(8,128)(2,1)} %get-tuple-element.239), channel_id=1, source_target_pairs={{3,0},{18,1},{17,2},{0,3},{7,4},{22,5},{21,6},{4,7},{11,8},{26,9},... | collective-permute-start | bytes 3145736 | tf_op jit(solution)/shard_map/ppermute | solution.py:385
  (125 other events, 2232.0 us)
Sparse Core Ops, SparseCore 0:
  994.8 124.2 all-reduce.9
  1122.3 222.8 all-reduce.11

commit v2 on v1

--- a/solution.py
+++ b/solution.py
@@ -378,6 +378,7 @@
 
 CHIPS = range(GROUP)
 FIRST_HOP = [(place(0, t), place(0, t ^ 1)) for t in CHIPS] + [(place(1, t), place(1, t ^ 2)) for t in CHIPS]
+LAST_HOP = [(place(c, t), place(c, t ^ 3)) for c in range(2) for t in CHIPS]
 SECOND_HOP = [(place(0, t), place(0, t ^ 2)) for t in CHIPS] + [(place(1, t), place(1, t ^ 1)) for t in CHIPS]
 
 
@@ -527,8 +528,8 @@
             ],
         ),
         out_shape=[jax.ShapeDtypeStruct((rows, width), bf16)] * 2,
-        compiler_params=pltpu.CompilerParams(vmem_limit_bytes=40 * MIB),
-        cost_estimate=pl.CostEstimate(
+        compiler_params=pltpu.CompilerParams(vmem_limit_bytes=60 * MIB),
+        cost_estimate=cost(
             flops=40 * 256 * seg * seg * pairs, bytes_accessed=rows * width * 14, transcendentals=10 * seg * seg * pairs
         ),
         name="attend",
@@ -624,26 +625,41 @@
             jax.ShapeDtypeStruct((2, rows, width), bf16),
             jax.ShapeDtypeStruct((2, rows, width), bf16),
         ],
-        compiler_params=pltpu.CompilerParams(vmem_limit_bytes=48 * MIB),
-        cost_estimate=pl.CostEstimate(
+        compiler_params=pltpu.CompilerParams(vmem_limit_bytes=60 * MIB),
+        cost_estimate=cost(
             flops=100 * 256 * seg * seg * pairs, bytes_accessed=rows * width * 26, transcendentals=10 * seg * seg * pairs
         ),
         name="attend_back",
     )(meta, q, kv, kvo, kcol, qx, do, o)
 
 
+PART = 8
+
+
+def cost(flops, bytes_accessed, transcendentals):
+    return pl.CostEstimate(flops=flops // PART, bytes_accessed=bytes_accessed // PART, transcendentals=transcendentals // PART)
+
+
 def fixed(shape):
     return pl.BlockSpec(shape, lambda *_: (0,) * len(shape), pipeline_mode=pl.Buffered(1))
 
 
-def joined(refs, *index):
-    return jnp.concatenate([ref[index] if index else ref[...] for ref in refs], axis=0) if len(refs) > 1 else refs[0][index] if index else refs[0][...]
+BIAS_ROWS = 16
+
+
+def units_of(piece):
+    return (piece.shape[0] - BIAS_ROWS) // 4
+
+
+def joined(refs, size=0, matrix=0):
+    parts = [ref[matrix * ref.shape[0] // size : (matrix + 1) * ref.shape[0] // size] if size else ref[...] for ref in refs]
+    return jnp.concatenate(parts, axis=0) if len(parts) > 1 else parts[0]
 
 
 def project_kernel(count, a, *refs):
     pieces, bias, q, kv = refs[:count], refs[count], refs[count + 1], refs[count + 2]
     step = pl.program_id(0)
-    result = (dot_nt(a[...], joined(pieces, 0)) + bias[0]).astype(bf16)
+    result = (dot_nt(a[...], joined(pieces)) + bias[0]).astype(bf16)
 
     @pl.when(step == 0)
     def _():
@@ -656,22 +672,22 @@
 
 def project_heads(a, pieces, bias):
     rows, width = a.shape
-    columns = sum(piece.shape[1] for piece in pieces)
+    columns = sum(units_of(piece) for piece in pieces)
     return pl.pallas_call(
         partial(project_kernel, len(pieces)),
         grid=(3,),
         in_specs=[fixed(a.shape)]
-        + [pl.BlockSpec((1,) + piece.shape[1:], lambda i: (i, 0, 0)) for piece in pieces]
+        + [pl.BlockSpec((units_of(piece), width), lambda i: (i, 0)) for piece in pieces]
         + [pl.BlockSpec((1, 1, columns), lambda i: (i, 0, 0))],
         out_specs=[
             pl.BlockSpec((rows, columns), lambda i: (0, 0)),
             pl.BlockSpec((1, rows, columns), lambda i: (jnp.maximum(i - 1, 0), 0, 0)),
         ],
         out_shape=[jax.ShapeDtypeStruct((rows, columns), bf16), jax.ShapeDtypeStruct((2, rows, columns), bf16)],
-        cost_estimate=pl.CostEstimate(
+        cost_estimate=cost(
             flops=6 * rows * width * columns, bytes_accessed=2 * rows * width + 6 * width * columns + 6 * rows * columns, transcendentals=0
         ),
-        compiler_params=pltpu.CompilerParams(vmem_limit_bytes=40 * MIB),
+        compiler_params=pltpu.CompilerParams(vmem_limit_bytes=60 * MIB),
         name="project",
     )(a, *pieces, bias)
 
@@ -710,33 +726,7 @@
     return jnp.concatenate([jnp.stack(rows), jnp.zeros((8 - len(rows), rows[0].shape[-1]), f32)])
 
 
-def mix_kernel(counts, *refs):
-    heads, weights = refs[: counts[0]], refs[counts[0] : sum(counts)]
-    x, vectors, out, normed = refs[sum(counts) :]
-    left = jnp.concatenate([ref[...] for ref in heads], axis=1) if len(heads) > 1 else heads[0][...]
-    total = x[...].astype(f32) + vectors[0:1] + dot_nn(left, joined(weights, 0))
-    out[...] = total
-    normed[...] = normed_rows(total, vectors)
-
-
-def mix(x, heads, pieces, vectors):
-    rows, width = x.shape
-    tile = rows // 2
-    return pl.pallas_call(
-        partial(mix_kernel, (len(heads), len(pieces))),
-        grid=(rows // tile,),
-        in_specs=[pl.BlockSpec((tile, h.shape[1]), lambda i: (i, 0)) for h in heads]
-        + [pl.BlockSpec((1,) + p.shape[1:], lambda i: (3, 0, 0), pipeline_mode=pl.Buffered(1)) for p in pieces]
-        + [pl.BlockSpec((tile, width), lambda i: (i, 0)), fixed(vectors.shape)],
-        out_specs=[pl.BlockSpec((tile, width), lambda i: (i, 0))] * 2,
-        out_shape=[jax.ShapeDtypeStruct((rows, width), f32), jax.ShapeDtypeStruct((rows, width), bf16)],
-        cost_estimate=pl.CostEstimate(flops=2 * rows * width * width, bytes_accessed=14 * rows * width, transcendentals=0),
-        compiler_params=pltpu.CompilerParams(vmem_limit_bytes=40 * MIB),
-        name="mix",
-    )(*heads, *pieces, x, vectors)
-
-
-STEPS = 8
+STEPS = 4
 GELU_A = 0.7978845608028654
 GELU_B = 0.044715
 
@@ -753,66 +743,110 @@
     return jnp.concatenate([own[matrix, core], own[matrix, 1 - core]] + [ref[matrix] for ref in refs[1:]], axis=0)
 
 
-def feed_kernel(meta, middle, after, vectors, bias, own, near, near_too, far, far_too, pre, hidden, out, normed, total):
+def feed_rows(middle, up, down, bias):
+    u = dot_nt(middle, up) + bias
+    square = u * u
+    t = jnp.tanh(u * (GELU_A + (GELU_A * GELU_B) * square))
+    half = 0.5 * u
+    value = (half + half * t).astype(bf16)
+    slope = 0.5 + 0.5 * t + (half - half * t * t) * (GELU_A + (3 * GELU_A * GELU_B) * square)
+    return slope.astype(bf16), value, dot_nn(value, down)
+
+
+def feed_kernel(counts, meta, *refs):
+    heads, weights = refs[: counts[0]], refs[counts[0] : sum(counts)]
+    x, vectors, bias, own, near, near_too, slope, hidden, after, middle, total = refs[sum(counts) :]
     core = meta[0]
-    step = pl.program_id(0)
-    refs = (own, near, near_too, far, far_too)
-    up, down = share(refs, 0, core), share(refs, 1, core)
-    units = up.shape[0]
-    parts = []
-    count = max(units // 256, 1)
-    size = units // count
-    for n in range(count):
-        at = slice(n * size, (n + 1) * size)
-        u = dot_nt(middle[...], up[at]) + bias[0, 0:1, at]
-        pre[0, :, at] = u.astype(bf16)
-        h = (0.5 * u * (1.0 + jnp.tanh(GELU_A * (u + GELU_B * u * u * u)))).astype(bf16)
-        hidden[0, :, at] = h
-        parts.append(dot_nn(h, down[at]))
-    term = parts[0]
-    for part in parts[1:]:
-        term = term + part
-
-    @pl.when(step == 0)
+    tile = total.shape[0] // 4
+
+    @pl.when(pl.program_id(0) == 0)
     def _():
-        total[...] = term
-
-    @pl.when(step > 0)
-    def _():
-        total[...] += term
-
-    @pl.when(step == pl.num_programs(0) - 1)
-    def _():
-        tile = total.shape[0] // 4
         for n in range(4):
             at = slice(n * tile, (n + 1) * tile)
-            value = (total[at] + after[at] + vectors[0:1]).astype(bf16)
-            out[at] = value
-            normed[at] = normed_rows(value.astype(f32), vectors)
-
-
-def feed(meta, middle, after, vectors, bias, pieces):
-    rows, width = middle.shape
-    units = 4 * pieces[1].shape[1]
+            left = jnp.concatenate([ref[at] for ref in heads], axis=1)
+            value = x[at].astype(f32) + vectors[0:1] + dot_nn(left, joined(weights))
+            after[at] = value
+            middle[at] = normed_rows(value, vectors)
+            total[at] = value + vectors[3:4]
+
+    refs = (own, near, near_too)
+    up, down = share(refs, 0, core), share(refs, 1, core)
+    for n in range(4):
+        at = slice(n * tile, (n + 1) * tile)
+        slope[0, at], hidden[0, at], term = feed_rows(middle[at], up, down, bias[0])
+        total[at] += term
+
+
+def feed(meta, x, heads, heads_pieces, vectors, bias, pieces):
+    rows, width = x.shape
+    units = 3 * pieces[1].shape[1]
     steps = STEPS
     wide = units // steps
+    per_step = pl.BlockSpec((1, rows, wide), lambda i, m: (i, 0, 0))
+    whole = pl.BlockSpec((rows, width), lambda i, m: (0, 0))
     return pl.pallas_call(
-        feed_kernel,
+        partial(feed_kernel, (len(heads), len(heads_pieces))),
         grid_spec=pltpu.PrefetchScalarGridSpec(
             num_scalar_prefetch=1,
             grid=(steps,),
-            in_specs=[fixed(middle.shape), fixed(after.shape), fixed(vectors.shape), pl.BlockSpec((1, 1, wide), lambda i, m: (i, 0, 0))]
-            + share_specs(pieces, steps),
-            out_specs=[pl.BlockSpec((1, rows, wide), lambda i, m: (i, 0, 0))] * 2 + [pl.BlockSpec((rows, width), lambda i, m: (0, 0))] * 2,
-            scratch_shapes=[pltpu.VMEM((rows, width), f32)],
+            in_specs=[fixed(h.shape) for h in heads]
+            + [pl.BlockSpec((units_of(p), width), lambda i, m: (3, 0), pipeline_mode=pl.Buffered(1)) for p in heads_pieces]
+            + [fixed(x.shape), fixed(vectors.shape), pl.BlockSpec((1, 1, wide), lambda i, m: (i, 0, 0))]
+            + share_specs(pieces[:3], steps),
+            out_specs=[per_step, per_step, whole, whole, whole],
         ),
+        out_shape=[jax.ShapeDtypeStruct((steps, rows, wide), bf16)] * 2
+        + [jax.ShapeDtypeStruct((rows, width), kind) for kind in (f32, bf16, f32)],
+        cost_estimate=cost(
+            flops=2 * rows * width * (2 * units + width), bytes_accessed=4 * units * (rows + width) + 16 * rows * width, transcendentals=rows * units
+        ),
+        compiler_params=pltpu.CompilerParams(vmem_limit_bytes=60 * MIB),
+        name="feed",
+    )(meta, *heads, *heads_pieces, x, vectors, bias, *pieces[:3])
+
+
+def feed_last_kernel(middle, so_far, vectors, bias, far, far_too, slope, hidden, out, normed, weights):
+    steps = slope.shape[0]
+
+    @pl.when(pl.program_id(0) == 0)
+    def _():
+        size = far.shape[1] // steps
+        for n in range(2):
+            for i in range(steps):
+                weights[n, 2 * i * size : (2 * i + 1) * size] = far[n, i * size : (i + 1) * size]
+                weights[n, (2 * i + 1) * size : (2 * i + 2) * size] = far_too[n, i * size : (i + 1) * size]
+
+    slopes, values, term = feed_rows(middle[...], weights[0], weights[1], bias[...])
+    wide = slope.shape[2]
+    for i in range(steps):
+        slope[i] = slopes[:, i * wide : (i + 1) * wide]
+        hidden[i] = values[:, i * wide : (i + 1) * wide]
+    value = (so_far[...] + term).astype(bf16)
+    out[...] = value
+    normed[...] = normed_rows(value.astype(f32), vectors)
+
+
+def feed_last(middle, so_far, vectors, bias, pieces):
+    rows, width = middle.shape
+    units = pieces[1].shape[1]
+    steps = STEPS
+    wide = units // steps
+    tile = rows // 4
+    slim = pl.BlockSpec((tile, width), lambda i: (i, 0))
+    per_step = pl.BlockSpec((steps, tile, wide), lambda i: (0, i, 0))
+    return pl.pallas_call(
+        feed_last_kernel,
+        grid=(rows // tile,),
+        in_specs=[slim, slim, fixed(vectors.shape), fixed(bias.shape), fixed(pieces[3].shape), fixed(pieces[4].shape)],
+        out_specs=[per_step, per_step, slim, slim],
         out_shape=[jax.ShapeDtypeStruct((steps, rows, wide), bf16)] * 2 + [jax.ShapeDtypeStruct((rows, width), bf16)] * 2,
-        cost_estimate=pl.CostEstimate(
+        scratch_shapes=[pltpu.VMEM((2, units, width), bf16)],
+        cost_estimate=cost(
             flops=4 * rows * width * units, bytes_accessed=4 * units * (rows + width) + 10 * rows * width, transcendentals=rows * units
         ),
-        compiler_params=pltpu.CompilerParams(vmem_limit_bytes=52 * MIB),
-        name="feed",
-    )(meta, middle, after, vectors, bias, *pieces)
+        compiler_params=pltpu.CompilerParams(vmem_limit_bytes=60 * MIB),
+        name="feed_last",
+    )(middle, so_far, vectors, bias, pieces[3], pieces[4])
 
 
 def norm_back_rows(total, value, above, gain):
@@ -823,7 +857,7 @@
     return above + factor * (scaled - first - normal * second), normal
 
 
-def norm_back_all(total, value, above, gain, out, low, sums):
+def norm_back_all(total, value, above, gain, low, sums):
     tile = total.shape[0] // 4
     rows = []
     for n in range(4):
@@ -831,8 +865,6 @@
         part = total[at]
         top = above[at].astype(f32)
         grad, normal = norm_back_rows(part, value[at].astype(f32), top, gain)
-        if out is not None:
-            out[at] = grad
         low[at] = grad.astype(bf16)
         rows.append([jnp.sum(v, axis=0, keepdims=True) for v in (part * normal, part, grad, top)])
     for n in range(4):
@@ -840,32 +872,17 @@
 
 
 def feed_back_kernel(
-    meta, above, middle, after, vectors, pre, hidden, own, near, near_too, far, far_too, keep, send, bias_sums, out, low, sums, total
+    meta, above, middle, after, vectors, slope, slope_last, hidden, hidden_last, own, near, near_too, far, far_too,
+    keep, send, bias_sums, low, sums, total
 ):
     core = meta[0]
     step = pl.program_id(0)
     refs = (own, near, near_too, far, far_too)
     up, down = share(refs, 0, core), share(refs, 1, core)
-    u = pre[0].astype(f32)
-    inner = GELU_A * (u + GELU_B * u * u * u)
-    t = jnp.tanh(inner)
-    slope = 0.5 * (1.0 + t) + 0.5 * u * (1.0 - t * t) * (GELU_A * (1.0 + 3.0 * GELU_B * u * u))
-    grad = dot_nt(above[...], down) * slope
-    low_grad = grad.astype(bf16)
-    bias_sums[0] = jnp.broadcast_to(jnp.sum(low_grad.astype(f32), axis=0, keepdims=True), bias_sums.shape[1:])
-    term = dot_nn(low_grad, up)
-
-    @pl.when(step == 0)
-    def _():
-        total[...] = term
-
-    @pl.when(step > 0)
-    def _():
-        total[...] += term
-
-    grads = (dot_tn(low_grad, middle[...]).astype(bf16), dot_tn(hidden[0], above[...]).astype(bf16))
     part = up.shape[0] // 8
-    for n, value in enumerate(grads):
+
+    def spread(n, value):
+        value = value.astype(bf16)
         keep[n, 0, 0 : 2 * part] = value[2 * part : 4 * part]
         keep[n, 0, 2 * part : 3 * part] = value[6 * part : 7 * part]
         keep[n, 0, 3 * part :] = value[0:part]
@@ -873,65 +890,76 @@
         send[n, 0, 2 * part : 3 * part] = value[7 * part :]
         send[n, 0, 3 * part :] = value[part : 2 * part]
 
+    @pl.when(step == 0)
+    def _():
+        total[...] = jnp.zeros_like(total)
+
+    slopes = jnp.concatenate([slope[0], slope_last[0]], axis=1)
+    values = jnp.concatenate([hidden[0], hidden_last[0]], axis=1)
+    grad = dot_nt(above[...], down) * slopes.astype(f32)
+    bias_sums[0] = jnp.broadcast_to(jnp.sum(grad, axis=0, keepdims=True), bias_sums.shape[1:])
+    low_grad = grad.astype(bf16)
+    spread(1, dot_tn(values, above[...]))
+    total[...] += dot_nn(low_grad, up)
+    spread(0, dot_tn(low_grad, middle[...]))
+
     @pl.when(step == pl.num_programs(0) - 1)
     def _():
-        norm_back_all(total, after, above, vectors[0:1], out, low, sums)
-
-
-def feed_back(meta, above, middle, after, gain, pre, hidden, pieces):
+        norm_back_all(total, after, above, vectors[0:1], low, sums)
+
+
+def feed_back(meta, above, middle, after, gain, slopes, values, pieces):
     rows, width = middle.shape
     units = 4 * pieces[1].shape[1]
     steps = STEPS
     wide = units // steps
     vectors = jnp.broadcast_to(gain[None], (8, width))
-    per_step = pl.BlockSpec((1, rows, wide), lambda i, m: (i, 0, 0))
+    per_step = [pl.BlockSpec((1, rows, v.shape[2]), lambda i, m: (i, 0, 0)) for v in slopes]
     grads = pl.BlockSpec((2, 1, wide // 2, width), lambda i, m: (0, i, 0, 0))
-    whole = pl.BlockSpec((rows, width), lambda i, m: (0, 0))
     return pl.pallas_call(
         feed_back_kernel,
         grid_spec=pltpu.PrefetchScalarGridSpec(
             num_scalar_prefetch=1,
             grid=(steps,),
-            in_specs=[fixed(above.shape), fixed(middle.shape), fixed(after.shape), fixed(vectors.shape), per_step, per_step]
+            in_specs=[fixed(above.shape), fixed(middle.shape), fixed(after.shape), fixed(vectors.shape)] + per_step * 2
             + share_specs(pieces, steps),
-            out_specs=[grads, grads, pl.BlockSpec((1, 8, wide), lambda i, m: (i, 0, 0)), whole, whole, pl.BlockSpec((8, width), lambda i, m: (0, 0))],
+            out_specs=[grads, grads, pl.BlockSpec((1, 8, wide), lambda i, m: (i, 0, 0)), pl.BlockSpec((rows, width), lambda i, m: (0, 0)), pl.BlockSpec((8, width), lambda i, m: (0, 0))],
             scratch_shapes=[pltpu.VMEM((rows, width), f32)],
         ),
         out_shape=[jax.ShapeDtypeStruct((2, steps, wide // 2, width), bf16)] * 2
         + [
             jax.ShapeDtypeStruct((steps, 8, wide), f32),
-            jax.ShapeDtypeStruct((rows, width), f32),
             jax.ShapeDtypeStruct((rows, width), bf16),
             jax.ShapeDtypeStruct((8, width), f32),
         ],
-        cost_estimate=pl.CostEstimate(
-            flops=8 * rows * width * units, bytes_accessed=12 * units * (rows + width) + 14 * rows * width, transcendentals=rows * units
+        cost_estimate=cost(
+            flops=8 * rows * width * units, bytes_accessed=12 * units * (rows + width) + 14 * rows * width, transcendentals=0
         ),
-        compiler_params=pltpu.CompilerParams(vmem_limit_bytes=58 * MIB),
+        compiler_params=pltpu.CompilerParams(vmem_limit_bytes=60 * MIB),
         name="feed_back",
-    )(meta, above, middle, after, vectors, pre, hidden, *pieces)
+    )(meta, above, middle, after, vectors, *slopes, *values, *pieces)
 
 
 def heads_back_kernel(count, low, *refs):
     pieces, out = refs[:count], refs[count]
-    out[...] = dot_nt(low[...], joined(pieces, 0)).astype(bf16)
+    out[...] = dot_nt(low[...], joined(pieces)).astype(bf16)
 
 
 def heads_back(low, pieces):
     rows, width = low.shape
-    columns = sum(piece.shape[1] for piece in pieces)
+    columns = sum(units_of(piece) for piece in pieces)
     tile = rows // 2
     return pl.pallas_call(
         partial(heads_back_kernel, len(pieces)),
         grid=(rows // tile,),
         in_specs=[pl.BlockSpec((tile, width), lambda i: (i, 0))]
-        + [pl.BlockSpec((1,) + p.shape[1:], lambda i: (3, 0, 0), pipeline_mode=pl.Buffered(1)) for p in pieces],
+        + [pl.BlockSpec((units_of(p), width), lambda i: (3, 0), pipeline_mode=pl.Buffered(1)) for p in pieces],
         out_specs=pl.BlockSpec((tile, columns), lambda i: (i, 0)),
         out_shape=jax.ShapeDtypeStruct((rows, columns), bf16),
-        cost_estimate=pl.CostEstimate(
+        cost_estimate=cost(
             flops=2 * rows * width * columns, bytes_accessed=2 * (rows * width + width * columns + rows * columns), transcendentals=0
         ),
-        compiler_params=pltpu.CompilerParams(vmem_limit_bytes=40 * MIB),
+        compiler_params=pltpu.CompilerParams(vmem_limit_bytes=60 * MIB),
         name="heads_back",
     )(low, *pieces)
 
@@ -946,30 +974,31 @@
         value, above, vectors = take(3)
     keep, send, bias_sums = take(3)
     outs = take(2) if last else take(1)
-    lefts, flipped = take(2)
+    lefts = refs.pop(0)
     total = refs.pop(0) if last else None
     step = pl.program_id(0)
     core = meta[0]
 
     @pl.when(step == 0)
     def _():
-        lefts[0] = dq[...]
+        bias_sums[0:1] = jnp.sum(dq[...].astype(f32), axis=0, keepdims=True)
         for n in range(2):
-            lefts[1 + n] = (dkv[n].astype(f32) + dkv_got[n].astype(f32)).astype(bf16)
-        for n in range(3):
-            flipped[n] = lefts[n].T
-        flipped[3] = o[...].T
-        for n, c in enumerate((0, 2)):
-            bias_sums[n : n + 1] = jnp.sum(lefts[c].astype(f32), axis=0, keepdims=True)
-
+            value_n = dkv[n].astype(f32) + dkv_got[n].astype(f32)
+            lefts[n] = value_n.astype(bf16)
+            if n == 1:
+                bias_sums[1:2] = jnp.sum(value_n, axis=0, keepdims=True)
+
+    sides = (dq, lefts.at[0], lefts.at[1], o)
+    term = None
     for c in range(4):
-        value_c = dot_nn(flipped[c], (low if c == 3 else a)[...]).astype(bf16)
+        value_c = dot_tn(sides[c][...], (low if c == 3 else a)[...]).astype(bf16)
         keep_at = send_at = at = 0
         for name, size in groups:
             if name == "own":
                 half = size // 2
-                keep[c, keep_at : keep_at + half] = jnp.where(core == 0, value_c[at : at + half], value_c[at + half : at + size])
-                send[c, send_at : send_at + half] = jnp.where(core == 0, value_c[at + half : at + size], value_c[at : at + half])
+                one, two = value_c[at : at + half], value_c[at + half : at + size]
+                keep[c, keep_at : keep_at + half] = jnp.where(core == 0, one, two)
+                send[c, send_at : send_at + half] = jnp.where(core == 0, two, one)
                 keep_at, send_at = keep_at + half, send_at + half
             elif name in ("near", "far"):
                 keep[c, keep_at : keep_at + size] = value_c[at : at + size]
@@ -978,40 +1007,39 @@
                 send[c, send_at : send_at + size] = value_c[at : at + size]
                 send_at += size
             at += size
-    term = None
-    for c in range(3):
-        part = dot_nn(lefts[c], joined(pieces, c))
-        term = part if term is None else term + part
+        if c < 3:
+            part = dot_nn(sides[c][...], joined(pieces, 3, c))
+            term = part if term is None else term + part
     if not first:
         term = term + so_far[...]
     if not last:
         outs[0][...] = term
         return
-    tile = total.shape[1] // pl.num_programs(0) if isinstance(pl.num_programs(0), int) else term.shape[1]
+    tile = term.shape[1]
     total[:, pl.ds(pl.multiple_of(step * tile, tile), tile)] = term
 
     @pl.when(step == pl.num_programs(0) - 1)
     def _():
-        norm_back_all(total, value, above, vectors[0:1], None, outs[0], outs[1])
+        norm_back_all(total, value, above, vectors[0:1], outs[0], outs[1])
 
 
 def project_back(meta, names, dq, dkv, dkv_got, o, a, low, pieces, so_far, norm):
     rows, width = a.shape
     columns = dq.shape[1]
-    groups = [(name, piece.shape[1]) for name, piece in zip(names, pieces)]
-    tiles = 4
+    groups = [(name, units_of(piece)) for name, piece in zip(names, pieces)]
+    tiles = 2
     tile = width // tiles
     slim = pl.BlockSpec((rows, tile), lambda i, m: (0, i))
     grads = pl.BlockSpec((4, columns // 2, tile), lambda i, m: (0, 0, i))
     args = [dq, dkv, dkv_got, o, a, low, *pieces]
     specs = [fixed(dq.shape), fixed(dkv.shape), fixed(dkv.shape), fixed(o.shape), slim, slim]
-    specs += [pl.BlockSpec((3, p.shape[1], tile), lambda i, m: (0, 0, i)) for p in pieces]
+    specs += [pl.BlockSpec((3 * units_of(p), tile), lambda i, m: (0, i)) for p in pieces]
     if so_far is not None:
         args.append(so_far)
         specs.append(slim)
     out_specs = [grads, grads, pl.BlockSpec((8, columns), lambda i, m: (0, 0))]
     out_shape = [jax.ShapeDtypeStruct((4, columns // 2, width), bf16)] * 2 + [jax.ShapeDtypeStruct((8, columns), f32)]
-    scratch = [pltpu.VMEM((3, rows, columns), bf16), pltpu.VMEM((4, columns, rows), bf16)]
+    scratch = [pltpu.VMEM((2, rows, columns), bf16)]
     if norm is None:
         out_specs.append(slim)
         out_shape.append(jax.ShapeDtypeStruct((rows, width), f32))
@@ -1028,20 +1056,16 @@
             num_scalar_prefetch=1, grid=(tiles,), in_specs=specs, out_specs=out_specs, scratch_shapes=scratch
         ),
         out_shape=out_shape,
-        cost_estimate=pl.CostEstimate(
+        cost_estimate=cost(
             flops=14 * rows * width * columns, bytes_accessed=2 * (6 * rows * columns + 7 * width * columns + 6 * rows * width), transcendentals=0
         ),
-        compiler_params=pltpu.CompilerParams(vmem_limit_bytes=58 * MIB),
+        compiler_params=pltpu.CompilerParams(vmem_limit_bytes=60 * MIB),
         name="project_back",
     )(meta, *args)
 
 
-def gathered(own, core):
-    near = hop(own, FIRST_HOP)
-    near_too = swap(near)
-    far = hop(half_of(near, 1, core), SECOND_HOP)
-    far_too = swap(far)
-    return {"own": own, "near": near, "near_too": near_too, "far": far, "far_too": far_too}
+def tie(values, *others):
+    return lax.optimization_barrier((values, others))[0]
 
 
 def plus(*values):
@@ -1051,15 +1075,175 @@
     return total.astype(bf16)
 
 
-def summed(near, far, own, core):
-    relayed = hop(far, SECOND_HOP)
-    matrices, units, width = near.shape
-    place_of_half = jnp.arange(2)[None, :, None, None] == core
-    near = near.reshape(matrices, 2, units // 2, width)
-    near = plus(near, jnp.where(place_of_half, relayed[:, None], jnp.zeros((), bf16)))
-    got = hop(near.reshape(matrices, units, width), FIRST_HOP)
-    total = plus(own, half_of(got, 1, core), swap(half_of(got, 1, 1 - core)))
-    return lax.psum(total, "dp")
+def meet_kernel(meta, keep_early, keep_late, got_early, got_late, far, own, early, late):
+    core = meta[0]
+    size = early.shape[1]
+    for half, out, kept, got in ((1 - core, early, keep_early, got_early), (core, late, keep_late, got_late)):
+        total = (kept[0, 0].astype(f32) + got[0, 0].astype(f32)).astype(bf16)
+        out[0] = total[:size]
+        far[0, half, 0] = total[size : size + size // 2]
+        own[0, half, 0] = total[size + size // 2 :]
+
+
+def meet(meta, keep, got):
+    matrices, steps, units, width = keep.shape
+    each = steps // 2
+    view = lambda late: pl.BlockSpec(
+        (1, 1, units, width), lambda n, j, m: (n, (m[0] if late else 1 - m[0]) * each + j, 0, 0)
+    )
+    halves = pl.BlockSpec((1, 2, 1, units // 4, width), lambda n, j, m: (n, 0, j, 0, 0))
+    rows = pl.BlockSpec((1, units // 2, width), lambda n, j, m: (n, j, 0))
+    both_shape = jax.ShapeDtypeStruct((matrices, 2, each, units // 4, width), bf16)
+    rows_shape = jax.ShapeDtypeStruct((matrices, each * units // 2, width), bf16)
+    far, own, early, late = pl.pallas_call(
+        meet_kernel,
+        grid_spec=pltpu.PrefetchScalarGridSpec(
+            num_scalar_prefetch=1,
+            grid=(matrices, each),
+            in_specs=[view(False), view(True)] * 2,
+            out_specs=[halves, halves, rows, rows],
+        ),
+        out_shape=[both_shape, both_shape, rows_shape, rows_shape],
+        cost_estimate=cost(flops=keep.size, bytes_accessed=6 * keep.size, transcendentals=0),
+        compiler_params=pltpu.CompilerParams(vmem_limit_bytes=60 * MIB),
+        name="meet",
+    )(meta, keep, keep, got, got)
+    flat = lambda value: value.reshape(matrices, -1, width)
+    return flat(far), flat(own), early, late
+
+
+def exchanged(value, axis, distance):
+    count = lax.axis_size(axis)
+    return lax.ppermute(value, axis, [(n, n ^ distance) for n in range(count)])
+
+
+def ordered(first, mine, other):
+    return jnp.where(first, jnp.concatenate([mine, other], axis=1), jnp.concatenate([other, mine], axis=1))
+
+
+class Send:
+    def __init__(self, transfer, value):
+        self.transfer, self.value = transfer, value
+
+
+def hopping(value, pairs):
+    return Send(lambda v: hop(v, pairs), value)
+
+
+def swapping(value):
+    return Send(swap, value)
+
+
+def exchanging(value, axis, distance):
+    return Send(lambda v: exchanged(v, axis, distance), value)
+
+
+class Chain:
+    def __init__(self, steps):
+        self.steps, self.result, self.done = steps, None, False
+        self.advance(None)
+
+    def advance(self, value):
+        self.pending, self.under_way = None, None
+        try:
+            self.pending, self.wait = self.steps.send(value)
+        except StopIteration as stop:
+            self.result, self.done = stop.value, True
+
+
+def once(sends, wait):
+    value = yield sends, wait
+    return value
+
+
+class Chains:
+    def __init__(self):
+        self.running = []
+
+    def start(self, steps):
+        chain = Chain(steps)
+        self.running.append(chain)
+        return chain
+
+    def turn(self, values):
+        self.running = [chain for chain in self.running if not chain.done]
+        due = []
+        for chain in self.running:
+            chain.wait -= 1
+            if chain.wait <= 0:
+                due.append(chain)
+        values, there = lax.optimization_barrier((values, [chain.under_way for chain in due]))
+        for chain, value in zip(due, there):
+            chain.advance(value)
+        return values
+
+    def launch(self, values):
+        chains = [chain for chain in self.running if chain.pending is not None]
+        sends = [chain.pending if isinstance(chain.pending, list) else [chain.pending] for chain in chains]
+        values, sent = lax.optimization_barrier((values, [[send.value for send in each] for each in sends]))
+        for chain, each, operands in zip(chains, sends, sent):
+            under_way = [send.transfer(value) for send, value in zip(each, operands)]
+            chain.under_way = under_way if isinstance(chain.pending, list) else under_way[0]
+            chain.pending = None
+        return values
+
+    def step(self, values, *new):
+        values = self.turn(values)
+        started = [self.start(make()) for make in new]
+        values = self.launch(values)
+        return (values, *started) if new else values
+
+
+def summed_feed(meta, keep, send, waits):
+    waits = iter(waits)
+    got = yield swapping(send), next(waits)
+    far, own, early, late = meet(meta, keep, got)
+    relayed, early = yield [hopping(far, SECOND_HOP), hopping(early, FIRST_HOP)], next(waits)
+    late, back = yield [hopping(plus(late, relayed), FIRST_HOP), swapping(early)], next(waits)
+    return (yield from summed_over_line(plus(own, late, back), waits))
+
+
+def summed_far(keep, send, waits):
+    waits = iter(waits)
+    got = yield swapping(send), next(waits)
+    return (yield hopping(plus(keep, got), LAST_HOP), next(waits))
+
+
+def summed_near(keep, send, core, waits):
+    waits = iter(waits)
+    got = yield swapping(send), next(waits)
+    near = yield hopping(plus(keep, got), FIRST_HOP), next(waits)
+    back = yield swapping(half_of(near, 1, 1 - core)), next(waits)
+    return half_of(near, 1, core), back
+
+
+def summed_over_line(total, waits):
+    if lax.axis_size("dp") != 4:
+        return lax.psum(total, "dp")
+    line = lax.axis_index("dp")
+    low, high = line & 1, line >> 1
+    got = yield exchanging(half_of(total, 1, 1 - low), "dp", 1), next(waits)
+    total = plus(half_of(total, 1, low), got)
+    got = yield exchanging(half_of(total, 1, 1 - high), "dp", 2), next(waits)
+    total = plus(half_of(total, 1, high), got)
+    got = yield exchanging(total, "dp", 2), next(waits)
+    total = ordered(high == 0, total, got)
+    got = yield exchanging(total, "dp", 1), next(waits)
+    return ordered(low == 0, total, got)
+
+
+def summed_everywhere(value):
+    for axis in ("section", "tensor", "dp"):
+        count = lax.axis_size(axis)
+        if count & (count - 1):
+            value = lax.psum(value, axis)
+            continue
+        distance = 1
+        while distance < count:
+            got = yield exchanging(value, axis, distance), 1
+            value = value + got
+            distance *= 2
+    return value
 
 
 def in_order(own, near, near_too, far, far_too, core, chip):
@@ -1071,7 +1255,8 @@
 
 
 PIECES = ("own", "near", "near_too", "far", "far_too")
-GROUPS = ((("own",), ("near", "near_too"), ("far", "far_too")), (PIECES,))
+GROUPS = (("own",), ("near", "near_too"), ("far", "far_too"))
+OWN, NEAR, FAR = range(3)
 
 
 def on_row(
@@ -1087,69 +1272,72 @@
     n_up = up_bias.shape[-1]
 
     def row_from(section):
-        got = [
-            hop(
+        return [
+            hopping(
                 lax.dynamic_index_in_dim(ends, chip ^ k, 0, keepdims=False),
                 [(place(section, t), place(core_of(t), t ^ k)) for t in CHIPS],
             )
             for k in CHIPS
         ]
 
+    def chosen_rows(got):
         def pick(k):
             return jnp.where(k == 0, got[0], jnp.where(k == 1, got[1], jnp.where(k == 2, got[2], got[3])))
 
         return jnp.concatenate([pick(chip ^ lo_segment), pick(chip ^ hi_segment)])
 
-    def row_to(section, row):
+    def row_to(section, row, distances):
         got = []
-        for k in CHIPS:
+        for k in distances:
             segment = chip ^ k
             sent = jnp.where(segment == lo_segment, row[:seg], row[seg:])
-            got.append(hop(sent, [(place(core_of(t), t ^ k), place(section, t)) for t in CHIPS]))
+            got.append(hopping(sent, [(place(core_of(t), t ^ k), place(section, t)) for t in CHIPS]))
         return got
 
     def both(mine):
         theirs = swap(mine)
         return (jnp.where(first_core, mine, theirs), jnp.where(first_core, theirs, mine))
 
-    vectors = jnp.concatenate(
-        [ln_gains[0].reshape(-1), ln_biases[0].reshape(-1), out_biases[0].reshape(-1), qv_bias[0].reshape(-1), up_bias[0]]
-    )
-    vectors = both(vectors[None])
-    x = row_from(0)
-    attention_own = both(jnp.concatenate([jnp.swapaxes(w_qkv[0], 1, 2), w_out]))
+    chains = Chains()
+    six = both(jnp.concatenate([ln_gains[0], ln_biases[0], out_biases[0]]))
+    bias = jnp.concatenate([qv_bias[0].reshape(-1), up_bias[0]])
+    bias = jnp.stack(three_parts(bias))
+    bias = jnp.pad(bias, ((0, 0), (0, -bias.shape[1] % D))).reshape(-1, D)
+    bias = jnp.pad(bias, ((0, BIAS_ROWS - bias.shape[0]), (0, 0)))
+    pack = jnp.concatenate([jnp.swapaxes(w_qkv[0], 1, 2).reshape(-1, D), w_out[0], bias])
+    x = chosen_rows([send.transfer(send.value) for send in row_from(0)])
+    attention_own = both(pack)
     feed_own = both(jnp.concatenate([w_up[0].T[None], w_down]))
-    biases = jnp.concatenate([v[:, 6 * D :] for v in vectors])
-    near = hop(biases, FIRST_HOP)
-    far = hop(near, SECOND_HOP)
-    bias_quarters = {"own": biases, "near": near, "near_too": swap(near), "far": far, "far_too": far}
+
+    def gathered_heads(own, pieces, waits):
+        pieces["own"] = own
+        near = yield hopping(own, FIRST_HOP), waits[0]
+        pieces["near"], pieces["near_too"] = near, swap(near)
+        heads = half_of(near[: 4 * n_qv].reshape(4, n_qv, D), 1, core).reshape(-1, D)
+        far = yield hopping(jnp.concatenate([heads, near[4 * n_qv :]]), SECOND_HOP), waits[1]
+        pieces["far"], pieces["far_too"] = far, swap(far)
+
+    def gathered_feed(own, pieces, waits):
+        near = yield hopping(own, FIRST_HOP), waits[0]
+        pieces += [own.reshape(2, 2, -1, D), near, swap(near)]
+        far = yield hopping(half_of(near, 1, core), SECOND_HOP), waits[1]
+        pieces += [far, swap(far)]
+
+    attention, feeding = ({}, {}), ([], [])
+    x, attention_own = tie((x, attention_own))
 
     def bias_of(name, layer, start, size):
-        part = bias_quarters[name][layer, start : start + size]
+        rows = attention[layer][name][-BIAS_ROWS:].astype(f32)
+        count = -(-(2 * n_qv + n_up) // D)
+        parts = rows[: 3 * count].reshape(3, -1)
+        part = ((parts[0] + parts[1]) + parts[2])[start : start + size]
         if name == "far":
             part = half_of(part, 0, core)
         if name == "far_too":
             part = half_of(part, 0, 1 - core)
         return part
 
-    weights = []
-    for layer in range(2):
-        own_bias = bias_quarters["own"][layer, 2 * n_qv :]
-        shares = [half_of(own_bias, 0, core), half_of(own_bias, 0, 1 - core)]
-        shares += [bias_of(name, layer, 2 * n_qv, n_up) for name in PIECES[1:]]
-        six = vectors[layer][0, : 6 * D].reshape(6, D)
-        attention, feeding = gathered(attention_own[layer], core), gathered(feed_own[layer], core)
-        feeding["own"] = feeding["own"].reshape(2, 2, -1, D)
-        weights.append(
-            dict(
-                gains=six[0:2],
-                shifts=six[2:4],
-                ends=six[4:6],
-                attention=attention,
-                feed=[feeding[name] for name in PIECES],
-                feed_bias=jnp.concatenate([part.reshape(STEPS, -1) for part in shares], axis=1)[:, None],
-            )
-        )
+    gains, shifts, end_biases = ([layer_six[n : n + 2] for layer_six in six] for n in (0, 2, 4))
 
     length = lax.dynamic_index_in_dim(lengths.reshape(-1), chip, 0, keepdims=False)
     segments = jnp.stack([lo_segment, hi_segment, 1 - core, 2 + core])
@@ -1180,92 +1368,96 @@
 
     groups = [
         [
-            dict(
-                names=names,
-                meta=group_meta(names),
-                qcol=query_columns(jnp.concatenate([slopes[name] for name in names])),
-                pieces=[weights[layer]["attention"][name] for name in names],
-                bias=jnp.stack(
-                    [
-                        jnp.concatenate([bias_of(name, layer, 0, n_qv) for name in names]),
-                        jnp.zeros((sum(pairs_of[name] for name in names) * 128,), f32),
-                        jnp.concatenate([bias_of(name, layer, n_qv, n_qv) for name in names]),
-                    ]
-                )[:, None],
-            )
-            for names in GROUPS[layer]
+            dict(names=names, meta=group_meta(names), qcol=query_columns(jnp.concatenate([slopes[name] for name in names])))
+            for names in GROUPS
         ]
         for layer in range(2)
     ]
+
+    def pieces_of(layer, index):
+        return [attention[layer][name] for name in groups[layer][index]["names"]]
+
+    def heads_bias(layer, index):
+        names = groups[layer][index]["names"]
+        return jnp.stack(
+            [
+                jnp.concatenate([bias_of(name, layer, 0, n_qv) for name in names]),
+                jnp.zeros((sum(pairs_of[name] for name in names) * 128,), f32),
+                jnp.concatenate([bias_of(name, layer, n_qv, n_qv) for name in names]),
+            ]
+        )[:, None]
+
     meta = core[None].astype(jnp.int32)
 
-    kept = []
-    normed = first_norm(x, eight_rows(jnp.zeros((D,), f32), weights[0]["gains"][0], weights[0]["shifts"][0]))
+    def into_heads(layer, index, normed):
+        q, kv = project_heads(normed, pieces_of(layer, index), heads_bias(layer, index))
+        return q, kv, swap(kv)
+
+    def attended(layer, index, projected):
+        group = groups[layer][index]
+        return tuple(projected) + tuple(attend(group["meta"], *projected, kcol, group["qcol"]))
+
+    def fed(layer, x, saved):
+        vectors = eight_rows(end_biases[layer][0], gains[layer][1], shifts[layer][1], end_biases[layer][1])
+        pieces = [p for index in range(len(saved)) for p in pieces_of(layer, index)]
+        bias = [bias_of("own", layer, 2 * n_qv, n_up)]
+        bias = [half_of(bias[0], 0, core), half_of(bias[0], 0, 1 - core)]
+        bias += [bias_of(name, layer, 2 * n_qv, n_up) for name in ("near", "near_too")]
+        bias = jnp.concatenate([part.reshape(STEPS, -1) for part in bias], axis=1)[:, None]
+        return feed(meta, x, [v[3] for v in saved], pieces, vectors, bias, feeding[layer])
+
+    def fed_last(layer, middle, total):
+        following = min(layer + 1, 1)
+        vectors = eight_rows(jnp.zeros((D,), f32), gains[following][0], shifts[following][0])
+        bias = [bias_of(name, layer, 2 * n_qv, n_up).reshape(STEPS, -1) for name in ("far", "far_too")]
+        return feed_last(middle, total, vectors, jnp.concatenate(bias, axis=1).reshape(1, -1), feeding[layer])
+
+    kept = [None, None]
+    chains.start(gathered_heads(attention_own[0], attention[0], (1, 1)))
+    x = chains.launch(x)
+    normed = first_norm(x, eight_rows(jnp.zeros((D,), f32), gains[0][0], shifts[0][0]))
     for layer in range(2):
-        w = weights[layer]
-        saved = []
-        for group in groups[layer]:
-            q, kv = project_heads(normed, group["pieces"], group["bias"])
-            kvo = swap(kv)
-            o, qx = attend(group["meta"], q, kv, kvo, kcol, group["qcol"])
-            saved.append((q, kv, kvo, o, qx))
-        after, middle = mix(
-            x,
-            [s[3] for s in saved],
-            [p for group in groups[layer] for p in group["pieces"]],
-            eight_rows(w["ends"][0], w["gains"][1], w["shifts"][1]),
+        saved = [None] * 3
+        saved[OWN] = attended(layer, OWN, into_heads(layer, OWN, normed))
+        (normed, saved[OWN], feed_own), _ = chains.step(
+            (normed, saved[OWN], feed_own), lambda: gathered_feed(feed_own[layer], feeding[layer], (2, 1))
         )
-        following = weights[min(layer + 1, 1)]
-        pre, hidden, result, normed_next = feed(
-            meta, middle, after, eight_rows(w["ends"][1], following["gains"][0], following["shifts"][0]), w["feed_bias"], w["feed"]
+        saved[NEAR] = attended(layer, NEAR, into_heads(layer, NEAR, normed))
+        normed, saved[NEAR] = chains.step((normed, saved[NEAR]))
+        saved[FAR] = attended(layer, FAR, into_heads(layer, FAR, normed))
+        saved = chains.step(saved)
+        slope, hidden, after, middle, total = fed(layer, x, saved)
+        (total, attention_own, ends), following = chains.step(
+            (total, attention_own, ends),
+            lambda: once(row_from(1), 1) if layer else gathered_heads(attention_own[1], attention[1], (2, 1)),
         )
-        kept.append((x, normed, saved, after, middle, pre, hidden))
-        x, normed = result, normed_next
-
-    sent_back = row_to(1, x)
-    grad = row_from(1)
-
-    matrices, vector_sums = [None, None], [None, None]
-    for layer in (1, 0):
-        w = weights[layer]
-        x_in, normed, saved, after, middle, pre, hidden = kept[layer]
-        keep, send, unit_sums, grad_after, low, sums_two = feed_back(
-            meta, grad, middle, after, w["gains"][1], pre, hidden, w["feed"]
+        slope_last, hidden_last, result, normed_next = fed_last(layer, middle, total)
+        kept[layer] = (x, normed, saved, after, middle, (slope, slope_last), (hidden, hidden_last))
+        if layer == 0:
+            x, normed = chains.step((result, normed_next))
+    x, *sent_back = chains.step(result, lambda: once(row_to(1, result, (0, 1)), 1))
+    grad = chosen_rows(following.result)
+
+    def heads_gradients(layer, index, low):
+        group = groups[layer][index]
+        q, kv, kvo, o, qx = kept[layer][2][index]
+        return attend_back(group["meta"], q, kv, kvo, kcol, qx, heads_back(low, pieces_of(layer, index)), o)
+
+    def weight_gradients(layer, index, grads, low, so_far, last):
+        group = groups[layer][index]
+        norm = (kept[layer][0], low, gains[layer][0]) if last else None
+        return project_back(
+            meta, group["names"], *grads, kept[layer][2][index][3], kept[layer][1], low, pieces_of(layer, index), so_far, norm
         )
-        total = plus(keep, swap(send))
-        part = total.shape[2] // 4
-        feed_grads = summed(
-            total[:, :, : 2 * part].reshape(2, -1, D), total[:, :, 2 * part : 3 * part].reshape(2, -1, D), total[:, :, 3 * part :].reshape(2, -1, D), core
-        )
-        so_far = None
-        sums_of, kept_rows = {}, {}
-        order = list(reversed(range(len(groups[layer]))))
-        for index in order:
-            group = groups[layer][index]
-            q, kv, kvo, o, qx = saved[index]
-            grad_heads = heads_back(low, group["pieces"])
-            dq, dkv, dkvo = attend_back(group["meta"], q, kv, kvo, kcol, qx, grad_heads, o)
-            got = swap(dkvo)
-            last = index == order[-1]
-            norm = (x_in, grad_after, w["gains"][0]) if last else None
-            results = project_back(meta, group["names"], dq, dkv, got, o, normed, low, group["pieces"], so_far, norm)
-            keep, send, bias_sums = results[:3]
-            if last:
-                grad, sums_one = results[3:]
-            else:
-                so_far = results[3]
-            total = plus(keep, swap(send))
-            at = at_kept = 0
+
+    def sums_of(layer, results, unit_sums, sums_one, sums_two):
+        parts = {}
+        for index, group in enumerate(groups[layer]):
+            at = 0
             for name in group["names"]:
                 size = pairs_of[name] * 128
-                sums_of[name] = bias_sums[0:2, at : at + size]
+                parts[name] = results[index][2][0:2, at : at + size]
                 at += size
-                if not name.endswith("_too"):
-                    size = size // 2 if name == "own" else size
-                    kept_rows[name] = total[:, at_kept : at_kept + size]
-                    at_kept += size
-        attention_grads = summed(kept_rows["near"], kept_rows["far"], kept_rows["own"], core)
-        matrices[layer] = (attention_grads, feed_grads)
         unit_sums = unit_sums[:, 0]
         part = unit_sums.shape[1] // 8
 
@@ -1274,16 +1466,66 @@
 
         own_keep, own_send = unit_part(0, 1), unit_part(1, 1)
         own = jnp.concatenate([jnp.where(first_core, own_keep, own_send), jnp.where(first_core, own_send, own_keep)])
-        flat = jnp.concatenate(
+        return jnp.concatenate(
             [
                 jnp.stack([sums_one[0], sums_two[0], sums_one[1], sums_two[1], sums_two[2], sums_two[3]]),
-                in_order(*[sums_of[name] for name in PIECES], core, chip),
+                in_order(*[parts[name] for name in PIECES], core, chip),
                 in_order(own, unit_part(2, 2), unit_part(4, 2), unit_part(6, 1), unit_part(7, 1), core, chip).reshape(-1, D),
             ]
         )
-        vector_sums[layer] = lax.psum(flat, ("section", "dp", "tensor"))
-
-    first_rows = row_to(0, grad)
+
+    def feed_gradients(layer, grad):
+        _, _, _, after, middle, slope, hidden = kept[layer]
+        return feed_back(meta, grad, middle, after, gains[layer][1], slope, hidden, feeding[layer])
+
+    def backward(layer, grad, others, *new):
+        keep, send, unit_sums, low, sums_two = feed_gradients(layer, grad)
+        (low, keep, send, others), feed_sums, *started = chains.step(
+            (low, keep, send, others),
+            lambda: summed_feed(meta, keep, send, (1, 2, 2, 2, 1, 1, 1)),
+            *(lambda make=make: make(others) for make in new),
+        )
+        results = [None] * 3
+        dq_far, dkv_far, sent_far = heads_gradients(layer, FAR, low)
+        (low, sent_far), got_far = chains.step((low, sent_far), lambda: once(swapping(sent_far), 1))
+        dq_near, dkv_near, sent_near = heads_gradients(layer, NEAR, low)
+        (low, sent_near), got_near = chains.step((low, sent_near), lambda: once(swapping(sent_near), 1))
+        results[FAR] = weight_gradients(layer, FAR, (dq_far, dkv_far, got_far.result), low, None, False)
+        (low, results[FAR]), far_sum = chains.step((low, results[FAR]), lambda: summed_far(*results[FAR][:2], (1, 1)))
+        results[NEAR] = weight_gradients(layer, NEAR, (dq_near, dkv_near, got_near.result), low, results[FAR][3], False)
+        (low, results[NEAR]), near_sum = chains.step(
+            (low, results[NEAR]), lambda: summed_near(*results[NEAR][:2], core, (1, 2, 1))
+        )
+        dq_own, dkv_own, sent_own = heads_gradients(layer, OWN, low)
+        (low, sent_own), got_own = chains.step((low, sent_own), lambda: once(swapping(sent_own), 1))
+        low, dq_own, dkv_own = chains.step((low, dq_own, dkv_own))
+        results[OWN] = weight_gradients(layer, OWN, (dq_own, dkv_own, got_own.result), low, results[NEAR][3], True)
+        grad, sums_one = results[OWN][3:]
+        sums = sums_of(layer, results, unit_sums, sums_one, sums_two)
+        return grad, results[OWN], sums, feed_sums, near_sum, far_sum, started
+
+    grad, own, sums_upper, upper_feed, near_sum, far_sum, again = backward(
+        1, grad, x, lambda row: once(row_to(1, row, (2, 3)), 1)
+    )
+    sent_back += again
+    (grad, own), own_sum = chains.step((grad, own), lambda: once(swapping(own[1]), 1))
+
+    def summed_heads(_, keep=own[0], own_sum=own_sum, near_sum=near_sum, far_sum=far_sum):
+        return summed_over_line(plus(keep, own_sum.result, *near_sum.result, far_sum.result), iter((1, 1, 1, 1)))
+
+    grad, own, sums_lower, lower_feed, near_sum, far_sum, (upper_heads,) = backward(0, grad, (), summed_heads)
+    (grad, sums_lower, own), first_one, own_sum, both_sums = chains.step(
+        (grad, sums_lower, own),
+        lambda: once(row_to(0, grad, (0, 1)), 1),
+        lambda: once(swapping(own[1]), 1),
+        lambda: summed_everywhere(jnp.stack([sums_lower, sums_upper])),
+    )
+    grad, first_two, lower_heads = chains.step(
+        grad,
+        lambda: once(row_to(0, grad, (2, 3)), 2),
+        lambda: summed_over_line(plus(own[0], own_sum.result, *near_sum.result, far_sum.result), iter((1, 1, 1, 1))),
+    )
+    first_rows = [first_one, first_two]
 
     def rows_of(got):
         return [
@@ -1292,9 +1534,6 @@
             )
             for row in CHIPS
         ]
-
-    ends_out = jnp.stack([jnp.where(first_core, a, b) for a, b in zip(rows_of(first_rows), rows_of(sent_back))])
-    ends_out = ends_out.astype(f32).reshape(1, micro, rows_here, seg, D)
 
     def finished(lower, upper):
         to_upper = lax.ppermute(upper, "section", [(0, 1)])
@@ -1305,8 +1544,29 @@
             jnp.concatenate([to_upper, upper], axis=1),
         ).astype(f32)
 
-    attention_grads, feed_grads = (finished(a, b) for a, b in zip(*matrices))
-    sums = jnp.where(first_core, vector_sums[0], vector_sums[1])
+    def feed_outputs():
+        grads = finished(lower_feed.result, upper_feed.result)
+        return grads[0].T[None], grads[1:]
+
+    def ends_outputs():
+        first, second = ([*chains_of[0].result, *chains_of[1].result] for chains_of in (first_rows, sent_back))
+        ends = jnp.stack([jnp.where(first_core, a, b) for a, b in zip(rows_of(first), rows_of(second))])
+        return ends.astype(f32).reshape(1, micro, rows_here, seg, D)
+
+    ready, waiting = {}, {"ends": (ends_outputs, first_rows), "feed": (feed_outputs, [lower_feed, upper_feed])}
+    while any(not chain.done for chain in chains.running):
+        ready = chains.step(ready)
+        for name in list(waiting):
+            make, needed = waiting[name]
+            if all(chain.done for chain in needed):
+                ready[name] = make()
+                del waiting[name]
+    for name, (make, _) in waiting.items():
+        ready[name] = make()
+    ends_out, (grad_up, grad_down) = ready["ends"], ready["feed"]
+    attention_grads = finished(lower_heads.result, upper_heads.result)
+    both_sums = both_sums.result
+    sums = jnp.where(first_core, both_sums[0], both_sums[1])
     grad_qv = lax.dynamic_slice_in_dim(sums[6:8], chip * n_qv, n_qv, 1)[None]
     grad_up_bias = lax.dynamic_slice_in_dim(sums[8:].reshape(-1), chip * n_up, n_up, 0)[None]
     return (
@@ -1316,9 +1576,9 @@
         jnp.swapaxes(attention_grads[:3], 1, 2)[None],
         grad_qv,
         attention_grads[3:],
-        feed_grads[0].T[None],
+        grad_up,
         grad_up_bias,
-        feed_grads[1:],
+        grad_down,
         sums[4:6][None],
     )
 

time: 1400 us -> 1060 us (0.76)
  waiting for transfers between devices: 533 us -> 156 us
  Pallas kernels: 541 us -> 595 us
  local copies, waits for them, and re-layouts: 101 us -> 80.5 us
    psum x2 -> x0, waiting for transfers between devices: 299 us -> none  [the longest x1 223 us: summed(): return lax.psum(total, 'dp')]
    ppermute x34, waiting for transfers between devices: 221 us -> 31.9 us  [hop(): return lax.ppermute(value, ST, pairs)]
    ppermute x0 -> x21, waiting for transfers between devices: none -> 106 us  [exchanged(): return lax.ppermute(value, axis, [(n, n ^ distance) for n in range(count)])]
    pallas_call x4 -> x6, Pallas kernels: 77.6 us -> 106 us  [the longest x2 60.1 us: feed(): pl.pallas_call(partial(feed_kernel, (len(heads), len(heads_pieces))), gri...]
    pallas_call x2, Pallas kernels: 124 us -> 98.9 us  [feed_back(): pl.pallas_call(feed_back_kernel, grid_spec=pltpu.PrefetchScalarGridSpec(n...]
    ppermute x0 -> x21, starting transfers between devices: none -> 23.9 us  [exchanged(): return lax.ppermute(value, axis, [(n, n ^ distance) for n in range(count)])]
    unnamed x234 -> x156, local copies, waits for them, and re-layouts: 50 us -> 28.3 us
    pallas_call x4 -> x6, Pallas kernels: 23.3 us -> 36.9 us  [project_heads(): pl.pallas_call(partial(project_kernel, len(pieces)), grid=(3,), in_specs=...]
  transfers between devices with their start and end apart: 70 -> 94, of which waited for: 14 -> 34; matrix products, arithmetic and copies ran while one was open for 10% -> 11% of each run, Pallas kernels for 27% -> 53%
where the time goes in v2:
time: 1060 us; the launch traced here: 1050 us
  Pallas kernels  595 us (56%)
  waiting for transfers between devices  156 us (15%)
  other arithmetic  108 us (10%)
  starting transfers between devices  107 us (10%)
  local copies, waits for them, and re-layouts  80.5 us (8%)
    pallas_call x6, Pallas kernels, attend_back(): pl.pallas_call(partial(attend_back_kernel, seg), grid_spec=pltpu.Prefetch...  146 us
    ppermute x21, waiting for transfers between devices, exchanged(): return lax.ppermute(value, axis, [(n, n ^ distance) for n in range(count)])  106 us
    pallas_call x6, Pallas kernels, attend(): pl.pallas_call(partial(attend_kernel, seg), grid_spec=pltpu.PrefetchScala...  101 us
    pallas_call x2, Pallas kernels, feed_back(): pl.pallas_call(feed_back_kernel, grid_spec=pltpu.PrefetchScalarGridSpec(n...  98.9 us
    pallas_call x6, Pallas kernels, project_back(): pl.pallas_call(partial(project_back_kernel, groups, so_far is None, norm...  80.7 us
    ppermute x34, starting transfers between devices, hop(): return lax.ppermute(value, ST, pairs)  67.4 us
    pallas_call x2, Pallas kernels, feed(): pl.pallas_call(partial(feed_kernel, (len(heads), len(heads_pieces))), gri...  60.1 us
    convert_element_type x18, other arithmetic, plus(): return total.astype(bf16)  42.2 us
  transfers between devices with their start and end apart: 94, of which 34 were waited for; matrix products, arithmetic and copies ran while one was open for 11% of the time, Pallas kernels for 53%

profile of v2, /device:TPU:0, one launch (start us, length us, event | category | flops | bytes accessed | tf_op | source)
XLA Modules:
  0.0 1050.2 jit_solution(13226065485317375134)
XLA Ops:
  5.0 9.6 collective-permute-start
  27.9 5.8 collective-permute-start.3
  60.1 5.4 project.6
  69.2 13.3 %attend.6 = (bf16[1024,256]{1,0:T(8,128)(2,1)}, bf16[1024,256]{1,0:T(8,128)(2,1)}) custom-call(s32[3]{0:T(128)} %pad_add_fusion.meta, bf16[1024,256]{1,0:T(8,128)(2,1)} %get-tuple-element.782.q, bf16[2,1024,256]{2,1,0:T(8,128)(2,1)} %get-tuple-element.783.kv, bf16[2,1024,256]{2,1,0:T(8,128)(2,1)} %collective-permute-done.6.kvo, ...), custom_call_target="tpu_custom_call" | custom-call | flops 671088640 | bytes 458752 | tf_op jit(solution)/shard_map/attend/pallas_call | solution.py:509
  82.5 5.8 broadcast_select_fusion
  94.7 7.7 project.7
  107.4 23.8 %attend.7 = (bf16[1024,512]{1,0:T(8,128)(2,1)}, bf16[1024,512]{1,0:T(8,128)(2,1)}) custom-call(s32[5]{0:T(128)} %pad_add_fusion.1.meta, bf16[1024,512]{1,0:T(8,128)(2,1)} %get-tuple-element.737.q, bf16[2,1024,512]{2,1,0:T(8,128)(2,1)} %get-tuple-element.738.kv, bf16[2,1024,512]{2,1,0:T(8,128)(2,1)} %collective-permute-done.10.kvo, ...), custom_call_target="tpu_custom_call" | custom-call | flops 1342177280 | bytes 917504 | tf_op jit(solution)/shard_map/attend/pallas_call | solution.py:509
  135.9 5.5 project.8
  145.2 13.4 %attend.8 = (bf16[1024,256]{1,0:T(8,128)(2,1)}, bf16[1024,256]{1,0:T(8,128)(2,1)}) custom-call(s32[3]{0:T(128)} %pad_add_fusion.2.meta, bf16[1024,256]{1,0:T(8,128)(2,1)} %get-tuple-element.722.q, bf16[2,1024,256]{2,1,0:T(8,128)(2,1)} %get-tuple-element.723.kv, bf16[2,1024,256]{2,1,0:T(8,128)(2,1)} %copy-done.41, bf16[2048,128]{1,0:T(8,128)(2,1)} %pad_maximum_fusion.6.kcol, ...), custom_call_target="tpu_custom_call" | custom-call | flops 671088640 | bytes 458752 | tf_op jit(solution)/shard_map/attend/pallas_call | solution.py:509
  170.8 30.1 %feed.2 = (bf16[4,1024,768]{2,1,0:T(8,128)(2,1)}, bf16[4,1024,768]{2,1,0:T(8,128)(2,1)}, f32[1024,1024]{1,0:T(8,128)}, bf16[1024,1024]{1,0:T(8,128)(2,1)}, f32[1024,1024]{1,0:T(8,128)}) custom-call(s32[1]{0:T(128)} %bitcast.meta, bf16[1024,256]{1,0:T(8,128)(2,1)} %get-tuple-element.508.refs_0_.o.refs_3_, ...), custom_call_target="tpu_custom_call" | custom-call | flops 1879048192 | bytes 5242880 | tf_op jit(solution)/shard_map/feed/pallas_call | solution.py:787
  205.4 13.3 %feed_last.2 = (bf16[4,1024,256]{2,1,0:T(8,128)(2,1)}, bf16[4,1024,256]{2,1,0:T(8,128)(2,1)}, bf16[1024,1024]{1,0:T(8,128)(2,1)}, bf16[1024,1024]{1,0:T(8,128)(2,1)}) custom-call(bf16[1024,1024]{1,0:T(8,128)(2,1)} %get-tuple-element.511.middle, f32[1024,1024]{1,0:T(8,128)} %get-tuple-element.517.so_far, f32[8,1024]{1,0:T(8,128)} %get-tuple-element.1060.vectors, ...), custom_call_target="tpu_custom_call" | custom-call | flops 536870912 | bytes 2359296 | tf_op jit(solution)/shard_map/feed_last/pallas_call | solution.py:837
  218.7 5.4 project.9
  228.0 13.5 %attend.9 = (bf16[1024,256]{1,0:T(8,128)(2,1)}, bf16[1024,256]{1,0:T(8,128)(2,1)}) custom-call(s32[3]{0:T(128)} %pad_add_fusion.meta, bf16[1024,256]{1,0:T(8,128)(2,1)} %get-tuple-element.666.q, bf16[2,1024,256]{2,1,0:T(8,128)(2,1)} %get-tuple-element.667.kv, bf16[2,1024,256]{2,1,0:T(8,128)(2,1)} %copy-done.42, bf16[2048,128]{1,0:T(8,128)(2,1)} %pad_maximum_fusion.6.kcol, ...), custom_call_target="tpu_custom_call" | custom-call | flops 671088640 | bytes 458752 | tf_op jit(solution)/shard_map/attend/pallas_call | solution.py:509
  247.4 7.5 project.10
  260.5 23.9 %attend.10 = (bf16[1024,512]{1,0:T(8,128)(2,1)}, bf16[1024,512]{1,0:T(8,128)(2,1)}) custom-call(s32[5]{0:T(128)} %pad_add_fusion.1.meta, bf16[1024,512]{1,0:T(8,128)(2,1)} %get-tuple-element.627.q, bf16[2,1024,512]{2,1,0:T(8,128)(2,1)} %get-tuple-element.628.kv, bf16[2,1024,512]{2,1,0:T(8,128)(2,1)} %copy-done.24, bf16[2048,128]{1,0:T(8,128)(2,1)} %pad_maximum_fusion.6.kcol, ...), custom_call_target="tpu_custom_call" | custom-call | flops 1342177280 | bytes 917504 | tf_op jit(solution)/shard_map/attend/pallas_call | solution.py:509
  288.2 5.4 project.11
  297.5 13.3 %attend.11 = (bf16[1024,256]{1,0:T(8,128)(2,1)}, bf16[1024,256]{1,0:T(8,128)(2,1)}) custom-call(s32[3]{0:T(128)} %pad_add_fusion.2.meta, bf16[1024,256]{1,0:T(8,128)(2,1)} %get-tuple-element.614.q, bf16[2,1024,256]{2,1,0:T(8,128)(2,1)} %get-tuple-element.615.kv, bf16[2,1024,256]{2,1,0:T(8,128)(2,1)} %copy-done.43, bf16[2048,128]{1,0:T(8,128)(2,1)} %pad_maximum_fusion.6.kcol, ...), custom_call_target="tpu_custom_call" | custom-call | flops 671088640 | bytes 458752 | tf_op jit(solution)/shard_map/attend/pallas_call | solution.py:509
  322.3 30.1 %feed.3 = (bf16[4,1024,768]{2,1,0:T(8,128)(2,1)}, bf16[4,1024,768]{2,1,0:T(8,128)(2,1)}, f32[1024,1024]{1,0:T(8,128)}, bf16[1024,1024]{1,0:T(8,128)(2,1)}, f32[1024,1024]{1,0:T(8,128)}) custom-call(s32[1]{0:T(128)} %bitcast.meta, bf16[1024,256]{1,0:T(8,128)(2,1)} %get-tuple-element.580.refs_0_.o.refs_3_, ...), custom_call_target="tpu_custom_call" | custom-call | flops 1879048192 | bytes 5242880 | tf_op jit(solution)/shard_map/feed/pallas_call | solution.py:787
  364.1 13.4 %feed_last.3 = (bf16[4,1024,256]{2,1,0:T(8,128)(2,1)}, bf16[4,1024,256]{2,1,0:T(8,128)(2,1)}, bf16[1024,1024]{1,0:T(8,128)(2,1)}, bf16[1024,1024]{1,0:T(8,128)(2,1)}) custom-call(bf16[1024,1024]{1,0:T(8,128)(2,1)} %get-tuple-element.584.middle, f32[1024,1024]{1,0:T(8,128)} %get-tuple-element.589.so_far, f32[8,1024]{1,0:T(8,128)} %get-tuple-element.1060.vectors, ...), custom_call_target="tpu_custom_call" | custom-call | flops 536870912 | bytes 2359296 | tf_op jit(solution)/shard_map/feed_last/pallas_call | solution.py:837
  377.6 10.1 collective-permute-done.32
  402.2 49.3 %feed_back.2 = (bf16[2,4,512,1024]{3,2,1,0:T(8,128)(2,1)}, bf16[2,4,512,1024]{3,2,1,0:T(8,128)(2,1)}, f32[4,8,1024]{2,1,0:T(8,128)}, bf16[1024,1024]{1,0:T(8,128)(2,1)}, f32[8,1024]{1,0:T(8,128)}) custom-call(s32[1]{0:T(128)} %bitcast.meta, bf16[1024,1024]{1,0:T(8,128)(2,1)} %pad_maximum_fusion.3.above, bf16[1024,1024]{1,0:T(8,128)(2,1)} %get-tuple-element.584.middle, ...), custom_call_target="tpu_custom_call" | custom-call | flops 4294967296 | bytes 14417920 | tf_op jit(solution)/shard_map/feed_back/pallas_call | solution.py:919
  452.8 7.0 collective-permute-start.37
  463.1 19.1 %attend_back.6 = (bf16[1024,256]{1,0:T(8,128)(2,1)}, bf16[2,1024,256]{2,1,0:T(8,128)(2,1)}, bf16[2,1024,256]{2,1,0:T(8,128)(2,1)}) custom-call(s32[3]{0:T(128)} %pad_add_fusion.2.meta, bf16[1024,256]{1,0:T(8,128)(2,1)} %get-tuple-element.614.q, bf16[2,1024,256]{2,1,0:T(8,128)(2,1)} %get-tuple-element.615.kv, bf16[2,1024,256]{2,1,0:T(8,128)(2,1)} %copy-done.43, ...), custom_call_target="tpu_custom_call" | custom-call | flops 1677721600 | bytes 851968 | tf_op jit(solution)/shard_map/attend_back/pallas_call | solution.py:603
  482.2 9.8 meet.2
  497.7 35.0 %attend_back.7 = (bf16[1024,512]{1,0:T(8,128)(2,1)}, bf16[2,1024,512]{2,1,0:T(8,128)(2,1)}, bf16[2,1024,512]{2,1,0:T(8,128)(2,1)}) custom-call(s32[5]{0:T(128)} %pad_add_fusion.1.meta, bf16[1024,512]{1,0:T(8,128)(2,1)} %get-tuple-element.627.q, bf16[2,1024,512]{2,1,0:T(8,128)(2,1)} %get-tuple-element.628.kv, bf16[2,1024,512]{2,1,0:T(8,128)(2,1)} %copy-done.24, ...), custom_call_target="tpu_custom_call" | custom-call | flops 3355443200 | bytes 1703936 | tf_op jit(solution)/shard_map/attend_back/pallas_call | solution.py:603
  533.6 9.3 project_back.6
  548.0 16.0 %project_back.7 = (bf16[4,256,1024]{2,1,0:T(8,128)(2,1)}, bf16[4,256,1024]{2,1,0:T(8,128)(2,1)}, f32[8,512]{1,0:T(8,128)}, f32[1024,1024]{1,0:T(8,128)}) custom-call(s32[1]{0:T(128)} %bitcast.meta, bf16[1024,512]{1,0:T(8,128)(2,1)} %get-tuple-element.652.refs_0_, bf16[2,1024,512]{2,1,0:T(8,128)(2,1)} %get-tuple-element.653.refs_1_, ...), custom_call_target="tpu_custom_call" | custom-call | flops 939524096 | bytes 3276800 | tf_op jit(solution)/shard_map/project_back/pallas_call | solution.py:1053
  571.6 19.2 %attend_back.8 = (bf16[1024,256]{1,0:T(8,128)(2,1)}, bf16[2,1024,256]{2,1,0:T(8,128)(2,1)}, bf16[2,1024,256]{2,1,0:T(8,128)(2,1)}) custom-call(s32[3]{0:T(128)} %pad_add_fusion.meta, bf16[1024,256]{1,0:T(8,128)(2,1)} %get-tuple-element.666.q, bf16[2,1024,256]{2,1,0:T(8,128)(2,1)} %get-tuple-element.667.kv, bf16[2,1024,256]{2,1,0:T(8,128)(2,1)} %copy-done.42, ...), custom_call_target="tpu_custom_call" | custom-call | flops 1677721600 | bytes 851968 | tf_op jit(solution)/shard_map/attend_back/pallas_call | solution.py:603
  590.9 5.0 collective-permute-done.45
  595.9 5.0 add_convert_fusion.2
  610.3 14.9 %project_back.8 = (bf16[4,128,1024]{2,1,0:T(8,128)(2,1)}, bf16[4,128,1024]{2,1,0:T(8,128)(2,1)}, f32[8,256]{1,0:T(8,128)}, bf16[1024,1024]{1,0:T(8,128)(2,1)}, f32[8,1024]{1,0:T(8,128)}) custom-call(s32[1]{0:T(128)} %bitcast.meta, bf16[1024,256]{1,0:T(8,128)(2,1)} %get-tuple-element.687.refs_0_, bf16[2,1024,256]{2,1,0:T(8,128)(2,1)} %get-tuple-element.688.refs_1_, ...), custom_call_target="tpu_custom_call" | custom-call | flops 469762048 | bytes 2424832 | tf_op jit(solution)/shard_map/project_back/pallas_call | solution.py:1053
  625.2 7.1 collective-permute-done.48
  640.8 49.6 %feed_back.3 = (bf16[2,4,512,1024]{3,2,1,0:T(8,128)(2,1)}, bf16[2,4,512,1024]{3,2,1,0:T(8,128)(2,1)}, f32[4,8,1024]{2,1,0:T(8,128)}, bf16[1024,1024]{1,0:T(8,128)(2,1)}, f32[8,1024]{1,0:T(8,128)}) custom-call(s32[1]{0:T(128)} %bitcast.meta, bf16[1024,1024]{1,0:T(8,128)(2,1)} %get-tuple-element.703.above, bf16[1024,1024]{1,0:T(8,128)(2,1)} %get-tuple-element.511.middle, ...), custom_call_target="tpu_custom_call" | custom-call | flops 4294967296 | bytes 14417920 | tf_op jit(solution)/shard_map/feed_back/pallas_call | solution.py:919
  701.7 19.1 %attend_back.9 = (bf16[1024,256]{1,0:T(8,128)(2,1)}, bf16[2,1024,256]{2,1,0:T(8,128)(2,1)}, bf16[2,1024,256]{2,1,0:T(8,128)(2,1)}) custom-call(s32[3]{0:T(128)} %pad_add_fusion.2.meta, bf16[1024,256]{1,0:T(8,128)(2,1)} %get-tuple-element.722.q, bf16[2,1024,256]{2,1,0:T(8,128)(2,1)} %get-tuple-element.723.kv, bf16[2,1024,256]{2,1,0:T(8,128)(2,1)} %copy-done.41, ...), custom_call_target="tpu_custom_call" | custom-call | flops 1677721600 | bytes 851968 | tf_op jit(solution)/shard_map/attend_back/pallas_call | solution.py:603
  723.8 9.4 meet.3
  743.3 34.8 %attend_back.10 = (bf16[1024,512]{1,0:T(8,128)(2,1)}, bf16[2,1024,512]{2,1,0:T(8,128)(2,1)}, bf16[2,1024,512]{2,1,0:T(8,128)(2,1)}) custom-call(s32[5]{0:T(128)} %pad_add_fusion.1.meta, bf16[1024,512]{1,0:T(8,128)(2,1)} %get-tuple-element.737.q, bf16[2,1024,512]{2,1,0:T(8,128)(2,1)} %get-tuple-element.738.kv, ...), custom_call_target="tpu_custom_call" | custom-call | flops 3355443200 | bytes 1703936 | tf_op jit(solution)/shard_map/attend_back/pallas_call | solution.py:603
  779.3 9.3 project_back.9
  788.7 5.7 collective-permute-done.61
  801.3 16.2 %project_back.10 = (bf16[4,256,1024]{2,1,0:T(8,128)(2,1)}, bf16[4,256,1024]{2,1,0:T(8,128)(2,1)}, f32[8,512]{1,0:T(8,128)}, f32[1024,1024]{1,0:T(8,128)}) custom-call(s32[1]{0:T(128)} %bitcast.meta, bf16[1024,512]{1,0:T(8,128)(2,1)} %get-tuple-element.767.refs_0_, bf16[2,1024,512]{2,1,0:T(8,128)(2,1)} %get-tuple-element.768.refs_1_, ...), custom_call_target="tpu_custom_call" | custom-call | flops 939524096 | bytes 3276800 | tf_op jit(solution)/shard_map/project_back/pallas_call | solution.py:1053
  829.3 19.2 %attend_back.11 = (bf16[1024,256]{1,0:T(8,128)(2,1)}, bf16[2,1024,256]{2,1,0:T(8,128)(2,1)}, bf16[2,1024,256]{2,1,0:T(8,128)(2,1)}) custom-call(s32[3]{0:T(128)} %pad_add_fusion.meta, bf16[1024,256]{1,0:T(8,128)(2,1)} %get-tuple-element.782.q, bf16[2,1024,256]{2,1,0:T(8,128)(2,1)} %get-tuple-element.783.kv, ...), custom_call_target="tpu_custom_call" | custom-call | flops 1677721600 | bytes 851968 | tf_op jit(solution)/shard_map/attend_back/pallas_call | solution.py:603
  865.1 14.9 %project_back.11 = (bf16[4,128,1024]{2,1,0:T(8,128)(2,1)}, bf16[4,128,1024]{2,1,0:T(8,128)(2,1)}, f32[8,256]{1,0:T(8,128)}, bf16[1024,1024]{1,0:T(8,128)(2,1)}, f32[8,1024]{1,0:T(8,128)}) custom-call(s32[1]{0:T(128)} %bitcast.meta, bf16[1024,256]{1,0:T(8,128)(2,1)} %get-tuple-element.803.refs_0_, bf16[2,1024,256]{2,1,0:T(8,128)(2,1)} %get-tuple-element.804.refs_1_, ...), custom_call_target="tpu_custom_call" | custom-call | flops 469762048 | bytes 2424832 | tf_op jit(solution)/shard_map/project_back/pallas_call | solution.py:1053
  883.4 5.0 collective-permute-done.70
  901.7 23.3 %collective-permute-done.72 = bf16[2,128,1024]{2,1,0:T(8,128)(2,1)S(1)} collective-permute-done((bf16[2,128,1024]{2,1,0:T(8,128)(2,1)S(1)}, bf16[2,128,1024]{2,1,0:T(8,128)(2,1)S(1)}, u32[]{:S(2)}, u32[]{:S(2)}) %collective-permute-start.72) | collective-permute-done | bytes 524320 | tf_op jit(solution)/shard_map/ppermute | solution.py:1117
  936.5 17.3 %collective-permute-done.78 = bf16[2,128,1024]{2,1,0:T(8,128)(2,1)S(1)} collective-permute-done((bf16[2,128,1024]{2,1,0:T(8,128)(2,1)S(1)}, bf16[2,128,1024]{2,1,0:T(8,128)(2,1)S(1)}, u32[]{:S(2)}, u32[]{:S(2)}) %collective-permute-start.78) | collective-permute-done | bytes 524320 | tf_op jit(solution)/shard_map/ppermute | solution.py:1117
  965.4 19.2 %collective-permute-done.85 = bf16[4,32,1024]{2,1,0:T(8,128)(2,1)} collective-permute-done((bf16[4,32,1024]{2,1,0:T(8,128)(2,1)}, bf16[4,32,1024]{2,1,0:T(8,128)(2,1)}, u32[]{:S(2)}, u32[]{:S(2)}) %collective-permute-start.85) | collective-permute-done | bytes 262176 | tf_op jit(solution)/shard_map/ppermute | solution.py:1117
  1010.1 7.8 collective-permute-done.89
  1023.7 9.0 collective-permute-done.90
  1036.7 5.3 copy.106
  (604 shorter events, 328.8 us)
Async XLA Ops:
  5.0 32.9 %collective-permute-start = (bf16[512,1024]{1,0:T(8,128)(2,1)}, bf16[512,1024]{1,0:T(8,128)(2,1)}, u32[]{:S(2)}, u32[]{:S(2)}) collective-permute-start(bf16[512,1024]{1,0:T(8,128)(2,1)} %get-tuple-element.960), channel_id=1, source_target_pairs={{0,0},{1,17},{2,18},{3,3},{4,4},{5,21},{6,22},{7,7},{8,8},{9,25},{... | collective-permute-start | bytes 3145736 | tf_op jit(solution)/shard_map/ppermute | solution.py:386
  22.8 28.0 %collective-permute-start.4 = (bf16[1040,1024]{1,0:T(8,128)(2,1)}, bf16[1040,1024]{1,0:T(8,128)(2,1)}, u32[]{:S(2)}, u32[]{:S(2)}) collective-permute-start(bf16[1040,1024]{1,0:T(8,128)(2,1)} %fusion.6), channel_id=1, source_target_pairs={{0,16},{16,0},{1,17},{17,1},{2,18},{18,2},{3,19},{19,3},{4,20},{20... | collective-permute-start | bytes 6389768 | tf_op jit(solution)/shard_map/ppermute | solution.py:390
  37.9 44.6 %collective-permute-start.7 = (bf16[2,1024,1024]{2,1,0:T(8,128)(2,1)}, bf16[2,1024,1024]{2,1,0:T(8,128)(2,1)}, u32[]{:S(2)}, u32[]{:S(2)}) collective-permute-start(bf16[2,1024,1024]{2,1,0:T(8,128)(2,1)} %pad_maximum_fusion), channel_id=1, source_target_pairs={{0,16},{16,0},{1,17},{17,1},{2,18},{18,2},{3,19},{19,3},{4,20},{20... | collective-permute-start | bytes 12582920 | tf_op jit(solution)/shard_map/ppermute | solution.py:390
  54.5 33.8 %collective-permute-start.8 = (bf16[1040,1024]{1,0:T(8,128)(2,1)S(1)}, bf16[1040,1024]{1,0:T(8,128)(2,1)}, u32[]{:S(2)}, u32[]{:S(2)}) collective-permute-start(bf16[1040,1024]{1,0:T(8,128)(2,1)S(1)} %get-tuple-element.454.refs_0_.refs_3_.refs_6_), channel_id=1, source_target_pairs={{0,1},{1,0},{2,3},{3,2},{16,18},{17,19},{18,16},{19,17},{4,5},{5,4... | collective-permute-start | bytes 6389768 | tf_op jit(solution)/shard_map/ppermute | solution.py:386
  102.5 28.8 %collective-permute-start.11 = (bf16[528,1024]{1,0:T(8,128)(2,1)}, bf16[528,1024]{1,0:T(8,128)(2,1)S(1)}, u32[]{:S(2)}, u32[]{:S(2)}) collective-permute-start(bf16[528,1024]{1,0:T(8,128)(2,1)} %pad_maximum_fusion.4), channel_id=1, source_target_pairs={{0,2},{1,3},{2,0},{3,1},{16,17},{17,16},{18,19},{19,18},{4,6},{5,7... | collective-permute-start | bytes 3244040 | tf_op jit(solution)/shard_map/ppermute | solution.py:386
  105.7 56.6 %collective-permute-start.14 = (bf16[2,1024,1024]{2,1,0:T(8,128)(2,1)}, bf16[2,1024,1024]{2,1,0:T(8,128)(2,1)}, u32[]{:S(2)}, u32[]{:S(2)}) collective-permute-start(bf16[2,1024,1024]{2,1,0:T(8,128)(2,1)} %get-tuple-element.491), channel_id=1, source_target_pairs={{0,1},{1,0},{2,3},{3,2},{16,18},{17,19},{18,16},{19,17},{4,5},{5,4... | collective-permute-start | bytes 12582920 | tf_op jit(solution)/shard_map/ppermute | solution.py:386
  166.8 34.1 %collective-permute-start.16 = (bf16[2,512,1024]{2,1,0:T(8,128)(2,1)}, bf16[2,512,1024]{2,1,0:T(8,128)(2,1)}, u32[]{:S(2)}, u32[]{:S(2)}) collective-permute-start(bf16[2,512,1024]{2,1,0:T(8,128)(2,1)} %constant_dynamic-slice_fusion.29), channel_id=1, source_target_pairs={{0,2},{1,3},{2,0},{3,1},{16,17},{17,16},{18,19},{19,18},{4,6},{5,7... | collective-permute-start | bytes 6291464 | tf_op jit(solution)/shard_map/ppermute | solution.py:386
  201.3 40.3 %collective-permute-start.19 = (bf16[1040,1024]{1,0:T(8,128)(2,1)S(1)}, bf16[1040,1024]{1,0:T(8,128)(2,1)}, u32[]{:S(2)}, u32[]{:S(2)}) collective-permute-start(bf16[1040,1024]{1,0:T(8,128)(2,1)S(1)} %copy-done.1), channel_id=1, source_target_pairs={{0,1},{1,0},{2,3},{3,2},{16,18},{17,19},{18,16},{19,17},{4,5},{5,4... | collective-permute-start | bytes 6389768 | tf_op jit(solution)/shard_map/ppermute | solution.py:386
  255.2 29.2 %collective-permute-start.22 = (bf16[528,1024]{1,0:T(8,128)(2,1)}, bf16[528,1024]{1,0:T(8,128)(2,1)S(1)}, u32[]{:S(2)}, u32[]{:S(2)}) collective-permute-start(bf16[528,1024]{1,0:T(8,128)(2,1)} %pad_maximum_fusion.5), channel_id=1, source_target_pairs={{0,2},{1,3},{2,0},{3,1},{16,17},{17,16},{18,19},{19,18},{4,6},{5,7... | collective-permute-start | bytes 3244040 | tf_op jit(solution)/shard_map/ppermute | solution.py:386
  257.2 57.6 %collective-permute-start.25 = (bf16[2,1024,1024]{2,1,0:T(8,128)(2,1)}, bf16[2,1024,1024]{2,1,0:T(8,128)(2,1)}, u32[]{:S(2)}, u32[]{:S(2)}) collective-permute-start(bf16[2,1024,1024]{2,1,0:T(8,128)(2,1)} %get-tuple-element.563), channel_id=1, source_target_pairs={{0,1},{1,0},{2,3},{3,2},{16,18},{17,19},{18,16},{19,17},{4,5},{5,4... | collective-permute-start | bytes 12582920 | tf_op jit(solution)/shard_map/ppermute | solution.py:386
  318.2 34.2 %collective-permute-start.27 = (bf16[2,512,1024]{2,1,0:T(8,128)(2,1)}, bf16[2,512,1024]{2,1,0:T(8,128)(2,1)S(1)}, u32[]{:S(2)}, u32[]{:S(2)}) collective-permute-start(bf16[2,512,1024]{2,1,0:T(8,128)(2,1)} %constant_dynamic-slice_fusion.27), channel_id=1, source_target_pairs={{0,2},{1,3},{2,0},{3,1},{16,17},{17,16},{18,19},{19,18},{4,6},{5,7... | collective-permute-start | bytes 6291464 | tf_op jit(solution)/shard_map/ppermute | solution.py:386
  390.7 60.8 %collective-permute-start.33 = (bf16[512,1024]{1,0:T(8,128)(2,1)}, bf16[512,1024]{1,0:T(8,128)(2,1)S(1)}, u32[]{:S(2)}, u32[]{:S(2)}) collective-permute-start(bf16[512,1024]{1,0:T(8,128)(2,1)} %get-tuple-element.610), channel_id=1, source_target_pairs={{0,16},{17,17},{18,18},{3,19},{4,20},{21,21},{22,22},{7,23},{8,24}... | collective-permute-start | bytes 3145736 | tf_op jit(solution)/shard_map/ppermute | solution.py:386
  394.9 56.6 %collective-permute-start.34 = (bf16[512,1024]{1,0:T(8,128)(2,1)}, bf16[512,1024]{1,0:T(8,128)(2,1)S(1)}, u32[]{:S(2)}, u32[]{:S(2)}) collective-permute-start(bf16[512,1024]{1,0:T(8,128)(2,1)} %get-tuple-element.611), channel_id=1, source_target_pairs={{1,16},{16,17},{19,18},{2,19},{5,20},{20,21},{23,22},{6,23},{9,24}... | collective-permute-start | bytes 3145736 | tf_op jit(solution)/shard_map/ppermute | solution.py:386
  451.5 30.7 %collective-permute-start.35 = (bf16[2,4,512,1024]{3,2,1,0:T(8,128)(2,1)}, bf16[2,4,512,1024]{3,2,1,0:T(8,128)(2,1)}, u32[]{:S(2)}, u32[]{:S(2)}) collective-permute-start(bf16[2,4,512,1024]{3,2,1,0:T(8,128)(2,1)} %get-tuple-element.619), channel_id=1, source_target_pairs={{0,16},{16,0},{1,17},{17,1},{2,18},{18,2},{3,19},{19,3},{4,20},{20... | collective-permute-start | bytes 25165832 | tf_op jit(solution)/shard_map/ppermute | solution.py:390
  452.1 30.1 %collective-permute-start.36 = (bf16[512,1024]{1,0:T(8,128)(2,1)}, bf16[512,1024]{1,0:T(8,128)(2,1)S(1)}, u32[]{:S(2)}, u32[]{:S(2)}) collective-permute-start(bf16[512,1024]{1,0:T(8,128)(2,1)} %get-tuple-element.620), channel_id=1, source_target_pairs={{2,16},{19,17},{16,18},{1,19},{6,20},{23,21},{20,22},{5,23},{10,24... | collective-permute-start | bytes 3145736 | tf_op jit(solution)/shard_map/ppermute | solution.py:386
  452.8 29.4 %collective-permute-start.37 = (bf16[512,1024]{1,0:T(8,128)(2,1)}, bf16[512,1024]{1,0:T(8,128)(2,1)}, u32[]{:S(2)}, u32[]{:S(2)}) collective-permute-start(bf16[512,1024]{1,0:T(8,128)(2,1)} %get-tuple-element.621), channel_id=1, source_target_pairs={{3,16},{18,17},{17,18},{0,19},{7,20},{22,21},{21,22},{4,23},{11,24... | collective-permute-start | bytes 3145736 | tf_op jit(solution)/shard_map/ppermute | solution.py:386
  492.0 40.6 %collective-permute-start.38 = (bf16[2,1024,256]{2,1,0:T(8,128)(2,1)}, bf16[2,1024,256]{2,1,0:T(8,128)(2,1)S(1)}, u32[]{:S(2)}, u32[]{:S(2)}) collective-permute-start(bf16[2,1024,256]{2,1,0:T(8,128)(2,1)} %get-tuple-element.632), channel_id=1, source_target_pairs={{0,16},{16,0},{1,17},{17,1},{2,18},{18,2},{3,19},{19,3},{4,20},{20... | collective-permute-start | bytes 3145736 | tf_op jit(solution)/shard_map/ppermute | solution.py:390
  492.1 50.9 %collective-permute-start.39 = (bf16[2,512,1024]{2,1,0:T(8,128)(2,1)}, bf16[2,512,1024]{2,1,0:T(8,128)(2,1)S(1)}, u32[]{:S(2)}, u32[]{:S(2)}) collective-permute-start(bf16[2,512,1024]{2,1,0:T(8,128)(2,1)} %bitcast.394), channel_id=1, source_target_pairs={{0,2},{1,3},{2,0},{3,1},{16,17},{17,16},{18,19},{19,18},{4,6},{5,7... | collective-permute-start | bytes 6291464 | tf_op jit(solution)/shard_map/ppermute | solution.py:386
  492.1 50.8 %collective-permute-start.40 = (bf16[2,512,1024]{2,1,0:T(8,128)(2,1)}, bf16[2,512,1024]{2,1,0:T(8,128)(2,1)}, u32[]{:S(2)}, u32[]{:S(2)}) collective-permute-start(bf16[2,512,1024]{2,1,0:T(8,128)(2,1)} %get-tuple-element.643), channel_id=1, source_target_pairs={{0,1},{1,0},{2,3},{3,2},{16,18},{17,19},{18,16},{19,17},{4,5},{5,4... | collective-permute-start | bytes 6291464 | tf_op jit(solution)/shard_map/ppermute | solution.py:386
  547.5 43.3 %collective-permute-start.43 = (bf16[2,512,1024]{2,1,0:T(8,128)(2,1)S(1)}, bf16[2,512,1024]{2,1,0:T(8,128)(2,1)}, u32[]{:S(2)}, u32[]{:S(2)}) collective-permute-start(bf16[2,512,1024]{2,1,0:T(8,128)(2,1)S(1)} %add_convert_fusion.3), channel_id=1, source_target_pairs={{0,1},{1,0},{2,3},{3,2},{16,18},{17,19},{18,16},{19,17},{4,5},{5,4... | collective-permute-start | bytes 6291464 | tf_op jit(solution)/shard_map/ppermute | solution.py:386
  548.0 42.9 %collective-permute-start.44 = (bf16[2,512,1024]{2,1,0:T(8,128)(2,1)}, bf16[2,512,1024]{2,1,0:T(8,128)(2,1)}, u32[]{:S(2)}, u32[]{:S(2)}) collective-permute-start(bf16[2,512,1024]{2,1,0:T(8,128)(2,1)} %collective-permute-done.40), channel_id=1, source_target_pairs={{0,16},{16,0},{1,17},{17,1},{2,18},{18,2},{3,19},{19,3},{4,20},{20... | collective-permute-start | bytes 6291464 | tf_op jit(solution)/shard_map/ppermute | solution.py:390
  566.7 29.2 %collective-permute-start.46 = (bf16[4,256,1024]{2,1,0:T(8,128)(2,1)}, bf16[4,256,1024]{2,1,0:T(8,128)(2,1)}, u32[]{:S(2)}, u32[]{:S(2)}) collective-permute-start(bf16[4,256,1024]{2,1,0:T(8,128)(2,1)} %get-tuple-element.674), channel_id=1, source_target_pairs={{0,16},{16,0},{1,17},{17,1},{2,18},{18,2},{3,19},{19,3},{4,20},{20... | collective-permute-start | bytes 6291464 | tf_op jit(solution)/shard_map/ppermute | solution.py:390
  567.2 28.8 %collective-permute-start.45 = (bf16[4,128,1024]{2,1,0:T(8,128)(2,1)}, bf16[4,128,1024]{2,1,0:T(8,128)(2,1)S(1)}, u32[]{:S(2)}, u32[]{:S(2)}) collective-permute-start(bf16[4,128,1024]{2,1,0:T(8,128)(2,1)} %add_convert_fusion.9), channel_id=1, source_target_pairs={{0,3},{1,2},{2,1},{3,0},{16,19},{17,18},{18,17},{19,16},{4,7},{5,6... | collective-permute-start | bytes 3145736 | tf_op jit(solution)/shard_map/ppermute | solution.py:386
  604.7 27.7 %collective-permute-start.49 = (bf16[4,256,1024]{2,1,0:T(8,128)(2,1)}, bf16[4,256,1024]{2,1,0:T(8,128)(2,1)}, u32[]{:S(2)}, u32[]{:S(2)}) collective-permute-start(bf16[4,256,1024]{2,1,0:T(8,128)(2,1)} %add_convert_fusion.2), channel_id=1, source_target_pairs={{0,1},{1,0},{2,3},{3,2},{16,18},{17,19},{18,16},{19,17},{4,5},{5,4... | collective-permute-start | bytes 6291464 | tf_op jit(solution)/shard_map/ppermute | solution.py:386
  637.1 53.3 %collective-permute-start.51 = (bf16[4,128,1024]{2,1,0:T(8,128)(2,1)}, bf16[4,128,1024]{2,1,0:T(8,128)(2,1)S(1)}, u32[]{:S(2)}, u32[]{:S(2)}) collective-permute-start(bf16[4,128,1024]{2,1,0:T(8,128)(2,1)} %constant_dynamic-slice_fusion.24), channel_id=1, source_target_pairs={{0,16},{16,0},{1,17},{17,1},{2,18},{18,2},{3,19},{19,3},{4,20},{20... | collective-permute-start | bytes 3145736 | tf_op jit(solution)/shard_map/ppermute | solution.py:390
  637.1 53.4 %collective-permute-start.52 = (bf16[4,128,1024]{2,1,0:T(8,128)(2,1)}, bf16[4,128,1024]{2,1,0:T(8,128)(2,1)S(1)}, u32[]{:S(2)}, u32[]{:S(2)}) collective-permute-start(bf16[4,128,1024]{2,1,0:T(8,128)(2,1)} %get-tuple-element.714), channel_id=1, source_target_pairs={{0,16},{16,0},{1,17},{17,1},{2,18},{18,2},{3,19},{19,3},{4,20},{20... | collective-permute-start | bytes 3145736 | tf_op jit(solution)/shard_map/ppermute | solution.py:390
  637.6 52.8 %collective-permute-start.50 = (bf16[2,128,1024]{2,1,0:T(8,128)(2,1)}, bf16[2,128,1024]{2,1,0:T(8,128)(2,1)}, u32[]{:S(2)}, u32[]{:S(2)}) collective-permute-start(bf16[2,128,1024]{2,1,0:T(8,128)(2,1)} %constant_dynamic-slice_fusion.25), channel_id=1, source_target_pairs={{0,8},{4,12},{8,0},{12,4},{1,9},{5,13},{9,1},{13,5},{2,10},{6,14},... | collective-permute-start | bytes 1572872 | tf_op jit(solution)/shard_map/ppermute | solution.py:1117
  696.4 26.6 %collective-permute-start.54 = (bf16[2,4,512,1024]{3,2,1,0:T(8,128)(2,1)}, bf16[2,4,512,1024]{3,2,1,0:T(8,128)(2,1)}, u32[]{:S(2)}, u32[]{:S(2)}) collective-permute-start(bf16[2,4,512,1024]{3,2,1,0:T(8,128)(2,1)} %get-tuple-element.728), channel_id=1, source_target_pairs={{0,16},{16,0},{1,17},{17,1},{2,18},{18,2},{3,19},{19,3},{4,20},{20... | collective-permute-start | bytes 25165832 | tf_op jit(solution)/shard_map/ppermute | solution.py:390
  696.5 26.5 %collective-permute-start.53 = (bf16[2,128,1024]{2,1,0:T(8,128)(2,1)S(1)}, bf16[2,128,1024]{2,1,0:T(8,128)(2,1)S(1)}, u32[]{:S(2)}, u32[]{:S(2)}) collective-permute-start(bf16[2,128,1024]{2,1,0:T(8,128)(2,1)S(1)} %add_convert_fusion.13), channel_id=1, source_target_pairs={{0,8},{4,12},{8,0},{12,4},{1,9},{5,13},{9,1},{13,5},{2,10},{6,14},... | collective-permute-start | bytes 1572872 | tf_op jit(solution)/shard_map/ppermute | solution.py:1117
  734.5 43.6 %collective-permute-start.56 = (bf16[2,256,1024]{2,1,0:T(8,128)(2,1)S(1)}, bf16[2,256,1024]{2,1,0:T(8,128)(2,1)}, u32[]{:S(2)}, u32[]{:S(2)}) collective-permute-start(bf16[2,256,1024]{2,1,0:T(8,128)(2,1)S(1)} %maximum_select_fusion.4), channel_id=1, source_target_pairs={{0,4},{4,0},{8,12},{12,8},{1,5},{5,1},{9,13},{13,9},{2,6},{6,2},{1... | collective-permute-start | bytes 3145736 | tf_op jit(solution)/shard_map/ppermute | solution.py:1117
  734.6 43.6 %collective-permute-start.58 = (bf16[2,1024,256]{2,1,0:T(8,128)(2,1)}, bf16[2,1024,256]{2,1,0:T(8,128)(2,1)}, u32[]{:S(2)}, u32[]{:S(2)}) collective-permute-start(bf16[2,1024,256]{2,1,0:T(8,128)(2,1)} %get-tuple-element.744), channel_id=1, source_target_pairs={{0,16},{16,0},{1,17},{17,1},{2,18},{18,2},{3,19},{19,3},{4,20},{20... | collective-permute-start | bytes 3145736 | tf_op jit(solution)/shard_map/ppermute | solution.py:390
  734.7 43.5 %collective-permute-start.57 = (bf16[4,32,1024]{2,1,0:T(8,128)(2,1)S(1)}, bf16[4,32,1024]{2,1,0:T(8,128)(2,1)}, u32[]{:S(2)}, u32[]{:S(2)}) collective-permute-start(bf16[4,32,1024]{2,1,0:T(8,128)(2,1)S(1)} %constant_dynamic-slice_fusion.22), channel_id=1, source_target_pairs={{0,8},{4,12},{8,0},{12,4},{1,9},{5,13},{9,1},{13,5},{2,10},{6,14},... | collective-permute-start | bytes 786440 | tf_op jit(solution)/shard_map/ppermute | solution.py:1117
  737.7 56.6 %collective-permute-start.59 = (bf16[2,512,1024]{2,1,0:T(8,128)(2,1)}, bf16[2,512,1024]{2,1,0:T(8,128)(2,1)S(1)}, u32[]{:S(2)}, u32[]{:S(2)}) collective-permute-start(bf16[2,512,1024]{2,1,0:T(8,128)(2,1)} %bitcast.393), channel_id=1, source_target_pairs={{0,2},{1,3},{2,0},{3,1},{16,17},{17,16},{18,19},{19,18},{4,6},{5,7... | collective-permute-start | bytes 6291464 | tf_op jit(solution)/shard_map/ppermute | solution.py:386
  738.2 56.2 %collective-permute-start.60 = (bf16[2,512,1024]{2,1,0:T(8,128)(2,1)}, bf16[2,512,1024]{2,1,0:T(8,128)(2,1)}, u32[]{:S(2)}, u32[]{:S(2)}) collective-permute-start(bf16[2,512,1024]{2,1,0:T(8,128)(2,1)} %get-tuple-element.756), channel_id=1, source_target_pairs={{0,1},{1,0},{2,3},{3,2},{16,18},{17,19},{18,16},{19,17},{4,5},{5,4... | collective-permute-start | bytes 6291464 | tf_op jit(solution)/shard_map/ppermute | solution.py:386
  800.2 48.3 %collective-permute-start.65 = (bf16[2,512,1024]{2,1,0:T(8,128)(2,1)S(1)}, bf16[2,512,1024]{2,1,0:T(8,128)(2,1)}, u32[]{:S(2)}, u32[]{:S(2)}) collective-permute-start(bf16[2,512,1024]{2,1,0:T(8,128)(2,1)S(1)} %add_convert_fusion.1), channel_id=1, source_target_pairs={{0,1},{1,0},{2,3},{3,2},{16,18},{17,19},{18,16},{19,17},{4,5},{5,4... | collective-permute-start | bytes 6291464 | tf_op jit(solution)/shard_map/ppermute | solution.py:386
  800.9 47.6 %collective-permute-start.66 = (bf16[2,512,1024]{2,1,0:T(8,128)(2,1)}, bf16[2,512,1024]{2,1,0:T(8,128)(2,1)}, u32[]{:S(2)}, u32[]{:S(2)}) collective-permute-start(bf16[2,512,1024]{2,1,0:T(8,128)(2,1)} %collective-permute-done.60), channel_id=1, source_target_pairs={{0,16},{16,0},{1,17},{17,1},{2,18},{18,2},{3,19},{19,3},{4,20},{20... | collective-permute-start | bytes 6291464 | tf_op jit(solution)/shard_map/ppermute | solution.py:390
  820.4 29.0 %collective-permute-start.68 = (bf16[4,256,1024]{2,1,0:T(8,128)(2,1)}, bf16[4,256,1024]{2,1,0:T(8,128)(2,1)}, u32[]{:S(2)}, u32[]{:S(2)}) collective-permute-start(bf16[4,256,1024]{2,1,0:T(8,128)(2,1)} %get-tuple-element.790), channel_id=1, source_target_pairs={{0,16},{16,0},{1,17},{17,1},{2,18},{18,2},{3,19},{19,3},{4,20},{20... | collective-permute-start | bytes 6291464 | tf_op jit(solution)/shard_map/ppermute | solution.py:390
  822.8 26.7 %collective-permute-start.67 = (bf16[4,128,1024]{2,1,0:T(8,128)(2,1)}, bf16[4,128,1024]{2,1,0:T(8,128)(2,1)}, u32[]{:S(2)}, u32[]{:S(2)}) collective-permute-start(bf16[4,128,1024]{2,1,0:T(8,128)(2,1)} %add_convert_fusion.6), channel_id=1, source_target_pairs={{0,3},{1,2},{2,1},{3,0},{16,19},{17,18},{18,17},{19,16},{4,7},{5,6... | collective-permute-start | bytes 3145736 | tf_op jit(solution)/shard_map/ppermute | solution.py:386
  859.8 28.6 %collective-permute-start.71 = (bf16[4,256,1024]{2,1,0:T(8,128)(2,1)}, bf16[4,256,1024]{2,1,0:T(8,128)(2,1)}, u32[]{:S(2)}, u32[]{:S(2)}) collective-permute-start(bf16[4,256,1024]{2,1,0:T(8,128)(2,1)} %add_convert_fusion), channel_id=1, source_target_pairs={{0,1},{1,0},{2,3},{3,2},{16,18},{17,19},{18,16},{19,17},{4,5},{5,4... | collective-permute-start | bytes 6291464 | tf_op jit(solution)/shard_map/ppermute | solution.py:386
  891.6 33.4 %collective-permute-start.73 = (bf16[4,128,1024]{2,1,0:T(8,128)(2,1)S(1)}, bf16[4,128,1024]{2,1,0:T(8,128)(2,1)S(1)}, u32[]{:S(2)}, u32[]{:S(2)}) collective-permute-start(bf16[4,128,1024]{2,1,0:T(8,128)(2,1)S(1)} %constant_dynamic-slice_fusion.11), channel_id=1, source_target_pairs={{0,16},{16,0},{1,17},{17,1},{2,18},{18,2},{3,19},{19,3},{4,20},{20... | collective-permute-start | bytes 3145736 | tf_op jit(solution)/shard_map/ppermute | solution.py:390
  891.7 33.3 %collective-permute-start.74 = (bf16[512,1024]{1,0:T(8,128)(2,1)S(1)}, bf16[512,1024]{1,0:T(8,128)(2,1)S(1)}, u32[]{:S(2)}, u32[]{:S(2)}) collective-permute-start(bf16[512,1024]{1,0:T(8,128)(2,1)S(1)} %get-tuple-element.830), channel_id=1, source_target_pairs={{0,0},{17,1},{18,2},{3,3},{4,4},{21,5},{22,6},{7,7},{8,8},{25,9},{... | collective-permute-start | bytes 3145736 | tf_op jit(solution)/shard_map/ppermute | solution.py:386
  892.5 32.5 %collective-permute-start.75 = (bf16[512,1024]{1,0:T(8,128)(2,1)S(1)}, bf16[512,1024]{1,0:T(8,128)(2,1)S(1)}, u32[]{:S(2)}, u32[]{:S(2)}) collective-permute-start(bf16[512,1024]{1,0:T(8,128)(2,1)S(1)} %get-tuple-element.831), channel_id=1, source_target_pairs={{1,0},{16,1},{19,2},{2,3},{5,4},{20,5},{23,6},{6,7},{9,8},{24,9},{... | collective-permute-start | bytes 3145736 | tf_op jit(solution)/shard_map/ppermute | solution.py:386
  894.1 31.0 %collective-permute-start.76 = (bf16[4,128,1024]{2,1,0:T(8,128)(2,1)S(1)}, bf16[4,128,1024]{2,1,0:T(8,128)(2,1)S(1)}, u32[]{:S(2)}, u32[]{:S(2)}) collective-permute-start(bf16[4,128,1024]{2,1,0:T(8,128)(2,1)S(1)} %copy-done.57), channel_id=1, source_target_pairs={{0,16},{16,0},{1,17},{17,1},{2,18},{18,2},{3,19},{19,3},{4,20},{20... | collective-permute-start | bytes 3145736 | tf_op jit(solution)/shard_map/ppermute | solution.py:390
  931.9 52.7 %collective-permute-start.83 = (bf16[512,1024]{1,0:T(8,128)(2,1)}, bf16[512,1024]{1,0:T(8,128)(2,1)}, u32[]{:S(2)}, u32[]{:S(2)}) collective-permute-start(bf16[512,1024]{1,0:T(8,128)(2,1)} %get-tuple-element.850), channel_id=1, source_target_pairs={{2,0},{19,1},{16,2},{1,3},{6,4},{23,5},{20,6},{5,7},{10,8},{27,9},... | collective-permute-start | bytes 3145736 | tf_op jit(solution)/shard_map/ppermute | solution.py:386
  933.2 51.4 %collective-permute-start.84 = (bf16[512,1024]{1,0:T(8,128)(2,1)}, bf16[512,1024]{1,0:T(8,128)(2,1)}, u32[]{:S(2)}, u32[]{:S(2)}) collective-permute-start(bf16[512,1024]{1,0:T(8,128)(2,1)} %get-tuple-element.851), channel_id=1, source_target_pairs={{3,0},{18,1},{17,2},{0,3},{7,4},{22,5},{21,6},{4,7},{11,8},{26,9},... | collective-permute-start | bytes 3145736 | tf_op jit(solution)/shard_map/ppermute | solution.py:386
  956.2 30.6 %collective-permute-start.81 = (bf16[2,256,1024]{2,1,0:T(8,128)(2,1)S(1)}, bf16[2,256,1024]{2,1,0:T(8,128)(2,1)}, u32[]{:S(2)}, u32[]{:S(2)}) collective-permute-start(bf16[2,256,1024]{2,1,0:T(8,128)(2,1)S(1)} %maximum_select_fusion.5), channel_id=1, source_target_pairs={{0,4},{4,0},{8,12},{12,8},{1,5},{5,1},{9,13},{13,9},{2,6},{6,2},{1... | collective-permute-start | bytes 3145736 | tf_op jit(solution)/shard_map/ppermute | solution.py:1117
  956.4 28.2 %collective-permute-start.85 = (bf16[4,32,1024]{2,1,0:T(8,128)(2,1)}, bf16[4,32,1024]{2,1,0:T(8,128)(2,1)}, u32[]{:S(2)}, u32[]{:S(2)}) collective-permute-start(bf16[4,32,1024]{2,1,0:T(8,128)(2,1)} %constant_dynamic-slice_fusion.1), channel_id=1, source_target_pairs={{0,8},{4,12},{8,0},{12,4},{1,9},{5,13},{9,1},{13,5},{2,10},{6,14},... | collective-permute-start | bytes 786440 | tf_op jit(solution)/shard_map/ppermute | solution.py:1117
  964.0 40.0 %collective-permute-start.87 = (bf16[2,512,1024]{2,1,0:T(8,128)(2,1)S(1)}, bf16[2,512,1024]{2,1,0:T(8,128)(2,1)S(1)}, u32[]{:S(2)}, u32[]{:S(2)}) collective-permute-start(bf16[2,512,1024]{2,1,0:T(8,128)(2,1)S(1)} %maximum_select_fusion.2), channel_id=1, source_target_pairs={{0,16},{1,17},{2,18},{3,19},{4,20},{5,21},{6,22},{7,23},{8,24},{9,... | collective-permute-start | bytes 6291464 | tf_op jit(solution)/shard_map/ppermute | solution.py:1539
  (107 other events, 1047.5 us)

commit v3 on v2

--- a/solution.py
+++ b/solution.py
@@ -415,6 +415,15 @@
     return first, second, third
 
 
+def three_rounded(value):
+    parts = []
+    for _ in range(3):
+        part = lax.reduce_precision(value, 8, 7)
+        parts.append(part.astype(bf16))
+        value = value - part
+    return tuple(parts)
+
+
 def key_columns(positions, length):
     high = (positions // 8 * 8).astype(f32)
     low = (positions % 8).astype(f32)
@@ -426,7 +435,7 @@
 
 
 def query_columns(slopes):
-    first, second, third = three_parts(slopes * 8.0)
+    first, second, third = three_rounded(slopes * 8.0)
     one = jnp.ones_like(first)
     columns = jnp.stack([first, second, third, first, second, third, one], axis=1)
     half = jnp.pad(columns, ((0, 0), (0, HEAD - 7))).reshape(-1, 2, HEAD)
@@ -434,7 +443,7 @@
     return jnp.broadcast_to(row[:, None, :], (row.shape[0], 8, 2 * HEAD))
 
 
-def attend_kernel(seg, meta, q, kv, kvo, kcol, qcol, o, qx, qp, kp, vp, st_m, st_a):
+def attend_kernel(seg, meta, q, kv, kvo, kcol, qcol, o, qx, qp, kp, vp):
     other = 1 - meta[0]
     lane = lax.broadcasted_iota(jnp.int32, (1, 128), 1)
     low = lane < 64
@@ -449,56 +458,54 @@
         vp[h, 0 : 2 * seg] = jnp.where(mine, kv[1], one)
         vp[h, 2 * seg :] = jnp.where(mine, kvo[1], one)
 
-    def scores_of(h, start, keys, masked):
-        queries = qp[h, pl.ds(start, seg)]
-        scores = []
-        for n, (key_start, key_count) in enumerate(keys):
-            part = dot_nt(queries, kp[h, pl.ds(key_start, key_count)])
-            if masked and n == len(keys) - 1:
-                row = lax.broadcasted_iota(jnp.int32, (seg, key_count), 0)
-                column = lax.broadcasted_iota(jnp.int32, (seg, key_count), 1)
-                part = jnp.where(column <= row, part, -1e30)
-            scores.append(part)
+    apart, first, second = range(3)
+    far = pl.multiple_of(2 * seg + other * seg, seg)
+    keys_of = ([far], [0], [0, 2 * seg, seg])
+    units = [(part, h) for part in (apart, first, second) for h in range(2)]
+
+    def scores_of(part, h):
+        start = pl.multiple_of(other * seg, seg) if part == apart else (part - first) * seg
+        scores = [dot_nt(qp[h, pl.ds(start, seg)], kp[h, pl.ds(key, seg)]) for key in keys_of[part]]
+        if part != apart:
+            row = lax.broadcasted_iota(jnp.int32, (seg, seg), 0)
+            column = lax.broadcasted_iota(jnp.int32, (seg, seg), 1)
+            scores[-1] = jnp.where(column <= row, scores[-1], -1e30)
+        return scores
+
+    done = {}
+
+    def weigh(part, h, scores):
         top = scores[0].max(axis=1, keepdims=True)
-        for part in scores[1:]:
-            top = jnp.maximum(top, part.max(axis=1, keepdims=True))
-        return scores, top
-
-    def weigh(h, scores, top, keys):
+        for score in scores[1:]:
+            top = jnp.maximum(top, score.max(axis=1, keepdims=True))
+        if part != apart:
+            use = other == part - first
+            apart_top, apart_total = done[apart, h]
+            apart_top = jnp.where(use, apart_top, -1e30)
+            top = jnp.maximum(top, apart_top)
+            weight = jnp.where(use, jnp.exp2((apart_top - top) * scale), 0.0)
         total = None
-        for part, (key_start, key_count) in zip(scores, keys):
-            powers = jnp.exp2((part - top) * scale).astype(bf16)
-            term = dot_nn(powers, vp[h, pl.ds(key_start, key_count)])
+        for score, key in zip(scores, keys_of[part]):
+            powers = jnp.exp2((score - top) * scale).astype(bf16)
+            term = dot_nn(powers, vp[h, pl.ds(key, seg)])
             total = term if total is None else total + term
-        return total
-
-    for h in range(2):
-        start = pl.multiple_of(other * seg, seg)
-        keys = [(pl.multiple_of(2 * seg + other * seg, seg), seg)]
-        scores, top = scores_of(h, start, keys, False)
-        st_a[h] = weigh(h, scores, top, keys)
-        st_m[h] = jnp.broadcast_to(top, (seg, 128))
+        done[part, h] = top, total if part == apart else total + weight * apart_total
+
+    scores = scores_of(*units[0])
+    for n, unit in enumerate(units):
+        following = scores_of(*units[n + 1]) if n + 1 < len(units) else None
+        weigh(*unit, scores)
+        scores = following
+    at = lane & 63
     for segment in range(2):
-        use = other == segment
         rows = slice(segment * seg, (segment + 1) * seg)
-        totals, tops = [], []
-        for h in range(2):
-            keys = [(segment * seg, seg)]
-            if segment == 1:
-                keys = [(0, seg), (2 * seg, seg)] + keys
-            scores, top = scores_of(h, segment * seg, keys, True)
-            fifth = jnp.where(use, st_m[h][:, 0:1], -1e30)
-            top = jnp.maximum(top, fifth)
-            weight = jnp.where(use, jnp.exp2((fifth - top) * scale), 0.0)
-            totals.append(weigh(h, scores, top, keys) + weight * st_a[h])
-            tops.append(top)
-        number = jnp.where(low, totals[0], totals[1])
-        sums = jnp.where(low, totals[1], totals[0])
+        (top_low, total_low), (top_high, total_high) = done[first + segment, 0], done[first + segment, 1]
+        number = jnp.where(low, total_low, total_high)
+        sums = jnp.where(low, total_high, total_low)
         o[rows] = (number / pltpu.roll(sums, 64, 1)).astype(bf16)
-        logs = jnp.where(low, tops[1], tops[0]) + jnp.log(sums) * 8.0
-        first, second, third = three_parts(logs)
-        at = lane & 63
-        qx[rows] = jnp.where(at == 7, -first, jnp.where(at == 8, -second, jnp.where(at == 9, -third, base)))
+        logs = jnp.where(low, top_high, top_low) + jnp.log(sums) * 8.0
+        parts = three_parts(logs)
+        qx[rows] = jnp.where(at == 7, -parts[0], jnp.where(at == 8, -parts[1], jnp.where(at == 9, -parts[2], base)))
 
 
 def attend(meta, q, kv, kvo, kcol, qcol):
@@ -523,8 +530,6 @@
                 pltpu.VMEM((2, rows, 128), bf16),
                 pltpu.VMEM((2, 2 * rows, 128), bf16),
                 pltpu.VMEM((2, 2 * rows, 128), bf16),
-                pltpu.VMEM((2, seg, 128), f32),
-                pltpu.VMEM((2, seg, 128), f32),
             ],
         ),
         out_shape=[jax.ShapeDtypeStruct((rows, width), bf16)] * 2,
@@ -537,15 +542,30 @@
 
 
 def attend_back_kernel(
-    seg, meta, q, kv, kvo, kcol, qx, do, o, dq, dkv, dkvo, qp, kp, vp, dp, kt, qm, dm, aq, ak, av
+    seg, starts, meta, q, kv, kvo, kcol, qx, low_grad, o, *refs
 ):
+    weights, (dq, dkv, dkvo, qp, kp, vp, dp, kt, qm, dm, aq, ak, av, both) = refs[: 2 * len(starts)], refs[2 * len(starts) :]
+    pair = pl.program_id(0)
+
+    @pl.when(pair % 2 == 0)
+    def _():
+        two = []
+        for n in range(2):
+            weight = weights[n][...]
+            for ref, start in zip(weights[2 + n :: 2], starts[1:]):
+                weight = jnp.where(pair + n < start, weight, ref[...])
+            two.append(weight)
+        grads = dot_nt(low_grad[...], jnp.concatenate(two, axis=0)).astype(bf16)
+        both[0], both[1] = grads[:, :128], grads[:, 128:]
+
+    do = both[pair % 2]
     other = 1 - meta[0]
     lane = lax.broadcasted_iota(jnp.int32, (1, 128), 1)
     low = lane < 64
     at = lane & 63
     scale = LOG2E / 8
     zero = jnp.zeros((1, 128), bf16)
-    product = do[...].astype(f32) * o[...].astype(f32)
+    product = do.astype(f32) * o[...].astype(f32)
     for h in range(2):
         mine = low if h == 0 else ~low
         qp[h] = jnp.where(mine, q[...], qx[...])
@@ -555,9 +575,9 @@
         vp[h, 2 * seg :] = jnp.where(mine, kvo[1], kcol[2 * seg :])
         first, second, third = three_parts(jnp.sum(jnp.where(mine, product, 0.0), axis=1, keepdims=True))
         extra = jnp.where(at == 7, -first, jnp.where(at == 8, -second, jnp.where(at == 9, -third, zero)))
-        dp[h] = jnp.where(mine, do[...], extra)
+        dp[h] = jnp.where(mine, do, extra)
         qm[h] = jnp.where(mine, q[...], zero)
-        dm[h] = jnp.where(mine, do[...], zero)
+        dm[h] = jnp.where(mine, do, zero)
     kt[:, 0 : 2 * seg] = kv[0].T
     kt[:, 2 * seg :] = kvo[0].T
     aq[...] = jnp.zeros_like(aq)
@@ -593,19 +613,28 @@
     dkvo[1] = av[2 * seg :].astype(bf16)
 
 
-def attend_back(meta, q, kv, kvo, kcol, qx, do, o):
+def attend_back(meta, q, kv, kvo, kcol, qx, low_grad, o, pieces):
     rows, width = q.shape
     seg = rows // 2
     pairs = width // 128
     block = pl.BlockSpec((rows, 128), lambda i, m: (0, i))
     mine = pl.BlockSpec((2, rows, 128), lambda i, m: (0, 0, i))
     theirs = pl.BlockSpec((2, rows, 128), lambda i, m: (0, 0, m[1 + i]))
+    starts, at, weights = [], 0, []
+    for piece in pieces:
+        count = units_of(piece) // 128
+        for n in range(2):
+            place_of = lambda i, m, at=at, count=count, n=n: (3 * count + jnp.clip(i // 2 * 2 + n - at, 0, count - 1), 0)
+            weights.append(pl.BlockSpec((128, piece.shape[1]), place_of))
+        starts.append(at)
+        at += count
     return pl.pallas_call(
-        partial(attend_back_kernel, seg),
+        partial(attend_back_kernel, seg, starts),
         grid_spec=pltpu.PrefetchScalarGridSpec(
             num_scalar_prefetch=1,
             grid=(pairs,),
-            in_specs=[block, mine, theirs, pl.BlockSpec((2 * rows, 128), lambda i, m: (0, 0))] + [block] * 3,
+            in_specs=[block, mine, theirs, pl.BlockSpec((2 * rows, 128), lambda i, m: (0, 0))] + [block, fixed(low_grad.shape), block]
+            + weights,
             out_specs=[block, mine, theirs],
             scratch_shapes=[
                 pltpu.VMEM((2, rows, 128), bf16),
@@ -618,6 +647,7 @@
                 pltpu.VMEM((128, rows), f32),
                 pltpu.VMEM((2 * rows, 128), f32),
                 pltpu.VMEM((2 * rows, 128), f32),
+                pltpu.VMEM((2, rows, 128), bf16),
             ],
         ),
         out_shape=[
@@ -627,13 +657,13 @@
         ],
         compiler_params=pltpu.CompilerParams(vmem_limit_bytes=60 * MIB),
         cost_estimate=cost(
-            flops=100 * 256 * seg * seg * pairs, bytes_accessed=rows * width * 26, transcendentals=10 * seg * seg * pairs
+            flops=100 * 256 * seg * seg * pairs + 512 * rows * low_grad.shape[1] * pairs, bytes_accessed=rows * width * 26, transcendentals=10 * seg * seg * pairs
         ),
         name="attend_back",
-    )(meta, q, kv, kvo, kcol, qx, do, o)
-
-
-PART = 8
+    )(meta, q, kv, kvo, kcol, qx, low_grad, o, *(piece for piece in pieces for _ in range(2)))
+
+
+PART = 64
 
 
 def cost(flops, bytes_accessed, transcendentals):
@@ -644,7 +674,7 @@
     return pl.BlockSpec(shape, lambda *_: (0,) * len(shape), pipeline_mode=pl.Buffered(1))
 
 
-BIAS_ROWS = 16
+BIAS_ROWS = 32
 
 
 def units_of(piece):
@@ -656,40 +686,38 @@
     return jnp.concatenate(parts, axis=0) if len(parts) > 1 else parts[0]
 
 
-def project_kernel(count, a, *refs):
-    pieces, bias, q, kv = refs[:count], refs[count], refs[count + 1], refs[count + 2]
-    step = pl.program_id(0)
-    result = (dot_nt(a[...], joined(pieces)) + bias[0]).astype(bf16)
-
-    @pl.when(step == 0)
-    def _():
-        q[...] = result
-
-    @pl.when(step > 0)
-    def _():
-        kv[0] = result
+def project_kernel(a, bias, *refs):
+    pieces, (q, kv) = refs[:-2], refs[-2:]
+    at = 0
+    for piece in pieces:
+        units = piece.shape[0] // 3
+        result = dot_nt(a[...], piece[...])
+        for n in range(3):
+            part = (result[:, n * units : (n + 1) * units] + bias[n, :, at : at + units]).astype(bf16)
+            if n == 0:
+                q[:, at : at + units] = part
+            else:
+                kv[n - 1, :, at : at + units] = part
+        at += units
 
 
 def project_heads(a, pieces, bias):
     rows, width = a.shape
     columns = sum(units_of(piece) for piece in pieces)
+    tile = rows // 4
     return pl.pallas_call(
-        partial(project_kernel, len(pieces)),
-        grid=(3,),
-        in_specs=[fixed(a.shape)]
-        + [pl.BlockSpec((units_of(piece), width), lambda i: (i, 0)) for piece in pieces]
-        + [pl.BlockSpec((1, 1, columns), lambda i: (i, 0, 0))],
-        out_specs=[
-            pl.BlockSpec((rows, columns), lambda i: (0, 0)),
-            pl.BlockSpec((1, rows, columns), lambda i: (jnp.maximum(i - 1, 0), 0, 0)),
-        ],
+        project_kernel,
+        grid=(rows // tile,),
+        in_specs=[pl.BlockSpec((tile, width), lambda i: (i, 0)), fixed(bias.shape)]
+        + [pl.BlockSpec((3 * units_of(piece), width), lambda i: (0, 0), pipeline_mode=pl.Buffered(1)) for piece in pieces],
+        out_specs=[pl.BlockSpec((tile, columns), lambda i: (i, 0)), pl.BlockSpec((2, tile, columns), lambda i: (0, i, 0))],
         out_shape=[jax.ShapeDtypeStruct((rows, columns), bf16), jax.ShapeDtypeStruct((2, rows, columns), bf16)],
         cost_estimate=cost(
             flops=6 * rows * width * columns, bytes_accessed=2 * rows * width + 6 * width * columns + 6 * rows * columns, transcendentals=0
         ),
         compiler_params=pltpu.CompilerParams(vmem_limit_bytes=60 * MIB),
         name="project",
-    )(a, *pieces, bias)
+    )(a, bias, *pieces)
 
 
 def normalize(value):
@@ -743,14 +771,20 @@
     return jnp.concatenate([own[matrix, core], own[matrix, 1 - core]] + [ref[matrix] for ref in refs[1:]], axis=0)
 
 
-def feed_rows(middle, up, down, bias):
-    u = dot_nt(middle, up) + bias
+def gelu_parts(u):
     square = u * u
     t = jnp.tanh(u * (GELU_A + (GELU_A * GELU_B) * square))
     half = 0.5 * u
-    value = (half + half * t).astype(bf16)
     slope = 0.5 + 0.5 * t + (half - half * t * t) * (GELU_A + (3 * GELU_A * GELU_B) * square)
-    return slope.astype(bf16), value, dot_nn(value, down)
+    return slope.astype(bf16), (half + half * t).astype(bf16)
+
+
+def in_turn(count, first, second):
+    value = first(0)
+    for n in range(count):
+        following = first(n + 1) if n + 1 < count else None
+        second(n, value)
+        value = following
 
 
 def feed_kernel(counts, meta, *refs):
@@ -771,10 +805,14 @@
 
     refs = (own, near, near_too)
     up, down = share(refs, 0, core), share(refs, 1, core)
-    for n in range(4):
-        at = slice(n * tile, (n + 1) * tile)
-        slope[0, at], hidden[0, at], term = feed_rows(middle[at], up, down, bias[0])
-        total[at] += term
+    rows_of = lambda n: slice(n * tile, (n + 1) * tile)
+
+    def rest(n, u):
+        slope[0, rows_of(n)], value = gelu_parts(u)
+        hidden[0, rows_of(n)] = value
+        total[rows_of(n)] += dot_nn(value, down)
+
+    in_turn(4, lambda n: dot_nt(middle[rows_of(n)], up) + bias[0], rest)
 
 
 def feed(meta, x, heads, heads_pieces, vectors, bias, pieces):
@@ -816,14 +854,21 @@
                 weights[n, 2 * i * size : (2 * i + 1) * size] = far[n, i * size : (i + 1) * size]
                 weights[n, (2 * i + 1) * size : (2 * i + 2) * size] = far_too[n, i * size : (i + 1) * size]
 
-    slopes, values, term = feed_rows(middle[...], weights[0], weights[1], bias[...])
     wide = slope.shape[2]
-    for i in range(steps):
-        slope[i] = slopes[:, i * wide : (i + 1) * wide]
-        hidden[i] = values[:, i * wide : (i + 1) * wide]
-    value = (so_far[...] + term).astype(bf16)
-    out[...] = value
-    normed[...] = normed_rows(value.astype(f32), vectors)
+    count = 2
+    tile = middle.shape[0] // count
+    rows_of = lambda n: slice(n * tile, (n + 1) * tile)
+
+    def rest(n, u):
+        slopes, values = gelu_parts(u)
+        for i in range(steps):
+            slope[i, rows_of(n)] = slopes[:, i * wide : (i + 1) * wide]
+            hidden[i, rows_of(n)] = values[:, i * wide : (i + 1) * wide]
+        value = (so_far[rows_of(n)] + dot_nn(values, weights[1])).astype(bf16)
+        out[rows_of(n)] = value
+        normed[rows_of(n)] = normed_rows(value.astype(f32), vectors)
+
+    in_turn(count, lambda n: dot_nt(middle[rows_of(n)], weights[0]) + bias[...], rest)
 
 
 def feed_last(middle, so_far, vectors, bias, pieces):
@@ -831,7 +876,7 @@
     units = pieces[1].shape[1]
     steps = STEPS
     wide = units // steps
-    tile = rows // 4
+    tile = rows // 2
     slim = pl.BlockSpec((tile, width), lambda i: (i, 0))
     per_step = pl.BlockSpec((steps, tile, wide), lambda i: (0, i, 0))
     return pl.pallas_call(
@@ -940,30 +985,6 @@
     )(meta, above, middle, after, vectors, *slopes, *values, *pieces)
 
 
-def heads_back_kernel(count, low, *refs):
-    pieces, out = refs[:count], refs[count]
-    out[...] = dot_nt(low[...], joined(pieces)).astype(bf16)
-
-
-def heads_back(low, pieces):
-    rows, width = low.shape
-    columns = sum(units_of(piece) for piece in pieces)
-    tile = rows // 2
-    return pl.pallas_call(
-        partial(heads_back_kernel, len(pieces)),
-        grid=(rows // tile,),
-        in_specs=[pl.BlockSpec((tile, width), lambda i: (i, 0))]
-        + [pl.BlockSpec((units_of(p), width), lambda i: (3, 0), pipeline_mode=pl.Buffered(1)) for p in pieces],
-        out_specs=pl.BlockSpec((tile, columns), lambda i: (i, 0)),
-        out_shape=jax.ShapeDtypeStruct((rows, columns), bf16),
-        cost_estimate=cost(
-            flops=2 * rows * width * columns, bytes_accessed=2 * (rows * width + width * columns + rows * columns), transcendentals=0
-        ),
-        compiler_params=pltpu.CompilerParams(vmem_limit_bytes=60 * MIB),
-        name="heads_back",
-    )(low, *pieces)
-
-
 def project_back_kernel(groups, first, last, meta, *refs):
     refs = list(refs)
     take = lambda n: [refs.pop(0) for _ in range(n)]
@@ -1027,7 +1048,7 @@
     rows, width = a.shape
     columns = dq.shape[1]
     groups = [(name, units_of(piece)) for name, piece in zip(names, pieces)]
-    tiles = 2
+    tiles = 4
     tile = width // tiles
     slim = pl.BlockSpec((rows, tile), lambda i, m: (0, i))
     grads = pl.BlockSpec((4, columns // 2, tile), lambda i, m: (0, 0, i))
@@ -1069,6 +1090,8 @@
 
 
 def plus(*values):
+    if len(values) == 2:
+        return values[0] + values[1]
     total = values[0].astype(f32)
     for value in values[1:]:
         total = total + value.astype(f32)
@@ -1172,25 +1195,29 @@
             chain.wait -= 1
             if chain.wait <= 0:
                 due.append(chain)
-        values, there = lax.optimization_barrier((values, [chain.under_way for chain in due]))
+        there = [lax.optimization_barrier((chain.under_way, values))[0] for chain in due]
+        values = lax.optimization_barrier((values, [chain.under_way for chain in due]))[0]
         for chain, value in zip(due, there):
             chain.advance(value)
         return values
 
     def launch(self, values):
         chains = [chain for chain in self.running if chain.pending is not None]
-        sends = [chain.pending if isinstance(chain.pending, list) else [chain.pending] for chain in chains]
-        values, sent = lax.optimization_barrier((values, [[send.value for send in each] for each in sends]))
-        for chain, each, operands in zip(chains, sends, sent):
-            under_way = [send.transfer(value) for send, value in zip(each, operands)]
+        for chain in chains:
+            sends = chain.pending if isinstance(chain.pending, list) else [chain.pending]
+            values, sent = lax.optimization_barrier((values, [send.value for send in sends]))
+            under_way = [send.transfer(value) for send, value in zip(sends, sent)]
             chain.under_way = under_way if isinstance(chain.pending, list) else under_way[0]
             chain.pending = None
         return values
 
-    def step(self, values, *new):
+    def stepped(self, values, new):
         values = self.turn(values)
         started = [self.start(make()) for make in new]
-        values = self.launch(values)
+        return [self.launch(values), *started]
+
+    def step(self, values, *new):
+        values, *started = self.stepped(values, new)
         return (values, *started) if new else values
 
 
@@ -1232,6 +1259,76 @@
     return ordered(low == 0, total, got)
 
 
+def ends_kernel(meta, *refs):
+    out = refs[-1]
+    for core in range(2):
+        for distance in range(GROUP):
+
+            @pl.when((meta[0] == core) & ((pl.program_id(1) ^ meta[1]) == distance))
+            def _(ref=refs[core * GROUP + distance]):
+                out[0] = ref[...].astype(f32)
+
+
+def ends_rows(meta, first, second):
+    rows, width = first[0].shape
+    tile = rows // 2
+    return pl.pallas_call(
+        ends_kernel,
+        grid_spec=pltpu.PrefetchScalarGridSpec(
+            num_scalar_prefetch=1,
+            grid=(rows // tile, GROUP),
+            in_specs=[pl.BlockSpec((tile, width), lambda j, n, m: (j, 0))] * (2 * GROUP),
+            out_specs=pl.BlockSpec((1, tile, width), lambda j, n, m: (n, j, 0)),
+        ),
+        out_shape=jax.ShapeDtypeStruct((GROUP, rows, width), f32),
+        cost_estimate=cost(flops=GROUP * rows * width, bytes_accessed=16 * GROUP * rows * width, transcendentals=0),
+        compiler_params=pltpu.CompilerParams(vmem_limit_bytes=60 * MIB),
+        name="ends_rows",
+    )(meta, *first, *second)
+
+
+def feed_out_kernel(meta, lower, upper, to_lower, to_upper, up, down):
+    for core, mine, other in ((0, lower, to_lower), (1, upper, to_upper)):
+        for same, ref in ((True, mine), (False, other)):
+
+            @pl.when((meta[0] == core) & ((pl.program_id(1) == core) == same))
+            def _(ref=ref):
+                up[...] = ref[0].astype(f32).T
+                down[...] = ref[1].astype(f32)
+
+
+def feed_out(meta, lower, upper, to_lower, to_upper):
+    _, units, width = lower.shape
+    tile = units // 2
+    return pl.pallas_call(
+        feed_out_kernel,
+        grid_spec=pltpu.PrefetchScalarGridSpec(
+            num_scalar_prefetch=1,
+            grid=(units // tile, 2),
+            in_specs=[pl.BlockSpec((2, tile, width), lambda j, h, m: (0, j, 0))] * 4,
+            out_specs=[
+                pl.BlockSpec((width, tile), lambda j, h, m: (0, h * 2 + j)),
+                pl.BlockSpec((tile, width), lambda j, h, m: (h * 2 + j, 0)),
+            ],
+        ),
+        out_shape=[jax.ShapeDtypeStruct((width, 2 * units), f32), jax.ShapeDtypeStruct((2 * units, width), f32)],
+        cost_estimate=cost(flops=4 * units * width, bytes_accessed=32 * units * width, transcendentals=0),
+        compiler_params=pltpu.CompilerParams(vmem_limit_bytes=60 * MIB),
+        name="feed_out",
+    )(meta, lower, upper, to_lower, to_upper)
+
+
+def handed_over(steps, pairs, pause=0):
+    total = yield from steps
+    if pause:
+        yield [], pause
+    got = yield Send(lambda v: lax.ppermute(v, "section", pairs), total), 1
+    return total, got
+
+
+UP, DOWN = [(0, 1)], [(1, 0)]
+
+
 def summed_everywhere(value):
     for axis in ("section", "tensor", "dp"):
         count = lax.axis_size(axis)
@@ -1275,23 +1372,28 @@
         return [
             hopping(
                 lax.dynamic_index_in_dim(ends, chip ^ k, 0, keepdims=False),
-                [(place(section, t), place(core_of(t), t ^ k)) for t in CHIPS],
+                [(place(section, t), place(core_of(t), t ^ k)) for t in CHIPS if k or core_of(t) != section],
             )
             for k in CHIPS
         ]
 
-    def chosen_rows(got):
+    def chosen_rows(section, got):
+        here = lax.dynamic_index_in_dim(ends, chip, 0, keepdims=False)
+        got = [jnp.where(core == section, here, got[0]), *got[1:]]
+
         def pick(k):
             return jnp.where(k == 0, got[0], jnp.where(k == 1, got[1], jnp.where(k == 2, got[2], got[3])))
 
         return jnp.concatenate([pick(chip ^ lo_segment), pick(chip ^ hi_segment)])
+
+    def segment_of(row, distance):
+        return jnp.where(chip ^ distance == lo_segment, row[:seg], row[seg:])
 
     def row_to(section, row, distances):
         got = []
         for k in distances:
-            segment = chip ^ k
-            sent = jnp.where(segment == lo_segment, row[:seg], row[seg:])
-            got.append(hopping(sent, [(place(core_of(t), t ^ k), place(section, t)) for t in CHIPS]))
+            pairs = [(place(core_of(t), t ^ k), place(section, t)) for t in CHIPS if k or core_of(t) != section]
+            got.append(hopping(segment_of(row, k), pairs))
         return got
 
     def both(mine):
@@ -1299,15 +1401,24 @@
         return (jnp.where(first_core, mine, theirs), jnp.where(first_core, theirs, mine))
 
     chains = Chains()
-    six = both(jnp.concatenate([ln_gains[0], ln_biases[0], out_biases[0]]))
     bias = jnp.concatenate([qv_bias[0].reshape(-1), up_bias[0]])
-    bias = jnp.stack(three_parts(bias))
-    bias = jnp.pad(bias, ((0, 0), (0, -bias.shape[1] % D))).reshape(-1, D)
-    bias = jnp.pad(bias, ((0, BIAS_ROWS - bias.shape[0]), (0, 0)))
-    pack = jnp.concatenate([jnp.swapaxes(w_qkv[0], 1, 2).reshape(-1, D), w_out[0], bias])
-    x = chosen_rows([send.transfer(send.value) for send in row_from(0)])
+    bias_rows = -(-bias.shape[0] // D)
+    bias = jnp.pad(bias, (0, bias_rows * D - bias.shape[0])).reshape(-1, D)
+    extra = jnp.concatenate([bias, ln_gains[0], ln_biases[0], out_biases[0]])
+    extra_rows = extra.shape[0]
+    extra = jnp.concatenate(three_rounded(extra))
+    extra = jnp.pad(extra, ((0, BIAS_ROWS - extra.shape[0]), (0, 0)))
+
+    def extra_of(pack):
+        rows = pack[-BIAS_ROWS:].astype(f32)
+        return (rows[:extra_rows] + rows[extra_rows : 2 * extra_rows]) + rows[2 * extra_rows : 3 * extra_rows]
+
+    pack = jnp.concatenate([jnp.swapaxes(w_qkv[0], 1, 2).reshape(-1, D), w_out[0], extra])
+    sends = row_from(0)
     attention_own = both(pack)
-    feed_own = both(jnp.concatenate([w_up[0].T[None], w_down]))
+    x = chosen_rows(0, [send.transfer(send.value) for send in sends])
+    feed_mine = tie(jnp.concatenate([w_up[0].T[None], w_down]), x)
+    feed_own = both(feed_mine)
 
     def gathered_heads(own, pieces, waits):
         pieces["own"] = own
@@ -1327,16 +1438,14 @@
     x, attention_own = tie((x, attention_own))
 
     def bias_of(name, layer, start, size):
-        rows = attention[layer][name][-BIAS_ROWS:].astype(f32)
-        count = -(-(2 * n_qv + n_up) // D)
-        parts = rows[: 3 * count].reshape(3, -1)
-        part = ((parts[0] + parts[1]) + parts[2])[start : start + size]
+        part = extra_of(attention[layer][name])[:bias_rows].reshape(-1)[start : start + size]
         if name == "far":
             part = half_of(part, 0, core)
         if name == "far_too":
             part = half_of(part, 0, 1 - core)
         return part
 
+    six = [extra_of(own)[bias_rows:] for own in attention_own]
     gains, shifts, end_biases = ([layer_six[n : n + 2] for layer_six in six] for n in (0, 2, 4))
 
     length = lax.dynamic_index_in_dim(lengths.reshape(-1), chip, 0, keepdims=False)
@@ -1419,8 +1528,9 @@
     for layer in range(2):
         saved = [None] * 3
         saved[OWN] = attended(layer, OWN, into_heads(layer, OWN, normed))
-        (normed, saved[OWN], feed_own), _ = chains.step(
-            (normed, saved[OWN], feed_own), lambda: gathered_feed(feed_own[layer], feeding[layer], (2, 1))
+        (normed, saved[OWN], feed_own), *_ = chains.stepped(
+            (normed, saved[OWN], feed_own),
+            [] if layer else [lambda: gathered_feed(feed_own[0], feeding[0], (2, 1))],
         )
         saved[NEAR] = attended(layer, NEAR, into_heads(layer, NEAR, normed))
         normed, saved[NEAR] = chains.step((normed, saved[NEAR]))
@@ -1434,14 +1544,16 @@
         slope_last, hidden_last, result, normed_next = fed_last(layer, middle, total)
         kept[layer] = (x, normed, saved, after, middle, (slope, slope_last), (hidden, hidden_last))
         if layer == 0:
-            x, normed = chains.step((result, normed_next))
+            (x, normed, feed_own), _ = chains.step(
+                (result, normed_next, feed_own), lambda: gathered_feed(feed_own[1], feeding[1], (3, 1))
+            )
     x, *sent_back = chains.step(result, lambda: once(row_to(1, result, (0, 1)), 1))
-    grad = chosen_rows(following.result)
+    grad = chosen_rows(1, following.result)
 
     def heads_gradients(layer, index, low):
         group = groups[layer][index]
         q, kv, kvo, o, qx = kept[layer][2][index]
-        return attend_back(group["meta"], q, kv, kvo, kcol, qx, heads_back(low, pieces_of(layer, index)), o)
+        return attend_back(group["meta"], q, kv, kvo, kcol, qx, low, o, pieces_of(layer, index))
 
     def weight_gradients(layer, index, grads, low, so_far, last):
         group = groups[layer][index]
@@ -1478,20 +1590,25 @@
         _, _, _, after, middle, slope, hidden = kept[layer]
         return feed_back(meta, grad, middle, after, gains[layer][1], slope, hidden, feeding[layer])
 
-    def backward(layer, grad, others, *new):
+    def backward(layer, grad, others, new, late):
         keep, send, unit_sums, low, sums_two = feed_gradients(layer, grad)
         (low, keep, send, others), feed_sums, *started = chains.step(
             (low, keep, send, others),
-            lambda: summed_feed(meta, keep, send, (1, 2, 2, 2, 1, 1, 1)),
+            lambda: handed_over(
+                summed_feed(meta, keep, send, (1, 2, 1, 1, 2, 1, 1) if layer else (1, 2, 1, 1, 2, 2, 1)), UP if layer else DOWN, 4 if layer else 0
+            ),
             *(lambda make=make: make(others) for make in new),
         )
+
         results = [None] * 3
         dq_far, dkv_far, sent_far = heads_gradients(layer, FAR, low)
         (low, sent_far), got_far = chains.step((low, sent_far), lambda: once(swapping(sent_far), 1))
         dq_near, dkv_near, sent_near = heads_gradients(layer, NEAR, low)
         (low, sent_near), got_near = chains.step((low, sent_near), lambda: once(swapping(sent_near), 1))
         results[FAR] = weight_gradients(layer, FAR, (dq_far, dkv_far, got_far.result), low, None, False)
-        (low, results[FAR]), far_sum = chains.step((low, results[FAR]), lambda: summed_far(*results[FAR][:2], (1, 1)))
+        (low, results[FAR]), far_sum, *started_late = chains.stepped(
+            (low, results[FAR]), [lambda: summed_far(*results[FAR][:2], (1, 1)), *late]
+        )
         results[NEAR] = weight_gradients(layer, NEAR, (dq_near, dkv_near, got_near.result), low, results[FAR][3], False)
         (low, results[NEAR]), near_sum = chains.step(
             (low, results[NEAR]), lambda: summed_near(*results[NEAR][:2], core, (1, 2, 1))
@@ -1502,69 +1619,63 @@
         results[OWN] = weight_gradients(layer, OWN, (dq_own, dkv_own, got_own.result), low, results[NEAR][3], True)
         grad, sums_one = results[OWN][3:]
         sums = sums_of(layer, results, unit_sums, sums_one, sums_two)
-        return grad, results[OWN], sums, feed_sums, near_sum, far_sum, started
+        return grad, results[OWN], sums, feed_sums, near_sum, far_sum, started + started_late
 
     grad, own, sums_upper, upper_feed, near_sum, far_sum, again = backward(
-        1, grad, x, lambda row: once(row_to(1, row, (2, 3)), 1)
+        1, grad, x, [lambda row: once(row_to(1, row, (2, 3)), 1)], []
     )
     sent_back += again
     (grad, own), own_sum = chains.step((grad, own), lambda: once(swapping(own[1]), 1))
 
-    def summed_heads(_, keep=own[0], own_sum=own_sum, near_sum=near_sum, far_sum=far_sum):
-        return summed_over_line(plus(keep, own_sum.result, *near_sum.result, far_sum.result), iter((1, 1, 1, 1)))
-
-    grad, own, sums_lower, lower_feed, near_sum, far_sum, (upper_heads,) = backward(0, grad, (), summed_heads)
-    (grad, sums_lower, own), first_one, own_sum, both_sums = chains.step(
+    def summed_heads(pairs, keep, own_sum, near_sum, far_sum):
+        total = plus(keep, own_sum.result, *near_sum.result, far_sum.result)
+        return handed_over(summed_over_line(total, iter((1, 1, 1, 1))), pairs)
+
+    upper_parts = own[0], own_sum, near_sum, far_sum
+    grad, own, sums_lower, lower_feed, near_sum, far_sum, (upper_heads,) = backward(
+        0, grad, (), [lambda _: summed_heads(UP, *upper_parts)], []
+    )
+    (grad, sums_lower, own), own_sum, zero, both_sums = chains.step(
         (grad, sums_lower, own),
-        lambda: once(row_to(0, grad, (0, 1)), 1),
         lambda: once(swapping(own[1]), 1),
+        lambda: once(row_to(0, grad, (0,)), 1),
         lambda: summed_everywhere(jnp.stack([sums_lower, sums_upper])),
     )
-    grad, first_two, lower_heads = chains.step(
-        grad,
-        lambda: once(row_to(0, grad, (2, 3)), 2),
-        lambda: summed_over_line(plus(own[0], own_sum.result, *near_sum.result, far_sum.result), iter((1, 1, 1, 1))),
-    )
-    first_rows = [first_one, first_two]
-
-    def rows_of(got):
-        return [
-            jnp.where(
-                row == chip, got[0], jnp.where(row == chip ^ 1, got[1], jnp.where(row == chip ^ 2, got[2], got[3]))
-            )
-            for row in CHIPS
-        ]
-
-    def finished(lower, upper):
-        to_upper = lax.ppermute(upper, "section", [(0, 1)])
-        to_lower = lax.ppermute(lower, "section", [(1, 0)])
-        return jnp.where(
-            first_core,
-            jnp.concatenate([lower, to_lower], axis=1),
-            jnp.concatenate([to_upper, upper], axis=1),
-        ).astype(f32)
+    grad, lower_heads = chains.step(
+        grad, lambda: summed_heads(DOWN, own[0], own_sum, near_sum, far_sum)
+    )
+    grad, three = chains.step(grad, lambda: once(row_to(0, grad, (3,)), 2))
+    grad, one, two = chains.step(grad, lambda: once(row_to(0, grad, (1,)), 1), lambda: once(row_to(0, grad, (2,)), 1))
+    first_rows = [zero, one, two, three]
 
     def feed_outputs():
-        grads = finished(lower_feed.result, upper_feed.result)
-        return grads[0].T[None], grads[1:]
+        (lower, to_lower), (upper, to_upper) = lower_feed.result, upper_feed.result
+        return feed_out(meta, lower, upper, to_lower, to_upper)
 
     def ends_outputs():
-        first, second = ([*chains_of[0].result, *chains_of[1].result] for chains_of in (first_rows, sent_back))
-        ends = jnp.stack([jnp.where(first_core, a, b) for a, b in zip(rows_of(first), rows_of(second))])
-        return ends.astype(f32).reshape(1, micro, rows_here, seg, D)
-
-    ready, waiting = {}, {"ends": (ends_outputs, first_rows), "feed": (feed_outputs, [lower_feed, upper_feed])}
+        place_here = jnp.stack([core, chip]).astype(jnp.int32)
+        first, second = [chain.result[0] for chain in first_rows], [*sent_back[0].result, *sent_back[1].result]
+        own_core = core_of(chip)
+        first[0] = jnp.where(own_core == 0, segment_of(grad, 0), first[0])
+        second[0] = jnp.where(own_core == 1, segment_of(result, 0), second[0])
+        rows = ends_rows(place_here, first, second)
+        return rows.reshape(1, micro, rows_here, seg, D)
+
+    ready, waiting = {}, {"feed": (feed_outputs, [lower_feed, upper_feed]), "ends": (ends_outputs, first_rows)}
     while any(not chain.done for chain in chains.running):
-        ready = chains.step(ready)
         for name in list(waiting):
             make, needed = waiting[name]
             if all(chain.done for chain in needed):
                 ready[name] = make()
                 del waiting[name]
+        ready, grad = chains.step((ready, grad))
     for name, (make, _) in waiting.items():
         ready[name] = make()
     ends_out, (grad_up, grad_down) = ready["ends"], ready["feed"]
-    attention_grads = finished(lower_heads.result, upper_heads.result)
+    (lower, to_lower), (upper, to_upper) = lower_heads.result, upper_heads.result
+    attention_grads = jnp.where(
+        first_core, jnp.concatenate([lower, to_lower], axis=1), jnp.concatenate([to_upper, upper], axis=1)
+    ).astype(f32)
     both_sums = both_sums.result
     sums = jnp.where(first_core, both_sums[0], both_sums[1])
     grad_qv = lax.dynamic_slice_in_dim(sums[6:8], chip * n_qv, n_qv, 1)[None]
@@ -1576,9 +1687,9 @@
         jnp.swapaxes(attention_grads[:3], 1, 2)[None],
         grad_qv,
         attention_grads[3:],
-        grad_up,
+        grad_up[None],
         grad_up_bias,
-        grad_down,
+        grad_down[None],
         sums[4:6][None],
     )
 

time: 1060 us -> 1040 us (0.981)
  Pallas kernels: 595 us -> 578 us
  local copies, waits for them, and re-layouts: 80.5 us -> 67.6 us
    add x4 -> x20, other arithmetic: 0.04 us -> 29.4 us  [the longest x14 29.3 us: plus(): return values[0] + values[1]]
    convert_element_type x18 -> x4, other arithmetic: 42.2 us -> 14.4 us  [plus(): return total.astype(bf16)]
    ppermute x34, waiting for transfers between devices: 31.9 us -> 53.6 us  [hop(): return lax.ppermute(value, ST, pairs)]
    pallas_call x6, Pallas kernels: 101 us -> 83.2 us  [attend(): pl.pallas_call(partial(attend_kernel, seg), grid_spec=pltpu.PrefetchScala...]
    ppermute x21, waiting for transfers between devices: 106 us -> 90.6 us  [exchanged(): return lax.ppermute(value, axis, [(n, n ^ distance) for n in range(count)])]
    unnamed x156 -> x152, local copies, waits for them, and re-layouts: 28.3 us -> 18.1 us
    pallas_call x18 -> x14, Pallas kernels: 203 us -> 212 us  [the longest x6 157 us: attend_back(): pl.pallas_call(partial(attend_back_kernel, seg, starts), grid_spec=pltpu....]
  transfers between devices with their start and end apart: 94 -> 93, of which waited for: 34 -> 33; matrix products, arithmetic and copies ran while one was open for 11% -> 13% of each run, Pallas kernels for 53% -> 55%
where the time goes in v3:
time: 1040 us; the launch traced here: 1020 us
  Pallas kernels  578 us (56%)
  waiting for transfers between devices  165 us (16%)
  other arithmetic  105 us (10%)
  starting transfers between devices  105 us (10%)
  local copies, waits for them, and re-layouts  67.6 us (6%)
    pallas_call x6, Pallas kernels, attend_back(): pl.pallas_call(partial(attend_back_kernel, seg, starts), grid_spec=pltpu....  157 us
    pallas_call x2, Pallas kernels, feed_back(): pl.pallas_call(feed_back_kernel, grid_spec=pltpu.PrefetchScalarGridSpec(n...  99 us
    ppermute x21, waiting for transfers between devices, exchanged(): return lax.ppermute(value, axis, [(n, n ^ distance) for n in range(count)])  90.6 us
    pallas_call x6, Pallas kernels, attend(): pl.pallas_call(partial(attend_kernel, seg), grid_spec=pltpu.PrefetchScala...  83.2 us
    pallas_call x6, Pallas kernels, project_back(): pl.pallas_call(partial(project_back_kernel, groups, so_far is None, norm...  80.5 us
    ppermute x34, starting transfers between devices, hop(): return lax.ppermute(value, ST, pairs)  62.4 us
    pallas_call x2, Pallas kernels, feed(): pl.pallas_call(partial(feed_kernel, (len(heads), len(heads_pieces))), gri...  55.3 us
    ppermute x34, waiting for transfers between devices, hop(): return lax.ppermute(value, ST, pairs)  53.6 us
  transfers between devices with their start and end apart: 93, of which 33 were waited for; matrix products, arithmetic and copies ran while one was open for 13% of the time, Pallas kernels for 55%

profile of v3, /device:TPU:0, one launch (start us, length us, event | category | flops | bytes accessed | tf_op | source)
XLA Modules:
  0.0 1024.4 jit_solution(3141227995720965280)
XLA Ops:
  10.1 5.3 collective-permute-start.3
  32.0 7.3 collective-permute-done.2
  54.6 5.4 project.6
  65.8 11.1 %attend.6 = (bf16[1024,256]{1,0:T(8,128)(2,1)}, bf16[1024,256]{1,0:T(8,128)(2,1)}) custom-call(s32[3]{0:T(128)} %pad_add_fusion.1.meta, bf16[1024,256]{1,0:T(8,128)(2,1)} %get-tuple-element.912.q, bf16[2,1024,256]{2,1,0:T(8,128)(2,1)} %get-tuple-element.913.kv, bf16[2,1024,256]{2,1,0:T(8,128)(2,1)} %copy-done.21, bf16[2048,128]{1,0:T(8,128)(2,1)} %pad_maximum_fusion.6.kcol, ...), custom_call_target="tpu_custom_call" | custom-call | flops 83886080 | bytes 57344 | tf_op jit(solution)/shard_map/attend/pallas_call | solution.py:516
  76.9 5.8 broadcast_select_fusion
  88.7 7.2 project.7
  101.6 19.3 %attend.7 = (bf16[1024,512]{1,0:T(8,128)(2,1)}, bf16[1024,512]{1,0:T(8,128)(2,1)}) custom-call(s32[5]{0:T(128)} %pad_add_fusion.2.meta, bf16[1024,512]{1,0:T(8,128)(2,1)} %get-tuple-element.846.q, bf16[2,1024,512]{2,1,0:T(8,128)(2,1)} %get-tuple-element.847.kv, bf16[2,1024,512]{2,1,0:T(8,128)(2,1)} %copy-done.14, bf16[2048,128]{1,0:T(8,128)(2,1)} %pad_maximum_fusion.6.kcol, ...), custom_call_target="tpu_custom_call" | custom-call | flops 167772160 | bytes 114688 | tf_op jit(solution)/shard_map/attend/pallas_call | solution.py:516
  127.4 5.7 project.8
  137.0 11.0 %attend.8 = (bf16[1024,256]{1,0:T(8,128)(2,1)}, bf16[1024,256]{1,0:T(8,128)(2,1)}) custom-call(s32[3]{0:T(128)} %pad_add_fusion.3.meta, bf16[1024,256]{1,0:T(8,128)(2,1)} %get-tuple-element.830.q, bf16[2,1024,256]{2,1,0:T(8,128)(2,1)} %get-tuple-element.831.kv, bf16[2,1024,256]{2,1,0:T(8,128)(2,1)} %copy-done.22, bf16[2048,128]{1,0:T(8,128)(2,1)} %pad_maximum_fusion.6.kcol, ...), custom_call_target="tpu_custom_call" | custom-call | flops 83886080 | bytes 57344 | tf_op jit(solution)/shard_map/attend/pallas_call | solution.py:516
  148.0 8.2 collective-permute-done.13.refs_12_.near
  164.0 27.9 %feed.2 = (bf16[4,1024,768]{2,1,0:T(8,128)(2,1)}, bf16[4,1024,768]{2,1,0:T(8,128)(2,1)}, f32[1024,1024]{1,0:T(8,128)}, bf16[1024,1024]{1,0:T(8,128)(2,1)}, f32[1024,1024]{1,0:T(8,128)}) custom-call(s32[1]{0:T(128)} %bitcast.meta, bf16[1024,256]{1,0:T(8,128)(2,1)} %get-tuple-element.591.refs_0_.o.refs_3_, ...), custom_call_target="tpu_custom_call" | custom-call | flops 234881024 | bytes 655360 | tf_op jit(solution)/shard_map/feed/pallas_call | solution.py:825
  196.6 12.4 %feed_last.2 = (bf16[4,1024,256]{2,1,0:T(8,128)(2,1)}, bf16[4,1024,256]{2,1,0:T(8,128)(2,1)}, bf16[1024,1024]{1,0:T(8,128)(2,1)}, bf16[1024,1024]{1,0:T(8,128)(2,1)}) custom-call(bf16[1024,1024]{1,0:T(8,128)(2,1)} %get-tuple-element.594.middle, f32[1024,1024]{1,0:T(8,128)} %get-tuple-element.602.so_far, f32[8,1024]{1,0:T(8,128)} %get-tuple-element.1233.vectors, ...), custom_call_target="tpu_custom_call" | custom-call | flops 67108864 | bytes 294912 | tf_op jit(solution)/shard_map/feed_last/pallas_call | solution.py:882
  209.0 5.4 project.9
  218.2 11.3 %attend.9 = (bf16[1024,256]{1,0:T(8,128)(2,1)}, bf16[1024,256]{1,0:T(8,128)(2,1)}) custom-call(s32[3]{0:T(128)} %pad_add_fusion.1.meta, bf16[1024,256]{1,0:T(8,128)(2,1)} %get-tuple-element.772.q, bf16[2,1024,256]{2,1,0:T(8,128)(2,1)} %get-tuple-element.773.kv, bf16[2,1024,256]{2,1,0:T(8,128)(2,1)} %copy-done.23, bf16[2048,128]{1,0:T(8,128)(2,1)} %pad_maximum_fusion.6.kcol, ...), custom_call_target="tpu_custom_call" | custom-call | flops 83886080 | bytes 57344 | tf_op jit(solution)/shard_map/attend/pallas_call | solution.py:516
  235.3 7.3 project.10
  248.3 19.1 %attend.10 = (bf16[1024,512]{1,0:T(8,128)(2,1)}, bf16[1024,512]{1,0:T(8,128)(2,1)}) custom-call(s32[5]{0:T(128)} %pad_add_fusion.2.meta, bf16[1024,512]{1,0:T(8,128)(2,1)} %get-tuple-element.719.q, bf16[2,1024,512]{2,1,0:T(8,128)(2,1)} %get-tuple-element.720.kv, bf16[2,1024,512]{2,1,0:T(8,128)(2,1)} %copy-done.15, bf16[2048,128]{1,0:T(8,128)(2,1)} %pad_maximum_fusion.6.kcol, ...), custom_call_target="tpu_custom_call" | custom-call | flops 167772160 | bytes 114688 | tf_op jit(solution)/shard_map/attend/pallas_call | solution.py:516
  274.3 5.7 project.11
  283.8 11.5 %attend.11 = (bf16[1024,256]{1,0:T(8,128)(2,1)}, bf16[1024,256]{1,0:T(8,128)(2,1)}) custom-call(s32[3]{0:T(128)} %pad_add_fusion.3.meta, bf16[1024,256]{1,0:T(8,128)(2,1)} %get-tuple-element.705.q, bf16[2,1024,256]{2,1,0:T(8,128)(2,1)} %get-tuple-element.706.kv, bf16[2,1024,256]{2,1,0:T(8,128)(2,1)} %copy-done.24, bf16[2048,128]{1,0:T(8,128)(2,1)} %pad_maximum_fusion.6.kcol, ...), custom_call_target="tpu_custom_call" | custom-call | flops 83886080 | bytes 57344 | tf_op jit(solution)/shard_map/attend/pallas_call | solution.py:516
  295.3 7.6 collective-permute-done.24.refs_12_.near
  310.6 27.4 %feed.3 = (bf16[4,1024,768]{2,1,0:T(8,128)(2,1)}, bf16[4,1024,768]{2,1,0:T(8,128)(2,1)}, f32[1024,1024]{1,0:T(8,128)}, bf16[1024,1024]{1,0:T(8,128)(2,1)}, f32[1024,1024]{1,0:T(8,128)}) custom-call(s32[1]{0:T(128)} %bitcast.meta, bf16[1024,256]{1,0:T(8,128)(2,1)} %get-tuple-element.666.refs_0_.o.refs_3_, ...), custom_call_target="tpu_custom_call" | custom-call | flops 234881024 | bytes 655360 | tf_op jit(solution)/shard_map/feed/pallas_call | solution.py:825
  349.7 12.4 %feed_last.3 = (bf16[4,1024,256]{2,1,0:T(8,128)(2,1)}, bf16[4,1024,256]{2,1,0:T(8,128)(2,1)}, bf16[1024,1024]{1,0:T(8,128)(2,1)}, bf16[1024,1024]{1,0:T(8,128)(2,1)}) custom-call(bf16[1024,1024]{1,0:T(8,128)(2,1)} %get-tuple-element.682.middle, f32[1024,1024]{1,0:T(8,128)} %get-tuple-element.683.so_far, f32[8,1024]{1,0:T(8,128)} %get-tuple-element.1233.vectors, ...), custom_call_target="tpu_custom_call" | custom-call | flops 67108864 | bytes 294912 | tf_op jit(solution)/shard_map/feed_last/pallas_call | solution.py:882
  362.1 10.6 %collective-permute-done.30 = bf16[512,1024]{1,0:T(8,128)(2,1)} collective-permute-done((bf16[512,1024]{1,0:T(8,128)(2,1)}, bf16[512,1024]{1,0:T(8,128)(2,1)}, u32[]{:S(2)}, u32[]{:S(2)}) %collective-permute-start.30) | collective-permute-done | bytes 1048608 | tf_op jit(solution)/shard_map/ppermute | solution.py:386
  375.5 5.2 collective-permute-start.32
  387.0 49.3 %feed_back.2 = (bf16[2,4,512,1024]{3,2,1,0:T(8,128)(2,1)}, bf16[2,4,512,1024]{3,2,1,0:T(8,128)(2,1)}, f32[4,8,1024]{2,1,0:T(8,128)}, bf16[1024,1024]{1,0:T(8,128)(2,1)}, f32[8,1024]{1,0:T(8,128)}) custom-call(s32[1]{0:T(128)} %bitcast.meta, bf16[1024,1024]{1,0:T(8,128)(2,1)} %pad_maximum_fusion.3.above, bf16[1024,1024]{1,0:T(8,128)(2,1)} %get-tuple-element.682.middle, ...), custom_call_target="tpu_custom_call" | custom-call | flops 536870912 | bytes 1802240 | tf_op jit(solution)/shard_map/feed_back/pallas_call | solution.py:964
  438.2 5.9 collective-permute-start.36
  444.1 20.7 %attend_back.6 = (bf16[1024,256]{1,0:T(8,128)(2,1)}, bf16[2,1024,256]{2,1,0:T(8,128)(2,1)}, bf16[2,1024,256]{2,1,0:T(8,128)(2,1)}) custom-call(s32[3]{0:T(128)} %pad_add_fusion.3.meta, bf16[1024,256]{1,0:T(8,128)(2,1)} %get-tuple-element.705.q, bf16[2,1024,256]{2,1,0:T(8,128)(2,1)} %get-tuple-element.706.kv, bf16[2,1024,256]{2,1,0:T(8,128)(2,1)} %copy-done.24, ...), custom_call_target="tpu_custom_call" | custom-call | flops 226492416 | bytes 106496 | tf_op jit(solution)/shard_map/attend_back/pallas_call | solution.py:631
  464.8 9.4 meet.2
  476.4 37.4 %attend_back.7 = (bf16[1024,512]{1,0:T(8,128)(2,1)}, bf16[2,1024,512]{2,1,0:T(8,128)(2,1)}, bf16[2,1024,512]{2,1,0:T(8,128)(2,1)}) custom-call(s32[5]{0:T(128)} %pad_add_fusion.2.meta, bf16[1024,512]{1,0:T(8,128)(2,1)} %get-tuple-element.719.q, bf16[2,1024,512]{2,1,0:T(8,128)(2,1)} %get-tuple-element.720.kv, bf16[2,1024,512]{2,1,0:T(8,128)(2,1)} %copy-done.15, ...), custom_call_target="tpu_custom_call" | custom-call | flops 452984832 | bytes 212992 | tf_op jit(solution)/shard_map/attend_back/pallas_call | solution.py:631
  514.8 9.6 project_back.6
  529.0 15.1 %project_back.7 = (bf16[4,256,1024]{2,1,0:T(8,128)(2,1)}, bf16[4,256,1024]{2,1,0:T(8,128)(2,1)}, f32[8,512]{1,0:T(8,128)}, f32[1024,1024]{1,0:T(8,128)}) custom-call(s32[1]{0:T(128)} %bitcast.meta, bf16[1024,512]{1,0:T(8,128)(2,1)} %get-tuple-element.747.refs_0_, bf16[2,1024,512]{2,1,0:T(8,128)(2,1)} %get-tuple-element.748.refs_1_, ...), custom_call_target="tpu_custom_call" | custom-call | flops 117440512 | bytes 409600 | tf_op jit(solution)/shard_map/project_back/pallas_call | solution.py:1074
  546.9 7.7 collective-permute-done.41
  563.0 20.3 %attend_back.8 = (bf16[1024,256]{1,0:T(8,128)(2,1)}, bf16[2,1024,256]{2,1,0:T(8,128)(2,1)}, bf16[2,1024,256]{2,1,0:T(8,128)(2,1)}) custom-call(s32[3]{0:T(128)} %pad_add_fusion.1.meta, bf16[1024,256]{1,0:T(8,128)(2,1)} %get-tuple-element.772.q, bf16[2,1024,256]{2,1,0:T(8,128)(2,1)} %get-tuple-element.773.kv, bf16[2,1024,256]{2,1,0:T(8,128)(2,1)} %copy-done.23, ...), custom_call_target="tpu_custom_call" | custom-call | flops 226492416 | bytes 106496 | tf_op jit(solution)/shard_map/attend_back/pallas_call | solution.py:631
  595.8 15.4 %project_back.8 = (bf16[4,128,1024]{2,1,0:T(8,128)(2,1)}, bf16[4,128,1024]{2,1,0:T(8,128)(2,1)}, f32[8,256]{1,0:T(8,128)}, bf16[1024,1024]{1,0:T(8,128)(2,1)}, f32[8,1024]{1,0:T(8,128)}) custom-call(s32[1]{0:T(128)} %bitcast.meta, bf16[1024,256]{1,0:T(8,128)(2,1)} %get-tuple-element.789.refs_0_, bf16[2,1024,256]{2,1,0:T(8,128)(2,1)} %get-tuple-element.790.refs_1_, ...), custom_call_target="tpu_custom_call" | custom-call | flops 58720256 | bytes 303104 | tf_op jit(solution)/shard_map/project_back/pallas_call | solution.py:1074
  611.2 7.8 collective-permute-done.48
  623.3 49.7 %feed_back.3 = (bf16[2,4,512,1024]{3,2,1,0:T(8,128)(2,1)}, bf16[2,4,512,1024]{3,2,1,0:T(8,128)(2,1)}, f32[4,8,1024]{2,1,0:T(8,128)}, bf16[1024,1024]{1,0:T(8,128)(2,1)}, f32[8,1024]{1,0:T(8,128)}) custom-call(s32[1]{0:T(128)} %bitcast.meta, bf16[1024,1024]{1,0:T(8,128)(2,1)} %get-tuple-element.809.above, bf16[1024,1024]{1,0:T(8,128)(2,1)} %get-tuple-element.594.middle, ...), custom_call_target="tpu_custom_call" | custom-call | flops 536870912 | bytes 1802240 | tf_op jit(solution)/shard_map/feed_back/pallas_call | solution.py:964
  683.0 20.7 %attend_back.9 = (bf16[1024,256]{1,0:T(8,128)(2,1)}, bf16[2,1024,256]{2,1,0:T(8,128)(2,1)}, bf16[2,1024,256]{2,1,0:T(8,128)(2,1)}) custom-call(s32[3]{0:T(128)} %pad_add_fusion.3.meta, bf16[1024,256]{1,0:T(8,128)(2,1)} %get-tuple-element.830.q, bf16[2,1024,256]{2,1,0:T(8,128)(2,1)} %get-tuple-element.831.kv, bf16[2,1024,256]{2,1,0:T(8,128)(2,1)} %copy-done.22, ...), custom_call_target="tpu_custom_call" | custom-call | flops 226492416 | bytes 106496 | tf_op jit(solution)/shard_map/attend_back/pallas_call | solution.py:631
  703.7 10.6 %collective-permute-done.55 = bf16[4,64,1024]{2,1,0:T(8,128)(2,1)S(1)} collective-permute-done((bf16[4,64,1024]{2,1,0:T(8,128)(2,1)S(1)}, bf16[4,64,1024]{2,1,0:T(8,128)(2,1)S(1)}, u32[]{:S(2)}, u32[]{:S(2)}) %collective-permute-start.55) | collective-permute-done | bytes 524320 | tf_op jit(solution)/shard_map/ppermute | solution.py:1140
  714.6 9.5 meet.3
  726.8 37.2 %attend_back.10 = (bf16[1024,512]{1,0:T(8,128)(2,1)}, bf16[2,1024,512]{2,1,0:T(8,128)(2,1)}, bf16[2,1024,512]{2,1,0:T(8,128)(2,1)}) custom-call(s32[5]{0:T(128)} %pad_add_fusion.2.meta, bf16[1024,512]{1,0:T(8,128)(2,1)} %get-tuple-element.846.q, bf16[2,1024,512]{2,1,0:T(8,128)(2,1)} %get-tuple-element.847.kv, bf16[2,1024,512]{2,1,0:T(8,128)(2,1)} %copy-done.14, ...), custom_call_target="tpu_custom_call" | custom-call | flops 452984832 | bytes 212992 | tf_op jit(solution)/shard_map/attend_back/pallas_call | solution.py:631
  766.6 9.6 project_back.9
  784.7 15.3 %project_back.10 = (bf16[4,256,1024]{2,1,0:T(8,128)(2,1)}, bf16[4,256,1024]{2,1,0:T(8,128)(2,1)}, f32[8,512]{1,0:T(8,128)}, f32[1024,1024]{1,0:T(8,128)}) custom-call(s32[1]{0:T(128)} %bitcast.meta, bf16[1024,512]{1,0:T(8,128)(2,1)} %get-tuple-element.882.refs_0_, bf16[2,1024,512]{2,1,0:T(8,128)(2,1)} %get-tuple-element.883.refs_1_, ...), custom_call_target="tpu_custom_call" | custom-call | flops 117440512 | bytes 409600 | tf_op jit(solution)/shard_map/project_back/pallas_call | solution.py:1074
  823.4 20.5 %attend_back.11 = (bf16[1024,256]{1,0:T(8,128)(2,1)}, bf16[2,1024,256]{2,1,0:T(8,128)(2,1)}, bf16[2,1024,256]{2,1,0:T(8,128)(2,1)}) custom-call(s32[3]{0:T(128)} %pad_add_fusion.1.meta, bf16[1024,256]{1,0:T(8,128)(2,1)} %get-tuple-element.912.q, bf16[2,1024,256]{2,1,0:T(8,128)(2,1)} %get-tuple-element.913.kv, bf16[2,1024,256]{2,1,0:T(8,128)(2,1)} %copy-done.21, ...), custom_call_target="tpu_custom_call" | custom-call | flops 226492416 | bytes 106496 | tf_op jit(solution)/shard_map/attend_back/pallas_call | solution.py:631
  861.4 15.4 %project_back.11 = (bf16[4,128,1024]{2,1,0:T(8,128)(2,1)}, bf16[4,128,1024]{2,1,0:T(8,128)(2,1)}, f32[8,256]{1,0:T(8,128)}, bf16[1024,1024]{1,0:T(8,128)(2,1)}, f32[8,1024]{1,0:T(8,128)}) custom-call(s32[1]{0:T(128)} %bitcast.meta, bf16[1024,256]{1,0:T(8,128)(2,1)} %get-tuple-element.933.refs_0_, bf16[2,1024,256]{2,1,0:T(8,128)(2,1)} %get-tuple-element.934.refs_1_, ...), custom_call_target="tpu_custom_call" | custom-call | flops 58720256 | bytes 303104 | tf_op jit(solution)/shard_map/project_back/pallas_call | solution.py:1074
  901.7 17.8 %collective-permute-done.78 = bf16[2,128,1024]{2,1,0:T(8,128)(2,1)S(1)} collective-permute-done((bf16[2,128,1024]{2,1,0:T(8,128)(2,1)}, bf16[2,128,1024]{2,1,0:T(8,128)(2,1)S(1)}, u32[]{:S(2)}, u32[]{:S(2)}) %collective-permute-start.78) | collective-permute-done | bytes 524320 | tf_op jit(solution)/shard_map/ppermute | solution.py:1140
  929.4 25.3 %collective-permute-done.81 = bf16[2,256,1024]{2,1,0:T(8,128)(2,1)S(1)} collective-permute-done((bf16[2,256,1024]{2,1,0:T(8,128)(2,1)S(1)}, bf16[2,256,1024]{2,1,0:T(8,128)(2,1)S(1)}, u32[]{:S(2)}, u32[]{:S(2)}) %collective-permute-start.81) | collective-permute-done | bytes 1048608 | tf_op jit(solution)/shard_map/ppermute | solution.py:1140
  974.4 12.8 %collective-permute-done.86 = bf16[4,32,1024]{2,1,0:T(8,128)(2,1)} collective-permute-done((bf16[4,32,1024]{2,1,0:T(8,128)(2,1)S(1)}, bf16[4,32,1024]{2,1,0:T(8,128)(2,1)}, u32[]{:S(2)}, u32[]{:S(2)}) %collective-permute-start.86) | collective-permute-done | bytes 262176 | tf_op jit(solution)/shard_map/ppermute | solution.py:1140
  993.7 8.7 feed_out.1
  1002.4 9.5 ends_rows.1
  (594 shorter events, 310.1 us)
Async XLA Ops:
  5.7 38.5 %collective-permute-start.4 = (bf16[1056,1024]{1,0:T(8,128)(2,1)}, bf16[1056,1024]{1,0:T(8,128)(2,1)}, u32[]{:S(2)}, u32[]{:S(2)}) collective-permute-start(bf16[1056,1024]{1,0:T(8,128)(2,1)} %pad_maximum_fusion.1), channel_id=1, source_target_pairs={{0,16},{16,0},{1,17},{17,1},{2,18},{18,2},{3,19},{19,3},{4,20},{20... | collective-permute-start | bytes 6488072 | tf_op jit(solution)/shard_map/ppermute | solution.py:390
  43.0 33.8 %collective-permute-start.6 = (bf16[2,1024,1024]{2,1,0:T(8,128)(2,1)}, bf16[2,1024,1024]{2,1,0:T(8,128)(2,1)}, u32[]{:S(2)}, u32[]{:S(2)}) collective-permute-start(bf16[2,1024,1024]{2,1,0:T(8,128)(2,1)} %pad_maximum_fusion), channel_id=1, source_target_pairs={{0,16},{16,0},{1,17},{17,1},{2,18},{18,2},{3,19},{19,3},{4,20},{20... | collective-permute-start | bytes 12582920 | tf_op jit(solution)/shard_map/ppermute | solution.py:390
  46.6 36.1 %collective-permute-start.7 = (bf16[1056,1024]{1,0:T(8,128)(2,1)S(1)}, bf16[1056,1024]{1,0:T(8,128)(2,1)}, u32[]{:S(2)}, u32[]{:S(2)}) collective-permute-start(bf16[1056,1024]{1,0:T(8,128)(2,1)S(1)} %get-tuple-element.671.refs_0_.refs_3_.refs_1_.refs_6_), channel_id=1, source_target_pairs={{0,1},{1,0},{2,3},{3,2},{16,18},{17,19},{18,16},{19,17},{4,5},{5,4... | collective-permute-start | bytes 6488072 | tf_op jit(solution)/shard_map/ppermute | solution.py:386
  96.3 27.4 %collective-permute-start.10 = (bf16[544,1024]{1,0:T(8,128)(2,1)}, bf16[544,1024]{1,0:T(8,128)(2,1)S(1)}, u32[]{:S(2)}, u32[]{:S(2)}) collective-permute-start(bf16[544,1024]{1,0:T(8,128)(2,1)} %pad_maximum_fusion.4), channel_id=1, source_target_pairs={{0,2},{1,3},{2,0},{3,1},{16,17},{17,16},{18,19},{19,18},{4,6},{5,7... | collective-permute-start | bytes 3342344 | tf_op jit(solution)/shard_map/ppermute | solution.py:386
  97.8 58.5 %collective-permute-start.13 = (bf16[2,1024,1024]{2,1,0:T(8,128)(2,1)}, bf16[2,1024,1024]{2,1,0:T(8,128)(2,1)}, u32[]{:S(2)}, u32[]{:S(2)}) collective-permute-start(bf16[2,1024,1024]{2,1,0:T(8,128)(2,1)} %get-tuple-element.617), channel_id=1, source_target_pairs={{0,1},{1,0},{2,3},{3,2},{16,18},{17,19},{18,16},{19,17},{4,5},{5,4... | collective-permute-start | bytes 12582920 | tf_op jit(solution)/shard_map/ppermute | solution.py:386
  160.0 32.0 %collective-permute-start.15 = (bf16[2,512,1024]{2,1,0:T(8,128)(2,1)}, bf16[2,512,1024]{2,1,0:T(8,128)(2,1)}, u32[]{:S(2)}, u32[]{:S(2)}) collective-permute-start(bf16[2,512,1024]{2,1,0:T(8,128)(2,1)} %constant_dynamic-slice_fusion.29), channel_id=1, source_target_pairs={{0,2},{1,3},{2,0},{3,1},{16,17},{17,16},{18,19},{19,18},{4,6},{5,7... | collective-permute-start | bytes 6291464 | tf_op jit(solution)/shard_map/ppermute | solution.py:386
  192.4 37.0 %collective-permute-start.18 = (bf16[1056,1024]{1,0:T(8,128)(2,1)S(1)}, bf16[1056,1024]{1,0:T(8,128)(2,1)}, u32[]{:S(2)}, u32[]{:S(2)}) collective-permute-start(bf16[1056,1024]{1,0:T(8,128)(2,1)S(1)} %copy-done.2), channel_id=1, source_target_pairs={{0,1},{1,0},{2,3},{3,2},{16,18},{17,19},{18,16},{19,17},{4,5},{5,4... | collective-permute-start | bytes 6488072 | tf_op jit(solution)/shard_map/ppermute | solution.py:386
  242.9 27.6 %collective-permute-start.21 = (bf16[544,1024]{1,0:T(8,128)(2,1)}, bf16[544,1024]{1,0:T(8,128)(2,1)S(1)}, u32[]{:S(2)}, u32[]{:S(2)}) collective-permute-start(bf16[544,1024]{1,0:T(8,128)(2,1)} %pad_maximum_fusion.5), channel_id=1, source_target_pairs={{0,2},{1,3},{2,0},{3,1},{16,17},{17,16},{18,19},{19,18},{4,6},{5,7... | collective-permute-start | bytes 3342344 | tf_op jit(solution)/shard_map/ppermute | solution.py:386
  244.1 58.7 %collective-permute-start.24 = (bf16[2,1024,1024]{2,1,0:T(8,128)(2,1)}, bf16[2,1024,1024]{2,1,0:T(8,128)(2,1)}, u32[]{:S(2)}, u32[]{:S(2)}) collective-permute-start(bf16[2,1024,1024]{2,1,0:T(8,128)(2,1)} %get-tuple-element.649), channel_id=1, source_target_pairs={{0,1},{1,0},{2,3},{3,2},{16,18},{17,19},{18,16},{19,17},{4,5},{5,4... | collective-permute-start | bytes 12582920 | tf_op jit(solution)/shard_map/ppermute | solution.py:386
  306.6 31.4 %collective-permute-start.26 = (bf16[2,512,1024]{2,1,0:T(8,128)(2,1)}, bf16[2,512,1024]{2,1,0:T(8,128)(2,1)S(1)}, u32[]{:S(2)}, u32[]{:S(2)}) collective-permute-start(bf16[2,512,1024]{2,1,0:T(8,128)(2,1)} %constant_dynamic-slice_fusion.27), channel_id=1, source_target_pairs={{0,2},{1,3},{2,0},{3,1},{16,17},{17,16},{18,19},{19,18},{4,6},{5,7... | collective-permute-start | bytes 6291464 | tf_op jit(solution)/shard_map/ppermute | solution.py:386
  375.5 60.8 %collective-permute-start.32 = (bf16[512,1024]{1,0:T(8,128)(2,1)S(1)}, bf16[512,1024]{1,0:T(8,128)(2,1)}, u32[]{:S(2)}, u32[]{:S(2)}) collective-permute-start(bf16[512,1024]{1,0:T(8,128)(2,1)S(1)} %get-tuple-element.700), channel_id=1, source_target_pairs={{0,16},{3,19},{4,20},{7,23},{8,24},{11,27},{12,28},{15,31}} | collective-permute-start | bytes 3145736 | tf_op jit(solution)/shard_map/ppermute | solution.py:386
  380.6 55.6 %collective-permute-start.33 = (bf16[512,1024]{1,0:T(8,128)(2,1)}, bf16[512,1024]{1,0:T(8,128)(2,1)}, u32[]{:S(2)}, u32[]{:S(2)}) collective-permute-start(bf16[512,1024]{1,0:T(8,128)(2,1)} %get-tuple-element.701), channel_id=1, source_target_pairs={{1,16},{16,17},{19,18},{2,19},{5,20},{20,21},{23,22},{6,23},{9,24}... | collective-permute-start | bytes 3145736 | tf_op jit(solution)/shard_map/ppermute | solution.py:386
  436.3 28.5 %collective-permute-start.34 = (bf16[2,4,512,1024]{3,2,1,0:T(8,128)(2,1)}, bf16[2,4,512,1024]{3,2,1,0:T(8,128)(2,1)}, u32[]{:S(2)}, u32[]{:S(2)}) collective-permute-start(bf16[2,4,512,1024]{3,2,1,0:T(8,128)(2,1)} %get-tuple-element.710), channel_id=1, source_target_pairs={{0,16},{16,0},{1,17},{17,1},{2,18},{18,2},{3,19},{19,3},{4,20},{20... | collective-permute-start | bytes 25165832 | tf_op jit(solution)/shard_map/ppermute | solution.py:390
  437.5 36.8 %collective-permute-start.35 = (bf16[512,1024]{1,0:T(8,128)(2,1)}, bf16[512,1024]{1,0:T(8,128)(2,1)S(1)}, u32[]{:S(2)}, u32[]{:S(2)}) collective-permute-start(bf16[512,1024]{1,0:T(8,128)(2,1)} %get-tuple-element.711), channel_id=1, source_target_pairs={{2,16},{19,17},{16,18},{1,19},{6,20},{23,21},{20,22},{5,23},{10,24... | collective-permute-start | bytes 3145736 | tf_op jit(solution)/shard_map/ppermute | solution.py:386
  438.2 36.0 %collective-permute-start.36 = (bf16[512,1024]{1,0:T(8,128)(2,1)S(1)}, bf16[512,1024]{1,0:T(8,128)(2,1)S(1)}, u32[]{:S(2)}, u32[]{:S(2)}) collective-permute-start(bf16[512,1024]{1,0:T(8,128)(2,1)S(1)} %get-tuple-element.712), channel_id=1, source_target_pairs={{3,16},{18,17},{17,18},{0,19},{7,20},{22,21},{21,22},{4,23},{11,24... | collective-permute-start | bytes 3145736 | tf_op jit(solution)/shard_map/ppermute | solution.py:386
  474.3 39.5 %collective-permute-start.37 = (bf16[2,1024,256]{2,1,0:T(8,128)(2,1)}, bf16[2,1024,256]{2,1,0:T(8,128)(2,1)S(1)}, u32[]{:S(2)}, u32[]{:S(2)}) collective-permute-start(bf16[2,1024,256]{2,1,0:T(8,128)(2,1)} %get-tuple-element.724), channel_id=1, source_target_pairs={{0,16},{16,0},{1,17},{17,1},{2,18},{18,2},{3,19},{19,3},{4,20},{20... | collective-permute-start | bytes 3145736 | tf_op jit(solution)/shard_map/ppermute | solution.py:390
  474.4 50.1 %collective-permute-start.38 = (bf16[2,512,1024]{2,1,0:T(8,128)(2,1)}, bf16[2,512,1024]{2,1,0:T(8,128)(2,1)}, u32[]{:S(2)}, u32[]{:S(2)}) collective-permute-start(bf16[2,512,1024]{2,1,0:T(8,128)(2,1)} %bitcast.389), channel_id=1, source_target_pairs={{0,2},{1,3},{2,0},{3,1},{16,17},{17,16},{18,19},{19,18},{4,6},{5,7... | collective-permute-start | bytes 6291464 | tf_op jit(solution)/shard_map/ppermute | solution.py:386
  474.5 50.0 %collective-permute-start.39 = (bf16[2,512,1024]{2,1,0:T(8,128)(2,1)}, bf16[2,512,1024]{2,1,0:T(8,128)(2,1)}, u32[]{:S(2)}, u32[]{:S(2)}) collective-permute-start(bf16[2,512,1024]{2,1,0:T(8,128)(2,1)} %get-tuple-element.735), channel_id=1, source_target_pairs={{0,1},{1,0},{2,3},{3,2},{16,18},{17,19},{18,16},{19,17},{4,5},{5,4... | collective-permute-start | bytes 6291464 | tf_op jit(solution)/shard_map/ppermute | solution.py:386
  528.3 26.2 %collective-permute-start.41 = (bf16[2,512,1024]{2,1,0:T(8,128)(2,1)}, bf16[2,512,1024]{2,1,0:T(8,128)(2,1)S(1)}, u32[]{:S(2)}, u32[]{:S(2)}) collective-permute-start(bf16[2,512,1024]{2,1,0:T(8,128)(2,1)} %add.528), channel_id=1, source_target_pairs={{0,1},{1,0},{2,3},{3,2},{16,18},{17,19},{18,16},{19,17},{4,5},{5,4... | collective-permute-start | bytes 6291464 | tf_op jit(solution)/shard_map/ppermute | solution.py:386
  528.5 26.1 %collective-permute-start.42 = (bf16[2,512,1024]{2,1,0:T(8,128)(2,1)}, bf16[2,512,1024]{2,1,0:T(8,128)(2,1)}, u32[]{:S(2)}, u32[]{:S(2)}) collective-permute-start(bf16[2,512,1024]{2,1,0:T(8,128)(2,1)} %collective-permute-done.39), channel_id=1, source_target_pairs={{0,16},{16,0},{1,17},{17,1},{2,18},{18,2},{3,19},{19,3},{4,20},{20... | collective-permute-start | bytes 6291464 | tf_op jit(solution)/shard_map/ppermute | solution.py:390
  559.7 28.4 %collective-permute-start.46 = (bf16[4,256,1024]{2,1,0:T(8,128)(2,1)}, bf16[4,256,1024]{2,1,0:T(8,128)(2,1)}, u32[]{:S(2)}, u32[]{:S(2)}) collective-permute-start(bf16[4,256,1024]{2,1,0:T(8,128)(2,1)} %get-tuple-element.779), channel_id=1, source_target_pairs={{0,16},{16,0},{1,17},{17,1},{2,18},{18,2},{3,19},{19,3},{4,20},{20... | collective-permute-start | bytes 6291464 | tf_op jit(solution)/shard_map/ppermute | solution.py:390
  559.8 25.7 %collective-permute-start.44 = (bf16[2,256,1024]{2,1,0:T(8,128)(2,1)S(1)}, bf16[2,256,1024]{2,1,0:T(8,128)(2,1)}, u32[]{:S(2)}, u32[]{:S(2)}) collective-permute-start(bf16[2,256,1024]{2,1,0:T(8,128)(2,1)S(1)} %constant_dynamic-slice_fusion.26), channel_id=1, source_target_pairs={{0,4},{4,0},{8,12},{12,8},{1,5},{5,1},{9,13},{13,9},{2,6},{6,2},{1... | collective-permute-start | bytes 3145736 | tf_op jit(solution)/shard_map/ppermute | solution.py:1140
  561.4 30.6 %collective-permute-start.45 = (bf16[4,128,1024]{2,1,0:T(8,128)(2,1)}, bf16[4,128,1024]{2,1,0:T(8,128)(2,1)}, u32[]{:S(2)}, u32[]{:S(2)}) collective-permute-start(bf16[4,128,1024]{2,1,0:T(8,128)(2,1)} %add.532), channel_id=1, source_target_pairs={{0,3},{1,2},{2,1},{3,0},{16,19},{17,18},{18,17},{19,16},{4,7},{5,6... | collective-permute-start | bytes 3145736 | tf_op jit(solution)/shard_map/ppermute | solution.py:386
  592.0 29.1 %collective-permute-start.49 = (bf16[4,256,1024]{2,1,0:T(8,128)(2,1)}, bf16[4,256,1024]{2,1,0:T(8,128)(2,1)S(1)}, u32[]{:S(2)}, u32[]{:S(2)}) collective-permute-start(bf16[4,256,1024]{2,1,0:T(8,128)(2,1)} %add.536), channel_id=1, source_target_pairs={{0,1},{1,0},{2,3},{3,2},{16,18},{17,19},{18,16},{19,17},{4,5},{5,4... | collective-permute-start | bytes 6291464 | tf_op jit(solution)/shard_map/ppermute | solution.py:386
  592.2 26.8 %collective-permute-start.48 = (bf16[2,128,1024]{2,1,0:T(8,128)(2,1)}, bf16[2,128,1024]{2,1,0:T(8,128)(2,1)}, u32[]{:S(2)}, u32[]{:S(2)}) collective-permute-start(bf16[2,128,1024]{2,1,0:T(8,128)(2,1)} %constant_dynamic-slice_fusion.25), channel_id=1, source_target_pairs={{0,8},{4,12},{8,0},{12,4},{1,9},{5,13},{9,1},{13,5},{2,10},{6,14},... | collective-permute-start | bytes 1572872 | tf_op jit(solution)/shard_map/ppermute | solution.py:1140
  622.2 53.0 %collective-permute-start.52 = (bf16[4,128,1024]{2,1,0:T(8,128)(2,1)}, bf16[4,128,1024]{2,1,0:T(8,128)(2,1)}, u32[]{:S(2)}, u32[]{:S(2)}) collective-permute-start(bf16[4,128,1024]{2,1,0:T(8,128)(2,1)} %get-tuple-element.820), channel_id=1, source_target_pairs={{0,16},{16,0},{1,17},{17,1},{2,18},{18,2},{3,19},{19,3},{4,20},{20... | collective-permute-start | bytes 3145736 | tf_op jit(solution)/shard_map/ppermute | solution.py:390
  622.2 53.0 %collective-permute-start.51 = (bf16[4,128,1024]{2,1,0:T(8,128)(2,1)}, bf16[4,128,1024]{2,1,0:T(8,128)(2,1)}, u32[]{:S(2)}, u32[]{:S(2)}) collective-permute-start(bf16[4,128,1024]{2,1,0:T(8,128)(2,1)} %constant_dynamic-slice_fusion.24), channel_id=1, source_target_pairs={{0,16},{16,0},{1,17},{17,1},{2,18},{18,2},{3,19},{19,3},{4,20},{20... | collective-permute-start | bytes 3145736 | tf_op jit(solution)/shard_map/ppermute | solution.py:390
  622.7 50.4 %collective-permute-start.50 = (bf16[2,128,1024]{2,1,0:T(8,128)(2,1)}, bf16[2,128,1024]{2,1,0:T(8,128)(2,1)}, u32[]{:S(2)}, u32[]{:S(2)}) collective-permute-start(bf16[2,128,1024]{2,1,0:T(8,128)(2,1)} %dynamic-slice_add_fusion.5), channel_id=1, source_target_pairs={{0,8},{4,12},{8,0},{12,4},{1,9},{5,13},{9,1},{13,5},{2,10},{6,14},... | collective-permute-start | bytes 1572872 | tf_op jit(solution)/shard_map/ppermute | solution.py:1140
  675.2 39.4 %collective-permute-start.54 = (bf16[2,4,512,1024]{3,2,1,0:T(8,128)(2,1)}, bf16[2,4,512,1024]{3,2,1,0:T(8,128)(2,1)}, u32[]{:S(2)}, u32[]{:S(2)}) collective-permute-start(bf16[2,4,512,1024]{3,2,1,0:T(8,128)(2,1)} %get-tuple-element.836), channel_id=1, source_target_pairs={{0,16},{16,0},{1,17},{17,1},{2,18},{18,2},{3,19},{19,3},{4,20},{20... | collective-permute-start | bytes 25165832 | tf_op jit(solution)/shard_map/ppermute | solution.py:390
  675.2 48.8 %collective-permute-start.53 = (bf16[2,256,1024]{2,1,0:T(8,128)(2,1)S(1)}, bf16[2,256,1024]{2,1,0:T(8,128)(2,1)}, u32[]{:S(2)}, u32[]{:S(2)}) collective-permute-start(bf16[2,256,1024]{2,1,0:T(8,128)(2,1)S(1)} %maximum_select_fusion.3), channel_id=1, source_target_pairs={{0,4},{4,0},{8,12},{12,8},{1,5},{5,1},{9,13},{13,9},{2,6},{6,2},{1... | collective-permute-start | bytes 3145736 | tf_op jit(solution)/shard_map/ppermute | solution.py:1140
  682.8 31.6 %collective-permute-start.55 = (bf16[4,64,1024]{2,1,0:T(8,128)(2,1)S(1)}, bf16[4,64,1024]{2,1,0:T(8,128)(2,1)S(1)}, u32[]{:S(2)}, u32[]{:S(2)}) collective-permute-start(bf16[4,64,1024]{2,1,0:T(8,128)(2,1)S(1)} %constant_dynamic-slice_fusion.23), channel_id=1, source_target_pairs={{0,4},{4,0},{8,12},{12,8},{1,5},{5,1},{9,13},{13,9},{2,6},{6,2},{1... | collective-permute-start | bytes 1572872 | tf_op jit(solution)/shard_map/ppermute | solution.py:1140
  724.1 40.1 %collective-permute-start.57 = (bf16[2,1024,256]{2,1,0:T(8,128)(2,1)}, bf16[2,1024,256]{2,1,0:T(8,128)(2,1)S(1)}, u32[]{:S(2)}, u32[]{:S(2)}) collective-permute-start(bf16[2,1024,256]{2,1,0:T(8,128)(2,1)} %get-tuple-element.852), channel_id=1, source_target_pairs={{0,16},{16,0},{1,17},{17,1},{2,18},{18,2},{3,19},{19,3},{4,20},{20... | collective-permute-start | bytes 3145736 | tf_op jit(solution)/shard_map/ppermute | solution.py:390
  724.1 39.9 %collective-permute-start.56 = (bf16[4,32,1024]{2,1,0:T(8,128)(2,1)S(1)}, bf16[4,32,1024]{2,1,0:T(8,128)(2,1)S(1)}, u32[]{:S(2)}, u32[]{:S(2)}) collective-permute-start(bf16[4,32,1024]{2,1,0:T(8,128)(2,1)S(1)} %constant_dynamic-slice_fusion.22), channel_id=1, source_target_pairs={{0,8},{4,12},{8,0},{12,4},{1,9},{5,13},{9,1},{13,5},{2,10},{6,14},... | collective-permute-start | bytes 786440 | tf_op jit(solution)/shard_map/ppermute | solution.py:1140
  724.9 51.4 %collective-permute-start.58 = (bf16[2,512,1024]{2,1,0:T(8,128)(2,1)}, bf16[2,512,1024]{2,1,0:T(8,128)(2,1)}, u32[]{:S(2)}, u32[]{:S(2)}) collective-permute-start(bf16[2,512,1024]{2,1,0:T(8,128)(2,1)} %bitcast.388), channel_id=1, source_target_pairs={{0,2},{1,3},{2,0},{3,1},{16,17},{17,16},{18,19},{19,18},{4,6},{5,7... | collective-permute-start | bytes 6291464 | tf_op jit(solution)/shard_map/ppermute | solution.py:386
  726.8 49.4 %collective-permute-start.59 = (bf16[2,512,1024]{2,1,0:T(8,128)(2,1)}, bf16[2,512,1024]{2,1,0:T(8,128)(2,1)}, u32[]{:S(2)}, u32[]{:S(2)}) collective-permute-start(bf16[2,512,1024]{2,1,0:T(8,128)(2,1)} %get-tuple-element.865), channel_id=1, source_target_pairs={{0,1},{1,0},{2,3},{3,2},{16,18},{17,19},{18,16},{19,17},{4,5},{5,4... | collective-permute-start | bytes 6291464 | tf_op jit(solution)/shard_map/ppermute | solution.py:386
  780.2 26.4 %collective-permute-start.62 = (bf16[2,512,1024]{2,1,0:T(8,128)(2,1)}, bf16[2,512,1024]{2,1,0:T(8,128)(2,1)}, u32[]{:S(2)}, u32[]{:S(2)}) collective-permute-start(bf16[2,512,1024]{2,1,0:T(8,128)(2,1)} %add.549), channel_id=1, source_target_pairs={{0,1},{1,0},{2,3},{3,2},{16,18},{17,19},{18,16},{19,17},{4,5},{5,4... | collective-permute-start | bytes 6291464 | tf_op jit(solution)/shard_map/ppermute | solution.py:386
  811.3 32.6 %collective-permute-start.69 = (bf16[4,256,1024]{2,1,0:T(8,128)(2,1)}, bf16[4,256,1024]{2,1,0:T(8,128)(2,1)}, u32[]{:S(2)}, u32[]{:S(2)}) collective-permute-start(bf16[4,256,1024]{2,1,0:T(8,128)(2,1)} %get-tuple-element.920), channel_id=1, source_target_pairs={{0,16},{16,0},{1,17},{17,1},{2,18},{18,2},{3,19},{19,3},{4,20},{20... | collective-permute-start | bytes 6291464 | tf_op jit(solution)/shard_map/ppermute | solution.py:390
  811.5 32.4 %collective-permute-start.68 = (bf16[4,128,1024]{2,1,0:T(8,128)(2,1)}, bf16[4,128,1024]{2,1,0:T(8,128)(2,1)}, u32[]{:S(2)}, u32[]{:S(2)}) collective-permute-start(bf16[4,128,1024]{2,1,0:T(8,128)(2,1)} %add.552), channel_id=1, source_target_pairs={{0,3},{1,2},{2,1},{3,0},{16,19},{17,18},{18,17},{19,16},{4,7},{5,6... | collective-permute-start | bytes 3145736 | tf_op jit(solution)/shard_map/ppermute | solution.py:386
  813.1 30.8 %collective-permute-start.67 = (bf16[4,128,1024]{2,1,0:T(8,128)(2,1)S(1)}, bf16[4,128,1024]{2,1,0:T(8,128)(2,1)}, u32[]{:S(2)}, u32[]{:S(2)}) collective-permute-start(bf16[4,128,1024]{2,1,0:T(8,128)(2,1)S(1)} %maximum_select_fusion.4), channel_id=1, source_target_pairs={{0,16},{1,17},{2,18},{3,19},{4,20},{5,21},{6,22},{7,23},{8,24},{9,... | collective-permute-start | bytes 3145736 | tf_op jit(solution)/shard_map/ppermute | solution.py:1325
  816.2 27.7 %collective-permute-start.66 = (bf16[2,256,1024]{2,1,0:T(8,128)(2,1)}, bf16[2,256,1024]{2,1,0:T(8,128)(2,1)}, u32[]{:S(2)}, u32[]{:S(2)}) collective-permute-start(bf16[2,256,1024]{2,1,0:T(8,128)(2,1)} %constant_dynamic-slice_fusion.21), channel_id=1, source_target_pairs={{0,4},{4,0},{8,12},{12,8},{1,5},{5,1},{9,13},{13,9},{2,6},{6,2},{1... | collective-permute-start | bytes 3145736 | tf_op jit(solution)/shard_map/ppermute | solution.py:1140
  855.7 26.4 %collective-permute-start.73 = (bf16[4,256,1024]{2,1,0:T(8,128)(2,1)}, bf16[4,256,1024]{2,1,0:T(8,128)(2,1)}, u32[]{:S(2)}, u32[]{:S(2)}) collective-permute-start(bf16[4,256,1024]{2,1,0:T(8,128)(2,1)} %add.554), channel_id=1, source_target_pairs={{0,1},{1,0},{2,3},{3,2},{16,18},{17,19},{18,16},{19,17},{4,5},{5,4... | collective-permute-start | bytes 6291464 | tf_op jit(solution)/shard_map/ppermute | solution.py:386
  859.2 26.5 %collective-permute-start.72 = (bf16[2,128,1024]{2,1,0:T(8,128)(2,1)}, bf16[2,128,1024]{2,1,0:T(8,128)(2,1)}, u32[]{:S(2)}, u32[]{:S(2)}) collective-permute-start(bf16[2,128,1024]{2,1,0:T(8,128)(2,1)} %constant_dynamic-slice_fusion.20), channel_id=1, source_target_pairs={{0,8},{4,12},{8,0},{12,4},{1,9},{5,13},{9,1},{13,5},{2,10},{6,14},... | collective-permute-start | bytes 1572872 | tf_op jit(solution)/shard_map/ppermute | solution.py:1140
  899.5 25.2 %collective-permute-start.80 = (bf16[4,64,1024]{2,1,0:T(8,128)(2,1)S(1)}, bf16[4,64,1024]{2,1,0:T(8,128)(2,1)S(1)}, u32[]{:S(2)}, u32[]{:S(2)}) collective-permute-start(bf16[4,64,1024]{2,1,0:T(8,128)(2,1)S(1)} %constant_dynamic-slice_fusion.2), channel_id=1, source_target_pairs={{0,4},{4,0},{8,12},{12,8},{1,5},{5,1},{9,13},{13,9},{2,6},{6,2},{1... | collective-permute-start | bytes 1572872 | tf_op jit(solution)/shard_map/ppermute | solution.py:1140
  924.7 30.0 %collective-permute-start.81 = (bf16[2,256,1024]{2,1,0:T(8,128)(2,1)S(1)}, bf16[2,256,1024]{2,1,0:T(8,128)(2,1)S(1)}, u32[]{:S(2)}, u32[]{:S(2)}) collective-permute-start(bf16[2,256,1024]{2,1,0:T(8,128)(2,1)S(1)} %maximum_select_fusion.5), channel_id=1, source_target_pairs={{0,4},{4,0},{8,12},{12,8},{1,5},{5,1},{9,13},{13,9},{2,6},{6,2},{1... | collective-permute-start | bytes 3145736 | tf_op jit(solution)/shard_map/ppermute | solution.py:1140
  924.7 30.0 %collective-permute-start.82 = (f32[2,12,1024]{2,1,0:T(8,128)S(1)}, f32[2,12,1024]{2,1,0:T(8,128)S(1)}, u32[]{:S(2)}, u32[]{:S(2)}) collective-permute-start(f32[2,12,1024]{2,1,0:T(8,128)S(1)} %fusion.58), channel_id=1, source_target_pairs={{0,2},{1,3},{2,0},{3,1},{4,6},{5,7},{6,4},{7,5},{8,10},{9,11},{10,... | collective-permute-start | bytes 294920 | tf_op jit(solution)/shard_map/ppermute | solution.py:1140
  926.8 27.9 %collective-permute-start.83 = (bf16[4,32,1024]{2,1,0:T(8,128)(2,1)S(1)}, bf16[4,32,1024]{2,1,0:T(8,128)(2,1)S(1)}, u32[]{:S(2)}, u32[]{:S(2)}) collective-permute-start(bf16[4,32,1024]{2,1,0:T(8,128)(2,1)S(1)} %constant_dynamic-slice_fusion.1), channel_id=1, source_target_pairs={{0,8},{4,12},{8,0},{12,4},{1,9},{5,13},{9,1},{13,5},{2,10},{6,14},... | collective-permute-start | bytes 786440 | tf_op jit(solution)/shard_map/ppermute | solution.py:1140
  957.0 31.4 %collective-permute-start.84 = (bf16[2,512,1024]{2,1,0:T(8,128)(2,1)}, bf16[2,512,1024]{2,1,0:T(8,128)(2,1)}, u32[]{:S(2)}, u32[]{:S(2)}) collective-permute-start(bf16[2,512,1024]{2,1,0:T(8,128)(2,1)} %maximum_select_fusion.1.lower), channel_id=1, source_target_pairs={{16,0},{17,1},{18,2},{19,3},{20,4},{21,5},{22,6},{23,7},{24,8},{25... | collective-permute-start | bytes 6291464 | tf_op jit(solution)/shard_map/ppermute | solution.py:1325
  958.3 30.1 %collective-permute-start.87 = (bf16[512,1024]{1,0:T(8,128)(2,1)}, bf16[512,1024]{1,0:T(8,128)(2,1)}, u32[]{:S(2)}, u32[]{:S(2)}) collective-permute-start(bf16[512,1024]{1,0:T(8,128)(2,1)} %slice_select_fusion), channel_id=1, source_target_pairs={{3,0},{18,1},{17,2},{0,3},{7,4},{22,5},{21,6},{4,7},{11,8},{26,9},... | collective-permute-start | bytes 3145736 | tf_op jit(solution)/shard_map/ppermute | solution.py:386
  (104 other events, 1059.8 us)

commit v4 on v3

--- a/solution.py
+++ b/solution.py
@@ -686,12 +686,18 @@
     return jnp.concatenate(parts, axis=0) if len(parts) > 1 else parts[0]
 
 
-def project_kernel(a, bias, *refs):
+def project_kernel(first, a, bias, *refs):
+    refs = list(refs)
+    rows = a[...]
+    if first:
+        vectors, normed = refs.pop(0), refs.pop()
+        rows = normed_rows(rows.astype(f32), vectors)
+        normed[...] = rows
     pieces, (q, kv) = refs[:-2], refs[-2:]
     at = 0
     for piece in pieces:
         units = piece.shape[0] // 3
-        result = dot_nt(a[...], piece[...])
+        result = dot_nt(rows, piece[...])
         for n in range(3):
             part = (result[:, n * units : (n + 1) * units] + bias[n, :, at : at + units]).astype(bf16)
             if n == 0:
@@ -701,23 +707,29 @@
         at += units
 
 
-def project_heads(a, pieces, bias):
+def project_heads(a, pieces, bias, vectors=None):
     rows, width = a.shape
     columns = sum(units_of(piece) for piece in pieces)
     tile = rows // 4
+    slim = pl.BlockSpec((tile, width), lambda i: (i, 0))
+    first = vectors is not None
+    extra = [vectors] if first else []
     return pl.pallas_call(
-        project_kernel,
+        partial(project_kernel, first),
         grid=(rows // tile,),
-        in_specs=[pl.BlockSpec((tile, width), lambda i: (i, 0)), fixed(bias.shape)]
+        in_specs=[slim, fixed(bias.shape)]
+        + [fixed(v.shape) for v in extra]
         + [pl.BlockSpec((3 * units_of(piece), width), lambda i: (0, 0), pipeline_mode=pl.Buffered(1)) for piece in pieces],
-        out_specs=[pl.BlockSpec((tile, columns), lambda i: (i, 0)), pl.BlockSpec((2, tile, columns), lambda i: (0, i, 0))],
-        out_shape=[jax.ShapeDtypeStruct((rows, columns), bf16), jax.ShapeDtypeStruct((2, rows, columns), bf16)],
+        out_specs=[pl.BlockSpec((tile, columns), lambda i: (i, 0)), pl.BlockSpec((2, tile, columns), lambda i: (0, i, 0))]
+        + [slim] * len(extra),
+        out_shape=[jax.ShapeDtypeStruct((rows, columns), bf16), jax.ShapeDtypeStruct((2, rows, columns), bf16)]
+        + [jax.ShapeDtypeStruct((rows, width), bf16)] * len(extra),
         cost_estimate=cost(
             flops=6 * rows * width * columns, bytes_accessed=2 * rows * width + 6 * width * columns + 6 * rows * columns, transcendentals=0
         ),
         compiler_params=pltpu.CompilerParams(vmem_limit_bytes=60 * MIB),
         name="project",
-    )(a, bias, *pieces)
+    )(a, bias, *extra, *pieces)
 
 
 def normalize(value):
@@ -731,23 +743,6 @@
 def normed_rows(value, vectors):
     normal, _ = normalize(value)
     return (normal * vectors[1:2] + vectors[2:3]).astype(bf16)
-
-
-def first_norm_kernel(x, vectors, out):
-    out[...] = normed_rows(x[...].astype(f32), vectors)
-
-
-def first_norm(x, vectors):
-    rows, width = x.shape
-    tile = rows // 4
-    return pl.pallas_call(
-        first_norm_kernel,
-        grid=(rows // tile,),
-        in_specs=[pl.BlockSpec((tile, width), lambda i: (i, 0)), fixed(vectors.shape)],
-        out_specs=pl.BlockSpec((tile, width), lambda i: (i, 0)),
-        out_shape=jax.ShapeDtypeStruct((rows, width), bf16),
-        name="first_norm",
-    )(x, vectors)
 
 
 def eight_rows(*rows):
@@ -1032,9 +1027,9 @@
             part = dot_nn(sides[c][...], joined(pieces, 3, c))
             term = part if term is None else term + part
     if not first:
-        term = term + so_far[...]
+        term = term + so_far[...].astype(f32)
     if not last:
-        outs[0][...] = term
+        outs[0][...] = term.astype(bf16)
         return
     tile = term.shape[1]
     total[:, pl.ds(pl.multiple_of(step * tile, tile), tile)] = term
@@ -1063,7 +1058,7 @@
     scratch = [pltpu.VMEM((2, rows, columns), bf16)]
     if norm is None:
         out_specs.append(slim)
-        out_shape.append(jax.ShapeDtypeStruct((rows, width), f32))
+        out_shape.append(jax.ShapeDtypeStruct((rows, width), bf16))
     else:
         value, above, gain = norm
         args += [value, above, jnp.broadcast_to(gain[None], (8, width))]
@@ -1524,10 +1519,16 @@
     kept = [None, None]
     chains.start(gathered_heads(attention_own[0], attention[0], (1, 1)))
     x = chains.launch(x)
-    normed = first_norm(x, eight_rows(jnp.zeros((D,), f32), gains[0][0], shifts[0][0]))
+    normed = None
     for layer in range(2):
         saved = [None] * 3
-        saved[OWN] = attended(layer, OWN, into_heads(layer, OWN, normed))
+        if layer == 0:
+            first_vectors = eight_rows(jnp.zeros((D,), f32), gains[0][0], shifts[0][0])
+            q, kv, normed = project_heads(x, pieces_of(0, OWN), heads_bias(0, OWN), first_vectors)
+            projected, feed_own = lax.optimization_barrier(((q, kv, swap(kv)), feed_own))
+        else:
+            projected = into_heads(layer, OWN, normed)
+        saved[OWN] = attended(layer, OWN, projected)
         (normed, saved[OWN], feed_own), *_ = chains.stepped(
             (normed, saved[OWN], feed_own),
             [] if layer else [lambda: gathered_feed(feed_own[0], feeding[0], (2, 1))],
@@ -1641,11 +1642,14 @@
         lambda: once(row_to(0, grad, (0,)), 1),
         lambda: summed_everywhere(jnp.stack([sums_lower, sums_upper])),
     )
-    grad, lower_heads = chains.step(
-        grad, lambda: summed_heads(DOWN, own[0], own_sum, near_sum, far_sum)
-    )
-    grad, three = chains.step(grad, lambda: once(row_to(0, grad, (3,)), 2))
-    grad, one, two = chains.step(grad, lambda: once(row_to(0, grad, (1,)), 1), lambda: once(row_to(0, grad, (2,)), 1))
+    grad, lower_heads, three, one = chains.step(
+        grad,
+        lambda: summed_heads(DOWN, own[0], own_sum, near_sum, far_sum),
+        lambda: once(row_to(0, grad, (3,)), 1),
+        lambda: once(row_to(0, grad, (1,)), 1),
+    )
+    grad, two = chains.step(grad, lambda: once(row_to(0, grad, (2,)), 1))
+    grad = chains.step(grad)
     first_rows = [zero, one, two, three]
 
     def feed_outputs():

time: 1040 us -> 1020 us (0.981)
    pallas_call x7 -> x6, Pallas kernels: 41.2 us -> 37.9 us  [project_heads(): pl.pallas_call(partial(project_kernel, first), grid=(rows // tile,), in_s...]
  transfers between devices with their start and end apart: 93 -> 93, of which waited for: 33 -> 32; matrix products, arithmetic and copies ran while one was open for 13% -> 13% of each run, Pallas kernels for 55% -> 55%
where the time goes in v4:
time: 1020 us; the launch traced here: 1010 us
  Pallas kernels  572 us (56%)
  waiting for transfers between devices  155 us (15%)
  starting transfers between devices  108 us (11%)
  other arithmetic  105 us (10%)
  local copies, waits for them, and re-layouts  68 us (7%)
    pallas_call x6, Pallas kernels, attend_back(): pl.pallas_call(partial(attend_back_kernel, seg, starts), grid_spec=pltpu....  157 us
    pallas_call x2, Pallas kernels, feed_back(): pl.pallas_call(feed_back_kernel, grid_spec=pltpu.PrefetchScalarGridSpec(n...  99 us
    pallas_call x6, Pallas kernels, attend(): pl.pallas_call(partial(attend_kernel, seg), grid_spec=pltpu.PrefetchScala...  83.1 us
    ppermute x21, waiting for transfers between devices, exchanged(): return lax.ppermute(value, axis, [(n, n ^ distance) for n in range(count)])  81 us
    pallas_call x6, Pallas kernels, project_back(): pl.pallas_call(partial(project_back_kernel, groups, so_far is None, norm...  77.6 us
    ppermute x34, starting transfers between devices, hop(): return lax.ppermute(value, ST, pairs)  63 us
    pallas_call x2, Pallas kernels, feed(): pl.pallas_call(partial(feed_kernel, (len(heads), len(heads_pieces))), gri...  55.3 us
    ppermute x34, waiting for transfers between devices, hop(): return lax.ppermute(value, ST, pairs)  53.3 us
  transfers between devices with their start and end apart: 93, of which 32 were waited for; matrix products, arithmetic and copies ran while one was open for 13% of the time, Pallas kernels for 55%

profile of v4, /device:TPU:0, one launch (start us, length us, event | category | flops | bytes accessed | tf_op | source)
XLA Modules:
  0.0 1011.2 jit_solution(10851374311448023703)
XLA Ops:
  9.8 5.3 collective-permute-start.3
  33.8 5.3 collective-permute-done.2
  50.7 6.6 project.6
  59.4 5.8 broadcast_select_fusion
  66.3 11.0 %attend.6 = (bf16[1024,256]{1,0:T(8,128)(2,1)}, bf16[1024,256]{1,0:T(8,128)(2,1)}) custom-call(s32[3]{0:T(128)} %pad_add_fusion.1.meta, bf16[1024,256]{1,0:T(8,128)(2,1)} %get-tuple-element.927.q, bf16[2,1024,256]{2,1,0:T(8,128)(2,1)} %get-tuple-element.928.kv, bf16[2,1024,256]{2,1,0:T(8,128)(2,1)} %copy-done.18, bf16[2048,128]{1,0:T(8,128)(2,1)} %pad_maximum_fusion.6.kcol, ...), custom_call_target="tpu_custom_call" | custom-call | flops 83886080 | bytes 57344 | tf_op jit(solution)/shard_map/attend/pallas_call | solution.py:516
  83.2 7.2 project.7
  96.1 19.2 %attend.7 = (bf16[1024,512]{1,0:T(8,128)(2,1)}, bf16[1024,512]{1,0:T(8,128)(2,1)}) custom-call(s32[5]{0:T(128)} %pad_add_fusion.2.meta, bf16[1024,512]{1,0:T(8,128)(2,1)} %get-tuple-element.861.q, bf16[2,1024,512]{2,1,0:T(8,128)(2,1)} %get-tuple-element.862.kv, bf16[2,1024,512]{2,1,0:T(8,128)(2,1)} %copy-done.12, bf16[2048,128]{1,0:T(8,128)(2,1)} %pad_maximum_fusion.6.kcol, ...), custom_call_target="tpu_custom_call" | custom-call | flops 167772160 | bytes 114688 | tf_op jit(solution)/shard_map/attend/pallas_call | solution.py:516
  121.5 5.7 project.8
  131.0 11.0 %attend.8 = (bf16[1024,256]{1,0:T(8,128)(2,1)}, bf16[1024,256]{1,0:T(8,128)(2,1)}) custom-call(s32[3]{0:T(128)} %pad_add_fusion.3.meta, bf16[1024,256]{1,0:T(8,128)(2,1)} %get-tuple-element.845.q, bf16[2,1024,256]{2,1,0:T(8,128)(2,1)} %get-tuple-element.846.kv, bf16[2,1024,256]{2,1,0:T(8,128)(2,1)} %copy-done.19, bf16[2048,128]{1,0:T(8,128)(2,1)} %pad_maximum_fusion.6.kcol, ...), custom_call_target="tpu_custom_call" | custom-call | flops 83886080 | bytes 57344 | tf_op jit(solution)/shard_map/attend/pallas_call | solution.py:516
  142.0 8.7 collective-permute-done.13.refs_12_.near
  158.4 27.9 %feed.2 = (bf16[4,1024,768]{2,1,0:T(8,128)(2,1)}, bf16[4,1024,768]{2,1,0:T(8,128)(2,1)}, f32[1024,1024]{1,0:T(8,128)}, bf16[1024,1024]{1,0:T(8,128)(2,1)}, f32[1024,1024]{1,0:T(8,128)}) custom-call(s32[1]{0:T(128)} %bitcast.meta, bf16[1024,256]{1,0:T(8,128)(2,1)} %get-tuple-element.606.refs_0_.o.refs_3_, ...), custom_call_target="tpu_custom_call" | custom-call | flops 234881024 | bytes 655360 | tf_op jit(solution)/shard_map/feed/pallas_call | solution.py:820
  190.9 12.4 %feed_last.2 = (bf16[4,1024,256]{2,1,0:T(8,128)(2,1)}, bf16[4,1024,256]{2,1,0:T(8,128)(2,1)}, bf16[1024,1024]{1,0:T(8,128)(2,1)}, bf16[1024,1024]{1,0:T(8,128)(2,1)}) custom-call(bf16[1024,1024]{1,0:T(8,128)(2,1)} %get-tuple-element.609.middle, f32[1024,1024]{1,0:T(8,128)} %get-tuple-element.617.so_far, f32[8,1024]{1,0:T(8,128)} %get-tuple-element.1251.vectors, ...), custom_call_target="tpu_custom_call" | custom-call | flops 67108864 | bytes 294912 | tf_op jit(solution)/shard_map/feed_last/pallas_call | solution.py:877
  203.3 5.4 project.9
  212.5 11.3 %attend.9 = (bf16[1024,256]{1,0:T(8,128)(2,1)}, bf16[1024,256]{1,0:T(8,128)(2,1)}) custom-call(s32[3]{0:T(128)} %pad_add_fusion.1.meta, bf16[1024,256]{1,0:T(8,128)(2,1)} %get-tuple-element.787.q, bf16[2,1024,256]{2,1,0:T(8,128)(2,1)} %get-tuple-element.788.kv, bf16[2,1024,256]{2,1,0:T(8,128)(2,1)} %copy-done.20, bf16[2048,128]{1,0:T(8,128)(2,1)} %pad_maximum_fusion.6.kcol, ...), custom_call_target="tpu_custom_call" | custom-call | flops 83886080 | bytes 57344 | tf_op jit(solution)/shard_map/attend/pallas_call | solution.py:516
  229.7 7.2 project.10
  242.6 19.0 %attend.10 = (bf16[1024,512]{1,0:T(8,128)(2,1)}, bf16[1024,512]{1,0:T(8,128)(2,1)}) custom-call(s32[5]{0:T(128)} %pad_add_fusion.2.meta, bf16[1024,512]{1,0:T(8,128)(2,1)} %get-tuple-element.734.q, bf16[2,1024,512]{2,1,0:T(8,128)(2,1)} %get-tuple-element.735.kv, bf16[2,1024,512]{2,1,0:T(8,128)(2,1)} %copy-done.13, bf16[2048,128]{1,0:T(8,128)(2,1)} %pad_maximum_fusion.6.kcol, ...), custom_call_target="tpu_custom_call" | custom-call | flops 167772160 | bytes 114688 | tf_op jit(solution)/shard_map/attend/pallas_call | solution.py:516
  268.5 5.7 project.11
  278.0 11.5 %attend.11 = (bf16[1024,256]{1,0:T(8,128)(2,1)}, bf16[1024,256]{1,0:T(8,128)(2,1)}) custom-call(s32[3]{0:T(128)} %pad_add_fusion.3.meta, bf16[1024,256]{1,0:T(8,128)(2,1)} %get-tuple-element.720.q, bf16[2,1024,256]{2,1,0:T(8,128)(2,1)} %get-tuple-element.721.kv, bf16[2,1024,256]{2,1,0:T(8,128)(2,1)} %copy-done.21, bf16[2048,128]{1,0:T(8,128)(2,1)} %pad_maximum_fusion.6.kcol, ...), custom_call_target="tpu_custom_call" | custom-call | flops 83886080 | bytes 57344 | tf_op jit(solution)/shard_map/attend/pallas_call | solution.py:516
  289.5 7.7 collective-permute-done.24.refs_12_.near
  305.0 27.4 %feed.3 = (bf16[4,1024,768]{2,1,0:T(8,128)(2,1)}, bf16[4,1024,768]{2,1,0:T(8,128)(2,1)}, f32[1024,1024]{1,0:T(8,128)}, bf16[1024,1024]{1,0:T(8,128)(2,1)}, f32[1024,1024]{1,0:T(8,128)}) custom-call(s32[1]{0:T(128)} %bitcast.meta, bf16[1024,256]{1,0:T(8,128)(2,1)} %get-tuple-element.681.refs_0_.o.refs_3_, ...), custom_call_target="tpu_custom_call" | custom-call | flops 234881024 | bytes 655360 | tf_op jit(solution)/shard_map/feed/pallas_call | solution.py:820
  344.1 12.4 %feed_last.3 = (bf16[4,1024,256]{2,1,0:T(8,128)(2,1)}, bf16[4,1024,256]{2,1,0:T(8,128)(2,1)}, bf16[1024,1024]{1,0:T(8,128)(2,1)}, bf16[1024,1024]{1,0:T(8,128)(2,1)}) custom-call(bf16[1024,1024]{1,0:T(8,128)(2,1)} %get-tuple-element.697.middle, f32[1024,1024]{1,0:T(8,128)} %get-tuple-element.698.so_far, f32[8,1024]{1,0:T(8,128)} %get-tuple-element.1251.vectors, ...), custom_call_target="tpu_custom_call" | custom-call | flops 67108864 | bytes 294912 | tf_op jit(solution)/shard_map/feed_last/pallas_call | solution.py:877
  356.5 10.9 %collective-permute-done.30 = bf16[512,1024]{1,0:T(8,128)(2,1)} collective-permute-done((bf16[512,1024]{1,0:T(8,128)(2,1)}, bf16[512,1024]{1,0:T(8,128)(2,1)}, u32[]{:S(2)}, u32[]{:S(2)}) %collective-permute-start.30) | collective-permute-done | bytes 1048608 | tf_op jit(solution)/shard_map/ppermute | solution.py:386
  381.7 49.3 %feed_back.2 = (bf16[2,4,512,1024]{3,2,1,0:T(8,128)(2,1)}, bf16[2,4,512,1024]{3,2,1,0:T(8,128)(2,1)}, f32[4,8,1024]{2,1,0:T(8,128)}, bf16[1024,1024]{1,0:T(8,128)(2,1)}, f32[8,1024]{1,0:T(8,128)}) custom-call(s32[1]{0:T(128)} %bitcast.meta, bf16[1024,1024]{1,0:T(8,128)(2,1)} %pad_maximum_fusion.3.above, bf16[1024,1024]{1,0:T(8,128)(2,1)} %get-tuple-element.697.middle, ...), custom_call_target="tpu_custom_call" | custom-call | flops 536870912 | bytes 1802240 | tf_op jit(solution)/shard_map/feed_back/pallas_call | solution.py:959
  432.9 5.9 collective-permute-start.36
  438.8 20.7 %attend_back.6 = (bf16[1024,256]{1,0:T(8,128)(2,1)}, bf16[2,1024,256]{2,1,0:T(8,128)(2,1)}, bf16[2,1024,256]{2,1,0:T(8,128)(2,1)}) custom-call(s32[3]{0:T(128)} %pad_add_fusion.3.meta, bf16[1024,256]{1,0:T(8,128)(2,1)} %get-tuple-element.720.q, bf16[2,1024,256]{2,1,0:T(8,128)(2,1)} %get-tuple-element.721.kv, bf16[2,1024,256]{2,1,0:T(8,128)(2,1)} %copy-done.21, ...), custom_call_target="tpu_custom_call" | custom-call | flops 226492416 | bytes 106496 | tf_op jit(solution)/shard_map/attend_back/pallas_call | solution.py:631
  459.6 9.5 meet.2
  470.9 37.4 %attend_back.7 = (bf16[1024,512]{1,0:T(8,128)(2,1)}, bf16[2,1024,512]{2,1,0:T(8,128)(2,1)}, bf16[2,1024,512]{2,1,0:T(8,128)(2,1)}) custom-call(s32[5]{0:T(128)} %pad_add_fusion.2.meta, bf16[1024,512]{1,0:T(8,128)(2,1)} %get-tuple-element.734.q, bf16[2,1024,512]{2,1,0:T(8,128)(2,1)} %get-tuple-element.735.kv, bf16[2,1024,512]{2,1,0:T(8,128)(2,1)} %copy-done.13, ...), custom_call_target="tpu_custom_call" | custom-call | flops 452984832 | bytes 212992 | tf_op jit(solution)/shard_map/attend_back/pallas_call | solution.py:631
  509.4 9.2 project_back.6
  524.4 14.5 %project_back.7 = (bf16[4,256,1024]{2,1,0:T(8,128)(2,1)}, bf16[4,256,1024]{2,1,0:T(8,128)(2,1)}, f32[8,512]{1,0:T(8,128)}, bf16[1024,1024]{1,0:T(8,128)(2,1)}) custom-call(s32[1]{0:T(128)} %bitcast.meta, bf16[1024,512]{1,0:T(8,128)(2,1)} %get-tuple-element.762.refs_0_, bf16[2,1024,512]{2,1,0:T(8,128)(2,1)} %get-tuple-element.763.refs_1_, ...), custom_call_target="tpu_custom_call" | custom-call | flops 117440512 | bytes 409600 | tf_op jit(solution)/shard_map/project_back/pallas_call | solution.py:1069
  541.7 7.7 collective-permute-done.41
  556.7 20.3 %attend_back.8 = (bf16[1024,256]{1,0:T(8,128)(2,1)}, bf16[2,1024,256]{2,1,0:T(8,128)(2,1)}, bf16[2,1024,256]{2,1,0:T(8,128)(2,1)}) custom-call(s32[3]{0:T(128)} %pad_add_fusion.1.meta, bf16[1024,256]{1,0:T(8,128)(2,1)} %get-tuple-element.787.q, bf16[2,1024,256]{2,1,0:T(8,128)(2,1)} %get-tuple-element.788.kv, bf16[2,1024,256]{2,1,0:T(8,128)(2,1)} %copy-done.20, ...), custom_call_target="tpu_custom_call" | custom-call | flops 226492416 | bytes 106496 | tf_op jit(solution)/shard_map/attend_back/pallas_call | solution.py:631
  589.5 15.0 %project_back.8 = (bf16[4,128,1024]{2,1,0:T(8,128)(2,1)}, bf16[4,128,1024]{2,1,0:T(8,128)(2,1)}, f32[8,256]{1,0:T(8,128)}, bf16[1024,1024]{1,0:T(8,128)(2,1)}, f32[8,1024]{1,0:T(8,128)}) custom-call(s32[1]{0:T(128)} %bitcast.meta, bf16[1024,256]{1,0:T(8,128)(2,1)} %get-tuple-element.804.refs_0_, bf16[2,1024,256]{2,1,0:T(8,128)(2,1)} %get-tuple-element.805.refs_1_, ...), custom_call_target="tpu_custom_call" | custom-call | flops 58720256 | bytes 303104 | tf_op jit(solution)/shard_map/project_back/pallas_call | solution.py:1069
  604.5 8.2 collective-permute-done.48
  617.0 49.7 %feed_back.3 = (bf16[2,4,512,1024]{3,2,1,0:T(8,128)(2,1)}, bf16[2,4,512,1024]{3,2,1,0:T(8,128)(2,1)}, f32[4,8,1024]{2,1,0:T(8,128)}, bf16[1024,1024]{1,0:T(8,128)(2,1)}, f32[8,1024]{1,0:T(8,128)}) custom-call(s32[1]{0:T(128)} %bitcast.meta, bf16[1024,1024]{1,0:T(8,128)(2,1)} %get-tuple-element.824.above, bf16[1024,1024]{1,0:T(8,128)(2,1)} %get-tuple-element.609.middle, ...), custom_call_target="tpu_custom_call" | custom-call | flops 536870912 | bytes 1802240 | tf_op jit(solution)/shard_map/feed_back/pallas_call | solution.py:959
  676.7 20.7 %attend_back.9 = (bf16[1024,256]{1,0:T(8,128)(2,1)}, bf16[2,1024,256]{2,1,0:T(8,128)(2,1)}, bf16[2,1024,256]{2,1,0:T(8,128)(2,1)}) custom-call(s32[3]{0:T(128)} %pad_add_fusion.3.meta, bf16[1024,256]{1,0:T(8,128)(2,1)} %get-tuple-element.845.q, bf16[2,1024,256]{2,1,0:T(8,128)(2,1)} %get-tuple-element.846.kv, bf16[2,1024,256]{2,1,0:T(8,128)(2,1)} %copy-done.19, ...), custom_call_target="tpu_custom_call" | custom-call | flops 226492416 | bytes 106496 | tf_op jit(solution)/shard_map/attend_back/pallas_call | solution.py:631
  697.5 10.6 %collective-permute-done.55 = bf16[4,64,1024]{2,1,0:T(8,128)(2,1)S(1)} collective-permute-done((bf16[4,64,1024]{2,1,0:T(8,128)(2,1)S(1)}, bf16[4,64,1024]{2,1,0:T(8,128)(2,1)S(1)}, u32[]{:S(2)}, u32[]{:S(2)}) %collective-permute-start.55) | collective-permute-done | bytes 524320 | tf_op jit(solution)/shard_map/ppermute | solution.py:1135
  708.3 9.5 meet.3
  720.6 37.2 %attend_back.10 = (bf16[1024,512]{1,0:T(8,128)(2,1)}, bf16[2,1024,512]{2,1,0:T(8,128)(2,1)}, bf16[2,1024,512]{2,1,0:T(8,128)(2,1)}) custom-call(s32[5]{0:T(128)} %pad_add_fusion.2.meta, bf16[1024,512]{1,0:T(8,128)(2,1)} %get-tuple-element.861.q, bf16[2,1024,512]{2,1,0:T(8,128)(2,1)} %get-tuple-element.862.kv, bf16[2,1024,512]{2,1,0:T(8,128)(2,1)} %copy-done.12, ...), custom_call_target="tpu_custom_call" | custom-call | flops 452984832 | bytes 212992 | tf_op jit(solution)/shard_map/attend_back/pallas_call | solution.py:631
  760.3 9.2 project_back.9
  778.0 14.6 %project_back.10 = (bf16[4,256,1024]{2,1,0:T(8,128)(2,1)}, bf16[4,256,1024]{2,1,0:T(8,128)(2,1)}, f32[8,512]{1,0:T(8,128)}, bf16[1024,1024]{1,0:T(8,128)(2,1)}) custom-call(s32[1]{0:T(128)} %bitcast.meta, bf16[1024,512]{1,0:T(8,128)(2,1)} %get-tuple-element.897.refs_0_, bf16[2,1024,512]{2,1,0:T(8,128)(2,1)} %get-tuple-element.898.refs_1_, ...), custom_call_target="tpu_custom_call" | custom-call | flops 117440512 | bytes 409600 | tf_op jit(solution)/shard_map/project_back/pallas_call | solution.py:1069
  816.8 20.5 %attend_back.11 = (bf16[1024,256]{1,0:T(8,128)(2,1)}, bf16[2,1024,256]{2,1,0:T(8,128)(2,1)}, bf16[2,1024,256]{2,1,0:T(8,128)(2,1)}) custom-call(s32[3]{0:T(128)} %pad_add_fusion.1.meta, bf16[1024,256]{1,0:T(8,128)(2,1)} %get-tuple-element.927.q, bf16[2,1024,256]{2,1,0:T(8,128)(2,1)} %get-tuple-element.928.kv, bf16[2,1024,256]{2,1,0:T(8,128)(2,1)} %copy-done.18, ...), custom_call_target="tpu_custom_call" | custom-call | flops 226492416 | bytes 106496 | tf_op jit(solution)/shard_map/attend_back/pallas_call | solution.py:631
  854.6 15.0 %project_back.11 = (bf16[4,128,1024]{2,1,0:T(8,128)(2,1)}, bf16[4,128,1024]{2,1,0:T(8,128)(2,1)}, f32[8,256]{1,0:T(8,128)}, bf16[1024,1024]{1,0:T(8,128)(2,1)}, f32[8,1024]{1,0:T(8,128)}) custom-call(s32[1]{0:T(128)} %bitcast.meta, bf16[1024,256]{1,0:T(8,128)(2,1)} %get-tuple-element.948.refs_0_, bf16[2,1024,256]{2,1,0:T(8,128)(2,1)} %get-tuple-element.949.refs_1_, ...), custom_call_target="tpu_custom_call" | custom-call | flops 58720256 | bytes 303104 | tf_op jit(solution)/shard_map/project_back/pallas_call | solution.py:1069
  900.2 12.9 %collective-permute-done.78 = bf16[2,128,1024]{2,1,0:T(8,128)(2,1)} collective-permute-done((bf16[2,128,1024]{2,1,0:T(8,128)(2,1)}, bf16[2,128,1024]{2,1,0:T(8,128)(2,1)}, u32[]{:S(2)}, u32[]{:S(2)}) %collective-permute-start.78) | collective-permute-done | bytes 524320 | tf_op jit(solution)/shard_map/ppermute | solution.py:1135
  915.0 9.4 collective-permute-done.79
  931.2 25.2 %collective-permute-done.83 = bf16[2,256,1024]{2,1,0:T(8,128)(2,1)S(1)} collective-permute-done((bf16[2,256,1024]{2,1,0:T(8,128)(2,1)S(1)}, bf16[2,256,1024]{2,1,0:T(8,128)(2,1)S(1)}, u32[]{:S(2)}, u32[]{:S(2)}) %collective-permute-start.83) | collective-permute-done | bytes 1048608 | tf_op jit(solution)/shard_map/ppermute | solution.py:1135
  967.4 9.7 ends_rows.1
  983.9 8.4 feed_out.1
  992.3 7.5 collective-permute-done.91
  (595 shorter events, 305.3 us)
Async XLA Ops:
  5.5 40.1 %collective-permute-start.4 = (bf16[1056,1024]{1,0:T(8,128)(2,1)}, bf16[1056,1024]{1,0:T(8,128)(2,1)}, u32[]{:S(2)}, u32[]{:S(2)}) collective-permute-start(bf16[1056,1024]{1,0:T(8,128)(2,1)} %pad_maximum_fusion.1), channel_id=1, source_target_pairs={{0,16},{16,0},{1,17},{17,1},{2,18},{18,2},{3,19},{19,3},{4,20},{20... | collective-permute-start | bytes 6488072 | tf_op jit(solution)/shard_map/ppermute | solution.py:390
  47.9 29.4 %collective-permute-start.7 = (bf16[1056,1024]{1,0:T(8,128)(2,1)S(1)}, bf16[1056,1024]{1,0:T(8,128)(2,1)}, u32[]{:S(2)}, u32[]{:S(2)}) collective-permute-start(bf16[1056,1024]{1,0:T(8,128)(2,1)S(1)} %get-tuple-element.686.refs_1_.refs_3_.refs_0_.refs_6_), channel_id=1, source_target_pairs={{0,1},{1,0},{2,3},{3,2},{16,18},{17,19},{18,16},{19,17},{4,5},{5,4... | collective-permute-start | bytes 6488072 | tf_op jit(solution)/shard_map/ppermute | solution.py:386
  90.7 27.0 %collective-permute-start.10 = (bf16[544,1024]{1,0:T(8,128)(2,1)}, bf16[544,1024]{1,0:T(8,128)(2,1)S(1)}, u32[]{:S(2)}, u32[]{:S(2)}) collective-permute-start(bf16[544,1024]{1,0:T(8,128)(2,1)} %pad_maximum_fusion.4), channel_id=1, source_target_pairs={{0,2},{1,3},{2,0},{3,1},{16,17},{17,16},{18,19},{19,18},{4,6},{5,7... | collective-permute-start | bytes 3342344 | tf_op jit(solution)/shard_map/ppermute | solution.py:386
  92.5 58.2 %collective-permute-start.13 = (bf16[2,1024,1024]{2,1,0:T(8,128)(2,1)}, bf16[2,1024,1024]{2,1,0:T(8,128)(2,1)}, u32[]{:S(2)}, u32[]{:S(2)}) collective-permute-start(bf16[2,1024,1024]{2,1,0:T(8,128)(2,1)} %get-tuple-element.632), channel_id=1, source_target_pairs={{0,1},{1,0},{2,3},{3,2},{16,18},{17,19},{18,16},{19,17},{4,5},{5,4... | collective-permute-start | bytes 12582920 | tf_op jit(solution)/shard_map/ppermute | solution.py:386
  154.4 32.0 %collective-permute-start.15 = (bf16[2,512,1024]{2,1,0:T(8,128)(2,1)}, bf16[2,512,1024]{2,1,0:T(8,128)(2,1)}, u32[]{:S(2)}, u32[]{:S(2)}) collective-permute-start(bf16[2,512,1024]{2,1,0:T(8,128)(2,1)} %constant_dynamic-slice_fusion.29), channel_id=1, source_target_pairs={{0,2},{1,3},{2,0},{3,1},{16,17},{17,16},{18,19},{19,18},{4,6},{5,7... | collective-permute-start | bytes 6291464 | tf_op jit(solution)/shard_map/ppermute | solution.py:386
  186.8 37.0 %collective-permute-start.18 = (bf16[1056,1024]{1,0:T(8,128)(2,1)S(1)}, bf16[1056,1024]{1,0:T(8,128)(2,1)}, u32[]{:S(2)}, u32[]{:S(2)}) collective-permute-start(bf16[1056,1024]{1,0:T(8,128)(2,1)S(1)} %copy-done.2), channel_id=1, source_target_pairs={{0,1},{1,0},{2,3},{3,2},{16,18},{17,19},{18,16},{19,17},{4,5},{5,4... | collective-permute-start | bytes 6488072 | tf_op jit(solution)/shard_map/ppermute | solution.py:386
  237.3 27.5 %collective-permute-start.21 = (bf16[544,1024]{1,0:T(8,128)(2,1)}, bf16[544,1024]{1,0:T(8,128)(2,1)S(1)}, u32[]{:S(2)}, u32[]{:S(2)}) collective-permute-start(bf16[544,1024]{1,0:T(8,128)(2,1)} %pad_maximum_fusion.5), channel_id=1, source_target_pairs={{0,2},{1,3},{2,0},{3,1},{16,17},{17,16},{18,19},{19,18},{4,6},{5,7... | collective-permute-start | bytes 3342344 | tf_op jit(solution)/shard_map/ppermute | solution.py:386
  238.8 58.4 %collective-permute-start.24 = (bf16[2,1024,1024]{2,1,0:T(8,128)(2,1)}, bf16[2,1024,1024]{2,1,0:T(8,128)(2,1)}, u32[]{:S(2)}, u32[]{:S(2)}) collective-permute-start(bf16[2,1024,1024]{2,1,0:T(8,128)(2,1)} %get-tuple-element.664), channel_id=1, source_target_pairs={{0,1},{1,0},{2,3},{3,2},{16,18},{17,19},{18,16},{19,17},{4,5},{5,4... | collective-permute-start | bytes 12582920 | tf_op jit(solution)/shard_map/ppermute | solution.py:386
  300.9 31.5 %collective-permute-start.26 = (bf16[2,512,1024]{2,1,0:T(8,128)(2,1)}, bf16[2,512,1024]{2,1,0:T(8,128)(2,1)S(1)}, u32[]{:S(2)}, u32[]{:S(2)}) collective-permute-start(bf16[2,512,1024]{2,1,0:T(8,128)(2,1)} %constant_dynamic-slice_fusion.27), channel_id=1, source_target_pairs={{0,2},{1,3},{2,0},{3,1},{16,17},{17,16},{18,19},{19,18},{4,6},{5,7... | collective-permute-start | bytes 6291464 | tf_op jit(solution)/shard_map/ppermute | solution.py:386
  370.2 60.8 %collective-permute-start.32 = (bf16[512,1024]{1,0:T(8,128)(2,1)S(1)}, bf16[512,1024]{1,0:T(8,128)(2,1)}, u32[]{:S(2)}, u32[]{:S(2)}) collective-permute-start(bf16[512,1024]{1,0:T(8,128)(2,1)S(1)} %get-tuple-element.715), channel_id=1, source_target_pairs={{0,16},{3,19},{4,20},{7,23},{8,24},{11,27},{12,28},{15,31}} | collective-permute-start | bytes 3145736 | tf_op jit(solution)/shard_map/ppermute | solution.py:386
  375.3 55.6 %collective-permute-start.33 = (bf16[512,1024]{1,0:T(8,128)(2,1)}, bf16[512,1024]{1,0:T(8,128)(2,1)}, u32[]{:S(2)}, u32[]{:S(2)}) collective-permute-start(bf16[512,1024]{1,0:T(8,128)(2,1)} %get-tuple-element.716), channel_id=1, source_target_pairs={{1,16},{16,17},{19,18},{2,19},{5,20},{20,21},{23,22},{6,23},{9,24}... | collective-permute-start | bytes 3145736 | tf_op jit(solution)/shard_map/ppermute | solution.py:386
  431.0 28.6 %collective-permute-start.34 = (bf16[2,4,512,1024]{3,2,1,0:T(8,128)(2,1)}, bf16[2,4,512,1024]{3,2,1,0:T(8,128)(2,1)}, u32[]{:S(2)}, u32[]{:S(2)}) collective-permute-start(bf16[2,4,512,1024]{3,2,1,0:T(8,128)(2,1)} %get-tuple-element.725), channel_id=1, source_target_pairs={{0,16},{16,0},{1,17},{17,1},{2,18},{18,2},{3,19},{19,3},{4,20},{20... | collective-permute-start | bytes 25165832 | tf_op jit(solution)/shard_map/ppermute | solution.py:390
  432.2 36.9 %collective-permute-start.35 = (bf16[512,1024]{1,0:T(8,128)(2,1)}, bf16[512,1024]{1,0:T(8,128)(2,1)S(1)}, u32[]{:S(2)}, u32[]{:S(2)}) collective-permute-start(bf16[512,1024]{1,0:T(8,128)(2,1)} %get-tuple-element.726), channel_id=1, source_target_pairs={{2,16},{19,17},{16,18},{1,19},{6,20},{23,21},{20,22},{5,23},{10,24... | collective-permute-start | bytes 3145736 | tf_op jit(solution)/shard_map/ppermute | solution.py:386
  432.9 36.2 %collective-permute-start.36 = (bf16[512,1024]{1,0:T(8,128)(2,1)S(1)}, bf16[512,1024]{1,0:T(8,128)(2,1)S(1)}, u32[]{:S(2)}, u32[]{:S(2)}) collective-permute-start(bf16[512,1024]{1,0:T(8,128)(2,1)S(1)} %get-tuple-element.727), channel_id=1, source_target_pairs={{3,16},{18,17},{17,18},{0,19},{7,20},{22,21},{21,22},{4,23},{11,24... | collective-permute-start | bytes 3145736 | tf_op jit(solution)/shard_map/ppermute | solution.py:386
  469.1 39.3 %collective-permute-start.37 = (bf16[2,1024,256]{2,1,0:T(8,128)(2,1)}, bf16[2,1024,256]{2,1,0:T(8,128)(2,1)S(1)}, u32[]{:S(2)}, u32[]{:S(2)}) collective-permute-start(bf16[2,1024,256]{2,1,0:T(8,128)(2,1)} %get-tuple-element.739), channel_id=1, source_target_pairs={{0,16},{16,0},{1,17},{17,1},{2,18},{18,2},{3,19},{19,3},{4,20},{20... | collective-permute-start | bytes 3145736 | tf_op jit(solution)/shard_map/ppermute | solution.py:390
  469.2 49.4 %collective-permute-start.38 = (bf16[2,512,1024]{2,1,0:T(8,128)(2,1)}, bf16[2,512,1024]{2,1,0:T(8,128)(2,1)}, u32[]{:S(2)}, u32[]{:S(2)}) collective-permute-start(bf16[2,512,1024]{2,1,0:T(8,128)(2,1)} %bitcast.389), channel_id=1, source_target_pairs={{0,2},{1,3},{2,0},{3,1},{16,17},{17,16},{18,19},{19,18},{4,6},{5,7... | collective-permute-start | bytes 6291464 | tf_op jit(solution)/shard_map/ppermute | solution.py:386
  469.2 49.3 %collective-permute-start.39 = (bf16[2,512,1024]{2,1,0:T(8,128)(2,1)}, bf16[2,512,1024]{2,1,0:T(8,128)(2,1)}, u32[]{:S(2)}, u32[]{:S(2)}) collective-permute-start(bf16[2,512,1024]{2,1,0:T(8,128)(2,1)} %get-tuple-element.750), channel_id=1, source_target_pairs={{0,1},{1,0},{2,3},{3,2},{16,18},{17,19},{18,16},{19,17},{4,5},{5,4... | collective-permute-start | bytes 6291464 | tf_op jit(solution)/shard_map/ppermute | solution.py:386
  523.1 26.4 %collective-permute-start.41 = (bf16[2,512,1024]{2,1,0:T(8,128)(2,1)}, bf16[2,512,1024]{2,1,0:T(8,128)(2,1)}, u32[]{:S(2)}, u32[]{:S(2)}) collective-permute-start(bf16[2,512,1024]{2,1,0:T(8,128)(2,1)} %add.528), channel_id=1, source_target_pairs={{0,1},{1,0},{2,3},{3,2},{16,18},{17,19},{18,16},{19,17},{4,5},{5,4... | collective-permute-start | bytes 6291464 | tf_op jit(solution)/shard_map/ppermute | solution.py:386
  523.5 25.9 %collective-permute-start.42 = (bf16[2,512,1024]{2,1,0:T(8,128)(2,1)}, bf16[2,512,1024]{2,1,0:T(8,128)(2,1)}, u32[]{:S(2)}, u32[]{:S(2)}) collective-permute-start(bf16[2,512,1024]{2,1,0:T(8,128)(2,1)} %collective-permute-done.39), channel_id=1, source_target_pairs={{0,16},{16,0},{1,17},{17,1},{2,18},{18,2},{3,19},{19,3},{4,20},{20... | collective-permute-start | bytes 6291464 | tf_op jit(solution)/shard_map/ppermute | solution.py:390
  553.2 28.4 %collective-permute-start.46 = (bf16[4,256,1024]{2,1,0:T(8,128)(2,1)}, bf16[4,256,1024]{2,1,0:T(8,128)(2,1)}, u32[]{:S(2)}, u32[]{:S(2)}) collective-permute-start(bf16[4,256,1024]{2,1,0:T(8,128)(2,1)} %get-tuple-element.794), channel_id=1, source_target_pairs={{0,16},{16,0},{1,17},{17,1},{2,18},{18,2},{3,19},{19,3},{4,20},{20... | collective-permute-start | bytes 6291464 | tf_op jit(solution)/shard_map/ppermute | solution.py:390
  554.9 30.6 %collective-permute-start.45 = (bf16[4,128,1024]{2,1,0:T(8,128)(2,1)}, bf16[4,128,1024]{2,1,0:T(8,128)(2,1)}, u32[]{:S(2)}, u32[]{:S(2)}) collective-permute-start(bf16[4,128,1024]{2,1,0:T(8,128)(2,1)} %add.532), channel_id=1, source_target_pairs={{0,3},{1,2},{2,1},{3,0},{16,19},{17,18},{18,17},{19,16},{4,7},{5,6... | collective-permute-start | bytes 3145736 | tf_op jit(solution)/shard_map/ppermute | solution.py:386
  585.5 29.3 %collective-permute-start.49 = (bf16[4,256,1024]{2,1,0:T(8,128)(2,1)}, bf16[4,256,1024]{2,1,0:T(8,128)(2,1)S(1)}, u32[]{:S(2)}, u32[]{:S(2)}) collective-permute-start(bf16[4,256,1024]{2,1,0:T(8,128)(2,1)} %add.536), channel_id=1, source_target_pairs={{0,1},{1,0},{2,3},{3,2},{16,18},{17,19},{18,16},{19,17},{4,5},{5,4... | collective-permute-start | bytes 6291464 | tf_op jit(solution)/shard_map/ppermute | solution.py:386
  585.9 26.8 %collective-permute-start.48 = (bf16[2,128,1024]{2,1,0:T(8,128)(2,1)}, bf16[2,128,1024]{2,1,0:T(8,128)(2,1)}, u32[]{:S(2)}, u32[]{:S(2)}) collective-permute-start(bf16[2,128,1024]{2,1,0:T(8,128)(2,1)} %constant_dynamic-slice_fusion.25), channel_id=1, source_target_pairs={{0,8},{4,12},{8,0},{12,4},{1,9},{5,13},{9,1},{13,5},{2,10},{6,14},... | collective-permute-start | bytes 1572872 | tf_op jit(solution)/shard_map/ppermute | solution.py:1135
  615.9 52.9 %collective-permute-start.52 = (bf16[4,128,1024]{2,1,0:T(8,128)(2,1)}, bf16[4,128,1024]{2,1,0:T(8,128)(2,1)}, u32[]{:S(2)}, u32[]{:S(2)}) collective-permute-start(bf16[4,128,1024]{2,1,0:T(8,128)(2,1)} %get-tuple-element.835), channel_id=1, source_target_pairs={{0,16},{16,0},{1,17},{17,1},{2,18},{18,2},{3,19},{19,3},{4,20},{20... | collective-permute-start | bytes 3145736 | tf_op jit(solution)/shard_map/ppermute | solution.py:390
  615.9 53.0 %collective-permute-start.51 = (bf16[4,128,1024]{2,1,0:T(8,128)(2,1)}, bf16[4,128,1024]{2,1,0:T(8,128)(2,1)}, u32[]{:S(2)}, u32[]{:S(2)}) collective-permute-start(bf16[4,128,1024]{2,1,0:T(8,128)(2,1)} %constant_dynamic-slice_fusion.24), channel_id=1, source_target_pairs={{0,16},{16,0},{1,17},{17,1},{2,18},{18,2},{3,19},{19,3},{4,20},{20... | collective-permute-start | bytes 3145736 | tf_op jit(solution)/shard_map/ppermute | solution.py:390
  616.4 50.4 %collective-permute-start.50 = (bf16[2,128,1024]{2,1,0:T(8,128)(2,1)}, bf16[2,128,1024]{2,1,0:T(8,128)(2,1)}, u32[]{:S(2)}, u32[]{:S(2)}) collective-permute-start(bf16[2,128,1024]{2,1,0:T(8,128)(2,1)} %dynamic-slice_add_fusion.5), channel_id=1, source_target_pairs={{0,8},{4,12},{8,0},{12,4},{1,9},{5,13},{9,1},{13,5},{2,10},{6,14},... | collective-permute-start | bytes 1572872 | tf_op jit(solution)/shard_map/ppermute | solution.py:1135
  668.9 39.4 %collective-permute-start.54 = (bf16[2,4,512,1024]{3,2,1,0:T(8,128)(2,1)}, bf16[2,4,512,1024]{3,2,1,0:T(8,128)(2,1)}, u32[]{:S(2)}, u32[]{:S(2)}) collective-permute-start(bf16[2,4,512,1024]{3,2,1,0:T(8,128)(2,1)} %get-tuple-element.851), channel_id=1, source_target_pairs={{0,16},{16,0},{1,17},{17,1},{2,18},{18,2},{3,19},{19,3},{4,20},{20... | collective-permute-start | bytes 25165832 | tf_op jit(solution)/shard_map/ppermute | solution.py:390
  669.0 48.9 %collective-permute-start.53 = (bf16[2,256,1024]{2,1,0:T(8,128)(2,1)S(1)}, bf16[2,256,1024]{2,1,0:T(8,128)(2,1)}, u32[]{:S(2)}, u32[]{:S(2)}) collective-permute-start(bf16[2,256,1024]{2,1,0:T(8,128)(2,1)S(1)} %maximum_select_fusion.3), channel_id=1, source_target_pairs={{0,4},{4,0},{8,12},{12,8},{1,5},{5,1},{9,13},{13,9},{2,6},{6,2},{1... | collective-permute-start | bytes 3145736 | tf_op jit(solution)/shard_map/ppermute | solution.py:1135
  676.5 31.6 %collective-permute-start.55 = (bf16[4,64,1024]{2,1,0:T(8,128)(2,1)S(1)}, bf16[4,64,1024]{2,1,0:T(8,128)(2,1)S(1)}, u32[]{:S(2)}, u32[]{:S(2)}) collective-permute-start(bf16[4,64,1024]{2,1,0:T(8,128)(2,1)S(1)} %constant_dynamic-slice_fusion.23), channel_id=1, source_target_pairs={{0,4},{4,0},{8,12},{12,8},{1,5},{5,1},{9,13},{13,9},{2,6},{6,2},{1... | collective-permute-start | bytes 1572872 | tf_op jit(solution)/shard_map/ppermute | solution.py:1135
  717.8 40.0 %collective-permute-start.57 = (bf16[2,1024,256]{2,1,0:T(8,128)(2,1)}, bf16[2,1024,256]{2,1,0:T(8,128)(2,1)S(1)}, u32[]{:S(2)}, u32[]{:S(2)}) collective-permute-start(bf16[2,1024,256]{2,1,0:T(8,128)(2,1)} %get-tuple-element.867), channel_id=1, source_target_pairs={{0,16},{16,0},{1,17},{17,1},{2,18},{18,2},{3,19},{19,3},{4,20},{20... | collective-permute-start | bytes 3145736 | tf_op jit(solution)/shard_map/ppermute | solution.py:390
  717.9 39.9 %collective-permute-start.56 = (bf16[4,32,1024]{2,1,0:T(8,128)(2,1)S(1)}, bf16[4,32,1024]{2,1,0:T(8,128)(2,1)S(1)}, u32[]{:S(2)}, u32[]{:S(2)}) collective-permute-start(bf16[4,32,1024]{2,1,0:T(8,128)(2,1)S(1)} %constant_dynamic-slice_fusion.22), channel_id=1, source_target_pairs={{0,8},{4,12},{8,0},{12,4},{1,9},{5,13},{9,1},{13,5},{2,10},{6,14},... | collective-permute-start | bytes 786440 | tf_op jit(solution)/shard_map/ppermute | solution.py:1135
  718.6 50.9 %collective-permute-start.58 = (bf16[2,512,1024]{2,1,0:T(8,128)(2,1)}, bf16[2,512,1024]{2,1,0:T(8,128)(2,1)}, u32[]{:S(2)}, u32[]{:S(2)}) collective-permute-start(bf16[2,512,1024]{2,1,0:T(8,128)(2,1)} %bitcast.388), channel_id=1, source_target_pairs={{0,2},{1,3},{2,0},{3,1},{16,17},{17,16},{18,19},{19,18},{4,6},{5,7... | collective-permute-start | bytes 6291464 | tf_op jit(solution)/shard_map/ppermute | solution.py:386
  720.6 49.0 %collective-permute-start.59 = (bf16[2,512,1024]{2,1,0:T(8,128)(2,1)}, bf16[2,512,1024]{2,1,0:T(8,128)(2,1)}, u32[]{:S(2)}, u32[]{:S(2)}) collective-permute-start(bf16[2,512,1024]{2,1,0:T(8,128)(2,1)} %get-tuple-element.880), channel_id=1, source_target_pairs={{0,1},{1,0},{2,3},{3,2},{16,18},{17,19},{18,16},{19,17},{4,5},{5,4... | collective-permute-start | bytes 6291464 | tf_op jit(solution)/shard_map/ppermute | solution.py:386
  773.6 26.4 %collective-permute-start.62 = (bf16[2,512,1024]{2,1,0:T(8,128)(2,1)}, bf16[2,512,1024]{2,1,0:T(8,128)(2,1)}, u32[]{:S(2)}, u32[]{:S(2)}) collective-permute-start(bf16[2,512,1024]{2,1,0:T(8,128)(2,1)} %add.549), channel_id=1, source_target_pairs={{0,1},{1,0},{2,3},{3,2},{16,18},{17,19},{18,16},{19,17},{4,5},{5,4... | collective-permute-start | bytes 6291464 | tf_op jit(solution)/shard_map/ppermute | solution.py:386
  804.7 32.6 %collective-permute-start.69 = (bf16[4,256,1024]{2,1,0:T(8,128)(2,1)}, bf16[4,256,1024]{2,1,0:T(8,128)(2,1)}, u32[]{:S(2)}, u32[]{:S(2)}) collective-permute-start(bf16[4,256,1024]{2,1,0:T(8,128)(2,1)} %get-tuple-element.935), channel_id=1, source_target_pairs={{0,16},{16,0},{1,17},{17,1},{2,18},{18,2},{3,19},{19,3},{4,20},{20... | collective-permute-start | bytes 6291464 | tf_op jit(solution)/shard_map/ppermute | solution.py:390
  804.8 32.4 %collective-permute-start.68 = (bf16[4,128,1024]{2,1,0:T(8,128)(2,1)}, bf16[4,128,1024]{2,1,0:T(8,128)(2,1)}, u32[]{:S(2)}, u32[]{:S(2)}) collective-permute-start(bf16[4,128,1024]{2,1,0:T(8,128)(2,1)} %add.552), channel_id=1, source_target_pairs={{0,3},{1,2},{2,1},{3,0},{16,19},{17,18},{18,17},{19,16},{4,7},{5,6... | collective-permute-start | bytes 3145736 | tf_op jit(solution)/shard_map/ppermute | solution.py:386
  806.4 30.8 %collective-permute-start.67 = (bf16[4,128,1024]{2,1,0:T(8,128)(2,1)S(1)}, bf16[4,128,1024]{2,1,0:T(8,128)(2,1)}, u32[]{:S(2)}, u32[]{:S(2)}) collective-permute-start(bf16[4,128,1024]{2,1,0:T(8,128)(2,1)S(1)} %maximum_select_fusion.4), channel_id=1, source_target_pairs={{0,16},{1,17},{2,18},{3,19},{4,20},{5,21},{6,22},{7,23},{8,24},{9,... | collective-permute-start | bytes 3145736 | tf_op jit(solution)/shard_map/ppermute | solution.py:1320
  809.5 27.8 %collective-permute-start.66 = (bf16[2,256,1024]{2,1,0:T(8,128)(2,1)}, bf16[2,256,1024]{2,1,0:T(8,128)(2,1)}, u32[]{:S(2)}, u32[]{:S(2)}) collective-permute-start(bf16[2,256,1024]{2,1,0:T(8,128)(2,1)} %constant_dynamic-slice_fusion.21), channel_id=1, source_target_pairs={{0,4},{4,0},{8,12},{12,8},{1,5},{5,1},{9,13},{13,9},{2,6},{6,2},{1... | collective-permute-start | bytes 3145736 | tf_op jit(solution)/shard_map/ppermute | solution.py:1135
  849.1 26.2 %collective-permute-start.73 = (bf16[4,256,1024]{2,1,0:T(8,128)(2,1)}, bf16[4,256,1024]{2,1,0:T(8,128)(2,1)S(1)}, u32[]{:S(2)}, u32[]{:S(2)}) collective-permute-start(bf16[4,256,1024]{2,1,0:T(8,128)(2,1)} %add.554), channel_id=1, source_target_pairs={{0,1},{1,0},{2,3},{3,2},{16,18},{17,19},{18,16},{19,17},{4,5},{5,4... | collective-permute-start | bytes 6291464 | tf_op jit(solution)/shard_map/ppermute | solution.py:386
  852.4 26.9 %collective-permute-start.72 = (bf16[2,128,1024]{2,1,0:T(8,128)(2,1)}, bf16[2,128,1024]{2,1,0:T(8,128)(2,1)}, u32[]{:S(2)}, u32[]{:S(2)}) collective-permute-start(bf16[2,128,1024]{2,1,0:T(8,128)(2,1)} %constant_dynamic-slice_fusion.20), channel_id=1, source_target_pairs={{0,8},{4,12},{8,0},{12,4},{1,9},{5,13},{9,1},{13,5},{2,10},{6,14},... | collective-permute-start | bytes 1572872 | tf_op jit(solution)/shard_map/ppermute | solution.py:1135
  887.0 26.2 %collective-permute-start.78 = (bf16[2,128,1024]{2,1,0:T(8,128)(2,1)}, bf16[2,128,1024]{2,1,0:T(8,128)(2,1)}, u32[]{:S(2)}, u32[]{:S(2)}) collective-permute-start(bf16[2,128,1024]{2,1,0:T(8,128)(2,1)} %dynamic-slice_add_fusion.3), channel_id=1, source_target_pairs={{0,8},{4,12},{8,0},{12,4},{1,9},{5,13},{9,1},{13,5},{2,10},{6,14},... | collective-permute-start | bytes 1572872 | tf_op jit(solution)/shard_map/ppermute | solution.py:1135
  893.7 31.0 %collective-permute-start.82 = (bf16[512,1024]{1,0:T(8,128)(2,1)S(1)}, bf16[512,1024]{1,0:T(8,128)(2,1)S(1)}, u32[]{:S(2)}, u32[]{:S(2)}) collective-permute-start(bf16[512,1024]{1,0:T(8,128)(2,1)S(1)} %get-tuple-element.999), channel_id=1, source_target_pairs={{1,0},{16,1},{19,2},{2,3},{5,4},{20,5},{23,6},{6,7},{9,8},{24,9},{... | collective-permute-start | bytes 3145736 | tf_op jit(solution)/shard_map/ppermute | solution.py:386
  895.2 29.6 %collective-permute-start.81 = (bf16[512,1024]{1,0:T(8,128)(2,1)S(1)}, bf16[512,1024]{1,0:T(8,128)(2,1)S(1)}, u32[]{:S(2)}, u32[]{:S(2)}) collective-permute-start(bf16[512,1024]{1,0:T(8,128)(2,1)S(1)} %get-tuple-element.998), channel_id=1, source_target_pairs={{3,0},{18,1},{17,2},{0,3},{7,4},{22,5},{21,6},{4,7},{11,8},{26,9},... | collective-permute-start | bytes 3145736 | tf_op jit(solution)/shard_map/ppermute | solution.py:386
  898.5 25.9 %collective-permute-start.79 = (f32[2,12,1024]{2,1,0:T(8,128)S(1)}, f32[2,12,1024]{2,1,0:T(8,128)S(1)}, u32[]{:S(2)}, u32[]{:S(2)}) collective-permute-start(f32[2,12,1024]{2,1,0:T(8,128)S(1)} %fusion.31), channel_id=1, source_target_pairs={{0,1},{1,0},{2,3},{3,2},{4,5},{5,4},{6,7},{7,6},{8,9},{9,8},{10,11... | collective-permute-start | bytes 294920 | tf_op jit(solution)/shard_map/ppermute | solution.py:1135
  924.7 31.6 %collective-permute-start.83 = (bf16[2,256,1024]{2,1,0:T(8,128)(2,1)S(1)}, bf16[2,256,1024]{2,1,0:T(8,128)(2,1)S(1)}, u32[]{:S(2)}, u32[]{:S(2)}) collective-permute-start(bf16[2,256,1024]{2,1,0:T(8,128)(2,1)S(1)} %maximum_select_fusion.5), channel_id=1, source_target_pairs={{0,4},{4,0},{8,12},{12,8},{1,5},{5,1},{9,13},{13,9},{2,6},{6,2},{1... | collective-permute-start | bytes 3145736 | tf_op jit(solution)/shard_map/ppermute | solution.py:1135
  925.0 32.1 %collective-permute-start.86 = (bf16[512,1024]{1,0:T(8,128)(2,1)S(1)}, bf16[512,1024]{1,0:T(8,128)(2,1)}, u32[]{:S(2)}, u32[]{:S(2)}) collective-permute-start(bf16[512,1024]{1,0:T(8,128)(2,1)S(1)} %slice_select_fusion), channel_id=1, source_target_pairs={{2,0},{19,1},{16,2},{1,3},{6,4},{23,5},{20,6},{5,7},{10,8},{27,9},... | collective-permute-start | bytes 3145736 | tf_op jit(solution)/shard_map/ppermute | solution.py:386
  926.3 30.0 %collective-permute-start.85 = (bf16[4,32,1024]{2,1,0:T(8,128)(2,1)S(1)}, bf16[4,32,1024]{2,1,0:T(8,128)(2,1)S(1)}, u32[]{:S(2)}, u32[]{:S(2)}) collective-permute-start(bf16[4,32,1024]{2,1,0:T(8,128)(2,1)S(1)} %constant_dynamic-slice_fusion.1), channel_id=1, source_target_pairs={{0,8},{4,12},{8,0},{12,4},{1,9},{5,13},{9,1},{13,5},{2,10},{6,14},... | collective-permute-start | bytes 786440 | tf_op jit(solution)/shard_map/ppermute | solution.py:1135
  927.8 28.6 %collective-permute-start.84 = (f32[2,12,1024]{2,1,0:T(8,128)S(1)}, f32[2,12,1024]{2,1,0:T(8,128)S(1)}, u32[]{:S(2)}, u32[]{:S(2)}) collective-permute-start(f32[2,12,1024]{2,1,0:T(8,128)S(1)} %fusion.58), channel_id=1, source_target_pairs={{0,2},{1,3},{2,0},{3,1},{4,6},{5,7},{6,4},{7,5},{8,10},{9,11},{10,... | collective-permute-start | bytes 294920 | tf_op jit(solution)/shard_map/ppermute | solution.py:1135
  (105 other events, 1100.4 us)
